TPU v7x, 32 devices: a whole 2x2x4 slice. The times are simulated.
32 devices in a mesh: groups: 2 (over x), tier: 16 (over z, y, core).
Axes of the slice: x: 2, y: 2, z: 4, core: 2. Of those that a mesh axis runs over, the one named last changes fastest.
Arguments:
- rho: float32 [256, 2, 256, 256], P(('groups', 'tier')), parts along dimension 0, may hold values from -6 to 6
- hamiltonian: float32 [256, 256], replicated, may hold values from -0.375 to 0.375
- couplings: float32 [4, 256, 256], replicated, may hold values from -0.375 to 0.375
- bath_coef: float32 [8, 2], P('groups'), parts along dimension 0, may hold values from 0.3 to 1.5
- damping: float32 [256], P(('groups', 'tier')), parts along dimension 0, may hold values from 0.2 to 3
- match_edges: int32 [16, 4, 1, 5], P('tier'), may hold values from 0 to 7, as said below
- left_rows: int32 [16, 6, 5], replicated, may hold values from 0 to 127, as said below
- left_count: int32 [16], replicated, may hold values from 1 to 6, as said below
Outputs:
- rho_next: float32 [256, 2, 256, 256], P(('groups', 'tier')), parts along dimension 0
There are 2 independent parts, one for each index of `groups`. A program takes and returns all parts, laid end to end along the dimension named above; an argument that names none is the same for every part. Nothing has to cross between parts.
Inputs may be any that keep to these rules, and one draw needn't show every extreme that they name: match_edges[b, c, j] = (target slot, partner slot, mode, lower flag 0 or 1, occupation 1 to 3); the row (b XOR 2^c, c, j) describes the same edge from the partner's side: its target slot is this row's partner slot and the reverse, same mode and occupation, opposite lower flag. left_rows[b, j] = (target slot, source matrix index, mode, lower flag 0 or 1, occupation 1 to 3); the source's block lies at cyclic block distance 1 to 4 from b, and the rows of one block name distinct source blocks. Only the first left_count[b] rows of block b are live; some block has exactly 6.
All inputs are finite; a program needn't handle non-finite values.
Results may differ from a plain program's by a relative error of at most 0.00005.
Values sent between devices are 32-bit elements; how exact they have to be, the bound alone decides.
No kernel may reach another device: no remote copies, remote signals or barrier semaphores. Data moves between devices by JAX's collectives and lax.ppermute only.
A program may use at most 128 MiB of HBM per device.

v0:
```python
import functools

import jax
import jax.numpy as jnp
from jax import lax
from jax.experimental import pallas as pl
from jax.experimental.pallas import tpu as pltpu
from jax.sharding import PartitionSpec as P

REACH = 4
STEP = 0.1
F32, BF16 = jnp.float32, jnp.bfloat16
SMEM = pl.BlockSpec(memory_space=pltpu.SMEM)
VMEM = pl.BlockSpec(memory_space=pltpu.VMEM)
ANY = pl.BlockSpec(memory_space=pl.ANY)


class Exchange:
    def __init__(self, kind, step, size, colour=None, listed=True):
        self.kind, self.step, self.size, self.colour, self.listed = kind, step, size, colour, listed

    def peer(self, index, outgoing):
        size, step = self.size, self.step
        if self.kind == "swap":
            return index ^ step
        if self.kind == "other":
            lower = (index & step) == 0
            if isinstance(index, int):
                return (index + (-step if lower else step)) % size
            return lax.rem(index + jnp.where(lower, size - step, step), size)
        move = step if outgoing else size - step
        if isinstance(index, int):
            return (index + move) % size
        return lax.rem(index + move, size)

    def permute(self, value):
        return lax.ppermute(value, "tier", [(i, self.peer(i, True)) for i in range(self.size)])


def exchanges(size, colours):
    near, far = [], []
    for distance in range(1, REACH + 1):
        colour = distance.bit_length() - 1
        if distance == 1 << colour and colour < colours:
            group = [
                Exchange("swap", distance, size, colour),
                Exchange("other", distance, size),
            ]
        else:
            group = [Exchange("shift", distance, size), Exchange("shift", size - distance, size)]
        (near if distance < REACH else far).extend(group)
    for colour in range(colours):
        if 1 << colour > REACH:
            far.append(Exchange("swap", 1 << colour, size, colour, listed=False))
    return near + far


def payload(exchange, pairs):
    return (pairs if exchange.colour is not None else 0) + (1 if exchange.listed else 0)


def split(value):
    high = value.astype(BF16)
    return high, (value - high.astype(F32)).astype(BF16)


def product(left, right):
    dot = functools.partial(jnp.dot, preferred_element_type=F32)
    return dot(left[0], right[0]) + (dot(left[0], right[1]) + dot(left[1], right[0]))


def outgoing_slots(exchange, me, mats, left_ref, count_ref, match_ref):
    slots = []
    if exchange.colour is not None:
        for j in range(match_ref.shape[2]):
            slots.append(match_ref[0, exchange.colour, j, 0])
    if exchange.listed:
        peer = exchange.peer(me, True)
        slot = jnp.int32(0)
        for j in range(left_ref.shape[1]):
            source = left_ref[peer, j, 1]
            hit = (j < count_ref[peer]) & (lax.div(source, mats) == me)
            slot = jnp.where(hit, lax.rem(source, mats), slot)
        slots.append(slot)
    return slots


def incoming_rows(exchange, me, mats, left_ref, count_ref, match_ref, left_root, match_root, bath_ref):
    rows = []

    def row(live, target, mode, flag, root):
        lower = flag == 1
        a = jnp.where(lower, jnp.float32(1), bath_ref[mode, 0])
        b = jnp.where(lower, jnp.float32(0), bath_ref[mode, 1])
        rows.append((live, target, mode, a * root, b * root))

    if exchange.colour is not None:
        c = exchange.colour
        for j in range(match_ref.shape[2]):
            row(None, match_ref[0, c, j, 0], match_ref[0, c, j, 2], match_ref[0, c, j, 3], match_root[c, j])
    if exchange.listed:
        peer = exchange.peer(me, False)
        found = [jnp.int32(0)] * 4 + [jnp.float32(0)]
        for j in range(left_ref.shape[1]):
            hit = (j < count_ref[me]) & (lax.div(left_ref[me, j, 1], mats) == peer)
            here = [1, left_ref[me, j, 0], left_ref[me, j, 2], left_ref[me, j, 3], left_root[me, j]]
            found = [jnp.where(hit, new, old) for new, old in zip(here, found)]
        row(found[0] == 1, found[1], found[2], found[3], found[4])
    return rows


def pack_kernel(plan, mats, me_ref, left_ref, count_ref, match_ref, source, *rest):
    sends, sems = rest[:-1], rest[-1]
    pack(plan, mats, me_ref, left_ref, count_ref, match_ref, source, sends, sems)


def pack(plan, mats, me_ref, left_ref, count_ref, match_ref, source, sends, sems):
    copies = []
    for exchange, send in zip(plan, sends):
        slots = outgoing_slots(exchange, me_ref[0], mats, left_ref, count_ref, match_ref)
        for place, slot in enumerate(slots):
            copies.append(pltpu.make_async_copy(source.at[slot], send.at[place], sems.at[len(copies)]))
            copies[-1].start()
    for copy in copies:
        copy.wait()


def commutator(density, hamiltonian):
    parts = []
    for part in (density[0], density[1]):
        halves = split(part)
        parts.append(product(hamiltonian, halves) - product(halves, hamiltonian))
    return parts[1], -parts[0]


def first_local_kernel(damping_ref, hamiltonian_ref, rho_ref, out_ref):
    decay = damping_ref[pl.program_id(0)]
    density = (rho_ref[0, 0], rho_ref[0, 1])
    turned = commutator(density, split(hamiltonian_ref[...]))
    for part in range(2):
        out_ref[0, part] = turned[part] - decay * density[part]


def second_local_kernel(damping_ref, hamiltonian_ref, first_ref, rho_ref, out_ref):
    decay = damping_ref[pl.program_id(0)]
    density = (first_ref[0, 0], first_ref[0, 1])
    turned = commutator(density, split(hamiltonian_ref[...]))
    for part in range(2):
        slope = turned[part] - decay * density[part]
        out_ref[0, part] = rho_ref[0, part] + STEP * density[part] + (0.5 * STEP * STEP) * slope


def local_call(kernel, damping, hamiltonian, *densities):
    mats, _, order, _ = densities[0].shape
    block = pl.BlockSpec((1, 2, order, order), lambda n: (n, 0, 0, 0))
    return pl.pallas_call(
        kernel,
        grid=(mats,),
        in_specs=[SMEM, pl.BlockSpec((order, order), lambda n: (0, 0))] + [block] * len(densities),
        out_specs=block,
        out_shape=jax.ShapeDtypeStruct(densities[0].shape, F32),
        compiler_params=pltpu.CompilerParams(vmem_limit_bytes=32 * 1024 * 1024),
        cost_estimate=pl.CostEstimate(
            flops=mats * 24 * order**3, bytes_accessed=mats * 16 * order**2 * (1 + len(densities)), transcendentals=0
        ),
    )(damping, hamiltonian, *densities)


def rows_kernel(plan, packs, scale, refs_in, *refs):
    me_ref, left_ref, count_ref, match_ref, left_root, match_root, bath_ref = refs[:7]
    couplings_ref = refs[7]
    arrivals = refs[8 : 8 + len(plan)]
    acc_in = refs[8 + len(plan)]
    rest = refs[9 + len(plan) :]
    acc_out, sends = rest[0], rest[1 : 1 + len(packs)]
    acc, landed, acc_sems, land_sems, send_sems = rest[1 + len(packs) :]
    mats = acc.shape[0]
    loads = [pltpu.make_async_copy(acc_in.at[n], acc.at[n], acc_sems.at[n]) for n in range(mats)]
    rows, lands = [], []
    for exchange, arrival in zip(plan, arrivals):
        found = incoming_rows(
            exchange, me_ref[0], mats, left_ref, count_ref, match_ref, left_root, match_root, bath_ref
        )
        for place, row in enumerate(found):
            at = len(rows)
            lands.append(pltpu.make_async_copy(arrival.at[place], landed.at[at], land_sems.at[at]))
            rows.append(row)
    for land in lands:
        land.start()
    for load in loads:
        load.start()
    for load in loads:
        load.wait()
    for at, (live, target, mode, a, b) in enumerate(rows):
        lands[at].wait()

        def add(at=at, target=target, mode=mode, a=a, b=b):
            coupling = split(couplings_ref[mode])
            real, imag = split(landed[at, 0]), split(landed[at, 1])
            left_re, right_re = product(coupling, real), product(real, coupling)
            left_im, right_im = product(coupling, imag), product(imag, coupling)
            edge_re = a * (left_re - right_re) - b * (left_im + right_im)
            edge_im = a * (left_im - right_im) + b * (left_re + right_re)
            acc[target, 0] += scale * edge_im
            acc[target, 1] -= scale * edge_re

        if live is None:
            add()
        else:
            pl.when(live)(add)
    stores = [pltpu.make_async_copy(acc.at[n], acc_out.at[n], acc_sems.at[n]) for n in range(mats)]
    for store in stores:
        store.start()
    if packs:
        pack(packs, mats, me_ref, left_ref, count_ref, match_ref, acc, sends, send_sems)
    for store in stores:
        store.wait()


def rows_call(plan, packs, pairs, scale, tables, couplings, arrivals, acc):
    mats, _, order, _ = acc.shape
    count = sum(payload(e, pairs) for e in plan)
    sent = sum(payload(e, pairs) for e in packs)
    shapes = [jax.ShapeDtypeStruct(acc.shape, F32)]
    shapes += [jax.ShapeDtypeStruct((payload(e, pairs), 2, order, order), F32) for e in packs]
    return pl.pallas_call(
        functools.partial(rows_kernel, plan, packs, scale, None),
        in_specs=[SMEM] * 7 + [VMEM] + [ANY] * (len(plan) + 1),
        out_specs=[ANY] * len(shapes),
        out_shape=shapes,
        input_output_aliases={8 + len(plan): 0},
        scratch_shapes=[
            pltpu.VMEM((mats, 2, order, order), F32),
            pltpu.VMEM((count, 2, order, order), F32),
            pltpu.SemaphoreType.DMA((mats,)),
            pltpu.SemaphoreType.DMA((count,)),
            pltpu.SemaphoreType.DMA((max(sent, 1),)),
        ],
        compiler_params=pltpu.CompilerParams(vmem_limit_bytes=32 * 1024 * 1024),
        cost_estimate=pl.CostEstimate(
            flops=count * 24 * order**3, bytes_accessed=(count + 2 * mats + sent) * 8 * order**2, transcendentals=0
        ),
    )(*tables, couplings, *arrivals, acc)


def pack_call(plan, pairs, tables, source):
    mats, _, order, _ = source.shape
    sent = sum(payload(e, pairs) for e in plan)
    return pl.pallas_call(
        functools.partial(pack_kernel, plan, mats),
        in_specs=[SMEM] * 4 + [ANY],
        out_specs=[ANY] * len(plan),
        out_shape=[jax.ShapeDtypeStruct((payload(e, pairs), 2, order, order), F32) for e in plan],
        scratch_shapes=[pltpu.SemaphoreType.DMA((sent,))],
        cost_estimate=pl.CostEstimate(flops=0, bytes_accessed=sent * 16 * order**2, transcendentals=0),
    )(*tables[:4], source)


def body(rho, hamiltonian, couplings, bath_coef, damping, match_edges, left_rows, left_count):
    colours, pairs = match_edges.shape[1:3]
    plan = exchanges(lax.axis_size("tier"), colours)
    me = lax.axis_index("tier").astype(jnp.int32)[None]
    left_root = jnp.sqrt(left_rows[:, :, 4].astype(F32))
    match_root = jnp.sqrt(match_edges[0, :, :, 4].astype(F32))
    tables = (me, left_rows, left_count, match_edges, left_root, match_root, bath_coef)

    cuts = [0]
    for distance in (2, REACH - 1):
        cuts.append(max(i + 1 for i, e in enumerate(plan) if e.step in (distance, e.size - distance)))
    cuts.append(len(plan))
    groups = [slice(a, b) for a, b in zip(cuts, cuts[1:]) if a < b]

    def gather(sends, acc, scale, packs):
        arrived = [e.permute(s) for e, s in zip(plan, sends)]
        for group in groups:
            last = group is groups[-1]
            got = rows_call(
                plan[group], packs if last else [], pairs, scale, tables, couplings, arrived[group], acc
            )
            acc = got[0]
        return acc, got[1:]

    sends = pack_call(plan, pairs, tables, rho)
    first, sends = gather(sends, local_call(first_local_kernel, damping, hamiltonian, rho), 1.0, plan)
    base = local_call(second_local_kernel, damping, hamiltonian, first, rho)
    return gather(sends, base, 0.5 * STEP * STEP, [])[0]


def solution(mesh):
    placed = (
        P(("groups", "tier"), None, None, None),
        P(),
        P(),
        P("groups", None),
        P(("groups", "tier")),
        P("tier", None, None, None),
        P(),
        P(),
    )
    return jax.shard_map(
        body,
        mesh=mesh,
        in_specs=placed,
        out_specs=P(("groups", "tier"), None, None, None),
        check_vma=False,
    )
```

profile of v0, /device:TPU:13, one launch (start us, length us, event | category | flops | bytes accessed | tf_op | source)
XLA Modules:
  0.0 433.6 jit_solution(18225221154450598248)
XLA Ops:
  1.5 193.6 %shard_map.82 = (f32[2,2,256,256]{3,2,1,0:T(8,128)}, f32[1,2,256,256]{3,2,1,0:T(8,128)}, f32[2,2,256,256]{3,2,1,0:T(8,128)}, f32[1,2,256,256]{3,2,1,0:T(8,128)},...) custom-call(s32[1]{0:T(128)} %bitcast.me_ref.refs_0_, ...), custom_call_target="tpu_custom_call" | custom-call | bytes 12582912 | tf_op jit(solution)/shard_map/pallas_call | solution.py:249
  196.1 2.5 collective-permute-start.6
  199.0 2.3 copy-done.5
  201.3 5.4 %shard_map.83.refs_12_ = f32[8,2,256,256]{3,2,1,0:T(8,128)S(1)} custom-call(f32[8]{0:T(128)S(1)} %copy-done.15, f32[256,256]{1,0:T(8,128)S(1)} %copy-done.12, f32[8,2,256,256]{3,2,1,0:T(8,128)S(1)} %copy-done.5), custom_call_target="tpu_custom_call" | custom-call | flops 3221225472 | bytes 16777216 | tf_op jit(solution)/shard_map/pallas_call | solution.py:156
  210.8 40.5 %collective-permute-start.3 = (f32[1,2,256,256]{3,2,1,0:T(8,128)}, f32[1,2,256,256]{3,2,1,0:T(8,128)}, u32[]{:S(2)}, u32[]{:S(2)}) collective-permute-start(f32[1,2,256,256]{3,2,1,0:T(8,128)} %get-tuple-element.27), channel_id=1, source_target_pairs={{0,3},{1,4},{2,5},{3,6},{4,7},{5,8},{6,9},{7,10},{8,11},{9,12},{10... | collective-permute-start | bytes 1572872 | tf_op jit(solution)/shard_map/ppermute | solution.py:37
  255.4 2.2 copy-done.1
  259.7 4.8 %shard_map.84.refs_10_ = f32[8,2,256,256]{3,2,1,0:T(8,128)S(1)} custom-call(s32[1]{0:T(128)} %bitcast.me_ref.refs_0_, s32[16,6,5]{2,1,0:T(8,128)S(1)} %copy-done.7, s32[16]{0:T(128)S(1)} %copy-done.14, s32[1,4,1,5]{3,2,1,0:T(1,128)S(1)} %copy-done.13, f32[16,6]{1,0:T(8,128)S(1)} %copy.62.refs_4_, ...), custom_call_target="tpu_custom_call", output_to_operand_aliasing={{}: (12, {})} | custom-call | flops 2415919104 | bytes 11534336 | tf_op jit(solution)/shard_map/pallas_call | solution.py:226
  264.5 26.8 %collective-permute-done.3.refs_8_ = f32[1,2,256,256]{3,2,1,0:T(8,128)} collective-permute-done((f32[1,2,256,256]{3,2,1,0:T(8,128)}, f32[1,2,256,256]{3,2,1,0:T(8,128)}, u32[]{:S(2)}, u32[]{:S(2)}) %collective-permute-start.3) | collective-permute-done | bytes 524320 | tf_op jit(solution)/shard_map/ppermute | solution.py:37
  291.2 7.2 %collective-permute-done.4.refs_9_ = f32[1,2,256,256]{3,2,1,0:T(8,128)} collective-permute-done((f32[1,2,256,256]{3,2,1,0:T(8,128)}, f32[1,2,256,256]{3,2,1,0:T(8,128)}, u32[]{:S(2)}, u32[]{:S(2)}) %collective-permute-start.4) | collective-permute-done | bytes 524320 | tf_op jit(solution)/shard_map/ppermute | solution.py:37
  298.4 4.0 shard_map.85.refs_11_
  302.6 10.7 %collective-permute-done.2.refs_10_ = f32[1,2,256,256]{3,2,1,0:T(8,128)S(1)} collective-permute-done((f32[1,2,256,256]{3,2,1,0:T(8,128)}, f32[1,2,256,256]{3,2,1,0:T(8,128)S(1)}, u32[]{:S(2)}, u32[]{:S(2)}) %collective-permute-start.2) | collective-permute-done | bytes 524320 | tf_op jit(solution)/shard_map/ppermute | solution.py:37
  313.3 4.9 %shard_map.86 = (f32[8,2,256,256]{3,2,1,0:T(8,128)S(1)}, f32[2,2,256,256]{3,2,1,0:T(8,128)S(1)}, f32[1,2,256,256]{3,2,1,0:T(8,128)S(1)}, f32[2,2,256,256]{3,2,1,...) custom-call(s32[1]{0:T(128)} %bitcast.me_ref.refs_0_, ...), custom_call_target="tpu_custom_call", output_to_operand_aliasing={{0}: (11, {})} | custom-call | flops 1610612736 | bytes 16777216 | tf_op jit(solution)/shard_map/pallas_call | solution.py:226
  320.7 2.9 collective-permute-start.15
  324.7 10.1 %collective-permute-done.15.refs_9_ = f32[1,2,256,256]{3,2,1,0:T(8,128)S(1)} collective-permute-done((f32[1,2,256,256]{3,2,1,0:T(8,128)S(1)}, f32[1,2,256,256]{3,2,1,0:T(8,128)S(1)}, u32[]{:S(2)}, u32[]{:S(2)}) %collective-permute-start.15) | collective-permute-done | bytes 524320 | tf_op jit(solution)/shard_map/ppermute | solution.py:37
  336.9 4.0 collective-permute-done.17.refs_11_
  340.9 9.6 %collective-permute-start.11 = (f32[1,2,256,256]{3,2,1,0:T(8,128)S(1)}, f32[1,2,256,256]{3,2,1,0:T(8,128)S(1)}, u32[]{:S(2)}, u32[]{:S(2)}) collective-permute-start(f32[1,2,256,256]{3,2,1,0:T(8,128)S(1)} %get-tuple-element.35), channel_id=1, source_target_pairs={{0,8},{1,9},{2,10},{3,11},{4,12},{5,13},{6,14},{7,15},{8,0},{9,1},... | collective-permute-start | bytes 1572872 | tf_op jit(solution)/shard_map/ppermute | solution.py:37
  350.5 28.7 %collective-permute-start.12 = (f32[1,2,256,256]{3,2,1,0:T(8,128)S(1)}, f32[1,2,256,256]{3,2,1,0:T(8,128)S(1)}, u32[]{:S(2)}, u32[]{:S(2)}) collective-permute-start(f32[1,2,256,256]{3,2,1,0:T(8,128)S(1)} %get-tuple-element.36), channel_id=1, source_target_pairs={{0,3},{1,4},{2,5},{3,6},{4,7},{5,8},{6,9},{7,10},{8,11},{9,12},{10... | collective-permute-start | bytes 1572872 | tf_op jit(solution)/shard_map/ppermute | solution.py:37
  379.3 2.2 copy-done.3
  381.4 6.7 %shard_map.87.refs_12_ = f32[8,2,256,256]{3,2,1,0:T(8,128)} custom-call(f32[8]{0:T(128)S(1)} %copy-done.15, f32[256,256]{1,0:T(8,128)S(1)} %copy-done.12, f32[8,2,256,256]{3,2,1,0:T(8,128)S(1)} %copy-done.3, f32[8,2,256,256]{3,2,1,0:T(8,128)S(1)} %copy-done.6), custom_call_target="tpu_custom_call" | custom-call | flops 3221225472 | bytes 25165824 | tf_op jit(solution)/shard_map/pallas_call | solution.py:156
  388.2 8.5 %shard_map.88.refs_10_ = f32[8,2,256,256]{3,2,1,0:T(8,128)} custom-call(s32[1]{0:T(128)} %bitcast.me_ref.refs_0_, s32[16,6,5]{2,1,0:T(8,128)S(1)} %copy-done.7, s32[16]{0:T(128)S(1)} %copy-done.14, s32[1,4,1,5]{3,2,1,0:T(1,128)S(1)} %copy-done.13, f32[16,6]{1,0:T(8,128)S(1)} %copy.62.refs_4_, f32[4,1]{1,0:T(4,128)S(1)} %bitcast.7, ...), custom_call_target="tpu_custom_call", output_to_operand_aliasing={{}: (12, {})} | custom-call | flops 2415919104 | bytes 11534336 | tf_op jit(solution)/shard_map/pallas_call | solution.py:226
  396.7 4.2 collective-permute-done.12.refs_8_
  400.9 18.1 %collective-permute-done.13.refs_9_ = f32[1,2,256,256]{3,2,1,0:T(8,128)S(1)} collective-permute-done((f32[1,2,256,256]{3,2,1,0:T(8,128)S(1)}, f32[1,2,256,256]{3,2,1,0:T(8,128)S(1)}, u32[]{:S(2)}, u32[]{:S(2)}) %collective-permute-start.13) | collective-permute-done | bytes 524320 | tf_op jit(solution)/shard_map/ppermute | solution.py:37
  419.0 6.9 %shard_map.89.refs_11_ = f32[8,2,256,256]{3,2,1,0:T(8,128)} custom-call(s32[1]{0:T(128)} %bitcast.me_ref.refs_0_, s32[16,6,5]{2,1,0:T(8,128)S(1)} %copy-done.7, s32[16]{0:T(128)S(1)} %copy-done.14, s32[1,4,1,5]{3,2,1,0:T(1,128)S(1)} %copy-done.13, f32[16,6]{1,0:T(8,128)S(1)} %copy.62.refs_4_, f32[4,1]{1,0:T(4,128)S(1)} %bitcast.8, ...), custom_call_target="tpu_custom_call", output_to_operand_aliasing={{}: (10, {})} | custom-call | flops 805306368 | bytes 9437184 | tf_op jit(solution)/shard_map/pallas_call | solution.py:226
  425.9 7.6 %shard_map.90 = f32[8,2,256,256]{3,2,1,0:T(8,128)} custom-call(s32[1]{0:T(128)} %bitcast.me_ref.refs_0_, s32[16,6,5]{2,1,0:T(8,128)S(1)} %copy-done.7, s32[16]{0:T(128)S(1)} %copy-done.14, s32[1,4,1,5]{3,2,1,0:T(1,128)S(1)} %copy-done.13, f32[16,6]{1,0:T(8,128)S(1)} %copy.62.refs_4_, f32[4,1]{1,0:T(4,128)S(1)} %bitcast.9, ...), custom_call_target="tpu_custom_call", output_to_operand_aliasing={{}: (11, {})} | custom-call | flops 1610612736 | bytes 10485760 | tf_op jit(solution)/shard_map/pallas_call | solution.py:226
  (60 shorter events, 19.1 us)
Async XLA Ops:
  0.0 199.0 %copy-start.15 = (f32[8]{0:T(128)S(1)}, f32[8]{0:T(128)}, u32[]{:S(2)}) copy-start(f32[8]{0:T(128)} %damping_ref.3) | copy-start | bytes 100
  0.0 199.0 %copy-start.12 = (f32[256,256]{1,0:T(8,128)S(1)}, f32[256,256]{1,0:T(8,128)}, u32[]{:S(2)}) copy-start(f32[256,256]{1,0:T(8,128)} %hamiltonian_ref.3) | copy-start | bytes 786436
  195.1 57.9 %collective-permute-start.5 = (f32[2,2,256,256]{3,2,1,0:T(8,128)}, f32[2,2,256,256]{3,2,1,0:T(8,128)S(1)}, u32[]{:S(2)}, u32[]{:S(2)}) collective-permute-start(f32[2,2,256,256]{3,2,1,0:T(8,128)} %get-tuple-element.29), channel_id=1, source_target_pairs={{0,1},{1,0},{2,3},{3,2},{4,5},{5,4},{6,7},{7,6},{8,9},{9,8},{10,11... | collective-permute-start | bytes 3145736 | tf_op jit(solution)/shard_map/ppermute | solution.py:37
  195.8 58.5 %collective-permute-start.7 = (f32[2,2,256,256]{3,2,1,0:T(8,128)}, f32[2,2,256,256]{3,2,1,0:T(8,128)}, u32[]{:S(2)}, u32[]{:S(2)}) collective-permute-start(f32[2,2,256,256]{3,2,1,0:T(8,128)} %get-tuple-element.31), channel_id=1, source_target_pairs={{0,2},{1,3},{2,0},{3,1},{4,6},{5,7},{6,4},{7,5},{8,10},{9,11},{10,... | collective-permute-start | bytes 3145736 | tf_op jit(solution)/shard_map/ppermute | solution.py:37
  196.1 13.9 %collective-permute-start.6 = (f32[1,2,256,256]{3,2,1,0:T(8,128)}, f32[1,2,256,256]{3,2,1,0:T(8,128)S(1)}, u32[]{:S(2)}, u32[]{:S(2)}) collective-permute-start(f32[1,2,256,256]{3,2,1,0:T(8,128)} %get-tuple-element.30), channel_id=1, source_target_pairs={{0,15},{1,2},{2,1},{3,4},{4,3},{5,6},{6,5},{7,8},{8,7},{9,10},{10,... | collective-permute-start | bytes 1572872 | tf_op jit(solution)/shard_map/ppermute | solution.py:37
  198.6 52.7 %collective-permute-start.8 = (f32[1,2,256,256]{3,2,1,0:T(8,128)}, f32[1,2,256,256]{3,2,1,0:T(8,128)S(1)}, u32[]{:S(2)}, u32[]{:S(2)}) collective-permute-start(f32[1,2,256,256]{3,2,1,0:T(8,128)} %get-tuple-element.32), channel_id=1, source_target_pairs={{0,14},{1,15},{2,4},{3,5},{4,2},{5,3},{6,8},{7,9},{8,6},{9,7},{10,... | collective-permute-start | bytes 1572872 | tf_op jit(solution)/shard_map/ppermute | solution.py:37
  198.8 56.6 %copy-start.4 = (f32[4,256,256]{2,1,0:T(8,128)S(1)}, f32[4,256,256]{2,1,0:T(8,128)}, u32[]{:S(2)}) copy-start(f32[4,256,256]{2,1,0:T(8,128)} %refs_7_.11) | copy-start | bytes 3145732
  198.8 114.5 %collective-permute-start = (f32[2,2,256,256]{3,2,1,0:T(8,128)}, f32[2,2,256,256]{3,2,1,0:T(8,128)S(1)}, u32[]{:S(2)}, u32[]{:S(2)}) collective-permute-start(f32[2,2,256,256]{3,2,1,0:T(8,128)} %get-tuple-element.24), channel_id=1, source_target_pairs={{0,4},{1,5},{2,6},{3,7},{4,0},{5,1},{6,2},{7,3},{8,12},{9,13},{10,... | collective-permute-start | bytes 3145736 | tf_op jit(solution)/shard_map/ppermute | solution.py:37
  201.2 54.1 %copy-start.7 = (s32[16,6,5]{2,1,0:T(8,128)S(1)}, s32[16,6,5]{2,1,0:T(8,128)}, u32[]{:S(2)}) copy-start(s32[16,6,5]{2,1,0:T(8,128)} %copy.61.left_ref.refs_1_) | copy-start | bytes 5764
  201.3 54.1 %copy-start.14 = (s32[16]{0:T(128)S(1)}, s32[16]{0:T(128)}, u32[]{:S(2)}) copy-start(s32[16]{0:T(128)} %refs_2_.11) | copy-start | bytes 196
  210.8 80.4 %collective-permute-start.3 = (f32[1,2,256,256]{3,2,1,0:T(8,128)}, f32[1,2,256,256]{3,2,1,0:T(8,128)}, u32[]{:S(2)}, u32[]{:S(2)}) collective-permute-start(f32[1,2,256,256]{3,2,1,0:T(8,128)} %get-tuple-element.27), channel_id=1, source_target_pairs={{0,3},{1,4},{2,5},{3,6},{4,7},{5,8},{6,9},{7,10},{8,11},{9,12},{10... | collective-permute-start | bytes 1572872 | tf_op jit(solution)/shard_map/ppermute | solution.py:37
  252.1 46.3 %collective-permute-start.4 = (f32[1,2,256,256]{3,2,1,0:T(8,128)}, f32[1,2,256,256]{3,2,1,0:T(8,128)}, u32[]{:S(2)}, u32[]{:S(2)}) collective-permute-start(f32[1,2,256,256]{3,2,1,0:T(8,128)} %get-tuple-element.28), channel_id=1, source_target_pairs={{0,13},{1,14},{2,15},{3,0},{4,1},{5,2},{6,3},{7,4},{8,5},{9,6},{10... | collective-permute-start | bytes 1572872 | tf_op jit(solution)/shard_map/ppermute | solution.py:37
  253.0 49.6 %collective-permute-start.1 = (f32[1,2,256,256]{3,2,1,0:T(8,128)}, f32[1,2,256,256]{3,2,1,0:T(8,128)S(1)}, u32[]{:S(2)}, u32[]{:S(2)}) collective-permute-start(f32[1,2,256,256]{3,2,1,0:T(8,128)} %get-tuple-element.25), channel_id=1, source_target_pairs={{0,12},{1,13},{2,14},{3,15},{4,8},{5,9},{6,10},{7,11},{8,4},{9,5},... | collective-permute-start | bytes 1572872 | tf_op jit(solution)/shard_map/ppermute | solution.py:37
  254.3 59.0 %collective-permute-start.2 = (f32[1,2,256,256]{3,2,1,0:T(8,128)}, f32[1,2,256,256]{3,2,1,0:T(8,128)S(1)}, u32[]{:S(2)}, u32[]{:S(2)}) collective-permute-start(f32[1,2,256,256]{3,2,1,0:T(8,128)} %get-tuple-element.26), channel_id=1, source_target_pairs={{0,8},{1,9},{2,10},{3,11},{4,12},{5,13},{6,14},{7,15},{8,0},{9,1},... | collective-permute-start | bytes 1572872 | tf_op jit(solution)/shard_map/ppermute | solution.py:37
  302.4 76.8 %copy-start.6 = (f32[8,2,256,256]{3,2,1,0:T(8,128)S(1)}, f32[8,2,256,256]{3,2,1,0:T(8,128)}, u32[]{:S(2)}) copy-start(f32[8,2,256,256]{3,2,1,0:T(8,128)} %rho_ref.3) | copy-start | bytes 12582916
  320.2 30.3 %collective-permute-start.14 = (f32[2,2,256,256]{3,2,1,0:T(8,128)S(1)}, f32[2,2,256,256]{3,2,1,0:T(8,128)S(1)}, u32[]{:S(2)}, u32[]{:S(2)}) collective-permute-start(f32[2,2,256,256]{3,2,1,0:T(8,128)S(1)} %get-tuple-element.38), channel_id=1, source_target_pairs={{0,1},{1,0},{2,3},{3,2},{4,5},{5,4},{6,7},{7,6},{8,9},{9,8},{10,11... | collective-permute-start | bytes 3145736 | tf_op jit(solution)/shard_map/ppermute | solution.py:37
  320.7 58.6 %collective-permute-start.16 = (f32[2,2,256,256]{3,2,1,0:T(8,128)S(1)}, f32[2,2,256,256]{3,2,1,0:T(8,128)S(1)}, u32[]{:S(2)}, u32[]{:S(2)}) collective-permute-start(f32[2,2,256,256]{3,2,1,0:T(8,128)S(1)} %get-tuple-element.40), channel_id=1, source_target_pairs={{0,2},{1,3},{2,0},{3,1},{4,6},{5,7},{6,4},{7,5},{8,10},{9,11},{10,... | collective-permute-start | bytes 3145736 | tf_op jit(solution)/shard_map/ppermute | solution.py:37
  320.7 14.1 %collective-permute-start.15 = (f32[1,2,256,256]{3,2,1,0:T(8,128)S(1)}, f32[1,2,256,256]{3,2,1,0:T(8,128)S(1)}, u32[]{:S(2)}, u32[]{:S(2)}) collective-permute-start(f32[1,2,256,256]{3,2,1,0:T(8,128)S(1)} %get-tuple-element.39), channel_id=1, source_target_pairs={{0,15},{1,2},{2,1},{3,4},{4,3},{5,6},{6,5},{7,8},{8,7},{9,10},{10,... | collective-permute-start | bytes 1572872 | tf_op jit(solution)/shard_map/ppermute | solution.py:37
  323.5 17.4 %collective-permute-start.17 = (f32[1,2,256,256]{3,2,1,0:T(8,128)S(1)}, f32[1,2,256,256]{3,2,1,0:T(8,128)S(1)}, u32[]{:S(2)}, u32[]{:S(2)}) collective-permute-start(f32[1,2,256,256]{3,2,1,0:T(8,128)S(1)} %get-tuple-element.41), channel_id=1, source_target_pairs={{0,14},{1,15},{2,4},{3,5},{4,2},{5,3},{6,8},{7,9},{8,6},{9,7},{10,... | collective-permute-start | bytes 1572872 | tf_op jit(solution)/shard_map/ppermute | solution.py:37
  323.5 102.4 %collective-permute-start.9 = (f32[2,2,256,256]{3,2,1,0:T(8,128)S(1)}, f32[2,2,256,256]{3,2,1,0:T(8,128)S(1)}, u32[]{:S(2)}, u32[]{:S(2)}) collective-permute-start(f32[2,2,256,256]{3,2,1,0:T(8,128)S(1)} %get-tuple-element.33), channel_id=1, source_target_pairs={{0,4},{1,5},{2,6},{3,7},{4,0},{5,1},{6,2},{7,3},{8,12},{9,13},{10,... | collective-permute-start | bytes 3145736 | tf_op jit(solution)/shard_map/ppermute | solution.py:37
  334.8 91.1 %collective-permute-start.10 = (f32[1,2,256,256]{3,2,1,0:T(8,128)S(1)}, f32[1,2,256,256]{3,2,1,0:T(8,128)S(1)}, u32[]{:S(2)}, u32[]{:S(2)}) collective-permute-start(f32[1,2,256,256]{3,2,1,0:T(8,128)S(1)} %get-tuple-element.34), channel_id=1, source_target_pairs={{0,12},{1,13},{2,14},{3,15},{4,8},{5,9},{6,10},{7,11},{8,4},{9,5},... | collective-permute-start | bytes 1572872 | tf_op jit(solution)/shard_map/ppermute | solution.py:37
  340.9 84.9 %collective-permute-start.11 = (f32[1,2,256,256]{3,2,1,0:T(8,128)S(1)}, f32[1,2,256,256]{3,2,1,0:T(8,128)S(1)}, u32[]{:S(2)}, u32[]{:S(2)}) collective-permute-start(f32[1,2,256,256]{3,2,1,0:T(8,128)S(1)} %get-tuple-element.35), channel_id=1, source_target_pairs={{0,8},{1,9},{2,10},{3,11},{4,12},{5,13},{6,14},{7,15},{8,0},{9,1},... | collective-permute-start | bytes 1572872 | tf_op jit(solution)/shard_map/ppermute | solution.py:37
  350.5 50.4 %collective-permute-start.12 = (f32[1,2,256,256]{3,2,1,0:T(8,128)S(1)}, f32[1,2,256,256]{3,2,1,0:T(8,128)S(1)}, u32[]{:S(2)}, u32[]{:S(2)}) collective-permute-start(f32[1,2,256,256]{3,2,1,0:T(8,128)S(1)} %get-tuple-element.36), channel_id=1, source_target_pairs={{0,3},{1,4},{2,5},{3,6},{4,7},{5,8},{6,9},{7,10},{8,11},{9,12},{10... | collective-permute-start | bytes 1572872 | tf_op jit(solution)/shard_map/ppermute | solution.py:37
  379.2 39.8 %collective-permute-start.13 = (f32[1,2,256,256]{3,2,1,0:T(8,128)S(1)}, f32[1,2,256,256]{3,2,1,0:T(8,128)S(1)}, u32[]{:S(2)}, u32[]{:S(2)}) collective-permute-start(f32[1,2,256,256]{3,2,1,0:T(8,128)S(1)} %get-tuple-element.37), channel_id=1, source_target_pairs={{0,13},{1,14},{2,15},{3,0},{4,1},{5,2},{6,3},{7,4},{8,5},{9,6},{10... | collective-permute-start | bytes 1572872 | tf_op jit(solution)/shard_map/ppermute | solution.py:37
  (11 other events, 120.1 us)
where the time goes:
time: 434 us
  Pallas kernels  242 us (56%)
  starting transfers between devices  91.5 us (21%)
  waiting for transfers between devices  82.5 us (19%)
  local copies, waits for them, and re-layouts  16.1 us (4%)
    pallas_call x1, Pallas kernels, pack_call(): pl.pallas_call(functools.partial(pack_kernel, plan, mats), in_specs=[SMEM...  194 us
    ppermute x18, starting transfers between devices, permute(): lax.ppermute(value, 'tier', [(i, self.peer(i, True)) for i in range(self....  91.5 us
    ppermute x18, waiting for transfers between devices, permute(): lax.ppermute(value, 'tier', [(i, self.peer(i, True)) for i in range(self....  82.5 us
    pallas_call x6, Pallas kernels, rows_call(): pl.pallas_call(functools.partial(rows_kernel, plan, packs, scale, None),...  36.7 us
    unnamed x36, local copies, waits for them, and re-layouts  16.1 us
    pallas_call x2, Pallas kernels, local_call(): pl.pallas_call(kernel, grid=(mats,), in_specs=[SMEM, pl.BlockSpec((order,...  12.2 us
  transfers between devices with their start and end apart: 18, of which 9 were waited for; matrix products, arithmetic and copies ran while one was open for 0% of the time, Pallas kernels for 8%

commit v1 on v0

--- a/solution.py
+++ b/solution.py
@@ -110,8 +110,13 @@
 
 
 def pack_kernel(plan, mats, me_ref, left_ref, count_ref, match_ref, source, *rest):
-    sends, sems = rest[:-1], rest[-1]
-    pack(plan, mats, me_ref, left_ref, count_ref, match_ref, source, sends, sems)
+    sends, (held, load_sems, sems) = rest[:-3], rest[-3:]
+    loads = [pltpu.make_async_copy(source.at[n], held.at[n], load_sems.at[n]) for n in range(mats)]
+    for load in loads:
+        load.start()
+    for load in loads:
+        load.wait()
+    pack(plan, mats, me_ref, left_ref, count_ref, match_ref, held, sends, sems)
 
 
 def pack(plan, mats, me_ref, left_ref, count_ref, match_ref, source, sends, sems):
@@ -251,7 +256,12 @@
         in_specs=[SMEM] * 4 + [ANY],
         out_specs=[ANY] * len(plan),
         out_shape=[jax.ShapeDtypeStruct((payload(e, pairs), 2, order, order), F32) for e in plan],
-        scratch_shapes=[pltpu.SemaphoreType.DMA((sent,))],
+        scratch_shapes=[
+            pltpu.VMEM(source.shape, F32),
+            pltpu.SemaphoreType.DMA((mats,)),
+            pltpu.SemaphoreType.DMA((sent,)),
+        ],
+        compiler_params=pltpu.CompilerParams(vmem_limit_bytes=16 * 1024 * 1024),
         cost_estimate=pl.CostEstimate(flops=0, bytes_accessed=sent * 16 * order**2, transcendentals=0),
     )(*tables[:4], source)
 

time: 434 us -> 249 us (0.57)
  Pallas kernels: 242 us -> 54.1 us
    pallas_call x1, Pallas kernels: 194 us -> 4.09 us  [pack_call(): pl.pallas_call(functools.partial(pack_kernel, plan, mats), in_specs=[SMEM...]
    unnamed x36 -> x46, local copies, waits for them, and re-layouts: 16.1 us -> 19.3 us
  transfers between devices with their start and end apart: 18 -> 18, of which waited for: 9 -> 8; matrix products, arithmetic and copies ran while one was open for 0% -> 0% of each run, Pallas kernels for 8% -> 15%
where the time goes in v1:
time: 249 us
  starting transfers between devices  90.6 us (36%)
  waiting for transfers between devices  83.5 us (34%)
  Pallas kernels  54.1 us (22%)
  local copies, waits for them, and re-layouts  19.4 us (8%)
    ppermute x18, starting transfers between devices, permute(): lax.ppermute(value, 'tier', [(i, self.peer(i, True)) for i in range(self....  90.6 us
    ppermute x18, waiting for transfers between devices, permute(): lax.ppermute(value, 'tier', [(i, self.peer(i, True)) for i in range(self....  83.5 us
    pallas_call x6, Pallas kernels, rows_call(): pl.pallas_call(functools.partial(rows_kernel, plan, packs, scale, None),...  37.9 us
    unnamed x46, local copies, waits for them, and re-layouts  19.3 us
    pallas_call x2, Pallas kernels, local_call(): pl.pallas_call(kernel, grid=(mats,), in_specs=[SMEM, pl.BlockSpec((order,...  12.1 us
  transfers between devices with their start and end apart: 18, of which 8 were waited for; matrix products, arithmetic and copies ran while one was open for 0% of the time, Pallas kernels for 15%

profile of v1, /device:TPU:13, one launch (start us, length us, event | category | flops | bytes accessed | tf_op | source)
XLA Modules:
  0.0 248.6 jit_solution(15140630232977633768)
XLA Ops:
  0.9 2.2 copy-done.5
  4.4 4.1 %shard_map.82 = (f32[2,2,256,256]{3,2,1,0:T(8,128)}, f32[1,2,256,256]{3,2,1,0:T(8,128)S(1)}, f32[2,2,256,256]{3,2,1,0:T(8,128)}, f32[1,2,256,256]{3,2,1,0:T(8,12...) custom-call(s32[1]{0:T(128)} %bitcast.me_ref.refs_0_, ...), custom_call_target="tpu_custom_call" | custom-call | bytes 12582912 | tf_op jit(solution)/shard_map/pallas_call | solution.py:254
  11.0 2.4 collective-permute-start.6
  14.9 5.4 %shard_map.83.refs_12_ = f32[8,2,256,256]{3,2,1,0:T(8,128)S(1)} custom-call(f32[8]{0:T(128)S(1)} %copy-done.18, f32[256,256]{1,0:T(8,128)S(1)} %copy-done.12, f32[8,2,256,256]{3,2,1,0:T(8,128)S(1)} %copy-done.6), custom_call_target="tpu_custom_call" | custom-call | flops 3221225472 | bytes 16777216 | tf_op jit(solution)/shard_map/pallas_call | solution.py:161
  22.3 2.2 collective-permute-done.6.refs_9_
  25.3 41.0 %collective-permute-start.3 = (f32[1,2,256,256]{3,2,1,0:T(8,128)}, f32[1,2,256,256]{3,2,1,0:T(8,128)}, u32[]{:S(2)}, u32[]{:S(2)}) collective-permute-start(f32[1,2,256,256]{3,2,1,0:T(8,128)} %get-tuple-element.27), channel_id=1, source_target_pairs={{0,3},{1,4},{2,5},{3,6},{4,7},{5,8},{6,9},{7,10},{8,11},{9,12},{10... | collective-permute-start | bytes 1572872 | tf_op jit(solution)/shard_map/ppermute | solution.py:37
  70.4 2.2 copy-done.1
  74.7 5.4 %shard_map.84.refs_10_ = f32[8,2,256,256]{3,2,1,0:T(8,128)S(1)} custom-call(s32[1]{0:T(128)} %bitcast.me_ref.refs_0_, s32[16,6,5]{2,1,0:T(8,128)S(1)} %copy.61.left_ref.refs_1_, s32[16]{0:T(128)S(1)} %copy-done.17, s32[1,4,1,5]{3,2,1,0:T(1,128)S(1)} %copy-done.15, f32[16,6]{1,0:T(8,128)S(1)} %copy.62.refs_4_, ...), custom_call_target="tpu_custom_call", output_to_operand_aliasing={{}: (12, {})} | custom-call | flops 2415919104 | bytes 11534336 | tf_op jit(solution)/shard_map/pallas_call | solution.py:231
  80.1 26.2 %collective-permute-done.3.refs_8_ = f32[1,2,256,256]{3,2,1,0:T(8,128)} collective-permute-done((f32[1,2,256,256]{3,2,1,0:T(8,128)}, f32[1,2,256,256]{3,2,1,0:T(8,128)}, u32[]{:S(2)}, u32[]{:S(2)}) %collective-permute-start.3) | collective-permute-done | bytes 524320 | tf_op jit(solution)/shard_map/ppermute | solution.py:37
  106.3 7.2 %collective-permute-done.4.refs_9_ = f32[1,2,256,256]{3,2,1,0:T(8,128)} collective-permute-done((f32[1,2,256,256]{3,2,1,0:T(8,128)}, f32[1,2,256,256]{3,2,1,0:T(8,128)}, u32[]{:S(2)}, u32[]{:S(2)}) %collective-permute-start.4) | collective-permute-done | bytes 524320 | tf_op jit(solution)/shard_map/ppermute | solution.py:37
  113.4 4.1 %shard_map.85.refs_11_ = f32[8,2,256,256]{3,2,1,0:T(8,128)S(1)} custom-call(s32[1]{0:T(128)} %bitcast.me_ref.refs_0_, s32[16,6,5]{2,1,0:T(8,128)S(1)} %copy.61.left_ref.refs_1_, s32[16]{0:T(128)S(1)} %copy-done.17, s32[1,4,1,5]{3,2,1,0:T(1,128)S(1)} %copy-done.15, f32[16,6]{1,0:T(8,128)S(1)} %copy.62.refs_4_, ...), custom_call_target="tpu_custom_call", output_to_operand_aliasing={{}: (10, {})} | custom-call | flops 805306368 | bytes 9437184 | tf_op jit(solution)/shard_map/pallas_call | solution.py:231
  117.6 10.6 %collective-permute-done.2.refs_10_ = f32[1,2,256,256]{3,2,1,0:T(8,128)S(1)} collective-permute-done((f32[1,2,256,256]{3,2,1,0:T(8,128)}, f32[1,2,256,256]{3,2,1,0:T(8,128)S(1)}, u32[]{:S(2)}, u32[]{:S(2)}) %collective-permute-start.2) | collective-permute-done | bytes 524320 | tf_op jit(solution)/shard_map/ppermute | solution.py:37
  128.2 4.9 %shard_map.86 = (f32[8,2,256,256]{3,2,1,0:T(8,128)S(1)}, f32[2,2,256,256]{3,2,1,0:T(8,128)S(1)}, f32[1,2,256,256]{3,2,1,0:T(8,128)S(1)}, f32[2,2,256,256]{3,2,1,...) custom-call(s32[1]{0:T(128)} %bitcast.me_ref.refs_0_, ...), custom_call_target="tpu_custom_call", output_to_operand_aliasing={{0}: (11, {})} | custom-call | flops 1610612736 | bytes 16777216 | tf_op jit(solution)/shard_map/pallas_call | solution.py:231
  135.4 4.3 %collective-permute-start.15 = (f32[1,2,256,256]{3,2,1,0:T(8,128)S(1)}, f32[1,2,256,256]{3,2,1,0:T(8,128)S(1)}, u32[]{:S(2)}, u32[]{:S(2)}) collective-permute-start(f32[1,2,256,256]{3,2,1,0:T(8,128)S(1)} %get-tuple-element.39), channel_id=1, source_target_pairs={{0,15},{1,2},{2,1},{3,4},{4,3},{5,6},{6,5},{7,8},{8,7},{9,10},{10,... | collective-permute-start | bytes 1572872 | tf_op jit(solution)/shard_map/ppermute | solution.py:37
  139.8 11.2 %collective-permute-done.15.refs_9_ = f32[1,2,256,256]{3,2,1,0:T(8,128)S(1)} collective-permute-done((f32[1,2,256,256]{3,2,1,0:T(8,128)S(1)}, f32[1,2,256,256]{3,2,1,0:T(8,128)S(1)}, u32[]{:S(2)}, u32[]{:S(2)}) %collective-permute-start.15) | collective-permute-done | bytes 524320 | tf_op jit(solution)/shard_map/ppermute | solution.py:37
  152.6 4.6 %collective-permute-done.17.refs_11_ = f32[1,2,256,256]{3,2,1,0:T(8,128)S(1)} collective-permute-done((f32[1,2,256,256]{3,2,1,0:T(8,128)S(1)}, f32[1,2,256,256]{3,2,1,0:T(8,128)S(1)}, u32[]{:S(2)}, u32[]{:S(2)}) %collective-permute-start.17) | collective-permute-done | bytes 524320 | tf_op jit(solution)/shard_map/ppermute | solution.py:37
  157.2 8.4 %collective-permute-start.11 = (f32[1,2,256,256]{3,2,1,0:T(8,128)S(1)}, f32[1,2,256,256]{3,2,1,0:T(8,128)S(1)}, u32[]{:S(2)}, u32[]{:S(2)}) collective-permute-start(f32[1,2,256,256]{3,2,1,0:T(8,128)S(1)} %get-tuple-element.35), channel_id=1, source_target_pairs={{0,8},{1,9},{2,10},{3,11},{4,12},{5,13},{6,14},{7,15},{8,0},{9,1},... | collective-permute-start | bytes 1572872 | tf_op jit(solution)/shard_map/ppermute | solution.py:37
  165.6 29.0 %collective-permute-start.12 = (f32[1,2,256,256]{3,2,1,0:T(8,128)S(1)}, f32[1,2,256,256]{3,2,1,0:T(8,128)S(1)}, u32[]{:S(2)}, u32[]{:S(2)}) collective-permute-start(f32[1,2,256,256]{3,2,1,0:T(8,128)S(1)} %get-tuple-element.36), channel_id=1, source_target_pairs={{0,3},{1,4},{2,5},{3,6},{4,7},{5,8},{6,9},{7,10},{8,11},{9,12},{10... | collective-permute-start | bytes 1572872 | tf_op jit(solution)/shard_map/ppermute | solution.py:37
  196.7 6.7 %shard_map.87.refs_12_ = f32[8,2,256,256]{3,2,1,0:T(8,128)} custom-call(f32[8]{0:T(128)S(1)} %copy-done.18, f32[256,256]{1,0:T(8,128)S(1)} %copy-done.13, f32[8,2,256,256]{3,2,1,0:T(8,128)S(1)} %copy-done.3, f32[8,2,256,256]{3,2,1,0:T(8,128)S(1)} %copy-done.7), custom_call_target="tpu_custom_call" | custom-call | flops 3221225472 | bytes 25165824 | tf_op jit(solution)/shard_map/pallas_call | solution.py:161
  203.4 9.0 %shard_map.88.refs_10_ = f32[8,2,256,256]{3,2,1,0:T(8,128)} custom-call(s32[1]{0:T(128)} %bitcast.me_ref.refs_0_, s32[16,6,5]{2,1,0:T(8,128)S(1)} %copy.61.left_ref.refs_1_, s32[16]{0:T(128)S(1)} %copy-done.17, s32[1,4,1,5]{3,2,1,0:T(1,128)S(1)} %copy-done.15, f32[16,6]{1,0:T(8,128)S(1)} %copy.62.refs_4_, ...), custom_call_target="tpu_custom_call", output_to_operand_aliasing={{}: (12, {})} | custom-call | flops 2415919104 | bytes 11534336 | tf_op jit(solution)/shard_map/pallas_call | solution.py:231
  212.4 3.8 %collective-permute-done.12.refs_8_ = f32[1,2,256,256]{3,2,1,0:T(8,128)S(1)} collective-permute-done((f32[1,2,256,256]{3,2,1,0:T(8,128)S(1)}, f32[1,2,256,256]{3,2,1,0:T(8,128)S(1)}, u32[]{:S(2)}, u32[]{:S(2)}) %collective-permute-start.12) | collective-permute-done | bytes 524320 | tf_op jit(solution)/shard_map/ppermute | solution.py:37
  216.2 17.8 %collective-permute-done.13.refs_9_ = f32[1,2,256,256]{3,2,1,0:T(8,128)S(1)} collective-permute-done((f32[1,2,256,256]{3,2,1,0:T(8,128)S(1)}, f32[1,2,256,256]{3,2,1,0:T(8,128)S(1)}, u32[]{:S(2)}, u32[]{:S(2)}) %collective-permute-start.13) | collective-permute-done | bytes 524320 | tf_op jit(solution)/shard_map/ppermute | solution.py:37
  234.0 6.9 %shard_map.89.refs_11_ = f32[8,2,256,256]{3,2,1,0:T(8,128)} custom-call(s32[1]{0:T(128)} %bitcast.me_ref.refs_0_, s32[16,6,5]{2,1,0:T(8,128)S(1)} %copy.61.left_ref.refs_1_, s32[16]{0:T(128)S(1)} %copy-done.17, s32[1,4,1,5]{3,2,1,0:T(1,128)S(1)} %copy-done.15, f32[16,6]{1,0:T(8,128)S(1)} %copy.62.refs_4_, ...), custom_call_target="tpu_custom_call", output_to_operand_aliasing={{}: (10, {})} | custom-call | flops 805306368 | bytes 9437184 | tf_op jit(solution)/shard_map/pallas_call | solution.py:231
  240.9 7.6 %shard_map.90 = f32[8,2,256,256]{3,2,1,0:T(8,128)} custom-call(s32[1]{0:T(128)} %bitcast.me_ref.refs_0_, s32[16,6,5]{2,1,0:T(8,128)S(1)} %copy.61.left_ref.refs_1_, s32[16]{0:T(128)S(1)} %copy-done.17, s32[1,4,1,5]{3,2,1,0:T(1,128)S(1)} %copy-done.15, f32[16,6]{1,0:T(8,128)S(1)} %copy.62.refs_4_, ...), custom_call_target="tpu_custom_call", output_to_operand_aliasing={{}: (11, {})} | custom-call | flops 1610612736 | bytes 10485760 | tf_op jit(solution)/shard_map/pallas_call | solution.py:231
  (70 shorter events, 21.3 us)
Async XLA Ops:
  10.1 57.9 %collective-permute-start.5 = (f32[2,2,256,256]{3,2,1,0:T(8,128)}, f32[2,2,256,256]{3,2,1,0:T(8,128)S(1)}, u32[]{:S(2)}, u32[]{:S(2)}) collective-permute-start(f32[2,2,256,256]{3,2,1,0:T(8,128)} %get-tuple-element.29), channel_id=1, source_target_pairs={{0,1},{1,0},{2,3},{3,2},{4,5},{5,4},{6,7},{7,6},{8,9},{9,8},{10,11... | collective-permute-start | bytes 3145736 | tf_op jit(solution)/shard_map/ppermute | solution.py:37
  10.8 58.5 %collective-permute-start.7 = (f32[2,2,256,256]{3,2,1,0:T(8,128)}, f32[2,2,256,256]{3,2,1,0:T(8,128)}, u32[]{:S(2)}, u32[]{:S(2)}) collective-permute-start(f32[2,2,256,256]{3,2,1,0:T(8,128)} %get-tuple-element.31), channel_id=1, source_target_pairs={{0,2},{1,3},{2,0},{3,1},{4,6},{5,7},{6,4},{7,5},{8,10},{9,11},{10,... | collective-permute-start | bytes 3145736 | tf_op jit(solution)/shard_map/ppermute | solution.py:37
  11.0 13.4 %collective-permute-start.6 = (f32[1,2,256,256]{3,2,1,0:T(8,128)S(1)}, f32[1,2,256,256]{3,2,1,0:T(8,128)S(1)}, u32[]{:S(2)}, u32[]{:S(2)}) collective-permute-start(f32[1,2,256,256]{3,2,1,0:T(8,128)S(1)} %get-tuple-element.30), channel_id=1, source_target_pairs={{0,15},{1,2},{2,1},{3,4},{4,3},{5,6},{6,5},{7,8},{8,7},{9,10},{10,... | collective-permute-start | bytes 1572872 | tf_op jit(solution)/shard_map/ppermute | solution.py:37
  13.4 52.9 %collective-permute-start.8 = (f32[1,2,256,256]{3,2,1,0:T(8,128)S(1)}, f32[1,2,256,256]{3,2,1,0:T(8,128)S(1)}, u32[]{:S(2)}, u32[]{:S(2)}) collective-permute-start(f32[1,2,256,256]{3,2,1,0:T(8,128)S(1)} %get-tuple-element.32), channel_id=1, source_target_pairs={{0,14},{1,15},{2,4},{3,5},{4,2},{5,3},{6,8},{7,9},{8,6},{9,7},{10,... | collective-permute-start | bytes 1572872 | tf_op jit(solution)/shard_map/ppermute | solution.py:37
  13.7 56.7 %copy-start.4 = (f32[4,256,256]{2,1,0:T(8,128)S(1)}, f32[4,256,256]{2,1,0:T(8,128)}, u32[]{:S(2)}) copy-start(f32[4,256,256]{2,1,0:T(8,128)} %refs_7_.11) | copy-start | bytes 3145732
  13.7 114.5 %collective-permute-start = (f32[2,2,256,256]{3,2,1,0:T(8,128)}, f32[2,2,256,256]{3,2,1,0:T(8,128)S(1)}, u32[]{:S(2)}, u32[]{:S(2)}) collective-permute-start(f32[2,2,256,256]{3,2,1,0:T(8,128)} %get-tuple-element.24), channel_id=1, source_target_pairs={{0,4},{1,5},{2,6},{3,7},{4,0},{5,1},{6,2},{7,3},{8,12},{9,13},{10,... | collective-permute-start | bytes 3145736 | tf_op jit(solution)/shard_map/ppermute | solution.py:37
  14.9 53.0 %copy-start.21 = (f32[4,2]{0,1:T(2,128)S(1)}, f32[4,2]{0,1:T(2,128)}, u32[]{:S(2)}) copy-start(f32[4,2]{0,1:T(2,128)} %param.11) | copy-start | bytes 100
  14.9 55.4 %copy-start.15 = (s32[1,4,1,5]{3,2,1,0:T(1,128)S(1)}, s32[1,4,1,5]{3,2,1,0:T(1,128)}, u32[]{:S(2)}) copy-start(s32[1,4,1,5]{3,2,1,0:T(1,128)} %refs_3_.11) | copy-start | bytes 244
  14.9 55.5 %copy-start.17 = (s32[16]{0:T(128)S(1)}, s32[16]{0:T(128)}, u32[]{:S(2)}) copy-start(s32[16]{0:T(128)} %refs_2_.11) | copy-start | bytes 196
  25.3 81.0 %collective-permute-start.3 = (f32[1,2,256,256]{3,2,1,0:T(8,128)}, f32[1,2,256,256]{3,2,1,0:T(8,128)}, u32[]{:S(2)}, u32[]{:S(2)}) collective-permute-start(f32[1,2,256,256]{3,2,1,0:T(8,128)} %get-tuple-element.27), channel_id=1, source_target_pairs={{0,3},{1,4},{2,5},{3,6},{4,7},{5,8},{6,9},{7,10},{8,11},{9,12},{10... | collective-permute-start | bytes 1572872 | tf_op jit(solution)/shard_map/ppermute | solution.py:37
  67.1 46.3 %collective-permute-start.4 = (f32[1,2,256,256]{3,2,1,0:T(8,128)}, f32[1,2,256,256]{3,2,1,0:T(8,128)}, u32[]{:S(2)}, u32[]{:S(2)}) collective-permute-start(f32[1,2,256,256]{3,2,1,0:T(8,128)} %get-tuple-element.28), channel_id=1, source_target_pairs={{0,13},{1,14},{2,15},{3,0},{4,1},{5,2},{6,3},{7,4},{8,5},{9,6},{10... | collective-permute-start | bytes 1572872 | tf_op jit(solution)/shard_map/ppermute | solution.py:37
  68.0 49.6 %collective-permute-start.1 = (f32[1,2,256,256]{3,2,1,0:T(8,128)}, f32[1,2,256,256]{3,2,1,0:T(8,128)S(1)}, u32[]{:S(2)}, u32[]{:S(2)}) collective-permute-start(f32[1,2,256,256]{3,2,1,0:T(8,128)} %copy-done.20), channel_id=1, source_target_pairs={{0,12},{1,13},{2,14},{3,15},{4,8},{5,9},{6,10},{7,11},{8,4},{9,5},... | collective-permute-start | bytes 1572872 | tf_op jit(solution)/shard_map/ppermute | solution.py:37
  69.3 58.9 %collective-permute-start.2 = (f32[1,2,256,256]{3,2,1,0:T(8,128)}, f32[1,2,256,256]{3,2,1,0:T(8,128)S(1)}, u32[]{:S(2)}, u32[]{:S(2)}) collective-permute-start(f32[1,2,256,256]{3,2,1,0:T(8,128)} %copy-done.19), channel_id=1, source_target_pairs={{0,8},{1,9},{2,10},{3,11},{4,12},{5,13},{6,14},{7,15},{8,0},{9,1},... | collective-permute-start | bytes 1572872 | tf_op jit(solution)/shard_map/ppermute | solution.py:37
  117.6 76.9 %copy-start.7 = (f32[8,2,256,256]{3,2,1,0:T(8,128)S(1)}, f32[8,2,256,256]{3,2,1,0:T(8,128)}, u32[]{:S(2)}) copy-start(f32[8,2,256,256]{3,2,1,0:T(8,128)} %rho_ref.3) | copy-start | bytes 12582916
  117.6 76.9 %copy-start.13 = (f32[256,256]{1,0:T(8,128)S(1)}, f32[256,256]{1,0:T(8,128)}, u32[]{:S(2)}) copy-start(f32[256,256]{1,0:T(8,128)} %hamiltonian_ref.3) | copy-start | bytes 786436
  135.1 30.4 %collective-permute-start.14 = (f32[2,2,256,256]{3,2,1,0:T(8,128)S(1)}, f32[2,2,256,256]{3,2,1,0:T(8,128)S(1)}, u32[]{:S(2)}, u32[]{:S(2)}) collective-permute-start(f32[2,2,256,256]{3,2,1,0:T(8,128)S(1)} %get-tuple-element.38), channel_id=1, source_target_pairs={{0,1},{1,0},{2,3},{3,2},{4,5},{5,4},{6,7},{7,6},{8,9},{9,8},{10,11... | collective-permute-start | bytes 3145736 | tf_op jit(solution)/shard_map/ppermute | solution.py:37
  135.4 59.1 %collective-permute-start.16 = (f32[2,2,256,256]{3,2,1,0:T(8,128)S(1)}, f32[2,2,256,256]{3,2,1,0:T(8,128)S(1)}, u32[]{:S(2)}, u32[]{:S(2)}) collective-permute-start(f32[2,2,256,256]{3,2,1,0:T(8,128)S(1)} %get-tuple-element.40), channel_id=1, source_target_pairs={{0,2},{1,3},{2,0},{3,1},{4,6},{5,7},{6,4},{7,5},{8,10},{9,11},{10,... | collective-permute-start | bytes 3145736 | tf_op jit(solution)/shard_map/ppermute | solution.py:37
  135.4 15.6 %collective-permute-start.15 = (f32[1,2,256,256]{3,2,1,0:T(8,128)S(1)}, f32[1,2,256,256]{3,2,1,0:T(8,128)S(1)}, u32[]{:S(2)}, u32[]{:S(2)}) collective-permute-start(f32[1,2,256,256]{3,2,1,0:T(8,128)S(1)} %get-tuple-element.39), channel_id=1, source_target_pairs={{0,15},{1,2},{2,1},{3,4},{4,3},{5,6},{6,5},{7,8},{8,7},{9,10},{10,... | collective-permute-start | bytes 1572872 | tf_op jit(solution)/shard_map/ppermute | solution.py:37
  139.8 17.4 %collective-permute-start.17 = (f32[1,2,256,256]{3,2,1,0:T(8,128)S(1)}, f32[1,2,256,256]{3,2,1,0:T(8,128)S(1)}, u32[]{:S(2)}, u32[]{:S(2)}) collective-permute-start(f32[1,2,256,256]{3,2,1,0:T(8,128)S(1)} %get-tuple-element.41), channel_id=1, source_target_pairs={{0,14},{1,15},{2,4},{3,5},{4,2},{5,3},{6,8},{7,9},{8,6},{9,7},{10,... | collective-permute-start | bytes 1572872 | tf_op jit(solution)/shard_map/ppermute | solution.py:37
  139.8 101.1 %collective-permute-start.9 = (f32[2,2,256,256]{3,2,1,0:T(8,128)S(1)}, f32[2,2,256,256]{3,2,1,0:T(8,128)S(1)}, u32[]{:S(2)}, u32[]{:S(2)}) collective-permute-start(f32[2,2,256,256]{3,2,1,0:T(8,128)S(1)} %get-tuple-element.33), channel_id=1, source_target_pairs={{0,4},{1,5},{2,6},{3,7},{4,0},{5,1},{6,2},{7,3},{8,12},{9,13},{10,... | collective-permute-start | bytes 3145736 | tf_op jit(solution)/shard_map/ppermute | solution.py:37
  151.0 89.9 %collective-permute-start.10 = (f32[1,2,256,256]{3,2,1,0:T(8,128)S(1)}, f32[1,2,256,256]{3,2,1,0:T(8,128)S(1)}, u32[]{:S(2)}, u32[]{:S(2)}) collective-permute-start(f32[1,2,256,256]{3,2,1,0:T(8,128)S(1)} %get-tuple-element.34), channel_id=1, source_target_pairs={{0,12},{1,13},{2,14},{3,15},{4,8},{5,9},{6,10},{7,11},{8,4},{9,5},... | collective-permute-start | bytes 1572872 | tf_op jit(solution)/shard_map/ppermute | solution.py:37
  157.2 83.7 %collective-permute-start.11 = (f32[1,2,256,256]{3,2,1,0:T(8,128)S(1)}, f32[1,2,256,256]{3,2,1,0:T(8,128)S(1)}, u32[]{:S(2)}, u32[]{:S(2)}) collective-permute-start(f32[1,2,256,256]{3,2,1,0:T(8,128)S(1)} %get-tuple-element.35), channel_id=1, source_target_pairs={{0,8},{1,9},{2,10},{3,11},{4,12},{5,13},{6,14},{7,15},{8,0},{9,1},... | collective-permute-start | bytes 1572872 | tf_op jit(solution)/shard_map/ppermute | solution.py:37
  165.6 50.6 %collective-permute-start.12 = (f32[1,2,256,256]{3,2,1,0:T(8,128)S(1)}, f32[1,2,256,256]{3,2,1,0:T(8,128)S(1)}, u32[]{:S(2)}, u32[]{:S(2)}) collective-permute-start(f32[1,2,256,256]{3,2,1,0:T(8,128)S(1)} %get-tuple-element.36), channel_id=1, source_target_pairs={{0,3},{1,4},{2,5},{3,6},{4,7},{5,8},{6,9},{7,10},{8,11},{9,12},{10... | collective-permute-start | bytes 1572872 | tf_op jit(solution)/shard_map/ppermute | solution.py:37
  194.5 39.5 %collective-permute-start.13 = (f32[1,2,256,256]{3,2,1,0:T(8,128)S(1)}, f32[1,2,256,256]{3,2,1,0:T(8,128)S(1)}, u32[]{:S(2)}, u32[]{:S(2)}) collective-permute-start(f32[1,2,256,256]{3,2,1,0:T(8,128)S(1)} %get-tuple-element.37), channel_id=1, source_target_pairs={{0,13},{1,14},{2,15},{3,0},{4,1},{5,2},{6,3},{7,4},{8,5},{9,6},{10... | collective-permute-start | bytes 1572872 | tf_op jit(solution)/shard_map/ppermute | solution.py:37
  (16 other events, 41.6 us)

commit v2 on v1

--- a/solution.py
+++ b/solution.py
@@ -12,7 +12,8 @@
 F32, BF16 = jnp.float32, jnp.bfloat16
 SMEM = pl.BlockSpec(memory_space=pltpu.SMEM)
 VMEM = pl.BlockSpec(memory_space=pltpu.VMEM)
-ANY = pl.BlockSpec(memory_space=pl.ANY)
+HBM = pl.BlockSpec(memory_space=pltpu.HBM)
+GRANT = 56 * 1024 * 1024
 
 
 class Exchange:
@@ -38,25 +39,31 @@
 
 
 def exchanges(size, colours):
-    near, far = [], []
-    for distance in range(1, REACH + 1):
-        colour = distance.bit_length() - 1
-        if distance == 1 << colour and colour < colours:
-            group = [
-                Exchange("swap", distance, size, colour),
-                Exchange("other", distance, size),
-            ]
-        else:
-            group = [Exchange("shift", distance, size), Exchange("shift", size - distance, size)]
-        (near if distance < REACH else far).extend(group)
+    swaps, others, shifts, far = [], [], [], []
     for colour in range(colours):
         if 1 << colour > REACH:
             far.append(Exchange("swap", 1 << colour, size, colour, listed=False))
-    return near + far
+    for distance in range(1, REACH + 1):
+        colour = distance.bit_length() - 1
+        if distance != 1 << colour or colour >= colours:
+            shifts += [Exchange("shift", distance, size), Exchange("shift", size - distance, size)]
+        elif distance < REACH:
+            swaps.append(Exchange("swap", distance, size, colour))
+            others.insert(0, Exchange("other", distance, size))
+        else:
+            far += [Exchange("swap", distance, size, colour), Exchange("other", distance, size)]
+    return swaps, shifts + others, far
 
 
 def payload(exchange, pairs):
     return (pairs if exchange.colour is not None else 0) + (1 if exchange.listed else 0)
+
+
+def when(condition, action):
+    if condition is None:
+        action()
+    else:
+        pl.when(condition)(action)
 
 
 def split(value):
@@ -78,7 +85,7 @@
         peer = exchange.peer(me, True)
         slot = jnp.int32(0)
         for j in range(left_ref.shape[1]):
-            source = left_ref[peer, j, 1]
+            source = left_ref[1, j, peer]
             hit = (j < count_ref[peer]) & (lax.div(source, mats) == me)
             slot = jnp.where(hit, lax.rem(source, mats), slot)
         slots.append(slot)
@@ -90,8 +97,8 @@
 
     def row(live, target, mode, flag, root):
         lower = flag == 1
-        a = jnp.where(lower, jnp.float32(1), bath_ref[mode, 0])
-        b = jnp.where(lower, jnp.float32(0), bath_ref[mode, 1])
+        a = jnp.where(lower, jnp.float32(1), bath_ref[0, mode])
+        b = jnp.where(lower, jnp.float32(0), bath_ref[1, mode])
         rows.append((live, target, mode, a * root, b * root))
 
     if exchange.colour is not None:
@@ -102,8 +109,8 @@
         peer = exchange.peer(me, False)
         found = [jnp.int32(0)] * 4 + [jnp.float32(0)]
         for j in range(left_ref.shape[1]):
-            hit = (j < count_ref[me]) & (lax.div(left_ref[me, j, 1], mats) == peer)
-            here = [1, left_ref[me, j, 0], left_ref[me, j, 2], left_ref[me, j, 3], left_root[me, j]]
+            hit = (j < count_ref[me]) & (lax.div(left_ref[1, j, me], mats) == peer)
+            here = [1, left_ref[0, j, me], left_ref[2, j, me], left_ref[3, j, me], left_root[j, me]]
             found = [jnp.where(hit, new, old) for new, old in zip(here, found)]
         row(found[0] == 1, found[1], found[2], found[3], found[4])
     return rows
@@ -138,40 +145,54 @@
     return parts[1], -parts[0]
 
 
-def first_local_kernel(damping_ref, hamiltonian_ref, rho_ref, out_ref):
-    decay = damping_ref[pl.program_id(0)]
-    density = (rho_ref[0, 0], rho_ref[0, 1])
-    turned = commutator(density, split(hamiltonian_ref[...]))
-    for part in range(2):
-        out_ref[0, part] = turned[part] - decay * density[part]
-
-
-def second_local_kernel(damping_ref, hamiltonian_ref, first_ref, rho_ref, out_ref):
-    decay = damping_ref[pl.program_id(0)]
-    density = (first_ref[0, 0], first_ref[0, 1])
+def local_kernel(packs, second, me_ref, left_ref, count_ref, match_ref, damping_ref, hamiltonian_ref, *refs):
+    density_ref, refs = refs[0], refs[1:]
+    if second:
+        rho_ref, refs = refs[0], refs[1:]
+    out_ref, sends, sems = refs[0], refs[1:-1], refs[-1]
+    here, mats = pl.program_id(0), pl.num_programs(0)
+    copies = []
+    for exchange, send in zip(packs, sends):
+        slots = outgoing_slots(exchange, me_ref[0], mats, left_ref, count_ref, match_ref)
+        for place, slot in enumerate(slots):
+            copy = pltpu.make_async_copy(density_ref.at[0], send.at[place], sems.at[len(copies)])
+            copies.append((slot == here, copy))
+    for asked, copy in copies:
+        pl.when(asked)(copy.start)
+    decay = damping_ref[here]
+    density = (density_ref[0, 0], density_ref[0, 1])
     turned = commutator(density, split(hamiltonian_ref[...]))
     for part in range(2):
         slope = turned[part] - decay * density[part]
-        out_ref[0, part] = rho_ref[0, part] + STEP * density[part] + (0.5 * STEP * STEP) * slope
-
-
-def local_call(kernel, damping, hamiltonian, *densities):
+        if second:
+            slope = rho_ref[0, part] + STEP * density[part] + (0.5 * STEP * STEP) * slope
+        out_ref[0, part] = slope
+    for asked, copy in copies:
+        pl.when(asked)(copy.wait)
+
+
+def local_call(packs, pairs, tables, damping, hamiltonian, *densities):
     mats, _, order, _ = densities[0].shape
+    sent = sum(payload(e, pairs) for e in packs)
     block = pl.BlockSpec((1, 2, order, order), lambda n: (n, 0, 0, 0))
     return pl.pallas_call(
-        kernel,
+        functools.partial(local_kernel, packs, len(densities) == 2),
         grid=(mats,),
-        in_specs=[SMEM, pl.BlockSpec((order, order), lambda n: (0, 0))] + [block] * len(densities),
-        out_specs=block,
-        out_shape=jax.ShapeDtypeStruct(densities[0].shape, F32),
-        compiler_params=pltpu.CompilerParams(vmem_limit_bytes=32 * 1024 * 1024),
+        in_specs=[SMEM] * 5 + [pl.BlockSpec((order, order), lambda n: (0, 0))] + [block] * len(densities),
+        out_specs=[block] + [HBM] * len(packs),
+        out_shape=[jax.ShapeDtypeStruct(densities[0].shape, F32)]
+        + [jax.ShapeDtypeStruct((payload(e, pairs), 2, order, order), F32) for e in packs],
+        scratch_shapes=[pltpu.SemaphoreType.DMA((sent,))],
+        compiler_params=pltpu.CompilerParams(vmem_limit_bytes=GRANT),
         cost_estimate=pl.CostEstimate(
-            flops=mats * 24 * order**3, bytes_accessed=mats * 16 * order**2 * (1 + len(densities)), transcendentals=0
+            flops=mats * 24 * order**3,
+            bytes_accessed=(mats * (1 + len(densities)) + sent) * 8 * order**2,
+            transcendentals=0,
         ),
-    )(damping, hamiltonian, *densities)
-
-
-def rows_kernel(plan, packs, scale, refs_in, *refs):
+    )(*tables[:4], damping, hamiltonian, *densities)
+
+
+def rows_kernel(plan, packs, scale, *refs):
     me_ref, left_ref, count_ref, match_ref, left_root, match_root, bath_ref = refs[:7]
     couplings_ref = refs[7]
     arrivals = refs[8 : 8 + len(plan)]
@@ -190,16 +211,18 @@
             at = len(rows)
             lands.append(pltpu.make_async_copy(arrival.at[place], landed.at[at], land_sems.at[at]))
             rows.append(row)
-    for land in lands:
-        land.start()
-    for load in loads:
-        load.start()
-    for load in loads:
-        load.wait()
+    for (live, *_), land in zip(rows, lands):
+        when(live, land.start)
+    touched = []
+    for n in range(mats):
+        hits = [row[1] == n if row[0] is None else row[0] & (row[1] == n) for row in rows]
+        touched.append(None if packs else functools.reduce(jnp.logical_or, hits))
+        when(touched[n], loads[n].start)
+    for n in range(mats):
+        when(touched[n], loads[n].wait)
     for at, (live, target, mode, a, b) in enumerate(rows):
-        lands[at].wait()
-
         def add(at=at, target=target, mode=mode, a=a, b=b):
+            lands[at].wait()
             coupling = split(couplings_ref[mode])
             real, imag = split(landed[at, 0]), split(landed[at, 1])
             left_re, right_re = product(coupling, real), product(real, coupling)
@@ -209,17 +232,14 @@
             acc[target, 0] += scale * edge_im
             acc[target, 1] -= scale * edge_re
 
-        if live is None:
-            add()
-        else:
-            pl.when(live)(add)
+        when(live, add)
     stores = [pltpu.make_async_copy(acc.at[n], acc_out.at[n], acc_sems.at[n]) for n in range(mats)]
-    for store in stores:
-        store.start()
+    for n in range(mats):
+        when(touched[n], stores[n].start)
     if packs:
         pack(packs, mats, me_ref, left_ref, count_ref, match_ref, acc, sends, send_sems)
-    for store in stores:
-        store.wait()
+    for n in range(mats):
+        when(touched[n], stores[n].wait)
 
 
 def rows_call(plan, packs, pairs, scale, tables, couplings, arrivals, acc):
@@ -229,9 +249,9 @@
     shapes = [jax.ShapeDtypeStruct(acc.shape, F32)]
     shapes += [jax.ShapeDtypeStruct((payload(e, pairs), 2, order, order), F32) for e in packs]
     return pl.pallas_call(
-        functools.partial(rows_kernel, plan, packs, scale, None),
-        in_specs=[SMEM] * 7 + [VMEM] + [ANY] * (len(plan) + 1),
-        out_specs=[ANY] * len(shapes),
+        functools.partial(rows_kernel, plan, packs, scale),
+        in_specs=[SMEM] * 7 + [VMEM] + [HBM] * (len(plan) + 1),
+        out_specs=[HBM] * len(shapes),
         out_shape=shapes,
         input_output_aliases={8 + len(plan): 0},
         scratch_shapes=[
@@ -241,7 +261,7 @@
             pltpu.SemaphoreType.DMA((count,)),
             pltpu.SemaphoreType.DMA((max(sent, 1),)),
         ],
-        compiler_params=pltpu.CompilerParams(vmem_limit_bytes=32 * 1024 * 1024),
+        compiler_params=pltpu.CompilerParams(vmem_limit_bytes=GRANT),
         cost_estimate=pl.CostEstimate(
             flops=count * 24 * order**3, bytes_accessed=(count + 2 * mats + sent) * 8 * order**2, transcendentals=0
         ),
@@ -253,47 +273,44 @@
     sent = sum(payload(e, pairs) for e in plan)
     return pl.pallas_call(
         functools.partial(pack_kernel, plan, mats),
-        in_specs=[SMEM] * 4 + [ANY],
-        out_specs=[ANY] * len(plan),
+        in_specs=[SMEM] * 4 + [HBM],
+        out_specs=[HBM] * len(plan),
         out_shape=[jax.ShapeDtypeStruct((payload(e, pairs), 2, order, order), F32) for e in plan],
         scratch_shapes=[
             pltpu.VMEM(source.shape, F32),
             pltpu.SemaphoreType.DMA((mats,)),
             pltpu.SemaphoreType.DMA((sent,)),
         ],
-        compiler_params=pltpu.CompilerParams(vmem_limit_bytes=16 * 1024 * 1024),
+        compiler_params=pltpu.CompilerParams(vmem_limit_bytes=GRANT),
         cost_estimate=pl.CostEstimate(flops=0, bytes_accessed=sent * 16 * order**2, transcendentals=0),
     )(*tables[:4], source)
 
 
 def body(rho, hamiltonian, couplings, bath_coef, damping, match_edges, left_rows, left_count):
     colours, pairs = match_edges.shape[1:3]
-    plan = exchanges(lax.axis_size("tier"), colours)
+    swaps, shifts, far = exchanges(lax.axis_size("tier"), colours)
     me = lax.axis_index("tier").astype(jnp.int32)[None]
-    left_root = jnp.sqrt(left_rows[:, :, 4].astype(F32))
+    left_fields = jnp.transpose(left_rows, (2, 1, 0))
+    left_root = jnp.sqrt(left_fields[4].astype(F32))
     match_root = jnp.sqrt(match_edges[0, :, :, 4].astype(F32))
-    tables = (me, left_rows, left_count, match_edges, left_root, match_root, bath_coef)
-
-    cuts = [0]
-    for distance in (2, REACH - 1):
-        cuts.append(max(i + 1 for i, e in enumerate(plan) if e.step in (distance, e.size - distance)))
-    cuts.append(len(plan))
-    groups = [slice(a, b) for a, b in zip(cuts, cuts[1:]) if a < b]
-
-    def gather(sends, acc, scale, packs):
-        arrived = [e.permute(s) for e, s in zip(plan, sends)]
-        for group in groups:
-            last = group is groups[-1]
+    tables = (me, left_fields, left_count, match_edges, left_root, match_root, bath_coef.T)
+
+    def gather(near_sends, far_sends, acc, scale, packs):
+        sends = list(near_sends) + list(far_sends)
+        arrived = [e.permute(s) for e, s in zip(swaps + shifts + far, sends)]
+        for group in (swaps, shifts, far):
             got = rows_call(
-                plan[group], packs if last else [], pairs, scale, tables, couplings, arrived[group], acc
+                group, packs if group is far else [], pairs, scale, tables, couplings, arrived[: len(group)], acc
             )
-            acc = got[0]
+            acc, arrived = got[0], arrived[len(group) :]
         return acc, got[1:]
 
-    sends = pack_call(plan, pairs, tables, rho)
-    first, sends = gather(sends, local_call(first_local_kernel, damping, hamiltonian, rho), 1.0, plan)
-    base = local_call(second_local_kernel, damping, hamiltonian, first, rho)
-    return gather(sends, base, 0.5 * STEP * STEP, [])[0]
+    near = swaps + shifts
+    sends = pack_call(near, pairs, tables, rho)
+    base, *far_sends = local_call(far, pairs, tables, damping, hamiltonian, rho)
+    first, sends = gather(sends, far_sends, base, 1.0, near)
+    base, *far_sends = local_call(far, pairs, tables, damping, hamiltonian, first, rho)
+    return gather(sends, far_sends, base, 0.5 * STEP * STEP, [])[0]
 
 
 def solution(mesh):

time: 249 us -> 231 us (0.928)
  starting transfers between devices: 90.6 us -> 14.4 us
  waiting for transfers between devices: 83.5 us -> 146 us
  local copies, waits for them, and re-layouts: 19.4 us -> 5.33 us
  Pallas kernels: 54.1 us -> 60.9 us
    ppermute x18, starting transfers between devices: 90.6 us -> 14.4 us  [permute(): lax.ppermute(value, 'tier', [(i, self.peer(i, True)) for i in range(self....]
    ppermute x18, waiting for transfers between devices: 83.5 us -> 146 us  [permute(): lax.ppermute(value, 'tier', [(i, self.peer(i, True)) for i in range(self....]
    unnamed x46, local copies, waits for them, and re-layouts: 19.3 us -> 5.33 us
    pallas_call x8, Pallas kernels: 50 us -> 55.5 us  [the longest x6 33.5 us: rows_call(): pl.pallas_call(functools.partial(rows_kernel, plan, packs, scale), in_spe...]
  transfers between devices with their start and end apart: 18 -> 18, of which waited for: 8 -> 10; matrix products, arithmetic and copies ran while one was open for 0% -> 1% of each run, Pallas kernels for 15% -> 18%
where the time goes in v2:
time: 231 us; the launch traced here: 229 us
  waiting for transfers between devices  146 us (63%)
  Pallas kernels  60.9 us (26%)
  starting transfers between devices  14.4 us (6%)
  local copies, waits for them, and re-layouts  5.33 us (2%)
    ppermute x18, waiting for transfers between devices, permute(): lax.ppermute(value, 'tier', [(i, self.peer(i, True)) for i in range(self....  146 us
    pallas_call x6, Pallas kernels, rows_call(): pl.pallas_call(functools.partial(rows_kernel, plan, packs, scale), in_spe...  33.5 us
    pallas_call x2, Pallas kernels, local_call(): pl.pallas_call(functools.partial(local_kernel, packs, len(densities) == 2...  21.9 us
    ppermute x18, starting transfers between devices, permute(): lax.ppermute(value, 'tier', [(i, self.peer(i, True)) for i in range(self....  14.4 us
    pallas_call x1, Pallas kernels, pack_call(): pl.pallas_call(functools.partial(pack_kernel, plan, mats), in_specs=[SMEM...  5.42 us
    unnamed x46, local copies, waits for them, and re-layouts  5.33 us
  transfers between devices with their start and end apart: 18, of which 10 were waited for; matrix products, arithmetic and copies ran while one was open for 1% of the time, Pallas kernels for 18%

profile of v2, /device:TPU:13, one launch (start us, length us, event | category | flops | bytes accessed | tf_op | source)
XLA Modules:
  0.0 229.1 jit_solution(16259499316319483299)
XLA Ops:
  0.0 5.4 %shard_map.83 = (f32[2,2,256,256]{3,2,1,0:T(8,128)}, f32[2,2,256,256]{3,2,1,0:T(8,128)}, f32[1,2,256,256]{3,2,1,0:T(8,128)}, f32[1,2,256,256]{3,2,1,0:T(8,128)},...) custom-call(s32[1]{0:T(128)} %bitcast.me_ref.refs_0_, s32[5,6,16]{2,1,0:T(8,128)} %bitcast.6, s32[16]{0:T(128)} %refs_2_.11, ...), custom_call_target="tpu_custom_call" | custom-call | bytes 8388608 | tf_op jit(solution)/shard_map/pallas_call | solution.py:274
  6.4 1.5 collective-permute-start.3
  8.2 10.5 %shard_map.82 = (f32[8,2,256,256]{3,2,1,0:T(8,128)}, f32[1,2,256,256]{3,2,1,0:T(8,128)}, f32[2,2,256,256]{3,2,1,0:T(8,128)}, f32[1,2,256,256]{3,2,1,0:T(8,128)}) custom-call(s32[1]{0:T(128)} %bitcast.me_ref.refs_0_, s32[5,6,16]{2,1,0:T(8,128)} %bitcast.7, s32[16]{0:T(128)} %refs_2_.11, s32[1,4,1,5]{3,2,1,0:T(1,128)} %refs_3_.11, f32[8]{0:T(128)} %damping_ref.3, ...), custom_call_target="tpu_custom_call" | custom-call | flops 3221225472 | bytes 10485760 | tf_op jit(solution)/shard_map/pallas_call | solution.py:178
  18.8 24.0 %collective-permute-done.3.refs_8_ = f32[1,2,256,256]{3,2,1,0:T(8,128)S(1)} collective-permute-done((f32[1,2,256,256]{3,2,1,0:T(8,128)}, f32[1,2,256,256]{3,2,1,0:T(8,128)S(1)}, u32[]{:S(2)}, u32[]{:S(2)}) %collective-permute-start.3) | collective-permute-done | bytes 524320 | tf_op jit(solution)/shard_map/ppermute | solution.py:38
  42.8 1.5 collective-permute-start.6
  47.7 5.7 %shard_map.84.refs_12_ = f32[8,2,256,256]{3,2,1,0:T(8,128)} custom-call(s32[1]{0:T(128)} %bitcast.me_ref.refs_0_, s32[5,6,16]{2,1,0:T(8,128)} %bitcast.9, s32[16]{0:T(128)} %refs_2_.11, s32[1,4,1,5]{3,2,1,0:T(1,128)} %refs_3_.11, f32[6,16]{1,0:T(8,128)} %fusion.1.refs_4_, f32[4,1]{1,0:T(4,128)} %bitcast.16, ...), custom_call_target="tpu_custom_call", output_to_operand_aliasing={{}: (10, {})} | custom-call | flops 1610612736 | bytes 10485760 | tf_op jit(solution)/shard_map/pallas_call | solution.py:251
  53.4 4.1 %collective-permute-done.5.refs_10_ = f32[1,2,256,256]{3,2,1,0:T(8,128)S(1)} collective-permute-done((f32[1,2,256,256]{3,2,1,0:T(8,128)S(1)}, f32[1,2,256,256]{3,2,1,0:T(8,128)S(1)}, u32[]{:S(2)}, u32[]{:S(2)}) %collective-permute-start.5) | collective-permute-done | bytes 524320 | tf_op jit(solution)/shard_map/ppermute | solution.py:38
  57.5 9.3 %collective-permute-done.6.refs_11_ = f32[1,2,256,256]{3,2,1,0:T(8,128)S(1)} collective-permute-done((f32[1,2,256,256]{3,2,1,0:T(8,128)S(1)}, f32[1,2,256,256]{3,2,1,0:T(8,128)S(1)}, u32[]{:S(2)}, u32[]{:S(2)}) %collective-permute-start.6) | collective-permute-done | bytes 524320 | tf_op jit(solution)/shard_map/ppermute | solution.py:38
  67.6 4.1 %shard_map.85.refs_11_ = f32[8,2,256,256]{3,2,1,0:T(8,128)} custom-call(s32[1]{0:T(128)} %bitcast.me_ref.refs_0_, s32[5,6,16]{2,1,0:T(8,128)} %bitcast.10, s32[16]{0:T(128)} %refs_2_.11, s32[1,4,1,5]{3,2,1,0:T(1,128)} %refs_3_.11, f32[6,16]{1,0:T(8,128)} %fusion.1.refs_4_, f32[4,1]{1,0:T(4,128)} %bitcast.17, ...), custom_call_target="tpu_custom_call", output_to_operand_aliasing={{}: (12, {})} | custom-call | flops 1610612736 | bytes 10485760 | tf_op jit(solution)/shard_map/pallas_call | solution.py:251
  71.8 26.6 %collective-permute-done.refs_8_ = f32[1,2,256,256]{3,2,1,0:T(8,128)S(1)} collective-permute-done((f32[1,2,256,256]{3,2,1,0:T(8,128)}, f32[1,2,256,256]{3,2,1,0:T(8,128)S(1)}, u32[]{:S(2)}, u32[]{:S(2)}) %collective-permute-start) | collective-permute-done | bytes 524320 | tf_op jit(solution)/shard_map/ppermute | solution.py:38
  98.4 8.9 %collective-permute-done.2.refs_10_ = f32[1,2,256,256]{3,2,1,0:T(8,128)S(1)} collective-permute-done((f32[1,2,256,256]{3,2,1,0:T(8,128)}, f32[1,2,256,256]{3,2,1,0:T(8,128)S(1)}, u32[]{:S(2)}, u32[]{:S(2)}) %collective-permute-start.2) | collective-permute-done | bytes 524320 | tf_op jit(solution)/shard_map/ppermute | solution.py:38
  109.1 8.4 %shard_map.86 = (f32[8,2,256,256]{3,2,1,0:T(8,128)}, f32[2,2,256,256]{3,2,1,0:T(8,128)}, f32[2,2,256,256]{3,2,1,0:T(8,128)}, f32[1,2,256,256]{3,2,1,0:T(8,128)},...) custom-call(s32[1]{0:T(128)} %bitcast.me_ref.refs_0_, ...), custom_call_target="tpu_custom_call", output_to_operand_aliasing={{0}: (11, {})} | custom-call | flops 1610612736 | bytes 14680064 | tf_op jit(solution)/shard_map/pallas_call | solution.py:251
  117.5 2.4 %collective-permute-start.16 = (f32[2,2,256,256]{3,2,1,0:T(8,128)}, f32[2,2,256,256]{3,2,1,0:T(8,128)S(1)}, u32[]{:S(2)}, u32[]{:S(2)}) collective-permute-start(f32[2,2,256,256]{3,2,1,0:T(8,128)} %get-tuple-element.44), channel_id=1, source_target_pairs={{0,1},{1,0},{2,3},{3,2},{4,5},{5,4},{6,7},{7,6},{8,9},{9,8},{10,11... | collective-permute-start | bytes 3145736 | tf_op jit(solution)/shard_map/ppermute | solution.py:38
  120.8 1.8 collective-permute-start.12
  122.6 11.4 %shard_map.87 = (f32[8,2,256,256]{3,2,1,0:T(8,128)}, f32[1,2,256,256]{3,2,1,0:T(8,128)}, f32[2,2,256,256]{3,2,1,0:T(8,128)}, f32[1,2,256,256]{3,2,1,0:T(8,128)}) custom-call(s32[1]{0:T(128)} %bitcast.me_ref.refs_0_, s32[5,6,16]{2,1,0:T(8,128)} %bitcast.12, s32[16]{0:T(128)} %refs_2_.11, s32[1,4,1,5]{3,2,1,0:T(1,128)} %refs_3_.11, f32[8]{0:T(128)} %damping_ref.3, ...), custom_call_target="tpu_custom_call" | custom-call | flops 3221225472 | bytes 14680064 | tf_op jit(solution)/shard_map/pallas_call | solution.py:178
  134.3 22.3 %collective-permute-done.12.refs_8_ = f32[1,2,256,256]{3,2,1,0:T(8,128)S(1)} collective-permute-done((f32[1,2,256,256]{3,2,1,0:T(8,128)}, f32[1,2,256,256]{3,2,1,0:T(8,128)S(1)}, u32[]{:S(2)}, u32[]{:S(2)}) %collective-permute-start.12) | collective-permute-done | bytes 524320 | tf_op jit(solution)/shard_map/ppermute | solution.py:38
  156.7 2.1 collective-permute-start.15
  160.1 5.9 %shard_map.88.refs_12_ = f32[8,2,256,256]{3,2,1,0:T(8,128)} custom-call(s32[1]{0:T(128)} %bitcast.me_ref.refs_0_, s32[5,6,16]{2,1,0:T(8,128)} %bitcast.13, s32[16]{0:T(128)} %refs_2_.11, s32[1,4,1,5]{3,2,1,0:T(1,128)} %refs_3_.11, f32[6,16]{1,0:T(8,128)} %fusion.1.refs_4_, f32[4,1]{1,0:T(4,128)} %bitcast.19, ...), custom_call_target="tpu_custom_call", output_to_operand_aliasing={{}: (10, {})} | custom-call | flops 1610612736 | bytes 10485760 | tf_op jit(solution)/shard_map/pallas_call | solution.py:251
  166.0 5.3 %collective-permute-done.14.refs_10_ = f32[1,2,256,256]{3,2,1,0:T(8,128)S(1)} collective-permute-done((f32[1,2,256,256]{3,2,1,0:T(8,128)S(1)}, f32[1,2,256,256]{3,2,1,0:T(8,128)S(1)}, u32[]{:S(2)}, u32[]{:S(2)}) %collective-permute-start.14) | collective-permute-done | bytes 524320 | tf_op jit(solution)/shard_map/ppermute | solution.py:38
  171.3 29.5 %collective-permute-done.15.refs_11_ = f32[1,2,256,256]{3,2,1,0:T(8,128)S(1)} collective-permute-done((f32[1,2,256,256]{3,2,1,0:T(8,128)S(1)}, f32[1,2,256,256]{3,2,1,0:T(8,128)S(1)}, u32[]{:S(2)}, u32[]{:S(2)}) %collective-permute-start.15) | collective-permute-done | bytes 524320 | tf_op jit(solution)/shard_map/ppermute | solution.py:38
  201.6 4.1 %shard_map.89.refs_11_ = f32[8,2,256,256]{3,2,1,0:T(8,128)} custom-call(s32[1]{0:T(128)} %bitcast.me_ref.refs_0_, s32[5,6,16]{2,1,0:T(8,128)} %bitcast.14, s32[16]{0:T(128)} %refs_2_.11, s32[1,4,1,5]{3,2,1,0:T(1,128)} %refs_3_.11, f32[6,16]{1,0:T(8,128)} %fusion.1.refs_4_, f32[4,1]{1,0:T(4,128)} %bitcast.20, ...), custom_call_target="tpu_custom_call", output_to_operand_aliasing={{}: (12, {})} | custom-call | flops 1610612736 | bytes 10485760 | tf_op jit(solution)/shard_map/pallas_call | solution.py:251
  205.7 7.2 %collective-permute-done.9.refs_8_ = f32[1,2,256,256]{3,2,1,0:T(8,128)S(1)} collective-permute-done((f32[1,2,256,256]{3,2,1,0:T(8,128)}, f32[1,2,256,256]{3,2,1,0:T(8,128)S(1)}, u32[]{:S(2)}, u32[]{:S(2)}) %collective-permute-start.9) | collective-permute-done | bytes 524320 | tf_op jit(solution)/shard_map/ppermute | solution.py:38
  212.9 9.1 %collective-permute-done.11.refs_10_ = f32[1,2,256,256]{3,2,1,0:T(8,128)S(1)} collective-permute-done((f32[1,2,256,256]{3,2,1,0:T(8,128)}, f32[1,2,256,256]{3,2,1,0:T(8,128)S(1)}, u32[]{:S(2)}, u32[]{:S(2)}) %collective-permute-start.11) | collective-permute-done | bytes 524320 | tf_op jit(solution)/shard_map/ppermute | solution.py:38
  223.8 5.2 %shard_map.90 = f32[8,2,256,256]{3,2,1,0:T(8,128)} custom-call(s32[1]{0:T(128)} %bitcast.me_ref.refs_0_, s32[5,6,16]{2,1,0:T(8,128)} %bitcast.15, s32[16]{0:T(128)} %refs_2_.11, s32[1,4,1,5]{3,2,1,0:T(1,128)} %refs_3_.11, f32[6,16]{1,0:T(8,128)} %fusion.1.refs_4_, f32[4,1]{1,0:T(4,128)} %bitcast.21, ...), custom_call_target="tpu_custom_call", output_to_operand_aliasing={{}: (11, {})} | custom-call | flops 1610612736 | bytes 10485760 | tf_op jit(solution)/shard_map/pallas_call | solution.py:251
  (69 shorter events, 12.4 us)
Async XLA Ops:
  5.4 40.2 %collective-permute-start.7 = (f32[2,2,256,256]{3,2,1,0:T(8,128)}, f32[2,2,256,256]{3,2,1,0:T(8,128)S(1)}, u32[]{:S(2)}, u32[]{:S(2)}) collective-permute-start(f32[2,2,256,256]{3,2,1,0:T(8,128)} %get-tuple-element.33), channel_id=1, source_target_pairs={{0,1},{1,0},{2,3},{3,2},{4,5},{5,4},{6,7},{7,6},{8,9},{9,8},{10,11... | collective-permute-start | bytes 3145736 | tf_op jit(solution)/shard_map/ppermute | solution.py:38
  6.2 40.4 %collective-permute-start.8 = (f32[2,2,256,256]{3,2,1,0:T(8,128)}, f32[2,2,256,256]{3,2,1,0:T(8,128)S(1)}, u32[]{:S(2)}, u32[]{:S(2)}) collective-permute-start(f32[2,2,256,256]{3,2,1,0:T(8,128)} %get-tuple-element.34), channel_id=1, source_target_pairs={{0,2},{1,3},{2,0},{3,1},{4,6},{5,7},{6,4},{7,5},{8,10},{9,11},{10,... | collective-permute-start | bytes 3145736 | tf_op jit(solution)/shard_map/ppermute | solution.py:38
  6.4 36.4 %collective-permute-start.3 = (f32[1,2,256,256]{3,2,1,0:T(8,128)}, f32[1,2,256,256]{3,2,1,0:T(8,128)S(1)}, u32[]{:S(2)}, u32[]{:S(2)}) collective-permute-start(f32[1,2,256,256]{3,2,1,0:T(8,128)} %get-tuple-element.29), channel_id=1, source_target_pairs={{0,3},{1,4},{2,5},{3,6},{4,7},{5,8},{6,9},{7,10},{8,11},{9,12},{10... | collective-permute-start | bytes 1572872 | tf_op jit(solution)/shard_map/ppermute | solution.py:38
  7.9 34.9 %copy-start.22 = (f32[1,2,256,256]{3,2,1,0:T(8,128)S(1)}, f32[1,2,256,256]{3,2,1,0:T(8,128)}, u32[]{:S(2)}) copy-start(f32[1,2,256,256]{3,2,1,0:T(8,128)} %get-tuple-element.31) | copy-start | bytes 1572868
  7.9 34.9 %copy-start.20 = (f32[1,2,256,256]{3,2,1,0:T(8,128)S(1)}, f32[1,2,256,256]{3,2,1,0:T(8,128)}, u32[]{:S(2)}) copy-start(f32[1,2,256,256]{3,2,1,0:T(8,128)} %get-tuple-element.32) | copy-start | bytes 1572868
  7.9 39.1 %copy-start.18 = (s32[1,4,1,5]{3,2,1,0:T(1,128)S(1)}, s32[1,4,1,5]{3,2,1,0:T(1,128)}, u32[]{:S(2)}) copy-start(s32[1,4,1,5]{3,2,1,0:T(1,128)} %refs_3_.11) | copy-start | bytes 244
  7.9 34.9 %collective-permute-start.4 = (f32[1,2,256,256]{3,2,1,0:T(8,128)}, f32[1,2,256,256]{3,2,1,0:T(8,128)S(1)}, u32[]{:S(2)}, u32[]{:S(2)}) collective-permute-start(f32[1,2,256,256]{3,2,1,0:T(8,128)} %get-tuple-element.30), channel_id=1, source_target_pairs={{0,13},{1,14},{2,15},{3,0},{4,1},{5,2},{6,3},{7,4},{8,5},{9,6},{10... | collective-permute-start | bytes 1572872 | tf_op jit(solution)/shard_map/ppermute | solution.py:38
  18.7 88.6 %collective-permute-start.1 = (f32[2,2,256,256]{3,2,1,0:T(8,128)}, f32[2,2,256,256]{3,2,1,0:T(8,128)S(1)}, u32[]{:S(2)}, u32[]{:S(2)}) collective-permute-start(f32[2,2,256,256]{3,2,1,0:T(8,128)} %get-tuple-element.27), channel_id=1, source_target_pairs={{0,4},{1,5},{2,6},{3,7},{4,0},{5,1},{6,2},{7,3},{8,12},{9,13},{10,... | collective-permute-start | bytes 3145736 | tf_op jit(solution)/shard_map/ppermute | solution.py:38
  42.8 14.7 %collective-permute-start.5 = (f32[1,2,256,256]{3,2,1,0:T(8,128)S(1)}, f32[1,2,256,256]{3,2,1,0:T(8,128)S(1)}, u32[]{:S(2)}, u32[]{:S(2)}) collective-permute-start(f32[1,2,256,256]{3,2,1,0:T(8,128)S(1)} %copy-done.22), channel_id=1, source_target_pairs={{0,14},{1,15},{2,4},{3,5},{4,2},{5,3},{6,8},{7,9},{8,6},{9,7},{10,... | collective-permute-start | bytes 1572872 | tf_op jit(solution)/shard_map/ppermute | solution.py:38
  42.8 23.9 %collective-permute-start.6 = (f32[1,2,256,256]{3,2,1,0:T(8,128)S(1)}, f32[1,2,256,256]{3,2,1,0:T(8,128)S(1)}, u32[]{:S(2)}, u32[]{:S(2)}) collective-permute-start(f32[1,2,256,256]{3,2,1,0:T(8,128)S(1)} %copy-done.20), channel_id=1, source_target_pairs={{0,15},{1,2},{2,1},{3,4},{4,3},{5,6},{6,5},{7,8},{8,7},{9,10},{10,... | collective-permute-start | bytes 1572872 | tf_op jit(solution)/shard_map/ppermute | solution.py:38
  45.6 52.8 %collective-permute-start = (f32[1,2,256,256]{3,2,1,0:T(8,128)}, f32[1,2,256,256]{3,2,1,0:T(8,128)S(1)}, u32[]{:S(2)}, u32[]{:S(2)}) collective-permute-start(f32[1,2,256,256]{3,2,1,0:T(8,128)} %get-tuple-element.26), channel_id=1, source_target_pairs={{0,8},{1,9},{2,10},{3,11},{4,12},{5,13},{6,14},{7,15},{8,0},{9,1},... | collective-permute-start | bytes 1572872 | tf_op jit(solution)/shard_map/ppermute | solution.py:38
  46.6 60.7 %collective-permute-start.2 = (f32[1,2,256,256]{3,2,1,0:T(8,128)}, f32[1,2,256,256]{3,2,1,0:T(8,128)S(1)}, u32[]{:S(2)}, u32[]{:S(2)}) collective-permute-start(f32[1,2,256,256]{3,2,1,0:T(8,128)} %get-tuple-element.28), channel_id=1, source_target_pairs={{0,12},{1,13},{2,14},{3,15},{4,8},{5,9},{6,10},{7,11},{8,4},{9,5},... | collective-permute-start | bytes 1572872 | tf_op jit(solution)/shard_map/ppermute | solution.py:38
  117.5 41.2 %collective-permute-start.16 = (f32[2,2,256,256]{3,2,1,0:T(8,128)}, f32[2,2,256,256]{3,2,1,0:T(8,128)S(1)}, u32[]{:S(2)}, u32[]{:S(2)}) collective-permute-start(f32[2,2,256,256]{3,2,1,0:T(8,128)} %get-tuple-element.44), channel_id=1, source_target_pairs={{0,1},{1,0},{2,3},{3,2},{4,5},{5,4},{6,7},{7,6},{8,9},{9,8},{10,11... | collective-permute-start | bytes 3145736 | tf_op jit(solution)/shard_map/ppermute | solution.py:38
  120.0 38.8 %collective-permute-start.17 = (f32[2,2,256,256]{3,2,1,0:T(8,128)}, f32[2,2,256,256]{3,2,1,0:T(8,128)S(1)}, u32[]{:S(2)}, u32[]{:S(2)}) collective-permute-start(f32[2,2,256,256]{3,2,1,0:T(8,128)} %get-tuple-element.45), channel_id=1, source_target_pairs={{0,2},{1,3},{2,0},{3,1},{4,6},{5,7},{6,4},{7,5},{8,10},{9,11},{10,... | collective-permute-start | bytes 3145736 | tf_op jit(solution)/shard_map/ppermute | solution.py:38
  120.8 35.8 %collective-permute-start.12 = (f32[1,2,256,256]{3,2,1,0:T(8,128)}, f32[1,2,256,256]{3,2,1,0:T(8,128)S(1)}, u32[]{:S(2)}, u32[]{:S(2)}) collective-permute-start(f32[1,2,256,256]{3,2,1,0:T(8,128)} %get-tuple-element.40), channel_id=1, source_target_pairs={{0,3},{1,4},{2,5},{3,6},{4,7},{5,8},{6,9},{7,10},{8,11},{9,12},{10... | collective-permute-start | bytes 1572872 | tf_op jit(solution)/shard_map/ppermute | solution.py:38
  122.6 34.0 %collective-permute-start.13 = (f32[1,2,256,256]{3,2,1,0:T(8,128)}, f32[1,2,256,256]{3,2,1,0:T(8,128)S(1)}, u32[]{:S(2)}, u32[]{:S(2)}) collective-permute-start(f32[1,2,256,256]{3,2,1,0:T(8,128)} %get-tuple-element.41), channel_id=1, source_target_pairs={{0,13},{1,14},{2,15},{3,0},{4,1},{5,2},{6,3},{7,4},{8,5},{9,6},{10... | collective-permute-start | bytes 1572872 | tf_op jit(solution)/shard_map/ppermute | solution.py:38
  122.6 34.1 %copy-start.19 = (f32[1,2,256,256]{3,2,1,0:T(8,128)S(1)}, f32[1,2,256,256]{3,2,1,0:T(8,128)}, u32[]{:S(2)}) copy-start(f32[1,2,256,256]{3,2,1,0:T(8,128)} %get-tuple-element.43) | copy-start | bytes 1572868
  134.0 88.0 %collective-permute-start.10 = (f32[2,2,256,256]{3,2,1,0:T(8,128)}, f32[2,2,256,256]{3,2,1,0:T(8,128)S(1)}, u32[]{:S(2)}, u32[]{:S(2)}) collective-permute-start(f32[2,2,256,256]{3,2,1,0:T(8,128)} %get-tuple-element.38), channel_id=1, source_target_pairs={{0,4},{1,5},{2,6},{3,7},{4,0},{5,1},{6,2},{7,3},{8,12},{9,13},{10,... | collective-permute-start | bytes 3145736 | tf_op jit(solution)/shard_map/ppermute | solution.py:38
  156.6 44.2 %copy-start.7 = (f32[1,2,256,256]{3,2,1,0:T(8,128)}, f32[1,2,256,256]{3,2,1,0:T(8,128)S(1)}, u32[]{:S(2)}) copy-start(f32[1,2,256,256]{3,2,1,0:T(8,128)S(1)} %collective-permute-done.12.refs_8_) | copy-start | bytes 1572868
  156.6 14.7 %collective-permute-start.14 = (f32[1,2,256,256]{3,2,1,0:T(8,128)S(1)}, f32[1,2,256,256]{3,2,1,0:T(8,128)S(1)}, u32[]{:S(2)}, u32[]{:S(2)}) collective-permute-start(f32[1,2,256,256]{3,2,1,0:T(8,128)S(1)} %copy-done.21), channel_id=1, source_target_pairs={{0,14},{1,15},{2,4},{3,5},{4,2},{5,3},{6,8},{7,9},{8,6},{9,7},{10,... | collective-permute-start | bytes 1572872 | tf_op jit(solution)/shard_map/ppermute | solution.py:38
  156.6 44.2 %copy-start.9 = (f32[1,2,256,256]{3,2,1,0:T(8,128)}, f32[1,2,256,256]{3,2,1,0:T(8,128)S(1)}, u32[]{:S(2)}) copy-start(f32[1,2,256,256]{3,2,1,0:T(8,128)S(1)} %collective-permute-done.13.refs_9_) | copy-start | bytes 1572868
  156.7 44.1 %collective-permute-start.15 = (f32[1,2,256,256]{3,2,1,0:T(8,128)S(1)}, f32[1,2,256,256]{3,2,1,0:T(8,128)S(1)}, u32[]{:S(2)}, u32[]{:S(2)}) collective-permute-start(f32[1,2,256,256]{3,2,1,0:T(8,128)S(1)} %copy-done.19), channel_id=1, source_target_pairs={{0,15},{1,2},{2,1},{3,4},{4,3},{5,6},{6,5},{7,8},{8,7},{9,10},{10,... | collective-permute-start | bytes 1572872 | tf_op jit(solution)/shard_map/ppermute | solution.py:38
  158.8 54.1 %collective-permute-start.9 = (f32[1,2,256,256]{3,2,1,0:T(8,128)}, f32[1,2,256,256]{3,2,1,0:T(8,128)S(1)}, u32[]{:S(2)}, u32[]{:S(2)}) collective-permute-start(f32[1,2,256,256]{3,2,1,0:T(8,128)} %get-tuple-element.37), channel_id=1, source_target_pairs={{0,8},{1,9},{2,10},{3,11},{4,12},{5,13},{6,14},{7,15},{8,0},{9,1},... | collective-permute-start | bytes 1572872 | tf_op jit(solution)/shard_map/ppermute | solution.py:38
  158.8 63.2 %collective-permute-start.11 = (f32[1,2,256,256]{3,2,1,0:T(8,128)}, f32[1,2,256,256]{3,2,1,0:T(8,128)S(1)}, u32[]{:S(2)}, u32[]{:S(2)}) collective-permute-start(f32[1,2,256,256]{3,2,1,0:T(8,128)} %get-tuple-element.39), channel_id=1, source_target_pairs={{0,12},{1,13},{2,14},{3,15},{4,8},{5,9},{6,10},{7,11},{8,4},{9,5},... | collective-permute-start | bytes 1572872 | tf_op jit(solution)/shard_map/ppermute | solution.py:38
  (17 other events, 149.8 us)

commit v3 on v2

--- a/solution.py
+++ b/solution.py
@@ -11,9 +11,9 @@
 STEP = 0.1
 F32, BF16 = jnp.float32, jnp.bfloat16
 SMEM = pl.BlockSpec(memory_space=pltpu.SMEM)
-VMEM = pl.BlockSpec(memory_space=pltpu.VMEM)
 HBM = pl.BlockSpec(memory_space=pltpu.HBM)
-GRANT = 56 * 1024 * 1024
+ANY = pl.BlockSpec(memory_space=pl.ANY)
+GRANT = 48 * 1024 * 1024
 
 
 class Exchange:
@@ -117,24 +117,22 @@
 
 
 def pack_kernel(plan, mats, me_ref, left_ref, count_ref, match_ref, source, *rest):
-    sends, (held, load_sems, sems) = rest[:-3], rest[-3:]
-    loads = [pltpu.make_async_copy(source.at[n], held.at[n], load_sems.at[n]) for n in range(mats)]
-    for load in loads:
-        load.start()
-    for load in loads:
-        load.wait()
-    pack(plan, mats, me_ref, left_ref, count_ref, match_ref, held, sends, sems)
-
-
-def pack(plan, mats, me_ref, left_ref, count_ref, match_ref, source, sends, sems):
-    copies = []
+    rest, (held, load_sems, sems) = rest[:-3], rest[-3:]
+    sends = rest[len(rest) - len(plan) :]
+    loads, stores = [], []
     for exchange, send in zip(plan, sends):
         slots = outgoing_slots(exchange, me_ref[0], mats, left_ref, count_ref, match_ref)
         for place, slot in enumerate(slots):
-            copies.append(pltpu.make_async_copy(source.at[slot], send.at[place], sems.at[len(copies)]))
-            copies[-1].start()
-    for copy in copies:
-        copy.wait()
+            at = len(loads)
+            loads.append(pltpu.make_async_copy(source.at[slot], held.at[at], load_sems.at[at]))
+            stores.append(pltpu.make_async_copy(held.at[at], send.at[place], sems.at[at]))
+    for load in loads:
+        load.start()
+    for load, store in zip(loads, stores):
+        load.wait()
+        store.start()
+    for store in stores:
+        store.wait()
 
 
 def commutator(density, hamiltonian):
@@ -145,99 +143,105 @@
     return parts[1], -parts[0]
 
 
-def local_kernel(packs, second, me_ref, left_ref, count_ref, match_ref, damping_ref, hamiltonian_ref, *refs):
-    density_ref, refs = refs[0], refs[1:]
-    if second:
-        rho_ref, refs = refs[0], refs[1:]
-    out_ref, sends, sems = refs[0], refs[1:-1], refs[-1]
-    here, mats = pl.program_id(0), pl.num_programs(0)
-    copies = []
-    for exchange, send in zip(packs, sends):
-        slots = outgoing_slots(exchange, me_ref[0], mats, left_ref, count_ref, match_ref)
-        for place, slot in enumerate(slots):
-            copy = pltpu.make_async_copy(density_ref.at[0], send.at[place], sems.at[len(copies)])
-            copies.append((slot == here, copy))
-    for asked, copy in copies:
-        pl.when(asked)(copy.start)
-    decay = damping_ref[here]
+def local_kernel(second, damping_ref, hamiltonian_ref, density_ref, *refs):
+    out_ref = refs[-1]
+    decay = damping_ref[pl.program_id(0)]
     density = (density_ref[0, 0], density_ref[0, 1])
     turned = commutator(density, split(hamiltonian_ref[...]))
     for part in range(2):
         slope = turned[part] - decay * density[part]
         if second:
-            slope = rho_ref[0, part] + STEP * density[part] + (0.5 * STEP * STEP) * slope
+            slope = refs[0][0, part] + STEP * density[part] + (0.5 * STEP * STEP) * slope
         out_ref[0, part] = slope
-    for asked, copy in copies:
-        pl.when(asked)(copy.wait)
-
-
-def local_call(packs, pairs, tables, damping, hamiltonian, *densities):
+
+
+def local_call(damping, hamiltonian, *densities):
     mats, _, order, _ = densities[0].shape
-    sent = sum(payload(e, pairs) for e in packs)
     block = pl.BlockSpec((1, 2, order, order), lambda n: (n, 0, 0, 0))
     return pl.pallas_call(
-        functools.partial(local_kernel, packs, len(densities) == 2),
+        functools.partial(local_kernel, len(densities) == 2),
         grid=(mats,),
-        in_specs=[SMEM] * 5 + [pl.BlockSpec((order, order), lambda n: (0, 0))] + [block] * len(densities),
-        out_specs=[block] + [HBM] * len(packs),
-        out_shape=[jax.ShapeDtypeStruct(densities[0].shape, F32)]
-        + [jax.ShapeDtypeStruct((payload(e, pairs), 2, order, order), F32) for e in packs],
-        scratch_shapes=[pltpu.SemaphoreType.DMA((sent,))],
+        in_specs=[SMEM, pl.BlockSpec((order, order), lambda n: (0, 0))] + [block] * len(densities),
+        out_specs=block,
+        out_shape=jax.ShapeDtypeStruct(densities[0].shape, F32),
         compiler_params=pltpu.CompilerParams(vmem_limit_bytes=GRANT),
         cost_estimate=pl.CostEstimate(
-            flops=mats * 24 * order**3,
-            bytes_accessed=(mats * (1 + len(densities)) + sent) * 8 * order**2,
-            transcendentals=0,
+            flops=mats * 24 * order**3, bytes_accessed=mats * (1 + len(densities)) * 8 * order**2, transcendentals=0
         ),
-    )(*tables[:4], damping, hamiltonian, *densities)
+    )(damping, hamiltonian, *densities)
 
 
 def rows_kernel(plan, packs, scale, *refs):
-    me_ref, left_ref, count_ref, match_ref, left_root, match_root, bath_ref = refs[:7]
-    couplings_ref = refs[7]
+    me_ref, left_ref, count_ref, match_ref, left_root, match_root, bath_ref, couplings_ref = refs[:8]
     arrivals = refs[8 : 8 + len(plan)]
     acc_in = refs[8 + len(plan)]
     rest = refs[9 + len(plan) :]
     acc_out, sends = rest[0], rest[1 : 1 + len(packs)]
-    acc, landed, acc_sems, land_sems, send_sems = rest[1 + len(packs) :]
-    mats = acc.shape[0]
-    loads = [pltpu.make_async_copy(acc_in.at[n], acc.at[n], acc_sems.at[n]) for n in range(mats)]
-    rows, lands = [], []
+    acc, landed, chosen, acc_sems, land_sems, mode_sems, send_sems = rest[1 + len(packs) :]
+    mats, me = acc.shape[0], me_ref[0]
+    rows, lands, modes = [], [], []
     for exchange, arrival in zip(plan, arrivals):
-        found = incoming_rows(
-            exchange, me_ref[0], mats, left_ref, count_ref, match_ref, left_root, match_root, bath_ref
-        )
+        found = incoming_rows(exchange, me, mats, left_ref, count_ref, match_ref, left_root, match_root, bath_ref)
         for place, row in enumerate(found):
             at = len(rows)
             lands.append(pltpu.make_async_copy(arrival.at[place], landed.at[at], land_sems.at[at]))
+            modes.append(pltpu.make_async_copy(couplings_ref.at[row[2]], chosen.at[at], mode_sems.at[at]))
             rows.append(row)
-    for (live, *_), land in zip(rows, lands):
+    for (live, *_), land, mode in zip(rows, lands, modes):
         when(live, land.start)
-    touched = []
+        when(live, mode.start)
+
+    def touches(n):
+        return functools.reduce(
+            jnp.logical_or, [row[1] == n if row[0] is None else row[0] & (row[1] == n) for row in rows]
+        )
+
+    touched = [touches(n) for n in range(mats)]
+    loads = [pltpu.make_async_copy(acc_in.at[n], acc.at[n], acc_sems.at[n]) for n in range(mats)]
+    stores = [pltpu.make_async_copy(acc.at[n], acc_out.at[n], acc_sems.at[n]) for n in range(mats)]
     for n in range(mats):
-        hits = [row[1] == n if row[0] is None else row[0] & (row[1] == n) for row in rows]
-        touched.append(None if packs else functools.reduce(jnp.logical_or, hits))
-        when(touched[n], loads[n].start)
-    for n in range(mats):
-        when(touched[n], loads[n].wait)
-    for at, (live, target, mode, a, b) in enumerate(rows):
-        def add(at=at, target=target, mode=mode, a=a, b=b):
+        when(None if packs else touched[n], loads[n].start)
+
+    def loaded():
+        for n in range(mats):
+            when(None if packs else touched[n], loads[n].wait)
+        for untouched, copy in early:
+            when(untouched, copy.start)
+
+    early, late, copies = [], [], []
+    for exchange, send in zip(packs, sends):
+        slots = outgoing_slots(exchange, me, mats, left_ref, count_ref, match_ref)
+        for place, slot in enumerate(slots):
+            copy = pltpu.make_async_copy(acc.at[slot], send.at[place], send_sems.at[len(copies)])
+            busy = touches(slot)
+            copies.append(copy)
+            late.append((busy, copy))
+            early.append((jnp.logical_not(busy), copy))
+    if rows[0][0] is not None:
+        loaded()
+    for at, (live, target, _, a, b) in enumerate(rows):
+
+        def add(at=at, target=target, a=a, b=b, first=at == 0 and live is None):
+            modes[at].wait()
             lands[at].wait()
-            coupling = split(couplings_ref[mode])
+            coupling = split(chosen[at])
             real, imag = split(landed[at, 0]), split(landed[at, 1])
             left_re, right_re = product(coupling, real), product(real, coupling)
             left_im, right_im = product(coupling, imag), product(imag, coupling)
             edge_re = a * (left_re - right_re) - b * (left_im + right_im)
             edge_im = a * (left_im - right_im) + b * (left_re + right_re)
+            if first:
+                loaded()
             acc[target, 0] += scale * edge_im
             acc[target, 1] -= scale * edge_re
 
         when(live, add)
-    stores = [pltpu.make_async_copy(acc.at[n], acc_out.at[n], acc_sems.at[n]) for n in range(mats)]
+    for busy, copy in late:
+        when(busy, copy.start)
     for n in range(mats):
         when(touched[n], stores[n].start)
-    if packs:
-        pack(packs, mats, me_ref, left_ref, count_ref, match_ref, acc, sends, send_sems)
+    for copy in copies:
+        copy.wait()
     for n in range(mats):
         when(touched[n], stores[n].wait)
 
@@ -250,14 +254,16 @@
     shapes += [jax.ShapeDtypeStruct((payload(e, pairs), 2, order, order), F32) for e in packs]
     return pl.pallas_call(
         functools.partial(rows_kernel, plan, packs, scale),
-        in_specs=[SMEM] * 7 + [VMEM] + [HBM] * (len(plan) + 1),
+        in_specs=[SMEM] * 7 + [HBM] + [ANY] * len(plan) + [HBM],
         out_specs=[HBM] * len(shapes),
         out_shape=shapes,
         input_output_aliases={8 + len(plan): 0},
         scratch_shapes=[
             pltpu.VMEM((mats, 2, order, order), F32),
             pltpu.VMEM((count, 2, order, order), F32),
+            pltpu.VMEM((count, order, order), F32),
             pltpu.SemaphoreType.DMA((mats,)),
+            pltpu.SemaphoreType.DMA((count,)),
             pltpu.SemaphoreType.DMA((count,)),
             pltpu.SemaphoreType.DMA((max(sent, 1),)),
         ],
@@ -268,22 +274,22 @@
     )(*tables, couplings, *arrivals, acc)
 
 
-def pack_call(plan, pairs, tables, source):
+def pack_call(plan, pairs, tables, source, *after):
     mats, _, order, _ = source.shape
     sent = sum(payload(e, pairs) for e in plan)
     return pl.pallas_call(
         functools.partial(pack_kernel, plan, mats),
-        in_specs=[SMEM] * 4 + [HBM],
+        in_specs=[SMEM] * 4 + [HBM] + [ANY] * len(after),
         out_specs=[HBM] * len(plan),
         out_shape=[jax.ShapeDtypeStruct((payload(e, pairs), 2, order, order), F32) for e in plan],
         scratch_shapes=[
-            pltpu.VMEM(source.shape, F32),
-            pltpu.SemaphoreType.DMA((mats,)),
+            pltpu.VMEM((sent, 2, order, order), F32),
+            pltpu.SemaphoreType.DMA((sent,)),
             pltpu.SemaphoreType.DMA((sent,)),
         ],
         compiler_params=pltpu.CompilerParams(vmem_limit_bytes=GRANT),
         cost_estimate=pl.CostEstimate(flops=0, bytes_accessed=sent * 16 * order**2, transcendentals=0),
-    )(*tables[:4], source)
+    )(*tables[:4], source, *after)
 
 
 def body(rho, hamiltonian, couplings, bath_coef, damping, match_edges, left_rows, left_count):
@@ -295,9 +301,12 @@
     match_root = jnp.sqrt(match_edges[0, :, :, 4].astype(F32))
     tables = (me, left_fields, left_count, match_edges, left_root, match_root, bath_coef.T)
 
-    def gather(near_sends, far_sends, acc, scale, packs):
-        sends = list(near_sends) + list(far_sends)
-        arrived = [e.permute(s) for e, s in zip(swaps + shifts + far, sends)]
+    near = swaps + shifts
+
+    def gather(density, near_sends, acc, scale, packs):
+        arrived = [e.permute(s) for e, s in zip(near, near_sends)]
+        far_sends = pack_call(far, pairs, tables, density, *arrived[: len(swaps)])
+        arrived += [e.permute(s) for e, s in zip(far, far_sends)]
         for group in (swaps, shifts, far):
             got = rows_call(
                 group, packs if group is far else [], pairs, scale, tables, couplings, arrived[: len(group)], acc
@@ -305,12 +314,9 @@
             acc, arrived = got[0], arrived[len(group) :]
         return acc, got[1:]
 
-    near = swaps + shifts
     sends = pack_call(near, pairs, tables, rho)
-    base, *far_sends = local_call(far, pairs, tables, damping, hamiltonian, rho)
-    first, sends = gather(sends, far_sends, base, 1.0, near)
-    base, *far_sends = local_call(far, pairs, tables, damping, hamiltonian, first, rho)
-    return gather(sends, far_sends, base, 0.5 * STEP * STEP, [])[0]
+    first, sends = gather(rho, sends, local_call(damping, hamiltonian, rho), 1.0, near)
+    return gather(first, sends, local_call(damping, hamiltonian, first, rho), 0.5 * STEP * STEP, [])[0]
 
 
 def solution(mesh):

time: 231 us -> 229 us (level)
  Pallas kernels: 60.9 us -> 47.6 us
  starting transfers between devices: 14.4 us -> 24 us
  waiting for transfers between devices: 146 us -> 150 us
    pallas_call x6, Pallas kernels: 33.5 us -> 23 us  [rows_call(): pl.pallas_call(functools.partial(rows_kernel, plan, packs, scale), in_spe...]
    ppermute x18, starting transfers between devices: 14.4 us -> 24 us  [permute(): lax.ppermute(value, 'tier', [(i, self.peer(i, True)) for i in range(self....]
    pallas_call x2, Pallas kernels: 21.9 us -> 16.2 us  [local_call(): pl.pallas_call(functools.partial(local_kernel, len(densities) == 2), grid...]
    ppermute x18, waiting for transfers between devices: 146 us -> 150 us  [permute(): lax.ppermute(value, 'tier', [(i, self.peer(i, True)) for i in range(self....]
    pallas_call x1 -> x3, Pallas kernels: 5.42 us -> 8.45 us  [pack_call(): pl.pallas_call(functools.partial(pack_kernel, plan, mats), in_specs=[SMEM...]
    unnamed x46 -> x22, local copies, waits for them, and re-layouts: 5.33 us -> 4.11 us
  transfers between devices with their start and end apart: 18 -> 18, of which waited for: 10 -> 7; matrix products, arithmetic and copies ran while one was open for 1% -> 0% of each run, Pallas kernels for 18% -> 15%
where the time goes in v3:
time: 229 us; the launch traced here: 226 us
  waiting for transfers between devices  150 us (66%)
  Pallas kernels  47.6 us (21%)
  starting transfers between devices  24 us (10%)
  local copies, waits for them, and re-layouts  4.11 us (2%)
    ppermute x18, waiting for transfers between devices, permute(): lax.ppermute(value, 'tier', [(i, self.peer(i, True)) for i in range(self....  150 us
    ppermute x18, starting transfers between devices, permute(): lax.ppermute(value, 'tier', [(i, self.peer(i, True)) for i in range(self....  24 us
    pallas_call x6, Pallas kernels, rows_call(): pl.pallas_call(functools.partial(rows_kernel, plan, packs, scale), in_spe...  23 us
    pallas_call x2, Pallas kernels, local_call(): pl.pallas_call(functools.partial(local_kernel, len(densities) == 2), grid...  16.2 us
    pallas_call x3, Pallas kernels, pack_call(): pl.pallas_call(functools.partial(pack_kernel, plan, mats), in_specs=[SMEM...  8.45 us
  transfers between devices with their start and end apart: 18, of which 7 were waited for; matrix products, arithmetic and copies ran while one was open for 0% of the time, Pallas kernels for 15%

profile of v3, /device:TPU:13, one launch (start us, length us, event | category | flops | bytes accessed | tf_op | source)
XLA Modules:
  0.0 226.3 jit_solution(14943736407539651462)
XLA Ops:
  2.1 3.3 %shard_map.82 = (f32[2,2,256,256]{3,2,1,0:T(8,128)S(1)}, f32[2,2,256,256]{3,2,1,0:T(8,128)S(1)}, f32[1,2,256,256]{3,2,1,0:T(8,128)S(1)}, f32[1,2,256,256]{3,2,1,...) custom-call(s32[1]{0:T(128)} %bitcast.me_ref.refs_0_, s32[5,6,16]{2,1,0:T(8,128)S(1)} %bitcast.6, ...), custom_call_target="tpu_custom_call" | custom-call | bytes 8388608 | tf_op jit(solution)/shard_map/pallas_call | solution.py:280
  6.4 1.8 collective-permute-start.5
  8.3 3.4 %collective-permute-start.7 = (f32[1,2,256,256]{3,2,1,0:T(8,128)S(1)}, f32[1,2,256,256]{3,2,1,0:T(8,128)S(1)}, u32[]{:S(2)}, u32[]{:S(2)}) collective-permute-start(f32[1,2,256,256]{3,2,1,0:T(8,128)S(1)} %get-tuple-element.31), channel_id=1, source_target_pairs={{0,14},{1,15},{2,4},{3,5},{4,2},{5,3},{6,8},{7,9},{8,6},{9,7},{10,... | collective-permute-start | bytes 1572872 | tf_op jit(solution)/shard_map/ppermute | solution.py:38
  12.0 41.6 %collective-permute-done.1.rest_1_.refs_9_ = f32[2,2,256,256]{3,2,1,0:T(8,128)S(1)} collective-permute-done((f32[2,2,256,256]{3,2,1,0:T(8,128)S(1)}, f32[2,2,256,256]{3,2,1,0:T(8,128)S(1)}, u32[]{:S(2)}, u32[]{:S(2)}) %collective-permute-start.1) | collective-permute-done | bytes 1048608 | tf_op jit(solution)/shard_map/ppermute | solution.py:38
  53.5 2.5 %shard_map.83 = (f32[1,2,256,256]{3,2,1,0:T(8,128)S(1)}, f32[2,2,256,256]{3,2,1,0:T(8,128)S(1)}, f32[1,2,256,256]{3,2,1,0:T(8,128)S(1)}) custom-call(s32[1]{0:T(128)} %bitcast.me_ref.refs_0_, s32[5,6,16]{2,1,0:T(8,128)S(1)} %bitcast.7, s32[16]{0:T(128)S(1)} %copy-done.8, s32[1,4,1,5]{3,2,1,0:T(1,128)S(1)} %copy-done.7, f32[8,2,256,256]{3,2,1,0:T(8,128)} %refs_0_.1, ...), custom_call_target="tpu_custom_call" | custom-call | bytes 4194304 | tf_op jit(solution)/shard_map/pallas_call | solution.py:280
  56.2 7.4 %shard_map.84.refs_10_ = f32[8,2,256,256]{3,2,1,0:T(8,128)S(1)} custom-call(f32[8]{0:T(128)S(1)} %copy-done.10, f32[256,256]{1,0:T(8,128)S(1)} %copy-done.6, f32[8,2,256,256]{3,2,1,0:T(8,128)} %refs_0_.1), custom_call_target="tpu_custom_call" | custom-call | flops 3221225472 | bytes 8388608 | tf_op jit(solution)/shard_map/pallas_call | solution.py:161
  63.7 2.0 copy-done
  65.7 2.6 %collective-permute-start.2 = (f32[1,2,256,256]{3,2,1,0:T(8,128)S(1)}, f32[1,2,256,256]{3,2,1,0:T(8,128)S(1)}, u32[]{:S(2)}, u32[]{:S(2)}) collective-permute-start(f32[1,2,256,256]{3,2,1,0:T(8,128)S(1)} %get-tuple-element.26), channel_id=1, source_target_pairs={{0,8},{1,9},{2,10},{3,11},{4,12},{5,13},{6,14},{7,15},{8,0},{9,1},... | collective-permute-start | bytes 1572872 | tf_op jit(solution)/shard_map/ppermute | solution.py:38
  68.4 4.9 %shard_map.85.refs_12_ = f32[8,2,256,256]{3,2,1,0:T(8,128)} custom-call(s32[1]{0:T(128)} %bitcast.me_ref.refs_0_, s32[5,6,16]{2,1,0:T(8,128)S(1)} %bitcast.9, s32[16]{0:T(128)S(1)} %copy-done.8, s32[1,4,1,5]{3,2,1,0:T(1,128)S(1)} %copy-done.7, f32[6,16]{1,0:T(8,128)S(1)} %fusion.1.refs_4_, f32[4,1]{1,0:T(4,128)S(1)} %bitcast.16, ...), custom_call_target="tpu_custom_call", output_to_operand_aliasing={{}: (10, {})} | custom-call | flops 1610612736 | bytes 10485760 | tf_op jit(solution)/shard_map/pallas_call | solution.py:255
  73.3 1.5 shard_map.86.refs_11_
  74.8 17.2 %collective-permute-done.2.refs_8_ = f32[1,2,256,256]{3,2,1,0:T(8,128)S(1)} collective-permute-done((f32[1,2,256,256]{3,2,1,0:T(8,128)S(1)}, f32[1,2,256,256]{3,2,1,0:T(8,128)S(1)}, u32[]{:S(2)}, u32[]{:S(2)}) %collective-permute-start.2) | collective-permute-done | bytes 524320 | tf_op jit(solution)/shard_map/ppermute | solution.py:38
  92.0 20.4 %collective-permute-done.4.refs_10_ = f32[1,2,256,256]{3,2,1,0:T(8,128)S(1)} collective-permute-done((f32[1,2,256,256]{3,2,1,0:T(8,128)S(1)}, f32[1,2,256,256]{3,2,1,0:T(8,128)S(1)}, u32[]{:S(2)}, u32[]{:S(2)}) %collective-permute-start.4) | collective-permute-done | bytes 524320 | tf_op jit(solution)/shard_map/ppermute | solution.py:38
  112.4 5.9 %shard_map.87 = (f32[8,2,256,256]{3,2,1,0:T(8,128)}, f32[2,2,256,256]{3,2,1,0:T(8,128)S(1)}, f32[2,2,256,256]{3,2,1,0:T(8,128)S(1)}, f32[1,2,256,256]{3,2,1,0:T(...) custom-call(s32[1]{0:T(128)} %bitcast.me_ref.refs_0_, ...), custom_call_target="tpu_custom_call", output_to_operand_aliasing={{0}: (11, {})} | custom-call | flops 1610612736 | bytes 14680064 | tf_op jit(solution)/shard_map/pallas_call | solution.py:255
  118.3 2.5 %collective-permute-start.9 = (f32[2,2,256,256]{3,2,1,0:T(8,128)S(1)}, f32[2,2,256,256]{3,2,1,0:T(8,128)S(1)}, u32[]{:S(2)}, u32[]{:S(2)}) collective-permute-start(f32[2,2,256,256]{3,2,1,0:T(8,128)S(1)} %get-tuple-element.34), channel_id=1, source_target_pairs={{0,1},{1,0},{2,3},{3,2},{4,5},{5,4},{6,7},{7,6},{8,9},{9,8},{10,11... | collective-permute-start | bytes 3145736 | tf_op jit(solution)/shard_map/ppermute | solution.py:38
  123.9 27.3 %collective-permute-done.10.rest_1_.refs_9_ = f32[2,2,256,256]{3,2,1,0:T(8,128)S(1)} collective-permute-done((f32[2,2,256,256]{3,2,1,0:T(8,128)S(1)}, f32[2,2,256,256]{3,2,1,0:T(8,128)S(1)}, u32[]{:S(2)}, u32[]{:S(2)}) %collective-permute-start.10) | collective-permute-done | bytes 1048608 | tf_op jit(solution)/shard_map/ppermute | solution.py:38
  151.2 2.5 %shard_map.88 = (f32[1,2,256,256]{3,2,1,0:T(8,128)S(1)}, f32[2,2,256,256]{3,2,1,0:T(8,128)S(1)}, f32[1,2,256,256]{3,2,1,0:T(8,128)S(1)}) custom-call(s32[1]{0:T(128)} %bitcast.me_ref.refs_0_, s32[5,6,16]{2,1,0:T(8,128)S(1)} %bitcast.12, s32[16]{0:T(128)S(1)} %copy-done.8, s32[1,4,1,5]{3,2,1,0:T(1,128)S(1)} %copy-done.7, ...), custom_call_target="tpu_custom_call" | custom-call | bytes 4194304 | tf_op jit(solution)/shard_map/pallas_call | solution.py:280
  153.8 2.2 collective-permute-start.16
  157.4 5.5 %collective-permute-start.11 = (f32[1,2,256,256]{3,2,1,0:T(8,128)S(1)}, f32[1,2,256,256]{3,2,1,0:T(8,128)S(1)}, u32[]{:S(2)}, u32[]{:S(2)}) collective-permute-start(f32[1,2,256,256]{3,2,1,0:T(8,128)S(1)} %get-tuple-element.36), channel_id=1, source_target_pairs={{0,8},{1,9},{2,10},{3,11},{4,12},{5,13},{6,14},{7,15},{8,0},{9,1},... | collective-permute-start | bytes 1572872 | tf_op jit(solution)/shard_map/ppermute | solution.py:38
  162.9 8.8 %shard_map.89.refs_10_ = f32[8,2,256,256]{3,2,1,0:T(8,128)} custom-call(f32[8]{0:T(128)S(1)} %copy-done.10, f32[256,256]{1,0:T(8,128)S(1)} %copy-done.6, f32[8,2,256,256]{3,2,1,0:T(8,128)S(1)} %copy-done.1, f32[8,2,256,256]{3,2,1,0:T(8,128)} %refs_0_.1), custom_call_target="tpu_custom_call" | custom-call | flops 3221225472 | bytes 12582912 | tf_op jit(solution)/shard_map/pallas_call | solution.py:161
  171.7 5.1 %shard_map.90.refs_12_ = f32[8,2,256,256]{3,2,1,0:T(8,128)} custom-call(s32[1]{0:T(128)} %bitcast.me_ref.refs_0_, s32[5,6,16]{2,1,0:T(8,128)S(1)} %bitcast.13, s32[16]{0:T(128)S(1)} %copy-done.8, s32[1,4,1,5]{3,2,1,0:T(1,128)S(1)} %copy-done.7, f32[6,16]{1,0:T(8,128)S(1)} %fusion.1.refs_4_, f32[4,1]{1,0:T(4,128)S(1)} %bitcast.19, ...), custom_call_target="tpu_custom_call", output_to_operand_aliasing={{}: (10, {})} | custom-call | flops 1610612736 | bytes 10485760 | tf_op jit(solution)/shard_map/pallas_call | solution.py:255
  176.8 4.4 %collective-permute-done.17.refs_11_ = f32[1,2,256,256]{3,2,1,0:T(8,128)S(1)} collective-permute-done((f32[1,2,256,256]{3,2,1,0:T(8,128)S(1)}, f32[1,2,256,256]{3,2,1,0:T(8,128)S(1)}, u32[]{:S(2)}, u32[]{:S(2)}) %collective-permute-start.17) | collective-permute-done | bytes 524320 | tf_op jit(solution)/shard_map/ppermute | solution.py:38
  182.6 30.3 %collective-permute-done.11.refs_8_ = f32[1,2,256,256]{3,2,1,0:T(8,128)S(1)} collective-permute-done((f32[1,2,256,256]{3,2,1,0:T(8,128)S(1)}, f32[1,2,256,256]{3,2,1,0:T(8,128)S(1)}, u32[]{:S(2)}, u32[]{:S(2)}) %collective-permute-start.11) | collective-permute-done | bytes 524320 | tf_op jit(solution)/shard_map/ppermute | solution.py:38
  212.9 8.9 %collective-permute-done.13.refs_10_ = f32[1,2,256,256]{3,2,1,0:T(8,128)S(1)} collective-permute-done((f32[1,2,256,256]{3,2,1,0:T(8,128)S(1)}, f32[1,2,256,256]{3,2,1,0:T(8,128)S(1)}, u32[]{:S(2)}, u32[]{:S(2)}) %collective-permute-start.13) | collective-permute-done | bytes 524320 | tf_op jit(solution)/shard_map/ppermute | solution.py:38
  221.9 4.3 %shard_map.92 = f32[8,2,256,256]{3,2,1,0:T(8,128)} custom-call(s32[1]{0:T(128)} %bitcast.me_ref.refs_0_, s32[5,6,16]{2,1,0:T(8,128)S(1)} %bitcast.15, s32[16]{0:T(128)S(1)} %copy-done.8, s32[1,4,1,5]{3,2,1,0:T(1,128)S(1)} %copy-done.7, f32[6,16]{1,0:T(8,128)S(1)} %fusion.1.refs_4_, f32[4,1]{1,0:T(4,128)S(1)} %bitcast.21, ...), custom_call_target="tpu_custom_call", output_to_operand_aliasing={{}: (11, {})} | custom-call | flops 1610612736 | bytes 10485760 | tf_op jit(solution)/shard_map/pallas_call | solution.py:255
  (47 shorter events, 9.6 us)
Async XLA Ops:
  5.4 50.8 %copy-start.6 = (f32[256,256]{1,0:T(8,128)S(1)}, f32[256,256]{1,0:T(8,128)}, u32[]{:S(2)}) copy-start(f32[256,256]{1,0:T(8,128)} %hamiltonian_ref.3) | copy-start | bytes 786436
  5.4 50.8 %copy-start.10 = (f32[8]{0:T(128)S(1)}, f32[8]{0:T(128)}, u32[]{:S(2)}) copy-start(f32[8]{0:T(128)} %damping_ref.3) | copy-start | bytes 100
  5.4 6.2 %collective-permute-start = (f32[2,2,256,256]{3,2,1,0:T(8,128)S(1)}, f32[2,2,256,256]{3,2,1,0:T(8,128)S(1)}, u32[]{:S(2)}, u32[]{:S(2)}) collective-permute-start(f32[2,2,256,256]{3,2,1,0:T(8,128)S(1)} %get-tuple-element.24), channel_id=1, source_target_pairs={{0,1},{1,0},{2,3},{3,2},{4,5},{5,4},{6,7},{7,6},{8,9},{9,8},{10,11... | collective-permute-start | bytes 3145736 | tf_op jit(solution)/shard_map/ppermute | solution.py:38
  6.3 47.2 %collective-permute-start.1 = (f32[2,2,256,256]{3,2,1,0:T(8,128)S(1)}, f32[2,2,256,256]{3,2,1,0:T(8,128)S(1)}, u32[]{:S(2)}, u32[]{:S(2)}) collective-permute-start(f32[2,2,256,256]{3,2,1,0:T(8,128)S(1)} %get-tuple-element.25), channel_id=1, source_target_pairs={{0,2},{1,3},{2,0},{3,1},{4,6},{5,7},{6,4},{7,5},{8,10},{9,11},{10,... | collective-permute-start | bytes 3145736 | tf_op jit(solution)/shard_map/ppermute | solution.py:38
  6.4 59.2 %collective-permute-start.5 = (f32[1,2,256,256]{3,2,1,0:T(8,128)S(1)}, f32[1,2,256,256]{3,2,1,0:T(8,128)S(1)}, u32[]{:S(2)}, u32[]{:S(2)}) collective-permute-start(f32[1,2,256,256]{3,2,1,0:T(8,128)S(1)} %get-tuple-element.29), channel_id=1, source_target_pairs={{0,3},{1,4},{2,5},{3,6},{4,7},{5,8},{6,9},{7,10},{8,11},{9,12},{10... | collective-permute-start | bytes 1572872 | tf_op jit(solution)/shard_map/ppermute | solution.py:38
  8.3 60.0 %collective-permute-start.6 = (f32[1,2,256,256]{3,2,1,0:T(8,128)S(1)}, f32[1,2,256,256]{3,2,1,0:T(8,128)S(1)}, u32[]{:S(2)}, u32[]{:S(2)}) collective-permute-start(f32[1,2,256,256]{3,2,1,0:T(8,128)S(1)} %get-tuple-element.30), channel_id=1, source_target_pairs={{0,13},{1,14},{2,15},{3,0},{4,1},{5,2},{6,3},{7,4},{8,5},{9,6},{10... | collective-permute-start | bytes 1572872 | tf_op jit(solution)/shard_map/ppermute | solution.py:38
  8.3 65.0 %collective-permute-start.7 = (f32[1,2,256,256]{3,2,1,0:T(8,128)S(1)}, f32[1,2,256,256]{3,2,1,0:T(8,128)S(1)}, u32[]{:S(2)}, u32[]{:S(2)}) collective-permute-start(f32[1,2,256,256]{3,2,1,0:T(8,128)S(1)} %get-tuple-element.31), channel_id=1, source_target_pairs={{0,14},{1,15},{2,4},{3,5},{4,2},{5,3},{6,8},{7,9},{8,6},{9,7},{10,... | collective-permute-start | bytes 1572872 | tf_op jit(solution)/shard_map/ppermute | solution.py:38
  11.6 61.7 %collective-permute-start.8 = (f32[1,2,256,256]{3,2,1,0:T(8,128)S(1)}, f32[1,2,256,256]{3,2,1,0:T(8,128)S(1)}, u32[]{:S(2)}, u32[]{:S(2)}) collective-permute-start(f32[1,2,256,256]{3,2,1,0:T(8,128)S(1)} %get-tuple-element.32), channel_id=1, source_target_pairs={{0,15},{1,2},{2,1},{3,4},{4,3},{5,6},{6,5},{7,8},{8,7},{9,10},{10,... | collective-permute-start | bytes 1572872 | tf_op jit(solution)/shard_map/ppermute | solution.py:38
  56.1 9.6 %copy-start.5 = (s32[16,6,5]{0,1,2:T(8,128)S(1)}, s32[16,6,5]{0,1,2:T(8,128)}, u32[]{:S(2)}) copy-start(s32[16,6,5]{0,1,2:T(8,128)} %param.14) | copy-start | bytes 5764
  56.1 12.3 %copy-start.2 = (f32[4,256,256]{2,1,0:T(8,128)S(1)}, f32[4,256,256]{2,1,0:T(8,128)}, u32[]{:S(2)}) copy-start(f32[4,256,256]{2,1,0:T(8,128)} %refs_7_.11) | copy-start | bytes 3145732
  56.1 12.3 %copy-start.9 = (f32[4,2]{0,1:T(2,128)S(1)}, f32[4,2]{0,1:T(2,128)}, u32[]{:S(2)}) copy-start(f32[4,2]{0,1:T(2,128)} %param.11) | copy-start | bytes 100
  56.1 56.3 %collective-permute-start.3 = (f32[2,2,256,256]{3,2,1,0:T(8,128)S(1)}, f32[2,2,256,256]{3,2,1,0:T(8,128)}, u32[]{:S(2)}, u32[]{:S(2)}) collective-permute-start(f32[2,2,256,256]{3,2,1,0:T(8,128)S(1)} %get-tuple-element.27), channel_id=1, source_target_pairs={{0,4},{1,5},{2,6},{3,7},{4,0},{5,1},{6,2},{7,3},{8,12},{9,13},{10,... | collective-permute-start | bytes 3145736 | tf_op jit(solution)/shard_map/ppermute | solution.py:38
  65.7 26.3 %collective-permute-start.2 = (f32[1,2,256,256]{3,2,1,0:T(8,128)S(1)}, f32[1,2,256,256]{3,2,1,0:T(8,128)S(1)}, u32[]{:S(2)}, u32[]{:S(2)}) collective-permute-start(f32[1,2,256,256]{3,2,1,0:T(8,128)S(1)} %get-tuple-element.26), channel_id=1, source_target_pairs={{0,8},{1,9},{2,10},{3,11},{4,12},{5,13},{6,14},{7,15},{8,0},{9,1},... | collective-permute-start | bytes 1572872 | tf_op jit(solution)/shard_map/ppermute | solution.py:38
  68.3 44.1 %collective-permute-start.4 = (f32[1,2,256,256]{3,2,1,0:T(8,128)S(1)}, f32[1,2,256,256]{3,2,1,0:T(8,128)S(1)}, u32[]{:S(2)}, u32[]{:S(2)}) collective-permute-start(f32[1,2,256,256]{3,2,1,0:T(8,128)S(1)} %get-tuple-element.28), channel_id=1, source_target_pairs={{0,12},{1,13},{2,14},{3,15},{4,8},{5,9},{6,10},{7,11},{8,4},{9,5},... | collective-permute-start | bytes 1572872 | tf_op jit(solution)/shard_map/ppermute | solution.py:38
  118.3 44.6 %copy-start.1 = (f32[8,2,256,256]{3,2,1,0:T(8,128)S(1)}, f32[8,2,256,256]{3,2,1,0:T(8,128)}, u32[]{:S(2)}) copy-start(f32[8,2,256,256]{3,2,1,0:T(8,128)} %get-tuple-element.33.source.density_ref) | copy-start | bytes 12582916
  118.3 5.6 %collective-permute-start.9 = (f32[2,2,256,256]{3,2,1,0:T(8,128)S(1)}, f32[2,2,256,256]{3,2,1,0:T(8,128)S(1)}, u32[]{:S(2)}, u32[]{:S(2)}) collective-permute-start(f32[2,2,256,256]{3,2,1,0:T(8,128)S(1)} %get-tuple-element.34), channel_id=1, source_target_pairs={{0,1},{1,0},{2,3},{3,2},{4,5},{5,4},{6,7},{7,6},{8,9},{9,8},{10,11... | collective-permute-start | bytes 3145736 | tf_op jit(solution)/shard_map/ppermute | solution.py:38
  120.8 30.4 %collective-permute-start.10 = (f32[2,2,256,256]{3,2,1,0:T(8,128)S(1)}, f32[2,2,256,256]{3,2,1,0:T(8,128)S(1)}, u32[]{:S(2)}, u32[]{:S(2)}) collective-permute-start(f32[2,2,256,256]{3,2,1,0:T(8,128)S(1)} %get-tuple-element.35), channel_id=1, source_target_pairs={{0,2},{1,3},{2,0},{3,1},{4,6},{5,7},{6,4},{7,5},{8,10},{9,11},{10,... | collective-permute-start | bytes 3145736 | tf_op jit(solution)/shard_map/ppermute | solution.py:38
  122.2 35.2 %collective-permute-start.14 = (f32[1,2,256,256]{3,2,1,0:T(8,128)S(1)}, f32[1,2,256,256]{3,2,1,0:T(8,128)S(1)}, u32[]{:S(2)}, u32[]{:S(2)}) collective-permute-start(f32[1,2,256,256]{3,2,1,0:T(8,128)S(1)} %get-tuple-element.39), channel_id=1, source_target_pairs={{0,3},{1,4},{2,5},{3,6},{4,7},{5,8},{6,9},{7,10},{8,11},{9,12},{10... | collective-permute-start | bytes 1572872 | tf_op jit(solution)/shard_map/ppermute | solution.py:38
  123.0 39.9 %collective-permute-start.15 = (f32[1,2,256,256]{3,2,1,0:T(8,128)S(1)}, f32[1,2,256,256]{3,2,1,0:T(8,128)S(1)}, u32[]{:S(2)}, u32[]{:S(2)}) collective-permute-start(f32[1,2,256,256]{3,2,1,0:T(8,128)S(1)} %get-tuple-element.40), channel_id=1, source_target_pairs={{0,13},{1,14},{2,15},{3,0},{4,1},{5,2},{6,3},{7,4},{8,5},{9,6},{10... | collective-permute-start | bytes 1572872 | tf_op jit(solution)/shard_map/ppermute | solution.py:38
  153.8 68.1 %collective-permute-start.12 = (f32[2,2,256,256]{3,2,1,0:T(8,128)S(1)}, f32[2,2,256,256]{3,2,1,0:T(8,128)S(1)}, u32[]{:S(2)}, u32[]{:S(2)}) collective-permute-start(f32[2,2,256,256]{3,2,1,0:T(8,128)S(1)} %get-tuple-element.37), channel_id=1, source_target_pairs={{0,4},{1,5},{2,6},{3,7},{4,0},{5,1},{6,2},{7,3},{8,12},{9,13},{10,... | collective-permute-start | bytes 3145736 | tf_op jit(solution)/shard_map/ppermute | solution.py:38
  153.8 23.0 %collective-permute-start.16 = (f32[1,2,256,256]{3,2,1,0:T(8,128)S(1)}, f32[1,2,256,256]{3,2,1,0:T(8,128)S(1)}, u32[]{:S(2)}, u32[]{:S(2)}) collective-permute-start(f32[1,2,256,256]{3,2,1,0:T(8,128)S(1)} %get-tuple-element.41), channel_id=1, source_target_pairs={{0,14},{1,15},{2,4},{3,5},{4,2},{5,3},{6,8},{7,9},{8,6},{9,7},{10,... | collective-permute-start | bytes 1572872 | tf_op jit(solution)/shard_map/ppermute | solution.py:38
  156.0 25.2 %collective-permute-start.17 = (f32[1,2,256,256]{3,2,1,0:T(8,128)S(1)}, f32[1,2,256,256]{3,2,1,0:T(8,128)S(1)}, u32[]{:S(2)}, u32[]{:S(2)}) collective-permute-start(f32[1,2,256,256]{3,2,1,0:T(8,128)S(1)} %get-tuple-element.42), channel_id=1, source_target_pairs={{0,15},{1,2},{2,1},{3,4},{4,3},{5,6},{6,5},{7,8},{8,7},{9,10},{10,... | collective-permute-start | bytes 1572872 | tf_op jit(solution)/shard_map/ppermute | solution.py:38
  157.4 55.6 %collective-permute-start.11 = (f32[1,2,256,256]{3,2,1,0:T(8,128)S(1)}, f32[1,2,256,256]{3,2,1,0:T(8,128)S(1)}, u32[]{:S(2)}, u32[]{:S(2)}) collective-permute-start(f32[1,2,256,256]{3,2,1,0:T(8,128)S(1)} %get-tuple-element.36), channel_id=1, source_target_pairs={{0,8},{1,9},{2,10},{3,11},{4,12},{5,13},{6,14},{7,15},{8,0},{9,1},... | collective-permute-start | bytes 1572872 | tf_op jit(solution)/shard_map/ppermute | solution.py:38
  162.9 58.9 %collective-permute-start.13 = (f32[1,2,256,256]{3,2,1,0:T(8,128)S(1)}, f32[1,2,256,256]{3,2,1,0:T(8,128)S(1)}, u32[]{:S(2)}, u32[]{:S(2)}) collective-permute-start(f32[1,2,256,256]{3,2,1,0:T(8,128)S(1)} %get-tuple-element.38), channel_id=1, source_target_pairs={{0,12},{1,13},{2,14},{3,15},{4,8},{5,9},{6,10},{7,11},{8,4},{9,5},... | collective-permute-start | bytes 1572872 | tf_op jit(solution)/shard_map/ppermute | solution.py:38
  (5 other events, 12.9 us)

commit v4 on v3

--- a/solution.py
+++ b/solution.py
@@ -39,20 +39,18 @@
 
 
 def exchanges(size, colours):
-    swaps, others, shifts, far = [], [], [], []
-    for colour in range(colours):
-        if 1 << colour > REACH:
-            far.append(Exchange("swap", 1 << colour, size, colour, listed=False))
+    shifts, others, swaps, far = [], [], [], []
     for distance in range(1, REACH + 1):
         colour = distance.bit_length() - 1
         if distance != 1 << colour or colour >= colours:
             shifts += [Exchange("shift", distance, size), Exchange("shift", size - distance, size)]
-        elif distance < REACH:
-            swaps.append(Exchange("swap", distance, size, colour))
-            others.insert(0, Exchange("other", distance, size))
-        else:
-            far += [Exchange("swap", distance, size, colour), Exchange("other", distance, size)]
-    return swaps, shifts + others, far
+            continue
+        swaps.append(Exchange("swap", distance, size, colour))
+        (others if distance < REACH else far).insert(0, Exchange("other", distance, size))
+    for colour in range(colours):
+        if 1 << colour > REACH:
+            far.insert(0, Exchange("swap", 1 << colour, size, colour, listed=False))
+    return shifts, others, swaps, far
 
 
 def payload(exchange, pairs):
@@ -294,24 +292,26 @@
 
 def body(rho, hamiltonian, couplings, bath_coef, damping, match_edges, left_rows, left_count):
     colours, pairs = match_edges.shape[1:3]
-    swaps, shifts, far = exchanges(lax.axis_size("tier"), colours)
+    shifts, others, swaps, far = exchanges(lax.axis_size("tier"), colours)
     me = lax.axis_index("tier").astype(jnp.int32)[None]
     left_fields = jnp.transpose(left_rows, (2, 1, 0))
     left_root = jnp.sqrt(left_fields[4].astype(F32))
     match_root = jnp.sqrt(match_edges[0, :, :, 4].astype(F32))
     tables = (me, left_fields, left_count, match_edges, left_root, match_root, bath_coef.T)
 
-    near = swaps + shifts
+    near, later = shifts + others + swaps[:1], swaps[1:] + far
 
     def gather(density, near_sends, acc, scale, packs):
         arrived = [e.permute(s) for e, s in zip(near, near_sends)]
-        far_sends = pack_call(far, pairs, tables, density, *arrived[: len(swaps)])
-        arrived += [e.permute(s) for e, s in zip(far, far_sends)]
-        for group in (swaps, shifts, far):
+        sends = pack_call(later, pairs, tables, density, *arrived[: len(shifts)])
+        arrived += [e.permute(s) for e, s in zip(later, sends)]
+        first, second = len(shifts + others), len(near) + 1
+        order = near + later
+        for a, b in ((0, first), (first, second), (second, len(order))):
             got = rows_call(
-                group, packs if group is far else [], pairs, scale, tables, couplings, arrived[: len(group)], acc
+                order[a:b], packs if b == len(order) else [], pairs, scale, tables, couplings, arrived[a:b], acc
             )
-            acc, arrived = got[0], arrived[len(group) :]
+            acc = got[0]
         return acc, got[1:]
 
     sends = pack_call(near, pairs, tables, rho)

time: 229 us -> 211 us (0.921)
  the two profiles are of different devices: /device:TPU:13 before, /device:TPU:14 now
where the time goes in v4:
time: 211 us; the launch traced here: 210 us
  waiting for transfers between devices  124 us (59%)
  Pallas kernels  55.2 us (26%)
  starting transfers between devices  25.2 us (12%)
  local copies, waits for them, and re-layouts  5.08 us (2%)
    ppermute x18, waiting for transfers between devices, permute(): lax.ppermute(value, 'tier', [(i, self.peer(i, True)) for i in range(self....  124 us
    pallas_call x6, Pallas kernels, rows_call(): pl.pallas_call(functools.partial(rows_kernel, plan, packs, scale), in_spe...  29 us
    ppermute x18, starting transfers between devices, permute(): lax.ppermute(value, 'tier', [(i, self.peer(i, True)) for i in range(self....  25.2 us
    pallas_call x2, Pallas kernels, local_call(): pl.pallas_call(functools.partial(local_kernel, len(densities) == 2), grid...  16.1 us
    pallas_call x3, Pallas kernels, pack_call(): pl.pallas_call(functools.partial(pack_kernel, plan, mats), in_specs=[SMEM...  10.1 us
    unnamed x22, local copies, waits for them, and re-layouts  5.08 us
  transfers between devices with their start and end apart: 18, of which 10 were waited for; matrix products, arithmetic and copies ran while one was open for 0% of the time, Pallas kernels for 20%

profile of v4, /device:TPU:14, one launch (start us, length us, event | category | flops | bytes accessed | tf_op | source)
XLA Modules:
  0.0 210.2 jit_solution(13935490790183528170)
XLA Ops:
  2.1 2.9 %shard_map.82 = (f32[1,2,256,256]{3,2,1,0:T(8,128)S(1)}, f32[1,2,256,256]{3,2,1,0:T(8,128)S(1)}, f32[1,2,256,256]{3,2,1,0:T(8,128)S(1)}, f32[1,2,256,256]{3,2,1,0:T(8,128)S(1)}, f32[2,2,256,256]{3,2,1,0:T(8,128)S(1)}) custom-call(s32[1]{0:T(128)} %bitcast.me_ref.refs_0_, s32[5,6,16]{2,1,0:T(8,128)S(1)} %bitcast.6, s32[16]{0:T(128)S(1)} %copy-done.7, ...), custom_call_target="tpu_custom_call" | custom-call | bytes 6291456 | tf_op jit(solution)/shard_map/pallas_call | solution.py:278
  7.0 12.1 %collective-permute-done.rest_0_.refs_8_ = f32[1,2,256,256]{3,2,1,0:T(8,128)S(1)} collective-permute-done((f32[1,2,256,256]{3,2,1,0:T(8,128)S(1)}, f32[1,2,256,256]{3,2,1,0:T(8,128)S(1)}, u32[]{:S(2)}, u32[]{:S(2)}) %collective-permute-start) | collective-permute-done | bytes 524320 | tf_op jit(solution)/shard_map/ppermute | solution.py:38
  19.1 6.6 %collective-permute-done.1.rest_1_.refs_9_ = f32[1,2,256,256]{3,2,1,0:T(8,128)S(1)} collective-permute-done((f32[1,2,256,256]{3,2,1,0:T(8,128)S(1)}, f32[1,2,256,256]{3,2,1,0:T(8,128)S(1)}, u32[]{:S(2)}, u32[]{:S(2)}) %collective-permute-start.1) | collective-permute-done | bytes 524320 | tf_op jit(solution)/shard_map/ppermute | solution.py:38
  25.7 3.2 %shard_map.83 = (f32[2,2,256,256]{3,2,1,0:T(8,128)S(1)}, f32[2,2,256,256]{3,2,1,0:T(8,128)S(1)}, f32[1,2,256,256]{3,2,1,0:T(8,128)S(1)}, f32[1,2,256,256]{3,2,1,0:T(8,128)S(1)}) custom-call(s32[1]{0:T(128)} %bitcast.me_ref.refs_0_, s32[5,6,16]{2,1,0:T(8,128)S(1)} %bitcast.7, s32[16]{0:T(128)S(1)} %copy-done.7, s32[1,4,1,5]{3,2,1,0:T(1,128)S(1)} %copy-done.6, ...), custom_call_target="tpu_custom_call" | custom-call | bytes 6291456 | tf_op jit(solution)/shard_map/pallas_call | solution.py:278
  33.0 7.4 %shard_map.84.refs_12_ = f32[8,2,256,256]{3,2,1,0:T(8,128)S(1)} custom-call(f32[8]{0:T(128)S(1)} %copy-done.9, f32[256,256]{1,0:T(8,128)S(1)} %copy-done.5, f32[8,2,256,256]{3,2,1,0:T(8,128)} %refs_0_.1), custom_call_target="tpu_custom_call" | custom-call | flops 3221225472 | bytes 8388608 | tf_op jit(solution)/shard_map/pallas_call | solution.py:159
  44.0 4.9 %collective-permute-start.3 = (f32[1,2,256,256]{3,2,1,0:T(8,128)S(1)}, f32[1,2,256,256]{3,2,1,0:T(8,128)S(1)}, u32[]{:S(2)}, u32[]{:S(2)}) collective-permute-start(f32[1,2,256,256]{3,2,1,0:T(8,128)S(1)} %get-tuple-element.27), channel_id=1, source_target_pairs={{0,8},{1,9},{2,10},{3,11},{4,12},{5,13},{6,14},{7,15},{8,0},{9,1},... | collective-permute-start | bytes 1572872 | tf_op jit(solution)/shard_map/ppermute | solution.py:38
  49.0 27.7 %collective-permute-done.8.refs_11_ = f32[1,2,256,256]{3,2,1,0:T(8,128)S(1)} collective-permute-done((f32[1,2,256,256]{3,2,1,0:T(8,128)S(1)}, f32[1,2,256,256]{3,2,1,0:T(8,128)S(1)}, u32[]{:S(2)}, u32[]{:S(2)}) %collective-permute-start.8) | collective-permute-done | bytes 524320 | tf_op jit(solution)/shard_map/ppermute | solution.py:38
  77.2 4.8 %shard_map.85.refs_10_ = f32[8,2,256,256]{3,2,1,0:T(8,128)} custom-call(s32[1]{0:T(128)} %bitcast.me_ref.refs_0_, s32[5,6,16]{2,1,0:T(8,128)S(1)} %bitcast.9, s32[16]{0:T(128)S(1)} %copy-done.7, s32[1,4,1,5]{3,2,1,0:T(1,128)S(1)} %copy-done.6, f32[6,16]{1,0:T(8,128)S(1)} %fusion.1.refs_4_, f32[4,1]{1,0:T(4,128)S(1)} %bitcast.16, ...), custom_call_target="tpu_custom_call", output_to_operand_aliasing={{}: (12, {})} | custom-call | flops 1610612736 | bytes 10485760 | tf_op jit(solution)/shard_map/pallas_call | solution.py:253
  82.1 4.2 %shard_map.86.refs_11_ = f32[8,2,256,256]{3,2,1,0:T(8,128)} custom-call(s32[1]{0:T(128)} %bitcast.me_ref.refs_0_, s32[5,6,16]{2,1,0:T(8,128)S(1)} %bitcast.10, s32[16]{0:T(128)S(1)} %copy-done.7, s32[1,4,1,5]{3,2,1,0:T(1,128)S(1)} %copy-done.6, f32[6,16]{1,0:T(8,128)S(1)} %fusion.1.refs_4_, f32[4,1]{1,0:T(4,128)S(1)} %bitcast.17, ...), custom_call_target="tpu_custom_call", output_to_operand_aliasing={{}: (10, {})} | custom-call | flops 1610612736 | bytes 10485760 | tf_op jit(solution)/shard_map/pallas_call | solution.py:253
  86.3 15.7 %collective-permute-done.4.refs_10_ = f32[1,2,256,256]{3,2,1,0:T(8,128)S(1)} collective-permute-done((f32[1,2,256,256]{3,2,1,0:T(8,128)S(1)}, f32[1,2,256,256]{3,2,1,0:T(8,128)S(1)}, u32[]{:S(2)}, u32[]{:S(2)}) %collective-permute-start.4) | collective-permute-done | bytes 524320 | tf_op jit(solution)/shard_map/ppermute | solution.py:38
  103.0 6.0 %shard_map.87 = (f32[8,2,256,256]{3,2,1,0:T(8,128)}, f32[1,2,256,256]{3,2,1,0:T(8,128)S(1)}, f32[1,2,256,256]{3,2,1,0:T(8,128)S(1)}, f32[1,2,256,256]{3,2,1,0:T(...) custom-call(s32[1]{0:T(128)} %bitcast.me_ref.refs_0_, ...), custom_call_target="tpu_custom_call", output_to_operand_aliasing={{0}: (11, {})} | custom-call | flops 1610612736 | bytes 13631488 | tf_op jit(solution)/shard_map/pallas_call | solution.py:253
  110.8 12.2 %collective-permute-done.9.rest_0_.refs_8_ = f32[1,2,256,256]{3,2,1,0:T(8,128)S(1)} collective-permute-done((f32[1,2,256,256]{3,2,1,0:T(8,128)S(1)}, f32[1,2,256,256]{3,2,1,0:T(8,128)S(1)}, u32[]{:S(2)}, u32[]{:S(2)}) %collective-permute-start.9) | collective-permute-done | bytes 524320 | tf_op jit(solution)/shard_map/ppermute | solution.py:38
  123.0 2.1 collective-permute-done.10.rest_1_.refs_9_
  125.1 3.9 %shard_map.88 = (f32[2,2,256,256]{3,2,1,0:T(8,128)S(1)}, f32[2,2,256,256]{3,2,1,0:T(8,128)S(1)}, f32[1,2,256,256]{3,2,1,0:T(8,128)}, f32[1,2,256,256]{3,2,1,0:T(8,128)S(1)}) custom-call(s32[1]{0:T(128)} %bitcast.me_ref.refs_0_, s32[5,6,16]{2,1,0:T(8,128)S(1)} %bitcast.12, s32[16]{0:T(128)S(1)} %copy-done.7, s32[1,4,1,5]{3,2,1,0:T(1,128)S(1)} %copy-done.6, ...), custom_call_target="tpu_custom_call" | custom-call | bytes 6291456 | tf_op jit(solution)/shard_map/pallas_call | solution.py:278
  129.0 3.0 %collective-permute-start.16 = (f32[1,2,256,256]{3,2,1,0:T(8,128)}, f32[1,2,256,256]{3,2,1,0:T(8,128)S(1)}, u32[]{:S(2)}, u32[]{:S(2)}) collective-permute-start(f32[1,2,256,256]{3,2,1,0:T(8,128)} %get-tuple-element.41), channel_id=1, source_target_pairs={{0,14},{1,15},{2,4},{3,5},{4,2},{5,3},{6,8},{7,9},{8,6},{9,7},{10,... | collective-permute-start | bytes 1572872 | tf_op jit(solution)/shard_map/ppermute | solution.py:38
  132.1 5.3 %collective-permute-start.11 = (f32[2,2,256,256]{3,2,1,0:T(8,128)S(1)}, f32[2,2,256,256]{3,2,1,0:T(8,128)S(1)}, u32[]{:S(2)}, u32[]{:S(2)}) collective-permute-start(f32[2,2,256,256]{3,2,1,0:T(8,128)S(1)} %get-tuple-element.36), channel_id=1, source_target_pairs={{0,4},{1,5},{2,6},{3,7},{4,0},{5,1},{6,2},{7,3},{8,12},{9,13},{10,... | collective-permute-start | bytes 3145736 | tf_op jit(solution)/shard_map/ppermute | solution.py:38
  137.4 7.8 %collective-permute-done.16.refs_10_ = f32[1,2,256,256]{3,2,1,0:T(8,128)S(1)} collective-permute-done((f32[1,2,256,256]{3,2,1,0:T(8,128)}, f32[1,2,256,256]{3,2,1,0:T(8,128)S(1)}, u32[]{:S(2)}, u32[]{:S(2)}) %collective-permute-start.16) | collective-permute-done | bytes 524320 | tf_op jit(solution)/shard_map/ppermute | solution.py:38
  145.2 3.6 %collective-permute-start.12 = (f32[1,2,256,256]{3,2,1,0:T(8,128)}, f32[1,2,256,256]{3,2,1,0:T(8,128)S(1)}, u32[]{:S(2)}, u32[]{:S(2)}) collective-permute-start(f32[1,2,256,256]{3,2,1,0:T(8,128)} %get-tuple-element.37), channel_id=1, source_target_pairs={{0,8},{1,9},{2,10},{3,11},{4,12},{5,13},{6,14},{7,15},{8,0},{9,1},... | collective-permute-start | bytes 1572872 | tf_op jit(solution)/shard_map/ppermute | solution.py:38
  148.7 27.5 %collective-permute-done.17.refs_11_ = f32[1,2,256,256]{3,2,1,0:T(8,128)S(1)} collective-permute-done((f32[1,2,256,256]{3,2,1,0:T(8,128)}, f32[1,2,256,256]{3,2,1,0:T(8,128)S(1)}, u32[]{:S(2)}, u32[]{:S(2)}) %collective-permute-start.17) | collective-permute-done | bytes 524320 | tf_op jit(solution)/shard_map/ppermute | solution.py:38
  176.2 8.7 %shard_map.89.refs_12_ = f32[8,2,256,256]{3,2,1,0:T(8,128)} custom-call(f32[8]{0:T(128)S(1)} %copy-done.9, f32[256,256]{1,0:T(8,128)S(1)} %copy-done.5, f32[8,2,256,256]{3,2,1,0:T(8,128)S(1)} %copy-done.1, f32[8,2,256,256]{3,2,1,0:T(8,128)} %refs_0_.1), custom_call_target="tpu_custom_call" | custom-call | flops 3221225472 | bytes 12582912 | tf_op jit(solution)/shard_map/pallas_call | solution.py:159
  184.9 5.0 %shard_map.90.refs_10_ = f32[8,2,256,256]{3,2,1,0:T(8,128)} custom-call(s32[1]{0:T(128)} %bitcast.me_ref.refs_0_, s32[5,6,16]{2,1,0:T(8,128)S(1)} %bitcast.13, s32[16]{0:T(128)S(1)} %copy-done.7, s32[1,4,1,5]{3,2,1,0:T(1,128)S(1)} %copy-done.6, f32[6,16]{1,0:T(8,128)S(1)} %fusion.1.refs_4_, f32[4,1]{1,0:T(4,128)S(1)} %bitcast.19, ...), custom_call_target="tpu_custom_call", output_to_operand_aliasing={{}: (12, {})} | custom-call | flops 1610612736 | bytes 10485760 | tf_op jit(solution)/shard_map/pallas_call | solution.py:253
  190.0 4.3 %shard_map.91.refs_11_ = f32[8,2,256,256]{3,2,1,0:T(8,128)} custom-call(s32[1]{0:T(128)} %bitcast.me_ref.refs_0_, s32[5,6,16]{2,1,0:T(8,128)S(1)} %bitcast.14, s32[16]{0:T(128)S(1)} %copy-done.7, s32[1,4,1,5]{3,2,1,0:T(1,128)S(1)} %copy-done.6, f32[6,16]{1,0:T(8,128)S(1)} %fusion.1.refs_4_, f32[4,1]{1,0:T(4,128)S(1)} %bitcast.20, ...), custom_call_target="tpu_custom_call", output_to_operand_aliasing={{}: (10, {})} | custom-call | flops 1610612736 | bytes 10485760 | tf_op jit(solution)/shard_map/pallas_call | solution.py:253
  194.3 11.2 %collective-permute-done.13.refs_10_ = f32[1,2,256,256]{3,2,1,0:T(8,128)S(1)} collective-permute-done((f32[1,2,256,256]{3,2,1,0:T(8,128)S(1)}, f32[1,2,256,256]{3,2,1,0:T(8,128)S(1)}, u32[]{:S(2)}, u32[]{:S(2)}) %collective-permute-start.13) | collective-permute-done | bytes 524320 | tf_op jit(solution)/shard_map/ppermute | solution.py:38
  205.5 4.6 %shard_map.92 = f32[8,2,256,256]{3,2,1,0:T(8,128)} custom-call(s32[1]{0:T(128)} %bitcast.me_ref.refs_0_, s32[5,6,16]{2,1,0:T(8,128)S(1)} %bitcast.15, s32[16]{0:T(128)S(1)} %copy-done.7, s32[1,4,1,5]{3,2,1,0:T(1,128)S(1)} %copy-done.6, f32[6,16]{1,0:T(8,128)S(1)} %fusion.1.refs_4_, f32[4,1]{1,0:T(4,128)S(1)} %bitcast.21, ...), custom_call_target="tpu_custom_call", output_to_operand_aliasing={{}: (11, {})} | custom-call | flops 1610612736 | bytes 10485760 | tf_op jit(solution)/shard_map/pallas_call | solution.py:253
  (47 shorter events, 15.1 us)
Async XLA Ops:
  2.1 30.9 %copy-start.5 = (f32[256,256]{1,0:T(8,128)S(1)}, f32[256,256]{1,0:T(8,128)}, u32[]{:S(2)}) copy-start(f32[256,256]{1,0:T(8,128)} %hamiltonian_ref.3) | copy-start | bytes 786436
  2.1 30.9 %copy-start.9 = (f32[8]{0:T(128)S(1)}, f32[8]{0:T(128)}, u32[]{:S(2)}) copy-start(f32[8]{0:T(128)} %damping_ref.3) | copy-start | bytes 100
  5.0 14.1 %collective-permute-start = (f32[1,2,256,256]{3,2,1,0:T(8,128)S(1)}, f32[1,2,256,256]{3,2,1,0:T(8,128)S(1)}, u32[]{:S(2)}, u32[]{:S(2)}) collective-permute-start(f32[1,2,256,256]{3,2,1,0:T(8,128)S(1)} %get-tuple-element.24), channel_id=1, source_target_pairs={{0,3},{1,4},{2,5},{3,6},{4,7},{5,8},{6,9},{7,10},{8,11},{9,12},{10... | collective-permute-start | bytes 1572872 | tf_op jit(solution)/shard_map/ppermute | solution.py:38
  6.3 19.4 %collective-permute-start.1 = (f32[1,2,256,256]{3,2,1,0:T(8,128)S(1)}, f32[1,2,256,256]{3,2,1,0:T(8,128)S(1)}, u32[]{:S(2)}, u32[]{:S(2)}) collective-permute-start(f32[1,2,256,256]{3,2,1,0:T(8,128)S(1)} %get-tuple-element.25), channel_id=1, source_target_pairs={{0,13},{1,14},{2,15},{3,0},{4,1},{5,2},{6,3},{7,4},{8,5},{9,6},{10... | collective-permute-start | bytes 1572872 | tf_op jit(solution)/shard_map/ppermute | solution.py:38
  6.8 75.2 %collective-permute-start.5 = (f32[2,2,256,256]{3,2,1,0:T(8,128)S(1)}, f32[2,2,256,256]{3,2,1,0:T(8,128)S(1)}, u32[]{:S(2)}, u32[]{:S(2)}) collective-permute-start(f32[2,2,256,256]{3,2,1,0:T(8,128)S(1)} %get-tuple-element.29), channel_id=1, source_target_pairs={{0,1},{1,0},{2,3},{3,2},{4,5},{5,4},{6,7},{7,6},{8,9},{9,8},{10,11... | collective-permute-start | bytes 3145736 | tf_op jit(solution)/shard_map/ppermute | solution.py:38
  29.0 53.1 %collective-permute-start.6 = (f32[2,2,256,256]{3,2,1,0:T(8,128)S(1)}, f32[2,2,256,256]{3,2,1,0:T(8,128)S(1)}, u32[]{:S(2)}, u32[]{:S(2)}) collective-permute-start(f32[2,2,256,256]{3,2,1,0:T(8,128)S(1)} %get-tuple-element.30), channel_id=1, source_target_pairs={{0,2},{1,3},{2,0},{3,1},{4,6},{5,7},{6,4},{7,5},{8,10},{9,11},{10,... | collective-permute-start | bytes 3145736 | tf_op jit(solution)/shard_map/ppermute | solution.py:38
  29.0 15.0 %collective-permute-start.7 = (f32[1,2,256,256]{3,2,1,0:T(8,128)S(1)}, f32[1,2,256,256]{3,2,1,0:T(8,128)S(1)}, u32[]{:S(2)}, u32[]{:S(2)}) collective-permute-start(f32[1,2,256,256]{3,2,1,0:T(8,128)S(1)} %get-tuple-element.31), channel_id=1, source_target_pairs={{0,14},{1,15},{2,4},{3,5},{4,2},{5,3},{6,8},{7,9},{8,6},{9,7},{10,... | collective-permute-start | bytes 1572872 | tf_op jit(solution)/shard_map/ppermute | solution.py:38
  30.7 45.9 %collective-permute-start.8 = (f32[1,2,256,256]{3,2,1,0:T(8,128)S(1)}, f32[1,2,256,256]{3,2,1,0:T(8,128)S(1)}, u32[]{:S(2)}, u32[]{:S(2)}) collective-permute-start(f32[1,2,256,256]{3,2,1,0:T(8,128)S(1)} %get-tuple-element.32), channel_id=1, source_target_pairs={{0,15},{1,2},{2,1},{3,4},{4,3},{5,6},{6,5},{7,8},{8,7},{9,10},{10,... | collective-permute-start | bytes 1572872 | tf_op jit(solution)/shard_map/ppermute | solution.py:38
  31.3 70.7 %collective-permute-start.2 = (f32[2,2,256,256]{3,2,1,0:T(8,128)S(1)}, f32[2,2,256,256]{3,2,1,0:T(8,128)S(1)}, u32[]{:S(2)}, u32[]{:S(2)}) collective-permute-start(f32[2,2,256,256]{3,2,1,0:T(8,128)S(1)} %get-tuple-element.26), channel_id=1, source_target_pairs={{0,4},{1,5},{2,6},{3,7},{4,0},{5,1},{6,2},{7,3},{8,12},{9,13},{10,... | collective-permute-start | bytes 3145736 | tf_op jit(solution)/shard_map/ppermute | solution.py:38
  33.0 44.2 %copy-start.2 = (f32[4,256,256]{2,1,0:T(8,128)S(1)}, f32[4,256,256]{2,1,0:T(8,128)}, u32[]{:S(2)}) copy-start(f32[4,256,256]{2,1,0:T(8,128)} %refs_7_.11) | copy-start | bytes 3145732
  33.0 44.2 %copy-start.4 = (s32[16,6,5]{0,1,2:T(8,128)S(1)}, s32[16,6,5]{0,1,2:T(8,128)}, u32[]{:S(2)}) copy-start(s32[16,6,5]{0,1,2:T(8,128)} %param.14) | copy-start | bytes 5764
  33.0 44.2 %copy-start.8 = (f32[4,2]{0,1:T(2,128)S(1)}, f32[4,2]{0,1:T(2,128)}, u32[]{:S(2)}) copy-start(f32[4,2]{0,1:T(2,128)} %param.11) | copy-start | bytes 100
  44.0 42.3 %collective-permute-start.3 = (f32[1,2,256,256]{3,2,1,0:T(8,128)S(1)}, f32[1,2,256,256]{3,2,1,0:T(8,128)S(1)}, u32[]{:S(2)}, u32[]{:S(2)}) collective-permute-start(f32[1,2,256,256]{3,2,1,0:T(8,128)S(1)} %get-tuple-element.27), channel_id=1, source_target_pairs={{0,8},{1,9},{2,10},{3,11},{4,12},{5,13},{6,14},{7,15},{8,0},{9,1},... | collective-permute-start | bytes 1572872 | tf_op jit(solution)/shard_map/ppermute | solution.py:38
  76.7 25.3 %collective-permute-start.4 = (f32[1,2,256,256]{3,2,1,0:T(8,128)S(1)}, f32[1,2,256,256]{3,2,1,0:T(8,128)S(1)}, u32[]{:S(2)}, u32[]{:S(2)}) collective-permute-start(f32[1,2,256,256]{3,2,1,0:T(8,128)S(1)} %get-tuple-element.28), channel_id=1, source_target_pairs={{0,12},{1,13},{2,14},{3,15},{4,8},{5,9},{6,10},{7,11},{8,4},{9,5},... | collective-permute-start | bytes 1572872 | tf_op jit(solution)/shard_map/ppermute | solution.py:38
  109.0 67.2 %copy-start.1 = (f32[8,2,256,256]{3,2,1,0:T(8,128)S(1)}, f32[8,2,256,256]{3,2,1,0:T(8,128)}, u32[]{:S(2)}) copy-start(f32[8,2,256,256]{3,2,1,0:T(8,128)} %get-tuple-element.33.source.density_ref) | copy-start | bytes 12582916
  109.0 14.0 %collective-permute-start.9 = (f32[1,2,256,256]{3,2,1,0:T(8,128)S(1)}, f32[1,2,256,256]{3,2,1,0:T(8,128)S(1)}, u32[]{:S(2)}, u32[]{:S(2)}) collective-permute-start(f32[1,2,256,256]{3,2,1,0:T(8,128)S(1)} %get-tuple-element.34), channel_id=1, source_target_pairs={{0,3},{1,4},{2,5},{3,6},{4,7},{5,8},{6,9},{7,10},{8,11},{9,12},{10... | collective-permute-start | bytes 1572872 | tf_op jit(solution)/shard_map/ppermute | solution.py:38
  109.1 16.0 %collective-permute-start.10 = (f32[1,2,256,256]{3,2,1,0:T(8,128)S(1)}, f32[1,2,256,256]{3,2,1,0:T(8,128)S(1)}, u32[]{:S(2)}, u32[]{:S(2)}) collective-permute-start(f32[1,2,256,256]{3,2,1,0:T(8,128)S(1)} %get-tuple-element.35), channel_id=1, source_target_pairs={{0,13},{1,14},{2,15},{3,0},{4,1},{5,2},{6,3},{7,4},{8,5},{9,6},{10... | collective-permute-start | bytes 1572872 | tf_op jit(solution)/shard_map/ppermute | solution.py:38
  110.8 79.2 %collective-permute-start.14 = (f32[2,2,256,256]{3,2,1,0:T(8,128)S(1)}, f32[2,2,256,256]{3,2,1,0:T(8,128)S(1)}, u32[]{:S(2)}, u32[]{:S(2)}) collective-permute-start(f32[2,2,256,256]{3,2,1,0:T(8,128)S(1)} %get-tuple-element.39), channel_id=1, source_target_pairs={{0,1},{1,0},{2,3},{3,2},{4,5},{5,4},{6,7},{7,6},{8,9},{9,8},{10,11... | collective-permute-start | bytes 3145736 | tf_op jit(solution)/shard_map/ppermute | solution.py:38
  129.0 61.0 %collective-permute-start.15 = (f32[2,2,256,256]{3,2,1,0:T(8,128)S(1)}, f32[2,2,256,256]{3,2,1,0:T(8,128)S(1)}, u32[]{:S(2)}, u32[]{:S(2)}) collective-permute-start(f32[2,2,256,256]{3,2,1,0:T(8,128)S(1)} %get-tuple-element.40), channel_id=1, source_target_pairs={{0,2},{1,3},{2,0},{3,1},{4,6},{5,7},{6,4},{7,5},{8,10},{9,11},{10,... | collective-permute-start | bytes 3145736 | tf_op jit(solution)/shard_map/ppermute | solution.py:38
  129.0 16.1 %collective-permute-start.16 = (f32[1,2,256,256]{3,2,1,0:T(8,128)}, f32[1,2,256,256]{3,2,1,0:T(8,128)S(1)}, u32[]{:S(2)}, u32[]{:S(2)}) collective-permute-start(f32[1,2,256,256]{3,2,1,0:T(8,128)} %get-tuple-element.41), channel_id=1, source_target_pairs={{0,14},{1,15},{2,4},{3,5},{4,2},{5,3},{6,8},{7,9},{8,6},{9,7},{10,... | collective-permute-start | bytes 1572872 | tf_op jit(solution)/shard_map/ppermute | solution.py:38
  132.1 44.1 %collective-permute-start.17 = (f32[1,2,256,256]{3,2,1,0:T(8,128)}, f32[1,2,256,256]{3,2,1,0:T(8,128)S(1)}, u32[]{:S(2)}, u32[]{:S(2)}) collective-permute-start(f32[1,2,256,256]{3,2,1,0:T(8,128)} %get-tuple-element.42), channel_id=1, source_target_pairs={{0,15},{1,2},{2,1},{3,4},{4,3},{5,6},{6,5},{7,8},{8,7},{9,10},{10,... | collective-permute-start | bytes 1572872 | tf_op jit(solution)/shard_map/ppermute | solution.py:38
  132.1 73.4 %collective-permute-start.11 = (f32[2,2,256,256]{3,2,1,0:T(8,128)S(1)}, f32[2,2,256,256]{3,2,1,0:T(8,128)S(1)}, u32[]{:S(2)}, u32[]{:S(2)}) collective-permute-start(f32[2,2,256,256]{3,2,1,0:T(8,128)S(1)} %get-tuple-element.36), channel_id=1, source_target_pairs={{0,4},{1,5},{2,6},{3,7},{4,0},{5,1},{6,2},{7,3},{8,12},{9,13},{10,... | collective-permute-start | bytes 3145736 | tf_op jit(solution)/shard_map/ppermute | solution.py:38
  145.2 49.1 %collective-permute-start.12 = (f32[1,2,256,256]{3,2,1,0:T(8,128)}, f32[1,2,256,256]{3,2,1,0:T(8,128)S(1)}, u32[]{:S(2)}, u32[]{:S(2)}) collective-permute-start(f32[1,2,256,256]{3,2,1,0:T(8,128)} %get-tuple-element.37), channel_id=1, source_target_pairs={{0,8},{1,9},{2,10},{3,11},{4,12},{5,13},{6,14},{7,15},{8,0},{9,1},... | collective-permute-start | bytes 1572872 | tf_op jit(solution)/shard_map/ppermute | solution.py:38
  176.2 29.3 %collective-permute-start.13 = (f32[1,2,256,256]{3,2,1,0:T(8,128)S(1)}, f32[1,2,256,256]{3,2,1,0:T(8,128)S(1)}, u32[]{:S(2)}, u32[]{:S(2)}) collective-permute-start(f32[1,2,256,256]{3,2,1,0:T(8,128)S(1)} %get-tuple-element.38), channel_id=1, source_target_pairs={{0,12},{1,13},{2,14},{3,15},{4,8},{5,9},{6,10},{7,11},{8,4},{9,5},... | collective-permute-start | bytes 1572872 | tf_op jit(solution)/shard_map/ppermute | solution.py:38
  (5 other events, 5.1 us)

commit v5 on v4

--- a/solution.py
+++ b/solution.py
@@ -49,8 +49,8 @@
         (others if distance < REACH else far).insert(0, Exchange("other", distance, size))
     for colour in range(colours):
         if 1 << colour > REACH:
-            far.insert(0, Exchange("swap", 1 << colour, size, colour, listed=False))
-    return shifts, others, swaps, far
+            swaps.insert(1, Exchange("swap", 1 << colour, size, colour, listed=False))
+    return shifts + others + swaps[:1], swaps[1:] + far
 
 
 def payload(exchange, pairs):
@@ -115,8 +115,7 @@
 
 
 def pack_kernel(plan, mats, me_ref, left_ref, count_ref, match_ref, source, *rest):
-    rest, (held, load_sems, sems) = rest[:-3], rest[-3:]
-    sends = rest[len(rest) - len(plan) :]
+    sends, (held, load_sems, sems) = rest[:-3], rest[-3:]
     loads, stores = [], []
     for exchange, send in zip(plan, sends):
         slots = outgoing_slots(exchange, me_ref[0], mats, left_ref, count_ref, match_ref)
@@ -272,12 +271,12 @@
     )(*tables, couplings, *arrivals, acc)
 
 
-def pack_call(plan, pairs, tables, source, *after):
+def pack_call(plan, pairs, tables, source):
     mats, _, order, _ = source.shape
     sent = sum(payload(e, pairs) for e in plan)
     return pl.pallas_call(
         functools.partial(pack_kernel, plan, mats),
-        in_specs=[SMEM] * 4 + [HBM] + [ANY] * len(after),
+        in_specs=[SMEM] * 4 + [HBM],
         out_specs=[HBM] * len(plan),
         out_shape=[jax.ShapeDtypeStruct((payload(e, pairs), 2, order, order), F32) for e in plan],
         scratch_shapes=[
@@ -287,36 +286,30 @@
         ],
         compiler_params=pltpu.CompilerParams(vmem_limit_bytes=GRANT),
         cost_estimate=pl.CostEstimate(flops=0, bytes_accessed=sent * 16 * order**2, transcendentals=0),
-    )(*tables[:4], source, *after)
+    )(*tables[:4], source)
 
 
 def body(rho, hamiltonian, couplings, bath_coef, damping, match_edges, left_rows, left_count):
     colours, pairs = match_edges.shape[1:3]
-    shifts, others, swaps, far = exchanges(lax.axis_size("tier"), colours)
+    early, late = exchanges(lax.axis_size("tier"), colours)
     me = lax.axis_index("tier").astype(jnp.int32)[None]
     left_fields = jnp.transpose(left_rows, (2, 1, 0))
     left_root = jnp.sqrt(left_fields[4].astype(F32))
     match_root = jnp.sqrt(match_edges[0, :, :, 4].astype(F32))
     tables = (me, left_fields, left_count, match_edges, left_root, match_root, bath_coef.T)
 
-    near, later = shifts + others + swaps[:1], swaps[1:] + far
-
-    def gather(density, near_sends, acc, scale, packs):
-        arrived = [e.permute(s) for e, s in zip(near, near_sends)]
-        sends = pack_call(later, pairs, tables, density, *arrived[: len(shifts)])
-        arrived += [e.permute(s) for e, s in zip(later, sends)]
-        first, second = len(shifts + others), len(near) + 1
-        order = near + later
-        for a, b in ((0, first), (first, second), (second, len(order))):
-            got = rows_call(
-                order[a:b], packs if b == len(order) else [], pairs, scale, tables, couplings, arrived[a:b], acc
-            )
-            acc = got[0]
-        return acc, got[1:]
-
-    sends = pack_call(near, pairs, tables, rho)
-    first, sends = gather(rho, sends, local_call(damping, hamiltonian, rho), 1.0, near)
-    return gather(first, sends, local_call(damping, hamiltonian, first, rho), 0.5 * STEP * STEP, [])[0]
+    plan = early + late
+
+    def gather(sends, acc, scale, packs):
+        arrived = [e.permute(s) for e, s in zip(plan, sends)]
+        cut = len(early)
+        acc = rows_call(early, [], pairs, scale, tables, couplings, arrived[:cut], acc)[0]
+        acc, *sends = rows_call(late, packs, pairs, scale, tables, couplings, arrived[cut:], acc)
+        return acc, sends
+
+    sends = pack_call(plan, pairs, tables, rho)
+    first, sends = gather(sends, local_call(damping, hamiltonian, rho), 1.0, plan)
+    return gather(sends, local_call(damping, hamiltonian, first, rho), 0.5 * STEP * STEP, [])[0]
 
 
 def solution(mesh):

time: 211 us -> 193 us (0.915)
  the two profiles are of different devices: /device:TPU:14 before, /device:TPU:0 now
where the time goes in v5:
time: 193 us; the launch traced here: 191 us
  waiting for transfers between devices  81.2 us (42%)
  starting transfers between devices  59 us (31%)
  Pallas kernels  43.5 us (23%)
  local copies, waits for them, and re-layouts  7.28 us (4%)
    ppermute x18, waiting for transfers between devices, permute(): lax.ppermute(value, 'tier', [(i, self.peer(i, True)) for i in range(self....  81.2 us
    ppermute x18, starting transfers between devices, permute(): lax.ppermute(value, 'tier', [(i, self.peer(i, True)) for i in range(self....  59 us
    pallas_call x4, Pallas kernels, rows_call(): pl.pallas_call(functools.partial(rows_kernel, plan, packs, scale), in_spe...  22.5 us
    pallas_call x2, Pallas kernels, local_call(): pl.pallas_call(functools.partial(local_kernel, len(densities) == 2), grid...  16.1 us
    unnamed x24, local copies, waits for them, and re-layouts  7.28 us
    pallas_call x1, Pallas kernels, pack_call(): pl.pallas_call(functools.partial(pack_kernel, plan, mats), in_specs=[SMEM...  4.86 us
  transfers between devices with their start and end apart: 18, of which 10 were waited for; matrix products, arithmetic and copies ran while one was open for 0% of the time, Pallas kernels for 13%

profile of v5, /device:TPU:0, one launch (start us, length us, event | category | flops | bytes accessed | tf_op | source)
XLA Modules:
  0.0 191.4 jit_solution(9883769609340654845)
XLA Ops:
  2.1 4.9 %shard_map.82 = (f32[1,2,256,256]{3,2,1,0:T(8,128)S(1)}, f32[1,2,256,256]{3,2,1,0:T(8,128)S(1)}, f32[1,2,256,256]{3,2,1,0:T(8,128)S(1)}, f32[1,2,256,256]{3,2,1,...) custom-call(s32[1]{0:T(128)} %bitcast.me_ref.refs_0_, ...), custom_call_target="tpu_custom_call" | custom-call | bytes 12582912 | tf_op jit(solution)/shard_map/pallas_call | solution.py:277
  6.9 3.2 %collective-permute-start.4 = (f32[1,2,256,256]{3,2,1,0:T(8,128)S(1)}, f32[1,2,256,256]{3,2,1,0:T(8,128)S(1)}, u32[]{:S(2)}, u32[]{:S(2)}) collective-permute-start(f32[1,2,256,256]{3,2,1,0:T(8,128)S(1)} %get-tuple-element.28), channel_id=1, source_target_pairs={{0,3},{1,4},{2,5},{3,6},{4,7},{5,8},{6,9},{7,10},{8,11},{9,12},{10... | collective-permute-start | bytes 1572872 | tf_op jit(solution)/shard_map/ppermute | solution.py:38
  17.7 3.7 %collective-permute-done.4.refs_8_ = f32[1,2,256,256]{3,2,1,0:T(8,128)S(1)} collective-permute-done((f32[1,2,256,256]{3,2,1,0:T(8,128)S(1)}, f32[1,2,256,256]{3,2,1,0:T(8,128)S(1)}, u32[]{:S(2)}, u32[]{:S(2)}) %collective-permute-start.4) | collective-permute-done | bytes 524320 | tf_op jit(solution)/shard_map/ppermute | solution.py:38
  21.5 4.8 %collective-permute-start.1 = (f32[2,2,256,256]{3,2,1,0:T(8,128)S(1)}, f32[2,2,256,256]{3,2,1,0:T(8,128)S(1)}, u32[]{:S(2)}, u32[]{:S(2)}) collective-permute-start(f32[2,2,256,256]{3,2,1,0:T(8,128)S(1)} %get-tuple-element.25), channel_id=1, source_target_pairs={{0,2},{1,3},{2,0},{3,1},{4,6},{5,7},{6,4},{7,5},{8,10},{9,11},{10,... | collective-permute-start | bytes 3145736 | tf_op jit(solution)/shard_map/ppermute | solution.py:38
  26.9 5.7 %collective-permute-start.2 = (f32[2,2,256,256]{3,2,1,0:T(8,128)}, f32[2,2,256,256]{3,2,1,0:T(8,128)}, u32[]{:S(2)}, u32[]{:S(2)}) collective-permute-start(f32[2,2,256,256]{3,2,1,0:T(8,128)} %get-tuple-element.26), channel_id=1, source_target_pairs={{0,4},{1,5},{2,6},{3,7},{4,0},{5,1},{6,2},{7,3},{8,12},{9,13},{10,... | collective-permute-start | bytes 3145736 | tf_op jit(solution)/shard_map/ppermute | solution.py:38
  32.8 16.0 %collective-permute-done.6.refs_10_ = f32[1,2,256,256]{3,2,1,0:T(8,128)S(1)} collective-permute-done((f32[1,2,256,256]{3,2,1,0:T(8,128)S(1)}, f32[1,2,256,256]{3,2,1,0:T(8,128)S(1)}, u32[]{:S(2)}, u32[]{:S(2)}) %collective-permute-start.6) | collective-permute-done | bytes 524320 | tf_op jit(solution)/shard_map/ppermute | solution.py:38
  50.8 7.3 %shard_map.83.refs_13_ = f32[8,2,256,256]{3,2,1,0:T(8,128)S(1)} custom-call(f32[8]{0:T(128)S(1)} %copy-done.10, f32[256,256]{1,0:T(8,128)S(1)} %copy-done.6, f32[8,2,256,256]{3,2,1,0:T(8,128)} %refs_0_.1), custom_call_target="tpu_custom_call" | custom-call | flops 3221225472 | bytes 8388608 | tf_op jit(solution)/shard_map/pallas_call | solution.py:158
  60.1 3.9 %shard_map.84.refs_12_ = f32[8,2,256,256]{3,2,1,0:T(8,128)} custom-call(s32[1]{0:T(128)} %bitcast.me_ref.refs_0_, s32[5,6,16]{2,1,0:T(8,128)S(1)} %bitcast.8, s32[16]{0:T(128)S(1)} %copy-done.9, s32[1,4,1,5]{3,2,1,0:T(1,128)S(1)} %copy-done.7, f32[6,16]{1,0:T(8,128)S(1)} %fusion.1.refs_4_, f32[4,1]{1,0:T(4,128)S(1)} %bitcast.12, ...), custom_call_target="tpu_custom_call", output_to_operand_aliasing={{}: (13, {})} | custom-call | flops 2415919104 | bytes 11534336 | tf_op jit(solution)/shard_map/pallas_call | solution.py:252
  64.1 16.5 %collective-permute-done.refs_8_ = f32[1,2,256,256]{3,2,1,0:T(8,128)S(1)} collective-permute-done((f32[1,2,256,256]{3,2,1,0:T(8,128)S(1)}, f32[1,2,256,256]{3,2,1,0:T(8,128)S(1)}, u32[]{:S(2)}, u32[]{:S(2)}) %collective-permute-start) | collective-permute-done | bytes 524320 | tf_op jit(solution)/shard_map/ppermute | solution.py:38
  80.6 11.3 %collective-permute-done.3.refs_11_ = f32[1,2,256,256]{3,2,1,0:T(8,128)S(1)} collective-permute-done((f32[1,2,256,256]{3,2,1,0:T(8,128)S(1)}, f32[1,2,256,256]{3,2,1,0:T(8,128)S(1)}, u32[]{:S(2)}, u32[]{:S(2)}) %collective-permute-start.3) | collective-permute-done | bytes 524320 | tf_op jit(solution)/shard_map/ppermute | solution.py:38
  92.9 8.3 %shard_map.85 = (f32[8,2,256,256]{3,2,1,0:T(8,128)}, f32[1,2,256,256]{3,2,1,0:T(8,128)S(1)}, f32[1,2,256,256]{3,2,1,0:T(8,128)S(1)}, f32[1,2,256,256]{3,2,1,0:T(...) custom-call(s32[1]{0:T(128)} %bitcast.me_ref.refs_0_, ...), custom_call_target="tpu_custom_call", output_to_operand_aliasing={{0}: (12, {})} | custom-call | flops 2415919104 | bytes 17825792 | tf_op jit(solution)/shard_map/pallas_call | solution.py:252
  101.2 3.5 %collective-permute-start.14 = (f32[1,2,256,256]{3,2,1,0:T(8,128)S(1)}, f32[1,2,256,256]{3,2,1,0:T(8,128)S(1)}, u32[]{:S(2)}, u32[]{:S(2)}) collective-permute-start(f32[1,2,256,256]{3,2,1,0:T(8,128)S(1)} %get-tuple-element.38), channel_id=1, source_target_pairs={{0,13},{1,14},{2,15},{3,0},{4,1},{5,2},{6,3},{7,4},{8,5},{9,6},{10... | collective-permute-start | bytes 1572872 | tf_op jit(solution)/shard_map/ppermute | solution.py:38
  104.8 3.3 %collective-permute-start.15 = (f32[1,2,256,256]{3,2,1,0:T(8,128)S(1)}, f32[1,2,256,256]{3,2,1,0:T(8,128)S(1)}, u32[]{:S(2)}, u32[]{:S(2)}) collective-permute-start(f32[1,2,256,256]{3,2,1,0:T(8,128)S(1)} %get-tuple-element.39), channel_id=1, source_target_pairs={{0,14},{1,15},{2,4},{3,5},{4,2},{5,3},{6,8},{7,9},{8,6},{9,7},{10,... | collective-permute-start | bytes 1572872 | tf_op jit(solution)/shard_map/ppermute | solution.py:38
  109.3 5.9 %collective-permute-done.13.refs_8_ = f32[1,2,256,256]{3,2,1,0:T(8,128)S(1)} collective-permute-done((f32[1,2,256,256]{3,2,1,0:T(8,128)S(1)}, f32[1,2,256,256]{3,2,1,0:T(8,128)S(1)}, u32[]{:S(2)}, u32[]{:S(2)}) %collective-permute-start.13) | collective-permute-done | bytes 524320 | tf_op jit(solution)/shard_map/ppermute | solution.py:38
  115.2 5.0 %collective-permute-start.10 = (f32[2,2,256,256]{3,2,1,0:T(8,128)}, f32[2,2,256,256]{3,2,1,0:T(8,128)S(1)}, u32[]{:S(2)}, u32[]{:S(2)}) collective-permute-start(f32[2,2,256,256]{3,2,1,0:T(8,128)} %get-tuple-element.34), channel_id=1, source_target_pairs={{0,2},{1,3},{2,0},{3,1},{4,6},{5,7},{6,4},{7,5},{8,10},{9,11},{10,... | collective-permute-start | bytes 3145736 | tf_op jit(solution)/shard_map/ppermute | solution.py:38
  120.2 6.2 %collective-permute-start.11 = (f32[2,2,256,256]{3,2,1,0:T(8,128)}, f32[2,2,256,256]{3,2,1,0:T(8,128)S(1)}, u32[]{:S(2)}, u32[]{:S(2)}) collective-permute-start(f32[2,2,256,256]{3,2,1,0:T(8,128)} %get-tuple-element.35), channel_id=1, source_target_pairs={{0,4},{1,5},{2,6},{3,7},{4,0},{5,1},{6,2},{7,3},{8,12},{9,13},{10,... | collective-permute-start | bytes 3145736 | tf_op jit(solution)/shard_map/ppermute | solution.py:38
  126.5 8.9 %collective-permute-done.15.refs_10_ = f32[1,2,256,256]{3,2,1,0:T(8,128)S(1)} collective-permute-done((f32[1,2,256,256]{3,2,1,0:T(8,128)S(1)}, f32[1,2,256,256]{3,2,1,0:T(8,128)S(1)}, u32[]{:S(2)}, u32[]{:S(2)}) %collective-permute-start.15) | collective-permute-done | bytes 524320 | tf_op jit(solution)/shard_map/ppermute | solution.py:38
  135.3 2.7 %collective-permute-start.9 = (f32[1,2,256,256]{3,2,1,0:T(8,128)S(1)}, f32[1,2,256,256]{3,2,1,0:T(8,128)S(1)}, u32[]{:S(2)}, u32[]{:S(2)}) collective-permute-start(f32[1,2,256,256]{3,2,1,0:T(8,128)S(1)} %get-tuple-element.33), channel_id=1, source_target_pairs={{0,8},{1,9},{2,10},{3,11},{4,12},{5,13},{6,14},{7,15},{8,0},{9,1},... | collective-permute-start | bytes 1572872 | tf_op jit(solution)/shard_map/ppermute | solution.py:38
  138.0 4.2 %collective-permute-done.16.refs_11_ = f32[1,2,256,256]{3,2,1,0:T(8,128)S(1)} collective-permute-done((f32[1,2,256,256]{3,2,1,0:T(8,128)S(1)}, f32[1,2,256,256]{3,2,1,0:T(8,128)S(1)}, u32[]{:S(2)}, u32[]{:S(2)}) %collective-permute-start.16) | collective-permute-done | bytes 524320 | tf_op jit(solution)/shard_map/ppermute | solution.py:38
  142.2 13.7 %collective-permute-start.12 = (f32[1,2,256,256]{3,2,1,0:T(8,128)S(1)}, f32[1,2,256,256]{3,2,1,0:T(8,128)S(1)}, u32[]{:S(2)}, u32[]{:S(2)}) collective-permute-start(f32[1,2,256,256]{3,2,1,0:T(8,128)S(1)} %get-tuple-element.36), channel_id=1, source_target_pairs={{0,12},{1,13},{2,14},{3,15},{4,8},{5,9},{6,10},{7,11},{8,4},{9,5},... | collective-permute-start | bytes 1572872 | tf_op jit(solution)/shard_map/ppermute | solution.py:38
  158.1 8.8 %shard_map.86.refs_13_ = f32[8,2,256,256]{3,2,1,0:T(8,128)} custom-call(f32[8]{0:T(128)S(1)} %copy-done.10, f32[256,256]{1,0:T(8,128)S(1)} %copy-done.6, f32[8,2,256,256]{3,2,1,0:T(8,128)S(1)} %copy-done.1, f32[8,2,256,256]{3,2,1,0:T(8,128)} %refs_0_.1), custom_call_target="tpu_custom_call" | custom-call | flops 3221225472 | bytes 12582912 | tf_op jit(solution)/shard_map/pallas_call | solution.py:158
  166.9 4.0 %shard_map.87.refs_12_ = f32[8,2,256,256]{3,2,1,0:T(8,128)} custom-call(s32[1]{0:T(128)} %bitcast.me_ref.refs_0_, s32[5,6,16]{2,1,0:T(8,128)S(1)} %bitcast.10, s32[16]{0:T(128)S(1)} %copy-done.9, s32[1,4,1,5]{3,2,1,0:T(1,128)S(1)} %copy-done.7, f32[6,16]{1,0:T(8,128)S(1)} %fusion.1.refs_4_, f32[4,1]{1,0:T(4,128)S(1)} %bitcast.14, ...), custom_call_target="tpu_custom_call", output_to_operand_aliasing={{}: (13, {})} | custom-call | flops 2415919104 | bytes 11534336 | tf_op jit(solution)/shard_map/pallas_call | solution.py:252
  173.4 11.4 %collective-permute-done.12.refs_11_ = f32[1,2,256,256]{3,2,1,0:T(8,128)S(1)} collective-permute-done((f32[1,2,256,256]{3,2,1,0:T(8,128)S(1)}, f32[1,2,256,256]{3,2,1,0:T(8,128)S(1)}, u32[]{:S(2)}, u32[]{:S(2)}) %collective-permute-start.12) | collective-permute-done | bytes 524320 | tf_op jit(solution)/shard_map/ppermute | solution.py:38
  184.9 6.3 %shard_map.88 = f32[8,2,256,256]{3,2,1,0:T(8,128)} custom-call(s32[1]{0:T(128)} %bitcast.me_ref.refs_0_, s32[5,6,16]{2,1,0:T(8,128)S(1)} %bitcast.11, s32[16]{0:T(128)S(1)} %copy-done.9, s32[1,4,1,5]{3,2,1,0:T(1,128)S(1)} %copy-done.7, f32[6,16]{1,0:T(8,128)S(1)} %fusion.1.refs_4_, f32[4,1]{1,0:T(4,128)S(1)} %bitcast.15, ...), custom_call_target="tpu_custom_call", output_to_operand_aliasing={{}: (12, {})} | custom-call | flops 2415919104 | bytes 11534336 | tf_op jit(solution)/shard_map/pallas_call | solution.py:252
  (45 shorter events, 21.4 us)
Async XLA Ops:
  0.0 50.8 %copy-start.10 = (f32[8]{0:T(128)S(1)}, f32[8]{0:T(128)}, u32[]{:S(2)}) copy-start(f32[8]{0:T(128)} %damping_ref.3) | copy-start | bytes 100
  2.1 48.7 %copy-start.6 = (f32[256,256]{1,0:T(8,128)S(1)}, f32[256,256]{1,0:T(8,128)}, u32[]{:S(2)}) copy-start(f32[256,256]{1,0:T(8,128)} %hamiltonian_ref.3) | copy-start | bytes 786436
  6.9 14.5 %collective-permute-start.4 = (f32[1,2,256,256]{3,2,1,0:T(8,128)S(1)}, f32[1,2,256,256]{3,2,1,0:T(8,128)S(1)}, u32[]{:S(2)}, u32[]{:S(2)}) collective-permute-start(f32[1,2,256,256]{3,2,1,0:T(8,128)S(1)} %get-tuple-element.28), channel_id=1, source_target_pairs={{0,3},{1,4},{2,5},{3,6},{4,7},{5,8},{6,9},{7,10},{8,11},{9,12},{10... | collective-permute-start | bytes 1572872 | tf_op jit(solution)/shard_map/ppermute | solution.py:38
  10.2 16.7 %collective-permute-start.5 = (f32[1,2,256,256]{3,2,1,0:T(8,128)S(1)}, f32[1,2,256,256]{3,2,1,0:T(8,128)S(1)}, u32[]{:S(2)}, u32[]{:S(2)}) collective-permute-start(f32[1,2,256,256]{3,2,1,0:T(8,128)S(1)} %get-tuple-element.29), channel_id=1, source_target_pairs={{0,13},{1,14},{2,15},{3,0},{4,1},{5,2},{6,3},{7,4},{8,5},{9,6},{10... | collective-permute-start | bytes 1572872 | tf_op jit(solution)/shard_map/ppermute | solution.py:38
  11.9 48.2 %collective-permute-start.8 = (f32[2,2,256,256]{3,2,1,0:T(8,128)S(1)}, f32[2,2,256,256]{3,2,1,0:T(8,128)S(1)}, u32[]{:S(2)}, u32[]{:S(2)}) collective-permute-start(f32[2,2,256,256]{3,2,1,0:T(8,128)S(1)} %get-tuple-element.32), channel_id=1, source_target_pairs={{0,1},{1,0},{2,3},{3,2},{4,5},{5,4},{6,7},{7,6},{8,9},{9,8},{10,11... | collective-permute-start | bytes 3145736 | tf_op jit(solution)/shard_map/ppermute | solution.py:38
  13.7 35.1 %collective-permute-start.6 = (f32[1,2,256,256]{3,2,1,0:T(8,128)S(1)}, f32[1,2,256,256]{3,2,1,0:T(8,128)S(1)}, u32[]{:S(2)}, u32[]{:S(2)}) collective-permute-start(f32[1,2,256,256]{3,2,1,0:T(8,128)S(1)} %get-tuple-element.30), channel_id=1, source_target_pairs={{0,14},{1,15},{2,4},{3,5},{4,2},{5,3},{6,8},{7,9},{8,6},{9,7},{10,... | collective-permute-start | bytes 1572872 | tf_op jit(solution)/shard_map/ppermute | solution.py:38
  15.3 33.5 %collective-permute-start.7 = (f32[1,2,256,256]{3,2,1,0:T(8,128)S(1)}, f32[1,2,256,256]{3,2,1,0:T(8,128)S(1)}, u32[]{:S(2)}, u32[]{:S(2)}) collective-permute-start(f32[1,2,256,256]{3,2,1,0:T(8,128)S(1)} %get-tuple-element.31), channel_id=1, source_target_pairs={{0,15},{1,2},{2,1},{3,4},{4,3},{5,6},{6,5},{7,8},{8,7},{9,10},{10,... | collective-permute-start | bytes 1572872 | tf_op jit(solution)/shard_map/ppermute | solution.py:38
  21.5 70.4 %collective-permute-start.1 = (f32[2,2,256,256]{3,2,1,0:T(8,128)S(1)}, f32[2,2,256,256]{3,2,1,0:T(8,128)S(1)}, u32[]{:S(2)}, u32[]{:S(2)}) collective-permute-start(f32[2,2,256,256]{3,2,1,0:T(8,128)S(1)} %get-tuple-element.25), channel_id=1, source_target_pairs={{0,2},{1,3},{2,0},{3,1},{4,6},{5,7},{6,4},{7,5},{8,10},{9,11},{10,... | collective-permute-start | bytes 3145736 | tf_op jit(solution)/shard_map/ppermute | solution.py:38
  26.9 64.9 %collective-permute-start.2 = (f32[2,2,256,256]{3,2,1,0:T(8,128)}, f32[2,2,256,256]{3,2,1,0:T(8,128)}, u32[]{:S(2)}, u32[]{:S(2)}) collective-permute-start(f32[2,2,256,256]{3,2,1,0:T(8,128)} %get-tuple-element.26), channel_id=1, source_target_pairs={{0,4},{1,5},{2,6},{3,7},{4,0},{5,1},{6,2},{7,3},{8,12},{9,13},{10,... | collective-permute-start | bytes 3145736 | tf_op jit(solution)/shard_map/ppermute | solution.py:38
  48.8 31.8 %collective-permute-start = (f32[1,2,256,256]{3,2,1,0:T(8,128)S(1)}, f32[1,2,256,256]{3,2,1,0:T(8,128)S(1)}, u32[]{:S(2)}, u32[]{:S(2)}) collective-permute-start(f32[1,2,256,256]{3,2,1,0:T(8,128)S(1)} %get-tuple-element.24), channel_id=1, source_target_pairs={{0,8},{1,9},{2,10},{3,11},{4,12},{5,13},{6,14},{7,15},{8,0},{9,1},... | collective-permute-start | bytes 1572872 | tf_op jit(solution)/shard_map/ppermute | solution.py:38
  48.8 11.4 %copy-start.2 = (f32[4,256,256]{2,1,0:T(8,128)S(1)}, f32[4,256,256]{2,1,0:T(8,128)}, u32[]{:S(2)}) copy-start(f32[4,256,256]{2,1,0:T(8,128)} %refs_7_.7) | copy-start | bytes 3145732
  48.8 11.4 %copy-start.5 = (s32[16,6,5]{0,1,2:T(8,128)S(1)}, s32[16,6,5]{0,1,2:T(8,128)}, u32[]{:S(2)}) copy-start(s32[16,6,5]{0,1,2:T(8,128)} %param.14) | copy-start | bytes 5764
  48.8 11.4 %copy-start.8 = (f32[4,2]{0,1:T(2,128)S(1)}, f32[4,2]{0,1:T(2,128)}, u32[]{:S(2)}) copy-start(f32[4,2]{0,1:T(2,128)} %param.11) | copy-start | bytes 100
  48.8 43.1 %collective-permute-start.3 = (f32[1,2,256,256]{3,2,1,0:T(8,128)S(1)}, f32[1,2,256,256]{3,2,1,0:T(8,128)S(1)}, u32[]{:S(2)}, u32[]{:S(2)}) collective-permute-start(f32[1,2,256,256]{3,2,1,0:T(8,128)S(1)} %get-tuple-element.27), channel_id=1, source_target_pairs={{0,12},{1,13},{2,14},{3,15},{4,8},{5,9},{6,10},{7,11},{8,4},{9,5},... | collective-permute-start | bytes 1572872 | tf_op jit(solution)/shard_map/ppermute | solution.py:38
  101.2 14.1 %collective-permute-start.13 = (f32[1,2,256,256]{3,2,1,0:T(8,128)S(1)}, f32[1,2,256,256]{3,2,1,0:T(8,128)S(1)}, u32[]{:S(2)}, u32[]{:S(2)}) collective-permute-start(f32[1,2,256,256]{3,2,1,0:T(8,128)S(1)} %get-tuple-element.37), channel_id=1, source_target_pairs={{0,3},{1,4},{2,5},{3,6},{4,7},{5,8},{6,9},{7,10},{8,11},{9,12},{10... | collective-permute-start | bytes 1572872 | tf_op jit(solution)/shard_map/ppermute | solution.py:38
  101.2 19.0 %collective-permute-start.14 = (f32[1,2,256,256]{3,2,1,0:T(8,128)S(1)}, f32[1,2,256,256]{3,2,1,0:T(8,128)S(1)}, u32[]{:S(2)}, u32[]{:S(2)}) collective-permute-start(f32[1,2,256,256]{3,2,1,0:T(8,128)S(1)} %get-tuple-element.38), channel_id=1, source_target_pairs={{0,13},{1,14},{2,15},{3,0},{4,1},{5,2},{6,3},{7,4},{8,5},{9,6},{10... | collective-permute-start | bytes 1572872 | tf_op jit(solution)/shard_map/ppermute | solution.py:38
  104.8 62.1 %collective-permute-start.17 = (f32[2,2,256,256]{3,2,1,0:T(8,128)S(1)}, f32[2,2,256,256]{3,2,1,0:T(8,128)S(1)}, u32[]{:S(2)}, u32[]{:S(2)}) collective-permute-start(f32[2,2,256,256]{3,2,1,0:T(8,128)S(1)} %get-tuple-element.41), channel_id=1, source_target_pairs={{0,1},{1,0},{2,3},{3,2},{4,5},{5,4},{6,7},{7,6},{8,9},{9,8},{10,11... | collective-permute-start | bytes 3145736 | tf_op jit(solution)/shard_map/ppermute | solution.py:38
  104.8 30.6 %collective-permute-start.15 = (f32[1,2,256,256]{3,2,1,0:T(8,128)S(1)}, f32[1,2,256,256]{3,2,1,0:T(8,128)S(1)}, u32[]{:S(2)}, u32[]{:S(2)}) collective-permute-start(f32[1,2,256,256]{3,2,1,0:T(8,128)S(1)} %get-tuple-element.39), channel_id=1, source_target_pairs={{0,14},{1,15},{2,4},{3,5},{4,2},{5,3},{6,8},{7,9},{8,6},{9,7},{10,... | collective-permute-start | bytes 1572872 | tf_op jit(solution)/shard_map/ppermute | solution.py:38
  108.1 34.1 %collective-permute-start.16 = (f32[1,2,256,256]{3,2,1,0:T(8,128)S(1)}, f32[1,2,256,256]{3,2,1,0:T(8,128)S(1)}, u32[]{:S(2)}, u32[]{:S(2)}) collective-permute-start(f32[1,2,256,256]{3,2,1,0:T(8,128)S(1)} %get-tuple-element.40), channel_id=1, source_target_pairs={{0,15},{1,2},{2,1},{3,4},{4,3},{5,6},{6,5},{7,8},{8,7},{9,10},{10,... | collective-permute-start | bytes 1572872 | tf_op jit(solution)/shard_map/ppermute | solution.py:38
  115.2 69.6 %collective-permute-start.10 = (f32[2,2,256,256]{3,2,1,0:T(8,128)}, f32[2,2,256,256]{3,2,1,0:T(8,128)S(1)}, u32[]{:S(2)}, u32[]{:S(2)}) collective-permute-start(f32[2,2,256,256]{3,2,1,0:T(8,128)} %get-tuple-element.34), channel_id=1, source_target_pairs={{0,2},{1,3},{2,0},{3,1},{4,6},{5,7},{6,4},{7,5},{8,10},{9,11},{10,... | collective-permute-start | bytes 3145736 | tf_op jit(solution)/shard_map/ppermute | solution.py:38
  120.2 64.6 %collective-permute-start.11 = (f32[2,2,256,256]{3,2,1,0:T(8,128)}, f32[2,2,256,256]{3,2,1,0:T(8,128)S(1)}, u32[]{:S(2)}, u32[]{:S(2)}) collective-permute-start(f32[2,2,256,256]{3,2,1,0:T(8,128)} %get-tuple-element.35), channel_id=1, source_target_pairs={{0,4},{1,5},{2,6},{3,7},{4,0},{5,1},{6,2},{7,3},{8,12},{9,13},{10,... | collective-permute-start | bytes 3145736 | tf_op jit(solution)/shard_map/ppermute | solution.py:38
  135.3 38.1 %collective-permute-start.9 = (f32[1,2,256,256]{3,2,1,0:T(8,128)S(1)}, f32[1,2,256,256]{3,2,1,0:T(8,128)S(1)}, u32[]{:S(2)}, u32[]{:S(2)}) collective-permute-start(f32[1,2,256,256]{3,2,1,0:T(8,128)S(1)} %get-tuple-element.33), channel_id=1, source_target_pairs={{0,8},{1,9},{2,10},{3,11},{4,12},{5,13},{6,14},{7,15},{8,0},{9,1},... | collective-permute-start | bytes 1572872 | tf_op jit(solution)/shard_map/ppermute | solution.py:38
  142.2 42.7 %collective-permute-start.12 = (f32[1,2,256,256]{3,2,1,0:T(8,128)S(1)}, f32[1,2,256,256]{3,2,1,0:T(8,128)S(1)}, u32[]{:S(2)}, u32[]{:S(2)}) collective-permute-start(f32[1,2,256,256]{3,2,1,0:T(8,128)S(1)} %get-tuple-element.36), channel_id=1, source_target_pairs={{0,12},{1,13},{2,14},{3,15},{4,8},{5,9},{6,10},{7,11},{8,4},{9,5},... | collective-permute-start | bytes 1572872 | tf_op jit(solution)/shard_map/ppermute | solution.py:38
  158.1 8.8 %copy-start.3 = (f32[4,256,256]{2,1,0:T(8,128)S(1)}, f32[4,256,256]{2,1,0:T(8,128)}, u32[]{:S(2)}) copy-start(f32[4,256,256]{2,1,0:T(8,128)} %refs_7_.7) | copy-start | bytes 3145732
  (6 other events, 7.3 us)

commit v6 on v5

--- a/solution.py
+++ b/solution.py
@@ -13,7 +13,7 @@
 SMEM = pl.BlockSpec(memory_space=pltpu.SMEM)
 HBM = pl.BlockSpec(memory_space=pltpu.HBM)
 ANY = pl.BlockSpec(memory_space=pl.ANY)
-GRANT = 48 * 1024 * 1024
+GRANT = 24 * 1024 * 1024
 
 
 class Exchange:
@@ -74,7 +74,7 @@
     return dot(left[0], right[0]) + (dot(left[0], right[1]) + dot(left[1], right[0]))
 
 
-def outgoing_slots(exchange, me, mats, left_ref, count_ref, match_ref):
+def outgoing_slots(exchange, me, mats, left_ref, match_ref):
     slots = []
     if exchange.colour is not None:
         for j in range(match_ref.shape[2]):
@@ -82,10 +82,9 @@
     if exchange.listed:
         peer = exchange.peer(me, True)
         slot = jnp.int32(0)
-        for j in range(left_ref.shape[1]):
+        for j in reversed(range(left_ref.shape[1])):
             source = left_ref[1, j, peer]
-            hit = (j < count_ref[peer]) & (lax.div(source, mats) == me)
-            slot = jnp.where(hit, lax.rem(source, mats), slot)
+            slot = jnp.where(lax.div(source, mats) == me, lax.rem(source, mats), slot)
         slots.append(slot)
     return slots
 
@@ -114,11 +113,11 @@
     return rows
 
 
-def pack_kernel(plan, mats, me_ref, left_ref, count_ref, match_ref, source, *rest):
+def pack_kernel(plan, mats, me_ref, left_ref, match_ref, source, *rest):
     sends, (held, load_sems, sems) = rest[:-3], rest[-3:]
     loads, stores = [], []
     for exchange, send in zip(plan, sends):
-        slots = outgoing_slots(exchange, me_ref[0], mats, left_ref, count_ref, match_ref)
+        slots = outgoing_slots(exchange, me_ref[0], mats, left_ref, match_ref)
         for place, slot in enumerate(slots):
             at = len(loads)
             loads.append(pltpu.make_async_copy(source.at[slot], held.at[at], load_sems.at[at]))
@@ -207,7 +206,7 @@
 
     early, late, copies = [], [], []
     for exchange, send in zip(packs, sends):
-        slots = outgoing_slots(exchange, me, mats, left_ref, count_ref, match_ref)
+        slots = outgoing_slots(exchange, me, mats, left_ref, match_ref)
         for place, slot in enumerate(slots):
             copy = pltpu.make_async_copy(acc.at[slot], send.at[place], send_sems.at[len(copies)])
             busy = touches(slot)
@@ -276,7 +275,7 @@
     sent = sum(payload(e, pairs) for e in plan)
     return pl.pallas_call(
         functools.partial(pack_kernel, plan, mats),
-        in_specs=[SMEM] * 4 + [HBM],
+        in_specs=[SMEM] * 3 + [HBM],
         out_specs=[HBM] * len(plan),
         out_shape=[jax.ShapeDtypeStruct((payload(e, pairs), 2, order, order), F32) for e in plan],
         scratch_shapes=[
@@ -286,7 +285,7 @@
         ],
         compiler_params=pltpu.CompilerParams(vmem_limit_bytes=GRANT),
         cost_estimate=pl.CostEstimate(flops=0, bytes_accessed=sent * 16 * order**2, transcendentals=0),
-    )(*tables[:4], source)
+    )(tables[0], tables[1], tables[3], source)
 
 
 def body(rho, hamiltonian, couplings, bath_coef, damping, match_edges, left_rows, left_count):
@@ -307,8 +306,9 @@
         acc, *sends = rows_call(late, packs, pairs, scale, tables, couplings, arrived[cut:], acc)
         return acc, sends
 
-    sends = pack_call(plan, pairs, tables, rho)
-    first, sends = gather(sends, local_call(damping, hamiltonian, rho), 1.0, plan)
+    sends = pack_call(early, pairs, tables, rho) + pack_call(late, pairs, tables, rho)
+    first, sends = gather(sends, local_call(damping, hamiltonian, rho), 1.0, early)
+    sends += pack_call(late, pairs, tables, first)
     return gather(sends, local_call(damping, hamiltonian, first, rho), 0.5 * STEP * STEP, [])[0]
 
 

time: 193 us -> 186 us (0.964)
  the two profiles are of different devices: /device:TPU:0 before, /device:TPU:13 now
where the time goes in v6:
time: 186 us; the launch traced here: 183 us
  waiting for transfers between devices  90.3 us (49%)
  starting transfers between devices  52.4 us (28%)
  Pallas kernels  36.1 us (19%)
  local copies, waits for them, and re-layouts  3.62 us (2%)
    ppermute x18, waiting for transfers between devices, permute(): lax.ppermute(value, 'tier', [(i, self.peer(i, True)) for i in range(self....  90.3 us
    ppermute x18, starting transfers between devices, permute(): lax.ppermute(value, 'tier', [(i, self.peer(i, True)) for i in range(self....  52.4 us
    pallas_call x4, Pallas kernels, rows_call(): pl.pallas_call(functools.partial(rows_kernel, plan, packs, scale), in_spe...  19.3 us
    pallas_call x2, Pallas kernels, local_call(): pl.pallas_call(functools.partial(local_kernel, len(densities) == 2), grid...  12.2 us
    pallas_call x3, Pallas kernels, pack_call(): pl.pallas_call(functools.partial(pack_kernel, plan, mats), in_specs=[SMEM...  4.66 us
  transfers between devices with their start and end apart: 18, of which 12 were waited for; matrix products, arithmetic and copies ran while one was open for 0% of the time, Pallas kernels for 13%

profile of v6, /device:TPU:13, one launch (start us, length us, event | category | flops | bytes accessed | tf_op | source)
XLA Modules:
  0.0 182.8 jit_solution(6595353138617200201)
XLA Ops:
  0.0 2.2 %copy-done = f32[8,2,256,256]{3,2,1,0:T(8,128)S(1)} copy-done((f32[8,2,256,256]{3,2,1,0:T(8,128)S(1)}, f32[8,2,256,256]{3,2,1,0:T(8,128)}, u32[]{:S(2)}) %copy-start) | copy-done | bytes 4194328
  11.8 7.1 %collective-permute-done.4.refs_8_ = f32[1,2,256,256]{3,2,1,0:T(8,128)S(1)} collective-permute-done((f32[1,2,256,256]{3,2,1,0:T(8,128)S(1)}, f32[1,2,256,256]{3,2,1,0:T(8,128)S(1)}, u32[]{:S(2)}, u32[]{:S(2)}) %collective-permute-start.4) | collective-permute-done | bytes 524320 | tf_op jit(solution)/shard_map/ppermute | solution.py:38
  20.6 11.4 %collective-permute-done.5.refs_9_ = f32[1,2,256,256]{3,2,1,0:T(8,128)S(1)} collective-permute-done((f32[1,2,256,256]{3,2,1,0:T(8,128)S(1)}, f32[1,2,256,256]{3,2,1,0:T(8,128)S(1)}, u32[]{:S(2)}, u32[]{:S(2)}) %collective-permute-start.5) | collective-permute-done | bytes 524320 | tf_op jit(solution)/shard_map/ppermute | solution.py:38
  33.3 3.6 %collective-permute-done.6.refs_10_ = f32[1,2,256,256]{3,2,1,0:T(8,128)S(1)} collective-permute-done((f32[1,2,256,256]{3,2,1,0:T(8,128)S(1)}, f32[1,2,256,256]{3,2,1,0:T(8,128)S(1)}, u32[]{:S(2)}, u32[]{:S(2)}) %collective-permute-start.6) | collective-permute-done | bytes 524320 | tf_op jit(solution)/shard_map/ppermute | solution.py:38
  36.9 5.2 %collective-permute-start = (f32[1,2,256,256]{3,2,1,0:T(8,128)S(1)}, f32[1,2,256,256]{3,2,1,0:T(8,128)S(1)}, u32[]{:S(2)}, u32[]{:S(2)}) collective-permute-start(f32[1,2,256,256]{3,2,1,0:T(8,128)S(1)} %get-tuple-element.24), channel_id=1, source_target_pairs={{0,8},{1,9},{2,10},{3,11},{4,12},{5,13},{6,14},{7,15},{8,0},{9,1},... | collective-permute-start | bytes 1572872 | tf_op jit(solution)/shard_map/ppermute | solution.py:38
  42.9 2.3 %collective-permute-start.3 = (f32[1,2,256,256]{3,2,1,0:T(8,128)S(1)}, f32[1,2,256,256]{3,2,1,0:T(8,128)S(1)}, u32[]{:S(2)}, u32[]{:S(2)}) collective-permute-start(f32[1,2,256,256]{3,2,1,0:T(8,128)S(1)} %get-tuple-element.27), channel_id=1, source_target_pairs={{0,12},{1,13},{2,14},{3,15},{4,8},{5,9},{6,10},{7,11},{8,4},{9,5},... | collective-permute-start | bytes 1572872 | tf_op jit(solution)/shard_map/ppermute | solution.py:38
  45.2 5.4 %shard_map.84.refs_13_ = f32[8,2,256,256]{3,2,1,0:T(8,128)S(1)} custom-call(f32[8]{0:T(128)S(1)} %copy-done.8, f32[256,256]{1,0:T(8,128)S(1)} %copy-done.4, f32[8,2,256,256]{3,2,1,0:T(8,128)S(1)} %copy-done.1), custom_call_target="tpu_custom_call" | custom-call | flops 3221225472 | bytes 8388608 | tf_op jit(solution)/shard_map/pallas_call | solution.py:157
  50.6 3.0 %shard_map.85.refs_12_ = f32[8,2,256,256]{3,2,1,0:T(8,128)S(1)} custom-call(s32[1]{0:T(128)} %bitcast.me_ref.refs_0_, s32[5,6,16]{2,1,0:T(8,128)S(1)} %bitcast.9, s32[16]{0:T(128)S(1)} %copy-done.7, s32[1,4,1,5]{3,2,1,0:T(1,128)S(1)} %copy-done.5, f32[6,16]{1,0:T(8,128)S(1)} %fusion.1.refs_4_, f32[4,1]{1,0:T(4,128)S(1)} %bitcast.14, ...), custom_call_target="tpu_custom_call", output_to_operand_aliasing={{}: (13, {})} | custom-call | flops 2415919104 | bytes 11534336 | tf_op jit(solution)/shard_map/pallas_call | solution.py:251
  53.7 21.3 %collective-permute-done.refs_8_ = f32[1,2,256,256]{3,2,1,0:T(8,128)S(1)} collective-permute-done((f32[1,2,256,256]{3,2,1,0:T(8,128)S(1)}, f32[1,2,256,256]{3,2,1,0:T(8,128)S(1)}, u32[]{:S(2)}, u32[]{:S(2)}) %collective-permute-start) | collective-permute-done | bytes 524320 | tf_op jit(solution)/shard_map/ppermute | solution.py:38
  74.9 2.5 %collective-permute-done.2.refs_10_ = f32[2,2,256,256]{3,2,1,0:T(8,128)S(1)} collective-permute-done((f32[2,2,256,256]{3,2,1,0:T(8,128)S(1)}, f32[2,2,256,256]{3,2,1,0:T(8,128)S(1)}, u32[]{:S(2)}, u32[]{:S(2)}) %collective-permute-start.2) | collective-permute-done | bytes 1048608 | tf_op jit(solution)/shard_map/ppermute | solution.py:38
  77.4 5.1 %shard_map.86 = (f32[8,2,256,256]{3,2,1,0:T(8,128)S(1)}, f32[1,2,256,256]{3,2,1,0:T(8,128)S(1)}, f32[1,2,256,256]{3,2,1,0:T(8,128)S(1)}, f32[1,2,256,256]{3,2,1,...) custom-call(s32[1]{0:T(128)} %bitcast.me_ref.refs_0_, ...), custom_call_target="tpu_custom_call", output_to_operand_aliasing={{0}: (12, {})} | custom-call | flops 2415919104 | bytes 14680064 | tf_op jit(solution)/shard_map/pallas_call | solution.py:251
  82.5 12.0 %collective-permute-start.13 = (f32[1,2,256,256]{3,2,1,0:T(8,128)S(1)}, f32[1,2,256,256]{3,2,1,0:T(8,128)S(1)}, u32[]{:S(2)}, u32[]{:S(2)}) collective-permute-start(f32[1,2,256,256]{3,2,1,0:T(8,128)S(1)} %get-tuple-element.38), channel_id=1, source_target_pairs={{0,3},{1,4},{2,5},{3,6},{4,7},{5,8},{6,9},{7,10},{8,11},{9,12},{10... | collective-permute-start | bytes 1572872 | tf_op jit(solution)/shard_map/ppermute | solution.py:38
  99.1 7.2 %collective-permute-done.13.refs_8_ = f32[1,2,256,256]{3,2,1,0:T(8,128)S(1)} collective-permute-done((f32[1,2,256,256]{3,2,1,0:T(8,128)S(1)}, f32[1,2,256,256]{3,2,1,0:T(8,128)S(1)}, u32[]{:S(2)}, u32[]{:S(2)}) %collective-permute-start.13) | collective-permute-done | bytes 524320 | tf_op jit(solution)/shard_map/ppermute | solution.py:38
  106.4 2.1 %collective-permute-start.10 = (f32[2,2,256,256]{3,2,1,0:T(8,128)S(1)}, f32[2,2,256,256]{3,2,1,0:T(8,128)S(1)}, u32[]{:S(2)}, u32[]{:S(2)}) collective-permute-start(f32[2,2,256,256]{3,2,1,0:T(8,128)S(1)} %get-tuple-element.35), channel_id=1, source_target_pairs={{0,2},{1,3},{2,0},{3,1},{4,6},{5,7},{6,4},{7,5},{8,10},{9,11},{10,... | collective-permute-start | bytes 3145736 | tf_op jit(solution)/shard_map/ppermute | solution.py:38
  108.5 8.9 %collective-permute-done.14.refs_9_ = f32[1,2,256,256]{3,2,1,0:T(8,128)S(1)} collective-permute-done((f32[1,2,256,256]{3,2,1,0:T(8,128)S(1)}, f32[1,2,256,256]{3,2,1,0:T(8,128)S(1)}, u32[]{:S(2)}, u32[]{:S(2)}) %collective-permute-start.14) | collective-permute-done | bytes 524320 | tf_op jit(solution)/shard_map/ppermute | solution.py:38
  117.3 6.5 %collective-permute-done.15.refs_10_ = f32[1,2,256,256]{3,2,1,0:T(8,128)S(1)} collective-permute-done((f32[1,2,256,256]{3,2,1,0:T(8,128)S(1)}, f32[1,2,256,256]{3,2,1,0:T(8,128)S(1)}, u32[]{:S(2)}, u32[]{:S(2)}) %collective-permute-start.15) | collective-permute-done | bytes 524320 | tf_op jit(solution)/shard_map/ppermute | solution.py:38
  123.9 5.0 %collective-permute-start.9 = (f32[1,2,256,256]{3,2,1,0:T(8,128)S(1)}, f32[1,2,256,256]{3,2,1,0:T(8,128)S(1)}, u32[]{:S(2)}, u32[]{:S(2)}) collective-permute-start(f32[1,2,256,256]{3,2,1,0:T(8,128)S(1)} %get-tuple-element.34), channel_id=1, source_target_pairs={{0,8},{1,9},{2,10},{3,11},{4,12},{5,13},{6,14},{7,15},{8,0},{9,1},... | collective-permute-start | bytes 1572872 | tf_op jit(solution)/shard_map/ppermute | solution.py:38
  128.9 2.4 %collective-permute-done.16.refs_11_ = f32[1,2,256,256]{3,2,1,0:T(8,128)S(1)} collective-permute-done((f32[1,2,256,256]{3,2,1,0:T(8,128)S(1)}, f32[1,2,256,256]{3,2,1,0:T(8,128)S(1)}, u32[]{:S(2)}, u32[]{:S(2)}) %collective-permute-start.16) | collective-permute-done | bytes 524320 | tf_op jit(solution)/shard_map/ppermute | solution.py:38
  131.3 14.9 %collective-permute-start.12 = (f32[1,2,256,256]{3,2,1,0:T(8,128)S(1)}, f32[1,2,256,256]{3,2,1,0:T(8,128)S(1)}, u32[]{:S(2)}, u32[]{:S(2)}) collective-permute-start(f32[1,2,256,256]{3,2,1,0:T(8,128)S(1)} %get-tuple-element.37), channel_id=1, source_target_pairs={{0,12},{1,13},{2,14},{3,15},{4,8},{5,9},{6,10},{7,11},{8,4},{9,5},... | collective-permute-start | bytes 1572872 | tf_op jit(solution)/shard_map/ppermute | solution.py:38
  146.2 6.7 %shard_map.88.refs_13_ = f32[8,2,256,256]{3,2,1,0:T(8,128)} custom-call(f32[8]{0:T(128)S(1)} %copy-done.8, f32[256,256]{1,0:T(8,128)S(1)} %copy-done.4, f32[8,2,256,256]{3,2,1,0:T(8,128)S(1)} %get-tuple-element.33.source.density_ref, f32[8,2,256,256]{3,2,1,0:T(8,128)S(1)} %copy-done.1), custom_call_target="tpu_custom_call" | custom-call | flops 3221225472 | bytes 12582912 | tf_op jit(solution)/shard_map/pallas_call | solution.py:157
  152.9 5.2 %shard_map.89.refs_12_ = f32[8,2,256,256]{3,2,1,0:T(8,128)} custom-call(s32[1]{0:T(128)} %bitcast.me_ref.refs_0_, s32[5,6,16]{2,1,0:T(8,128)S(1)} %bitcast.12, s32[16]{0:T(128)S(1)} %copy-done.7, s32[1,4,1,5]{3,2,1,0:T(1,128)S(1)} %copy-done.5, f32[6,16]{1,0:T(8,128)S(1)} %fusion.1.refs_4_, f32[4,1]{1,0:T(4,128)S(1)} %bitcast.16, ...), custom_call_target="tpu_custom_call", output_to_operand_aliasing={{}: (13, {})} | custom-call | flops 2415919104 | bytes 11534336 | tf_op jit(solution)/shard_map/pallas_call | solution.py:251
  158.1 7.3 %collective-permute-done.9.refs_8_ = f32[1,2,256,256]{3,2,1,0:T(8,128)S(1)} collective-permute-done((f32[1,2,256,256]{3,2,1,0:T(8,128)S(1)}, f32[1,2,256,256]{3,2,1,0:T(8,128)S(1)}, u32[]{:S(2)}, u32[]{:S(2)}) %collective-permute-start.9) | collective-permute-done | bytes 524320 | tf_op jit(solution)/shard_map/ppermute | solution.py:38
  165.4 11.3 %collective-permute-done.12.refs_11_ = f32[1,2,256,256]{3,2,1,0:T(8,128)S(1)} collective-permute-done((f32[1,2,256,256]{3,2,1,0:T(8,128)S(1)}, f32[1,2,256,256]{3,2,1,0:T(8,128)S(1)}, u32[]{:S(2)}, u32[]{:S(2)}) %collective-permute-start.12) | collective-permute-done | bytes 524320 | tf_op jit(solution)/shard_map/ppermute | solution.py:38
  176.7 6.0 %shard_map.90 = f32[8,2,256,256]{3,2,1,0:T(8,128)} custom-call(s32[1]{0:T(128)} %bitcast.me_ref.refs_0_, s32[5,6,16]{2,1,0:T(8,128)S(1)} %bitcast.13, s32[16]{0:T(128)S(1)} %copy-done.7, s32[1,4,1,5]{3,2,1,0:T(1,128)S(1)} %copy-done.5, f32[6,16]{1,0:T(8,128)S(1)} %fusion.1.refs_4_, f32[4,1]{1,0:T(4,128)S(1)} %bitcast.17, ...), custom_call_target="tpu_custom_call", output_to_operand_aliasing={{}: (12, {})} | custom-call | flops 2415919104 | bytes 11534336 | tf_op jit(solution)/shard_map/pallas_call | solution.py:251
  (41 shorter events, 18.0 us)
Async XLA Ops:
  3.6 41.6 %copy-start.1 = (f32[8,2,256,256]{3,2,1,0:T(8,128)S(1)}, f32[8,2,256,256]{3,2,1,0:T(8,128)}, u32[]{:S(2)}) copy-start(f32[8,2,256,256]{3,2,1,0:T(8,128)} %refs_0_.1) | copy-start | bytes 12582916
  3.6 41.6 %copy-start.4 = (f32[256,256]{1,0:T(8,128)S(1)}, f32[256,256]{1,0:T(8,128)}, u32[]{:S(2)}) copy-start(f32[256,256]{1,0:T(8,128)} %hamiltonian_ref.3) | copy-start | bytes 786436
  3.6 41.6 %copy-start.8 = (f32[8]{0:T(128)S(1)}, f32[8]{0:T(128)}, u32[]{:S(2)}) copy-start(f32[8]{0:T(128)} %damping_ref.3) | copy-start | bytes 100
  5.2 13.6 %collective-permute-start.4 = (f32[1,2,256,256]{3,2,1,0:T(8,128)S(1)}, f32[1,2,256,256]{3,2,1,0:T(8,128)S(1)}, u32[]{:S(2)}, u32[]{:S(2)}) collective-permute-start(f32[1,2,256,256]{3,2,1,0:T(8,128)S(1)} %get-tuple-element.28), channel_id=1, source_target_pairs={{0,3},{1,4},{2,5},{3,6},{4,7},{5,8},{6,9},{7,10},{8,11},{9,12},{10... | collective-permute-start | bytes 1572872 | tf_op jit(solution)/shard_map/ppermute | solution.py:38
  7.1 24.9 %collective-permute-start.5 = (f32[1,2,256,256]{3,2,1,0:T(8,128)S(1)}, f32[1,2,256,256]{3,2,1,0:T(8,128)S(1)}, u32[]{:S(2)}, u32[]{:S(2)}) collective-permute-start(f32[1,2,256,256]{3,2,1,0:T(8,128)S(1)} %get-tuple-element.29), channel_id=1, source_target_pairs={{0,13},{1,14},{2,15},{3,0},{4,1},{5,2},{6,3},{7,4},{8,5},{9,6},{10... | collective-permute-start | bytes 1572872 | tf_op jit(solution)/shard_map/ppermute | solution.py:38
  7.1 43.5 %collective-permute-start.8 = (f32[2,2,256,256]{3,2,1,0:T(8,128)S(1)}, f32[2,2,256,256]{3,2,1,0:T(8,128)S(1)}, u32[]{:S(2)}, u32[]{:S(2)}) collective-permute-start(f32[2,2,256,256]{3,2,1,0:T(8,128)S(1)} %get-tuple-element.32), channel_id=1, source_target_pairs={{0,1},{1,0},{2,3},{3,2},{4,5},{5,4},{6,7},{7,6},{8,9},{9,8},{10,11... | collective-permute-start | bytes 3145736 | tf_op jit(solution)/shard_map/ppermute | solution.py:38
  7.7 29.2 %collective-permute-start.6 = (f32[1,2,256,256]{3,2,1,0:T(8,128)S(1)}, f32[1,2,256,256]{3,2,1,0:T(8,128)S(1)}, u32[]{:S(2)}, u32[]{:S(2)}) collective-permute-start(f32[1,2,256,256]{3,2,1,0:T(8,128)S(1)} %get-tuple-element.30), channel_id=1, source_target_pairs={{0,14},{1,15},{2,4},{3,5},{4,2},{5,3},{6,8},{7,9},{8,6},{9,7},{10,... | collective-permute-start | bytes 1572872 | tf_op jit(solution)/shard_map/ppermute | solution.py:38
  9.1 33.7 %collective-permute-start.7 = (f32[1,2,256,256]{3,2,1,0:T(8,128)S(1)}, f32[1,2,256,256]{3,2,1,0:T(8,128)S(1)}, u32[]{:S(2)}, u32[]{:S(2)}) collective-permute-start(f32[1,2,256,256]{3,2,1,0:T(8,128)S(1)} %get-tuple-element.31), channel_id=1, source_target_pairs={{0,15},{1,2},{2,1},{3,4},{4,3},{5,6},{6,5},{7,8},{8,7},{9,10},{10,... | collective-permute-start | bytes 1572872 | tf_op jit(solution)/shard_map/ppermute | solution.py:38
  18.9 56.1 %collective-permute-start.1 = (f32[2,2,256,256]{3,2,1,0:T(8,128)S(1)}, f32[2,2,256,256]{3,2,1,0:T(8,128)S(1)}, u32[]{:S(2)}, u32[]{:S(2)}) collective-permute-start(f32[2,2,256,256]{3,2,1,0:T(8,128)S(1)} %get-tuple-element.25), channel_id=1, source_target_pairs={{0,2},{1,3},{2,0},{3,1},{4,6},{5,7},{6,4},{7,5},{8,10},{9,11},{10,... | collective-permute-start | bytes 3145736 | tf_op jit(solution)/shard_map/ppermute | solution.py:38
  32.0 45.4 %collective-permute-start.2 = (f32[2,2,256,256]{3,2,1,0:T(8,128)S(1)}, f32[2,2,256,256]{3,2,1,0:T(8,128)S(1)}, u32[]{:S(2)}, u32[]{:S(2)}) collective-permute-start(f32[2,2,256,256]{3,2,1,0:T(8,128)S(1)} %get-tuple-element.26), channel_id=1, source_target_pairs={{0,4},{1,5},{2,6},{3,7},{4,0},{5,1},{6,2},{7,3},{8,12},{9,13},{10,... | collective-permute-start | bytes 3145736 | tf_op jit(solution)/shard_map/ppermute | solution.py:38
  36.9 38.0 %collective-permute-start = (f32[1,2,256,256]{3,2,1,0:T(8,128)S(1)}, f32[1,2,256,256]{3,2,1,0:T(8,128)S(1)}, u32[]{:S(2)}, u32[]{:S(2)}) collective-permute-start(f32[1,2,256,256]{3,2,1,0:T(8,128)S(1)} %get-tuple-element.24), channel_id=1, source_target_pairs={{0,8},{1,9},{2,10},{3,11},{4,12},{5,13},{6,14},{7,15},{8,0},{9,1},... | collective-permute-start | bytes 1572872 | tf_op jit(solution)/shard_map/ppermute | solution.py:38
  42.9 7.7 %copy-start.2 = (f32[4,256,256]{2,1,0:T(8,128)S(1)}, f32[4,256,256]{2,1,0:T(8,128)}, u32[]{:S(2)}) copy-start(f32[4,256,256]{2,1,0:T(8,128)} %refs_7_.7) | copy-start | bytes 3145732
  42.9 7.7 %copy-start.6 = (f32[4,2]{0,1:T(2,128)S(1)}, f32[4,2]{0,1:T(2,128)}, u32[]{:S(2)}) copy-start(f32[4,2]{0,1:T(2,128)} %param.11) | copy-start | bytes 100
  42.9 7.7 %copy-start.7 = (s32[16]{0:T(128)S(1)}, s32[16]{0:T(128)}, u32[]{:S(2)}) copy-start(s32[16]{0:T(128)} %refs_2_.7) | copy-start | bytes 196
  42.9 32.1 %collective-permute-start.3 = (f32[1,2,256,256]{3,2,1,0:T(8,128)S(1)}, f32[1,2,256,256]{3,2,1,0:T(8,128)S(1)}, u32[]{:S(2)}, u32[]{:S(2)}) collective-permute-start(f32[1,2,256,256]{3,2,1,0:T(8,128)S(1)} %get-tuple-element.27), channel_id=1, source_target_pairs={{0,12},{1,13},{2,14},{3,15},{4,8},{5,9},{6,10},{7,11},{8,4},{9,5},... | collective-permute-start | bytes 1572872 | tf_op jit(solution)/shard_map/ppermute | solution.py:38
  82.5 23.8 %collective-permute-start.13 = (f32[1,2,256,256]{3,2,1,0:T(8,128)S(1)}, f32[1,2,256,256]{3,2,1,0:T(8,128)S(1)}, u32[]{:S(2)}, u32[]{:S(2)}) collective-permute-start(f32[1,2,256,256]{3,2,1,0:T(8,128)S(1)} %get-tuple-element.38), channel_id=1, source_target_pairs={{0,3},{1,4},{2,5},{3,6},{4,7},{5,8},{6,9},{7,10},{8,11},{9,12},{10... | collective-permute-start | bytes 1572872 | tf_op jit(solution)/shard_map/ppermute | solution.py:38
  94.5 22.8 %collective-permute-start.14 = (f32[1,2,256,256]{3,2,1,0:T(8,128)S(1)}, f32[1,2,256,256]{3,2,1,0:T(8,128)S(1)}, u32[]{:S(2)}, u32[]{:S(2)}) collective-permute-start(f32[1,2,256,256]{3,2,1,0:T(8,128)S(1)} %get-tuple-element.39), channel_id=1, source_target_pairs={{0,13},{1,14},{2,15},{3,0},{4,1},{5,2},{6,3},{7,4},{8,5},{9,6},{10... | collective-permute-start | bytes 1572872 | tf_op jit(solution)/shard_map/ppermute | solution.py:38
  94.6 58.4 %collective-permute-start.17 = (f32[2,2,256,256]{3,2,1,0:T(8,128)S(1)}, f32[2,2,256,256]{3,2,1,0:T(8,128)S(1)}, u32[]{:S(2)}, u32[]{:S(2)}) collective-permute-start(f32[2,2,256,256]{3,2,1,0:T(8,128)S(1)} %get-tuple-element.42), channel_id=1, source_target_pairs={{0,1},{1,0},{2,3},{3,2},{4,5},{5,4},{6,7},{7,6},{8,9},{9,8},{10,11... | collective-permute-start | bytes 3145736 | tf_op jit(solution)/shard_map/ppermute | solution.py:38
  94.6 29.3 %collective-permute-start.15 = (f32[1,2,256,256]{3,2,1,0:T(8,128)S(1)}, f32[1,2,256,256]{3,2,1,0:T(8,128)S(1)}, u32[]{:S(2)}, u32[]{:S(2)}) collective-permute-start(f32[1,2,256,256]{3,2,1,0:T(8,128)S(1)} %get-tuple-element.40), channel_id=1, source_target_pairs={{0,14},{1,15},{2,4},{3,5},{4,2},{5,3},{6,8},{7,9},{8,6},{9,7},{10,... | collective-permute-start | bytes 1572872 | tf_op jit(solution)/shard_map/ppermute | solution.py:38
  95.7 35.6 %collective-permute-start.16 = (f32[1,2,256,256]{3,2,1,0:T(8,128)S(1)}, f32[1,2,256,256]{3,2,1,0:T(8,128)S(1)}, u32[]{:S(2)}, u32[]{:S(2)}) collective-permute-start(f32[1,2,256,256]{3,2,1,0:T(8,128)S(1)} %get-tuple-element.41), channel_id=1, source_target_pairs={{0,15},{1,2},{2,1},{3,4},{4,3},{5,6},{6,5},{7,8},{8,7},{9,10},{10,... | collective-permute-start | bytes 1572872 | tf_op jit(solution)/shard_map/ppermute | solution.py:38
  106.4 70.3 %collective-permute-start.10 = (f32[2,2,256,256]{3,2,1,0:T(8,128)S(1)}, f32[2,2,256,256]{3,2,1,0:T(8,128)S(1)}, u32[]{:S(2)}, u32[]{:S(2)}) collective-permute-start(f32[2,2,256,256]{3,2,1,0:T(8,128)S(1)} %get-tuple-element.35), channel_id=1, source_target_pairs={{0,2},{1,3},{2,0},{3,1},{4,6},{5,7},{6,4},{7,5},{8,10},{9,11},{10,... | collective-permute-start | bytes 3145736 | tf_op jit(solution)/shard_map/ppermute | solution.py:38
  117.3 59.3 %collective-permute-start.11 = (f32[2,2,256,256]{3,2,1,0:T(8,128)S(1)}, f32[2,2,256,256]{3,2,1,0:T(8,128)S(1)}, u32[]{:S(2)}, u32[]{:S(2)}) collective-permute-start(f32[2,2,256,256]{3,2,1,0:T(8,128)S(1)} %get-tuple-element.36), channel_id=1, source_target_pairs={{0,4},{1,5},{2,6},{3,7},{4,0},{5,1},{6,2},{7,3},{8,12},{9,13},{10,... | collective-permute-start | bytes 3145736 | tf_op jit(solution)/shard_map/ppermute | solution.py:38
  123.9 41.5 %collective-permute-start.9 = (f32[1,2,256,256]{3,2,1,0:T(8,128)S(1)}, f32[1,2,256,256]{3,2,1,0:T(8,128)S(1)}, u32[]{:S(2)}, u32[]{:S(2)}) collective-permute-start(f32[1,2,256,256]{3,2,1,0:T(8,128)S(1)} %get-tuple-element.34), channel_id=1, source_target_pairs={{0,8},{1,9},{2,10},{3,11},{4,12},{5,13},{6,14},{7,15},{8,0},{9,1},... | collective-permute-start | bytes 1572872 | tf_op jit(solution)/shard_map/ppermute | solution.py:38
  131.3 45.4 %collective-permute-start.12 = (f32[1,2,256,256]{3,2,1,0:T(8,128)S(1)}, f32[1,2,256,256]{3,2,1,0:T(8,128)S(1)}, u32[]{:S(2)}, u32[]{:S(2)}) collective-permute-start(f32[1,2,256,256]{3,2,1,0:T(8,128)S(1)} %get-tuple-element.37), channel_id=1, source_target_pairs={{0,12},{1,13},{2,14},{3,15},{4,8},{5,9},{6,10},{7,11},{8,4},{9,5},... | collective-permute-start | bytes 1572872 | tf_op jit(solution)/shard_map/ppermute | solution.py:38
  (3 other events, 3.6 us)

commit v7 on v6

--- a/solution.py
+++ b/solution.py
@@ -13,7 +13,7 @@
 SMEM = pl.BlockSpec(memory_space=pltpu.SMEM)
 HBM = pl.BlockSpec(memory_space=pltpu.HBM)
 ANY = pl.BlockSpec(memory_space=pl.ANY)
-GRANT = 24 * 1024 * 1024
+GRANT, LARGE_GRANT = 24 * 1024 * 1024, 56 * 1024 * 1024
 
 
 class Exchange:
@@ -39,18 +39,22 @@
 
 
 def exchanges(size, colours):
-    shifts, others, swaps, far = [], [], [], []
+    shifts, others, swaps, far, last = [], [], [], [], []
     for distance in range(1, REACH + 1):
         colour = distance.bit_length() - 1
         if distance != 1 << colour or colour >= colours:
             shifts += [Exchange("shift", distance, size), Exchange("shift", size - distance, size)]
             continue
-        swaps.append(Exchange("swap", distance, size, colour))
-        (others if distance < REACH else far).insert(0, Exchange("other", distance, size))
+        pair = [Exchange("swap", distance, size, colour), Exchange("other", distance, size)]
+        if distance == REACH:
+            last = pair
+        else:
+            swaps.append(pair[0])
+            others.insert(0, pair[1])
     for colour in range(colours):
         if 1 << colour > REACH:
-            swaps.insert(1, Exchange("swap", 1 << colour, size, colour, listed=False))
-    return shifts + others + swaps[:1], swaps[1:] + far
+            far.append(Exchange("swap", 1 << colour, size, colour, listed=False))
+    return shifts, others + swaps[:1], far + swaps[1:], last
 
 
 def payload(exchange, pairs):
@@ -113,15 +117,35 @@
     return rows
 
 
-def pack_kernel(plan, mats, me_ref, left_ref, match_ref, source, *rest):
-    sends, (held, load_sems, sems) = rest[:-3], rest[-3:]
+def tables_kernel(plan, mats, me_ref, left_ref, count_ref, match_ref, left_root, match_root, bath_ref, whole, real):
+    at = 0
+    for exchange in plan:
+        me = me_ref[0]
+        slots = outgoing_slots(exchange, me, mats, left_ref, match_ref)
+        rows = incoming_rows(exchange, me, mats, left_ref, count_ref, match_ref, left_root, match_root, bath_ref)
+        for slot, (live, target, mode, a, b) in zip(slots, rows):
+            whole[at, 0] = jnp.int32(1) if live is None else live.astype(jnp.int32)
+            whole[at, 1], whole[at, 2], whole[at, 3] = target, mode, slot
+            real[at, 0], real[at, 1] = a, b
+            at += 1
+
+
+def tables_call(plan, pairs, mats, tables):
+    count = sum(payload(e, pairs) for e in plan)
+    return pl.pallas_call(
+        functools.partial(tables_kernel, plan, mats),
+        in_specs=[SMEM] * 7,
+        out_specs=[SMEM] * 2,
+        out_shape=[jax.ShapeDtypeStruct((count, 4), jnp.int32), jax.ShapeDtypeStruct((count, 2), F32)],
+        compiler_params=pltpu.CompilerParams(vmem_limit_bytes=GRANT),
+    )(*tables)
+
+
+def copy_slots(slots, source, sends, held, load_sems, sems):
     loads, stores = [], []
-    for exchange, send in zip(plan, sends):
-        slots = outgoing_slots(exchange, me_ref[0], mats, left_ref, match_ref)
-        for place, slot in enumerate(slots):
-            at = len(loads)
-            loads.append(pltpu.make_async_copy(source.at[slot], held.at[at], load_sems.at[at]))
-            stores.append(pltpu.make_async_copy(held.at[at], send.at[place], sems.at[at]))
+    for at, (slot, (send, place)) in enumerate(zip(slots, sends)):
+        loads.append(pltpu.make_async_copy(source.at[slot], held.at[at], load_sems.at[at]))
+        stores.append(pltpu.make_async_copy(held.at[at], send.at[place], sems.at[at]))
     for load in loads:
         load.start()
     for load, store in zip(loads, stores):
@@ -129,6 +153,42 @@
         store.start()
     for store in stores:
         store.wait()
+
+
+def places(plan, pairs, sends):
+    return [(send, place) for e, send in zip(plan, sends) for place in range(payload(e, pairs))]
+
+
+def first_pack_kernel(plan, pairs, mats, me_ref, left_ref, match_ref, source, *rest):
+    slots = []
+    for exchange in plan:
+        slots += outgoing_slots(exchange, me_ref[0], mats, left_ref, match_ref)
+    copy_slots(slots, source, places(plan, pairs, rest[:-3]), *rest[-3:])
+
+
+def next_pack_kernel(plan, pairs, offset, whole, source, *rest):
+    sends = places(plan, pairs, rest[:-3])
+    copy_slots([whole[offset + at, 3] for at in range(len(sends))], source, sends, *rest[-3:])
+
+
+def pack_call(kernel, plan, pairs, grant, scalars, source):
+    order = source.shape[-1]
+    sent = sum(payload(e, pairs) for e in plan)
+    return list(
+        pl.pallas_call(
+            kernel,
+            in_specs=[SMEM] * len(scalars) + [HBM],
+            out_specs=[HBM] * len(plan),
+            out_shape=[jax.ShapeDtypeStruct((payload(e, pairs), 2, order, order), F32) for e in plan],
+            scratch_shapes=[
+                pltpu.VMEM((sent, 2, order, order), F32),
+                pltpu.SemaphoreType.DMA((sent,)),
+                pltpu.SemaphoreType.DMA((sent,)),
+            ],
+            compiler_params=pltpu.CompilerParams(vmem_limit_bytes=grant),
+            cost_estimate=pl.CostEstimate(flops=0, bytes_accessed=sent * 16 * order**2, transcendentals=0),
+        )(*scalars, source)
+    )
 
 
 def commutator(density, hamiltonian):
@@ -167,19 +227,20 @@
     )(damping, hamiltonian, *densities)
 
 
-def rows_kernel(plan, packs, scale, *refs):
-    me_ref, left_ref, count_ref, match_ref, left_root, match_root, bath_ref, couplings_ref = refs[:8]
-    arrivals = refs[8 : 8 + len(plan)]
-    acc_in = refs[8 + len(plan)]
-    rest = refs[9 + len(plan) :]
+def rows_kernel(plan, packs, pairs, offset, scale, whole, real, couplings_ref, *refs):
+    arrivals = refs[: len(plan)]
+    acc_in = refs[len(plan)]
+    rest = refs[len(plan) + 1 :]
     acc_out, sends = rest[0], rest[1 : 1 + len(packs)]
     acc, landed, chosen, acc_sems, land_sems, mode_sems, send_sems = rest[1 + len(packs) :]
-    mats, me = acc.shape[0], me_ref[0]
+    mats = acc.shape[0]
     rows, lands, modes = [], [], []
     for exchange, arrival in zip(plan, arrivals):
-        found = incoming_rows(exchange, me, mats, left_ref, count_ref, match_ref, left_root, match_root, bath_ref)
-        for place, row in enumerate(found):
+        for place in range(payload(exchange, pairs)):
             at = len(rows)
+            index = offset + at
+            live = whole[index, 0] == 1 if exchange.listed and place == payload(exchange, pairs) - 1 else None
+            row = (live, whole[index, 1], whole[index, 2], real[index, 0], real[index, 1])
             lands.append(pltpu.make_async_copy(arrival.at[place], landed.at[at], land_sems.at[at]))
             modes.append(pltpu.make_async_copy(couplings_ref.at[row[2]], chosen.at[at], mode_sems.at[at]))
             rows.append(row)
@@ -205,14 +266,13 @@
             when(untouched, copy.start)
 
     early, late, copies = [], [], []
-    for exchange, send in zip(packs, sends):
-        slots = outgoing_slots(exchange, me, mats, left_ref, match_ref)
-        for place, slot in enumerate(slots):
-            copy = pltpu.make_async_copy(acc.at[slot], send.at[place], send_sems.at[len(copies)])
-            busy = touches(slot)
-            copies.append(copy)
-            late.append((busy, copy))
-            early.append((jnp.logical_not(busy), copy))
+    for at, (send, place) in enumerate(places(packs, pairs, sends)):
+        slot = whole[at, 3]
+        copy = pltpu.make_async_copy(acc.at[slot], send.at[place], send_sems.at[at])
+        busy = touches(slot)
+        copies.append(copy)
+        late.append((busy, copy))
+        early.append((jnp.logical_not(busy), copy))
     if rows[0][0] is not None:
         loaded()
     for at, (live, target, _, a, b) in enumerate(rows):
@@ -242,18 +302,18 @@
         when(touched[n], stores[n].wait)
 
 
-def rows_call(plan, packs, pairs, scale, tables, couplings, arrivals, acc):
+def rows_call(plan, packs, pairs, offset, scale, scalars, couplings, arrivals, acc):
     mats, _, order, _ = acc.shape
     count = sum(payload(e, pairs) for e in plan)
     sent = sum(payload(e, pairs) for e in packs)
     shapes = [jax.ShapeDtypeStruct(acc.shape, F32)]
     shapes += [jax.ShapeDtypeStruct((payload(e, pairs), 2, order, order), F32) for e in packs]
     return pl.pallas_call(
-        functools.partial(rows_kernel, plan, packs, scale),
-        in_specs=[SMEM] * 7 + [HBM] + [ANY] * len(plan) + [HBM],
+        functools.partial(rows_kernel, plan, packs, pairs, offset, scale),
+        in_specs=[SMEM] * 2 + [HBM] + [ANY] * len(plan) + [HBM],
         out_specs=[HBM] * len(shapes),
         out_shape=shapes,
-        input_output_aliases={8 + len(plan): 0},
+        input_output_aliases={3 + len(plan): 0},
         scratch_shapes=[
             pltpu.VMEM((mats, 2, order, order), F32),
             pltpu.VMEM((count, 2, order, order), F32),
@@ -264,52 +324,49 @@
             pltpu.SemaphoreType.DMA((max(sent, 1),)),
         ],
         compiler_params=pltpu.CompilerParams(vmem_limit_bytes=GRANT),
-        cost_estimate=pl.CostEstimate(
-            flops=count * 24 * order**3, bytes_accessed=(count + 2 * mats + sent) * 8 * order**2, transcendentals=0
-        ),
-    )(*tables, couplings, *arrivals, acc)
-
-
-def pack_call(plan, pairs, tables, source):
-    mats, _, order, _ = source.shape
-    sent = sum(payload(e, pairs) for e in plan)
-    return pl.pallas_call(
-        functools.partial(pack_kernel, plan, mats),
-        in_specs=[SMEM] * 3 + [HBM],
-        out_specs=[HBM] * len(plan),
-        out_shape=[jax.ShapeDtypeStruct((payload(e, pairs), 2, order, order), F32) for e in plan],
-        scratch_shapes=[
-            pltpu.VMEM((sent, 2, order, order), F32),
-            pltpu.SemaphoreType.DMA((sent,)),
-            pltpu.SemaphoreType.DMA((sent,)),
-        ],
-        compiler_params=pltpu.CompilerParams(vmem_limit_bytes=GRANT),
-        cost_estimate=pl.CostEstimate(flops=0, bytes_accessed=sent * 16 * order**2, transcendentals=0),
-    )(tables[0], tables[1], tables[3], source)
+        cost_estimate=pl.CostEstimate(flops=0, bytes_accessed=0, transcendentals=0),
+    )(*scalars, couplings, *arrivals, acc)
 
 
 def body(rho, hamiltonian, couplings, bath_coef, damping, match_edges, left_rows, left_count):
     colours, pairs = match_edges.shape[1:3]
-    early, late = exchanges(lax.axis_size("tier"), colours)
+    shifts, early, middle, last = exchanges(lax.axis_size("tier"), colours)
+    plan = shifts + early + middle + last
+    mats = rho.shape[0]
     me = lax.axis_index("tier").astype(jnp.int32)[None]
     left_fields = jnp.transpose(left_rows, (2, 1, 0))
     left_root = jnp.sqrt(left_fields[4].astype(F32))
     match_root = jnp.sqrt(match_edges[0, :, :, 4].astype(F32))
     tables = (me, left_fields, left_count, match_edges, left_root, match_root, bath_coef.T)
 
-    plan = early + late
-
-    def gather(sends, acc, scale, packs):
+    first_tables = (tables[0], tables[1], tables[3])
+    scalars = tables_call(plan, pairs, mats, tables)
+
+    def size(group):
+        return sum(payload(e, pairs) for e in group)
+
+    def gather(sends, acc, scale, packs, groups):
         arrived = [e.permute(s) for e, s in zip(plan, sends)]
-        cut = len(early)
-        acc = rows_call(early, [], pairs, scale, tables, couplings, arrived[:cut], acc)[0]
-        acc, *sends = rows_call(late, packs, pairs, scale, tables, couplings, arrived[cut:], acc)
-        return acc, sends
-
-    sends = pack_call(early, pairs, tables, rho) + pack_call(late, pairs, tables, rho)
-    first, sends = gather(sends, local_call(damping, hamiltonian, rho), 1.0, early)
-    sends += pack_call(late, pairs, tables, first)
-    return gather(sends, local_call(damping, hamiltonian, first, rho), 0.5 * STEP * STEP, [])[0]
+        at, offset = 0, 0
+        for group in groups:
+            sent = packs if group is groups[-1] else []
+            got = arrived[at : at + len(group)]
+            acc, *out = rows_call(group, sent, pairs, offset, scale, scalars, couplings, got, acc)
+            at, offset = at + len(group), offset + size(group)
+        return acc, out
+
+    rest = plan[len(shifts) :]
+    pack = functools.partial(first_pack_kernel, shifts, pairs, mats)
+    sends = pack_call(pack, shifts, pairs, LARGE_GRANT, first_tables, rho)
+    pack = functools.partial(first_pack_kernel, rest, pairs, mats)
+    sends += pack_call(pack, rest, pairs, GRANT, first_tables, rho)
+    groups = [group for group in (shifts + early, middle, last) if group]
+    first, sends = gather(sends, local_call(damping, hamiltonian, rho), 1.0, shifts, groups)
+
+    pack = functools.partial(next_pack_kernel, rest, pairs, size(shifts))
+    sends += pack_call(pack, rest, pairs, GRANT, scalars[:1], first)
+    groups = [group for group in (shifts + early, middle + last) if group]
+    return gather(sends, local_call(damping, hamiltonian, first, rho), 0.5 * STEP * STEP, [], groups)[0]
 
 
 def solution(mesh):

time: 186 us -> 183 us (0.984)
  waiting for transfers between devices: 90.3 us -> 101 us
  starting transfers between devices: 52.4 us -> 41.7 us
  local copies, waits for them, and re-layouts: 3.62 us -> 0.03 us
  Pallas kernels: 36.1 us -> 38.4 us
    ppermute x18, starting transfers between devices: 52.4 us -> 41.7 us  [permute(): lax.ppermute(value, 'tier', [(i, self.peer(i, True)) for i in range(self....]
    ppermute x18, waiting for transfers between devices: 90.3 us -> 101 us  [permute(): lax.ppermute(value, 'tier', [(i, self.peer(i, True)) for i in range(self....]
    unnamed x18 -> x16, local copies, waits for them, and re-layouts: 3.62 us -> 0.03 us
    pallas_call x7 -> x9, Pallas kernels: 23.9 us -> 26.3 us  [the longest x5 16.8 us: rows_call(): pl.pallas_call(functools.partial(rows_kernel, plan, packs, pairs, offset,...]
  transfers between devices with their start and end apart: 18 -> 18, of which waited for: 12 -> 9; matrix products, arithmetic and copies ran while one was open for 0% -> 0% of each run, Pallas kernels for 13% -> 15%
where the time goes in v7:
time: 183 us; the launch traced here: 182 us
  waiting for transfers between devices  101 us (55%)
  starting transfers between devices  41.7 us (23%)
  Pallas kernels  38.4 us (21%)
    ppermute x18, waiting for transfers between devices, permute(): lax.ppermute(value, 'tier', [(i, self.peer(i, True)) for i in range(self....  101 us
    ppermute x18, starting transfers between devices, permute(): lax.ppermute(value, 'tier', [(i, self.peer(i, True)) for i in range(self....  41.7 us
    pallas_call x5, Pallas kernels, rows_call(): pl.pallas_call(functools.partial(rows_kernel, plan, packs, pairs, offset,...  16.8 us
    pallas_call x2, Pallas kernels, local_call(): pl.pallas_call(functools.partial(local_kernel, len(densities) == 2), grid...  12.1 us
    pallas_call x3, Pallas kernels, pack_call(): pl.pallas_call(kernel, in_specs=[SMEM] * len(scalars) + [HBM], out_specs=...  7.05 us
  transfers between devices with their start and end apart: 18, of which 9 were waited for; matrix products, arithmetic and copies ran while one was open for 0% of the time, Pallas kernels for 15%

profile of v7, /device:TPU:13, one launch (start us, length us, event | category | flops | bytes accessed | tf_op | source)
XLA Modules:
  0.0 181.5 jit_solution(5022004833876912480)
XLA Ops:
  0.0 3.4 %shard_map.84 = (f32[1,2,256,256]{3,2,1,0:T(8,128)}, f32[1,2,256,256]{3,2,1,0:T(8,128)}) custom-call(s32[1]{0:T(128)} %bitcast.me_ref, s32[5,6,16]{2,1,0:T(8,128)} %bitcast.6, s32[1,4,1,5]{3,2,1,0:T(1,128)} %match_ref.5, f32[8,2,256,256]{3,2,1,0:T(8,128)} %refs_0_.1), custom_call_target="tpu_custom_call" | custom-call | bytes 2097152 | tf_op jit(solution)/shard_map/pallas_call | solution.py:178
  3.5 1.9 %collective-permute-start.4 = (f32[1,2,256,256]{3,2,1,0:T(8,128)}, f32[1,2,256,256]{3,2,1,0:T(8,128)S(1)}, u32[]{:S(2)}, u32[]{:S(2)}) collective-permute-start(f32[1,2,256,256]{3,2,1,0:T(8,128)} %get-tuple-element.32), channel_id=1, source_target_pairs={{0,3},{1,4},{2,5},{3,6},{4,7},{5,8},{6,9},{7,10},{8,11},{9,12},{10... | collective-permute-start | bytes 1572872 | tf_op jit(solution)/shard_map/ppermute | solution.py:38
  5.4 2.0 %shard_map.83 = (f32[1,2,256,256]{3,2,1,0:T(8,128)S(1)}, f32[1,2,256,256]{3,2,1,0:T(8,128)S(1)}, f32[2,2,256,256]{3,2,1,0:T(8,128)S(1)}, f32[1,2,256,256]{3,2,1,...) custom-call(s32[1]{0:T(128)} %bitcast.me_ref, ...), custom_call_target="tpu_custom_call" | custom-call | bytes 10485760 | tf_op jit(solution)/shard_map/pallas_call | solution.py:178
  7.4 2.1 %collective-permute-start.6 = (f32[1,2,256,256]{3,2,1,0:T(8,128)S(1)}, f32[1,2,256,256]{3,2,1,0:T(8,128)S(1)}, u32[]{:S(2)}, u32[]{:S(2)}) collective-permute-start(f32[1,2,256,256]{3,2,1,0:T(8,128)S(1)} %get-tuple-element.34), channel_id=1, source_target_pairs={{0,14},{1,15},{2,4},{3,5},{4,2},{5,3},{6,8},{7,9},{8,6},{9,7},{10,... | collective-permute-start | bytes 1572872 | tf_op jit(solution)/shard_map/ppermute | solution.py:38
  10.6 6.9 %collective-permute-done.4.refs_0_ = f32[1,2,256,256]{3,2,1,0:T(8,128)S(1)} collective-permute-done((f32[1,2,256,256]{3,2,1,0:T(8,128)}, f32[1,2,256,256]{3,2,1,0:T(8,128)S(1)}, u32[]{:S(2)}, u32[]{:S(2)}) %collective-permute-start.4) | collective-permute-done | bytes 524320 | tf_op jit(solution)/shard_map/ppermute | solution.py:38
  19.1 11.4 %collective-permute-done.5.refs_1_ = f32[1,2,256,256]{3,2,1,0:T(8,128)S(1)} collective-permute-done((f32[1,2,256,256]{3,2,1,0:T(8,128)}, f32[1,2,256,256]{3,2,1,0:T(8,128)S(1)}, u32[]{:S(2)}, u32[]{:S(2)}) %collective-permute-start.5) | collective-permute-done | bytes 524320 | tf_op jit(solution)/shard_map/ppermute | solution.py:38
  31.7 3.7 %collective-permute-done.6.refs_2_ = f32[1,2,256,256]{3,2,1,0:T(8,128)S(1)} collective-permute-done((f32[1,2,256,256]{3,2,1,0:T(8,128)S(1)}, f32[1,2,256,256]{3,2,1,0:T(8,128)S(1)}, u32[]{:S(2)}, u32[]{:S(2)}) %collective-permute-start.6) | collective-permute-done | bytes 524320 | tf_op jit(solution)/shard_map/ppermute | solution.py:38
  35.4 3.0 %collective-permute-start.1 = (f32[1,2,256,256]{3,2,1,0:T(8,128)S(1)}, f32[1,2,256,256]{3,2,1,0:T(8,128)S(1)}, u32[]{:S(2)}, u32[]{:S(2)}) collective-permute-start(f32[1,2,256,256]{3,2,1,0:T(8,128)S(1)} %get-tuple-element.29), channel_id=1, source_target_pairs={{0,12},{1,13},{2,14},{3,15},{4,8},{5,9},{6,10},{7,11},{8,4},{9,5},... | collective-permute-start | bytes 1572872 | tf_op jit(solution)/shard_map/ppermute | solution.py:38
  38.4 4.8 %collective-permute-done.7.refs_3_ = f32[1,2,256,256]{3,2,1,0:T(8,128)S(1)} collective-permute-done((f32[1,2,256,256]{3,2,1,0:T(8,128)S(1)}, f32[1,2,256,256]{3,2,1,0:T(8,128)S(1)}, u32[]{:S(2)}, u32[]{:S(2)}) %collective-permute-start.7) | collective-permute-done | bytes 524320 | tf_op jit(solution)/shard_map/ppermute | solution.py:38
  44.8 2.4 %shard_map.82 = (s32[12,4]{1,0:T(8,128)S(1)}, f32[12,2]{1,0:T(8,128)S(1)}) custom-call(s32[1]{0:T(128)} %bitcast.me_ref, s32[5,6,16]{2,1,0:T(8,128)S(1)} %bitcast.9, s32[16]{0:T(128)S(1)} %copy-done.6, s32[1,4,1,5]{3,2,1,0:T(1,128)S(1)} %copy-done.4, f32[6,16]{1,0:T(8,128)S(1)} %fusion.1.left_root, f32[4,1]{1,0:T(4,128)S(1)} %bitcast.10, f32[2,4]{1,0:T(2,128)S(1)} %bitcast.11), custom_call_target="tpu_custom_call" | custom-call | tf_op jit(solution)/shard_map/pallas_call | solution.py:135
  47.3 5.4 %shard_map.85.refs_5_ = f32[8,2,256,256]{3,2,1,0:T(8,128)S(1)} custom-call(f32[8]{0:T(128)S(1)} %copy-done.7, f32[256,256]{1,0:T(8,128)S(1)} %copy-done.2, f32[8,2,256,256]{3,2,1,0:T(8,128)S(1)} %copy-done), custom_call_target="tpu_custom_call" | custom-call | flops 3221225472 | bytes 8388608 | tf_op jit(solution)/shard_map/pallas_call | solution.py:217
  52.7 2.6 %shard_map.86.refs_2_ = f32[8,2,256,256]{3,2,1,0:T(8,128)S(1)} custom-call(s32[12,4]{1,0:T(8,128)S(1)} %get-tuple-element.26.whole, f32[12,2]{1,0:T(8,128)S(1)} %get-tuple-element.27.real, f32[4,256,256]{2,1,0:T(8,128)S(1)} %copy-done.1, f32[1,2,256,256]{3,2,1,0:T(8,128)S(1)} %collective-permute-done.4.refs_0_, ...), custom_call_target="tpu_custom_call", output_to_operand_aliasing={{}: (8, {})} | custom-call | tf_op jit(solution)/shard_map/pallas_call | solution.py:311
  55.3 29.4 %collective-permute-done.2.refs_0_ = f32[1,2,256,256]{3,2,1,0:T(8,128)S(1)} collective-permute-done((f32[1,2,256,256]{3,2,1,0:T(8,128)S(1)}, f32[1,2,256,256]{3,2,1,0:T(8,128)S(1)}, u32[]{:S(2)}, u32[]{:S(2)}) %collective-permute-start.2) | collective-permute-done | bytes 524320 | tf_op jit(solution)/shard_map/ppermute | solution.py:38
  84.7 2.5 %shard_map.87.refs_2_ = f32[8,2,256,256]{3,2,1,0:T(8,128)S(1)} custom-call(s32[12,4]{1,0:T(8,128)S(1)} %get-tuple-element.26.whole, f32[12,2]{1,0:T(8,128)S(1)} %get-tuple-element.27.real, f32[4,256,256]{2,1,0:T(8,128)S(1)} %copy-done.1, f32[1,2,256,256]{3,2,1,0:T(8,128)S(1)} %collective-permute-done.2.refs_0_, ...), custom_call_target="tpu_custom_call", output_to_operand_aliasing={{}: (5, {})} | custom-call | tf_op jit(solution)/shard_map/pallas_call | solution.py:311
  87.2 2.2 %shard_map.88 = (f32[8,2,256,256]{3,2,1,0:T(8,128)S(1)}, f32[1,2,256,256]{3,2,1,0:T(8,128)S(1)}, f32[1,2,256,256]{3,2,1,0:T(8,128)S(1)}) custom-call(s32[12,4]{1,0:T(8,128)S(1)} %get-tuple-element.26.whole, f32[12,2]{1,0:T(8,128)S(1)} %get-tuple-element.27.real, f32[4,256,256]{2,1,0:T(8,128)S(1)} %copy-done.1, ...), custom_call_target="tpu_custom_call", output_to_operand_aliasing={{0}: (5, {})} | custom-call | tf_op jit(solution)/shard_map/pallas_call | solution.py:311
  89.4 3.3 %collective-permute-start.13 = (f32[1,2,256,256]{3,2,1,0:T(8,128)S(1)}, f32[1,2,256,256]{3,2,1,0:T(8,128)S(1)}, u32[]{:S(2)}, u32[]{:S(2)}) collective-permute-start(f32[1,2,256,256]{3,2,1,0:T(8,128)S(1)} %get-tuple-element.42), channel_id=1, source_target_pairs={{0,3},{1,4},{2,5},{3,6},{4,7},{5,8},{6,9},{7,10},{8,11},{9,12},{10... | collective-permute-start | bytes 1572872 | tf_op jit(solution)/shard_map/ppermute | solution.py:38
  97.7 10.0 %collective-permute-done.13.refs_0_ = f32[1,2,256,256]{3,2,1,0:T(8,128)S(1)} collective-permute-done((f32[1,2,256,256]{3,2,1,0:T(8,128)S(1)}, f32[1,2,256,256]{3,2,1,0:T(8,128)S(1)}, u32[]{:S(2)}, u32[]{:S(2)}) %collective-permute-start.13) | collective-permute-done | bytes 524320 | tf_op jit(solution)/shard_map/ppermute | solution.py:38
  107.7 20.2 %collective-permute-start.10 = (f32[2,2,256,256]{3,2,1,0:T(8,128)S(1)}, f32[2,2,256,256]{3,2,1,0:T(8,128)S(1)}, u32[]{:S(2)}, u32[]{:S(2)}) collective-permute-start(f32[2,2,256,256]{3,2,1,0:T(8,128)S(1)} %get-tuple-element.39), channel_id=1, source_target_pairs={{0,2},{1,3},{2,0},{3,1},{4,6},{5,7},{6,4},{7,5},{8,10},{9,11},{10,... | collective-permute-start | bytes 3145736 | tf_op jit(solution)/shard_map/ppermute | solution.py:38
  128.3 2.3 %collective-permute-start.12 = (f32[1,2,256,256]{3,2,1,0:T(8,128)S(1)}, f32[1,2,256,256]{3,2,1,0:T(8,128)S(1)}, u32[]{:S(2)}, u32[]{:S(2)}) collective-permute-start(f32[1,2,256,256]{3,2,1,0:T(8,128)S(1)} %get-tuple-element.41), channel_id=1, source_target_pairs={{0,12},{1,13},{2,14},{3,15},{4,8},{5,9},{6,10},{7,11},{8,4},{9,5},... | collective-permute-start | bytes 1572872 | tf_op jit(solution)/shard_map/ppermute | solution.py:38
  130.6 6.8 %shard_map.90.refs_5_ = f32[8,2,256,256]{3,2,1,0:T(8,128)} custom-call(f32[8]{0:T(128)S(1)} %copy-done.7, f32[256,256]{1,0:T(8,128)S(1)} %copy-done.2, f32[8,2,256,256]{3,2,1,0:T(8,128)S(1)} %get-tuple-element.37.source.density_ref, f32[8,2,256,256]{3,2,1,0:T(8,128)S(1)} %copy-done), custom_call_target="tpu_custom_call" | custom-call | flops 3221225472 | bytes 12582912 | tf_op jit(solution)/shard_map/pallas_call | solution.py:217
  137.4 4.5 %shard_map.91.refs_4_ = f32[8,2,256,256]{3,2,1,0:T(8,128)} custom-call(s32[12,4]{1,0:T(8,128)S(1)} %get-tuple-element.26.whole, f32[12,2]{1,0:T(8,128)S(1)} %get-tuple-element.27.real, f32[4,256,256]{2,1,0:T(8,128)S(1)} %copy-done.1, f32[1,2,256,256]{3,2,1,0:T(8,128)S(1)} %collective-permute-done.13.refs_0_, ...), custom_call_target="tpu_custom_call", output_to_operand_aliasing={{}: (8, {})} | custom-call | tf_op jit(solution)/shard_map/pallas_call | solution.py:311
  141.9 13.6 %collective-permute-done.9.refs_0_ = f32[1,2,256,256]{3,2,1,0:T(8,128)S(1)} collective-permute-done((f32[1,2,256,256]{3,2,1,0:T(8,128)S(1)}, f32[1,2,256,256]{3,2,1,0:T(8,128)S(1)}, u32[]{:S(2)}, u32[]{:S(2)}) %collective-permute-start.9) | collective-permute-done | bytes 524320 | tf_op jit(solution)/shard_map/ppermute | solution.py:38
  155.5 20.9 %collective-permute-done.12.refs_3_ = f32[1,2,256,256]{3,2,1,0:T(8,128)S(1)} collective-permute-done((f32[1,2,256,256]{3,2,1,0:T(8,128)S(1)}, f32[1,2,256,256]{3,2,1,0:T(8,128)S(1)}, u32[]{:S(2)}, u32[]{:S(2)}) %collective-permute-start.12) | collective-permute-done | bytes 524320 | tf_op jit(solution)/shard_map/ppermute | solution.py:38
  176.4 5.0 %shard_map.92 = f32[8,2,256,256]{3,2,1,0:T(8,128)} custom-call(s32[12,4]{1,0:T(8,128)S(1)} %get-tuple-element.26.whole, f32[12,2]{1,0:T(8,128)S(1)} %get-tuple-element.27.real, f32[4,256,256]{2,1,0:T(8,128)S(1)} %copy-done.1, f32[1,2,256,256]{3,2,1,0:T(8,128)S(1)} %collective-permute-done.9.refs_0_, ...), custom_call_target="tpu_custom_call", output_to_operand_aliasing={{}: (7, {})} | custom-call | tf_op jit(solution)/shard_map/pallas_call | solution.py:311
  (41 shorter events, 11.0 us)
Async XLA Ops:
  0.0 5.4 %copy-start.4 = (s32[1,4,1,5]{3,2,1,0:T(1,128)S(1)}, s32[1,4,1,5]{3,2,1,0:T(1,128)}, u32[]{:S(2)}) copy-start(s32[1,4,1,5]{3,2,1,0:T(1,128)} %match_ref.5) | copy-start | bytes 244
  0.0 5.4 %copy-start = (f32[8,2,256,256]{3,2,1,0:T(8,128)S(1)}, f32[8,2,256,256]{3,2,1,0:T(8,128)}, u32[]{:S(2)}) copy-start(f32[8,2,256,256]{3,2,1,0:T(8,128)} %refs_0_.1) | copy-start | bytes 12582916
  0.0 44.8 %copy-start.5 = (f32[4,2]{0,1:T(2,128)S(1)}, f32[4,2]{0,1:T(2,128)}, u32[]{:S(2)}) copy-start(f32[4,2]{0,1:T(2,128)} %param.11) | copy-start | bytes 100
  0.0 44.8 %copy-start.6 = (s32[16]{0:T(128)S(1)}, s32[16]{0:T(128)}, u32[]{:S(2)}) copy-start(s32[16]{0:T(128)} %count_ref.1) | copy-start | bytes 196
  0.0 47.2 %copy-start.2 = (f32[256,256]{1,0:T(8,128)S(1)}, f32[256,256]{1,0:T(8,128)}, u32[]{:S(2)}) copy-start(f32[256,256]{1,0:T(8,128)} %hamiltonian_ref.3) | copy-start | bytes 786436
  0.0 47.2 %copy-start.7 = (f32[8]{0:T(128)S(1)}, f32[8]{0:T(128)}, u32[]{:S(2)}) copy-start(f32[8]{0:T(128)} %damping_ref.3) | copy-start | bytes 100
  3.5 14.0 %collective-permute-start.4 = (f32[1,2,256,256]{3,2,1,0:T(8,128)}, f32[1,2,256,256]{3,2,1,0:T(8,128)S(1)}, u32[]{:S(2)}, u32[]{:S(2)}) collective-permute-start(f32[1,2,256,256]{3,2,1,0:T(8,128)} %get-tuple-element.32), channel_id=1, source_target_pairs={{0,3},{1,4},{2,5},{3,6},{4,7},{5,8},{6,9},{7,10},{8,11},{9,12},{10... | collective-permute-start | bytes 1572872 | tf_op jit(solution)/shard_map/ppermute | solution.py:38
  5.4 25.1 %collective-permute-start.5 = (f32[1,2,256,256]{3,2,1,0:T(8,128)}, f32[1,2,256,256]{3,2,1,0:T(8,128)S(1)}, u32[]{:S(2)}, u32[]{:S(2)}) collective-permute-start(f32[1,2,256,256]{3,2,1,0:T(8,128)} %get-tuple-element.33), channel_id=1, source_target_pairs={{0,13},{1,14},{2,15},{3,0},{4,1},{5,2},{6,3},{7,4},{8,5},{9,6},{10... | collective-permute-start | bytes 1572872 | tf_op jit(solution)/shard_map/ppermute | solution.py:38
  7.4 27.9 %collective-permute-start.6 = (f32[1,2,256,256]{3,2,1,0:T(8,128)S(1)}, f32[1,2,256,256]{3,2,1,0:T(8,128)S(1)}, u32[]{:S(2)}, u32[]{:S(2)}) collective-permute-start(f32[1,2,256,256]{3,2,1,0:T(8,128)S(1)} %get-tuple-element.34), channel_id=1, source_target_pairs={{0,14},{1,15},{2,4},{3,5},{4,2},{5,3},{6,8},{7,9},{8,6},{9,7},{10,... | collective-permute-start | bytes 1572872 | tf_op jit(solution)/shard_map/ppermute | solution.py:38
  9.5 33.6 %collective-permute-start.7 = (f32[1,2,256,256]{3,2,1,0:T(8,128)S(1)}, f32[1,2,256,256]{3,2,1,0:T(8,128)S(1)}, u32[]{:S(2)}, u32[]{:S(2)}) collective-permute-start(f32[1,2,256,256]{3,2,1,0:T(8,128)S(1)} %get-tuple-element.35), channel_id=1, source_target_pairs={{0,15},{1,2},{2,1},{3,4},{4,3},{5,6},{6,5},{7,8},{8,7},{9,10},{10,... | collective-permute-start | bytes 1572872 | tf_op jit(solution)/shard_map/ppermute | solution.py:38
  10.6 42.0 %collective-permute-start.8 = (f32[2,2,256,256]{3,2,1,0:T(8,128)S(1)}, f32[2,2,256,256]{3,2,1,0:T(8,128)S(1)}, u32[]{:S(2)}, u32[]{:S(2)}) collective-permute-start(f32[2,2,256,256]{3,2,1,0:T(8,128)S(1)} %get-tuple-element.36), channel_id=1, source_target_pairs={{0,1},{1,0},{2,3},{3,2},{4,5},{5,4},{6,7},{7,6},{8,9},{9,8},{10,11... | collective-permute-start | bytes 3145736 | tf_op jit(solution)/shard_map/ppermute | solution.py:38
  17.5 67.2 %collective-permute-start.3 = (f32[2,2,256,256]{3,2,1,0:T(8,128)S(1)}, f32[2,2,256,256]{3,2,1,0:T(8,128)S(1)}, u32[]{:S(2)}, u32[]{:S(2)}) collective-permute-start(f32[2,2,256,256]{3,2,1,0:T(8,128)S(1)} %get-tuple-element.31), channel_id=1, source_target_pairs={{0,2},{1,3},{2,0},{3,1},{4,6},{5,7},{6,4},{7,5},{8,10},{9,11},{10,... | collective-permute-start | bytes 3145736 | tf_op jit(solution)/shard_map/ppermute | solution.py:38
  30.5 56.7 %collective-permute-start = (f32[2,2,256,256]{3,2,1,0:T(8,128)S(1)}, f32[2,2,256,256]{3,2,1,0:T(8,128)S(1)}, u32[]{:S(2)}, u32[]{:S(2)}) collective-permute-start(f32[2,2,256,256]{3,2,1,0:T(8,128)S(1)} %get-tuple-element.28), channel_id=1, source_target_pairs={{0,4},{1,5},{2,6},{3,7},{4,0},{5,1},{6,2},{7,3},{8,12},{9,13},{10,... | collective-permute-start | bytes 3145736 | tf_op jit(solution)/shard_map/ppermute | solution.py:38
  35.4 51.8 %collective-permute-start.1 = (f32[1,2,256,256]{3,2,1,0:T(8,128)S(1)}, f32[1,2,256,256]{3,2,1,0:T(8,128)S(1)}, u32[]{:S(2)}, u32[]{:S(2)}) collective-permute-start(f32[1,2,256,256]{3,2,1,0:T(8,128)S(1)} %get-tuple-element.29), channel_id=1, source_target_pairs={{0,12},{1,13},{2,14},{3,15},{4,8},{5,9},{6,10},{7,11},{8,4},{9,5},... | collective-permute-start | bytes 1572872 | tf_op jit(solution)/shard_map/ppermute | solution.py:38
  43.2 41.5 %collective-permute-start.2 = (f32[1,2,256,256]{3,2,1,0:T(8,128)S(1)}, f32[1,2,256,256]{3,2,1,0:T(8,128)S(1)}, u32[]{:S(2)}, u32[]{:S(2)}) collective-permute-start(f32[1,2,256,256]{3,2,1,0:T(8,128)S(1)} %get-tuple-element.30), channel_id=1, source_target_pairs={{0,8},{1,9},{2,10},{3,11},{4,12},{5,13},{6,14},{7,15},{8,0},{9,1},... | collective-permute-start | bytes 1572872 | tf_op jit(solution)/shard_map/ppermute | solution.py:38
  89.4 18.3 %collective-permute-start.13 = (f32[1,2,256,256]{3,2,1,0:T(8,128)S(1)}, f32[1,2,256,256]{3,2,1,0:T(8,128)S(1)}, u32[]{:S(2)}, u32[]{:S(2)}) collective-permute-start(f32[1,2,256,256]{3,2,1,0:T(8,128)S(1)} %get-tuple-element.42), channel_id=1, source_target_pairs={{0,3},{1,4},{2,5},{3,6},{4,7},{5,8},{6,9},{7,10},{8,11},{9,12},{10... | collective-permute-start | bytes 1572872 | tf_op jit(solution)/shard_map/ppermute | solution.py:38
  92.7 35.3 %collective-permute-start.14 = (f32[1,2,256,256]{3,2,1,0:T(8,128)S(1)}, f32[1,2,256,256]{3,2,1,0:T(8,128)S(1)}, u32[]{:S(2)}, u32[]{:S(2)}) collective-permute-start(f32[1,2,256,256]{3,2,1,0:T(8,128)S(1)} %get-tuple-element.43), channel_id=1, source_target_pairs={{0,13},{1,14},{2,15},{3,0},{4,1},{5,2},{6,3},{7,4},{8,5},{9,6},{10... | collective-permute-start | bytes 1572872 | tf_op jit(solution)/shard_map/ppermute | solution.py:38
  94.3 33.6 %collective-permute-start.15 = (f32[1,2,256,256]{3,2,1,0:T(8,128)S(1)}, f32[1,2,256,256]{3,2,1,0:T(8,128)S(1)}, u32[]{:S(2)}, u32[]{:S(2)}) collective-permute-start(f32[1,2,256,256]{3,2,1,0:T(8,128)S(1)} %get-tuple-element.44), channel_id=1, source_target_pairs={{0,14},{1,15},{2,4},{3,5},{4,2},{5,3},{6,8},{7,9},{8,6},{9,7},{10,... | collective-permute-start | bytes 1572872 | tf_op jit(solution)/shard_map/ppermute | solution.py:38
  95.9 32.4 %collective-permute-start.16 = (f32[1,2,256,256]{3,2,1,0:T(8,128)S(1)}, f32[1,2,256,256]{3,2,1,0:T(8,128)S(1)}, u32[]{:S(2)}, u32[]{:S(2)}) collective-permute-start(f32[1,2,256,256]{3,2,1,0:T(8,128)S(1)} %get-tuple-element.45), channel_id=1, source_target_pairs={{0,15},{1,2},{2,1},{3,4},{4,3},{5,6},{6,5},{7,8},{8,7},{9,10},{10,... | collective-permute-start | bytes 1572872 | tf_op jit(solution)/shard_map/ppermute | solution.py:38
  97.7 39.7 %collective-permute-start.17 = (f32[2,2,256,256]{3,2,1,0:T(8,128)S(1)}, f32[2,2,256,256]{3,2,1,0:T(8,128)S(1)}, u32[]{:S(2)}, u32[]{:S(2)}) collective-permute-start(f32[2,2,256,256]{3,2,1,0:T(8,128)S(1)} %get-tuple-element.46), channel_id=1, source_target_pairs={{0,1},{1,0},{2,3},{3,2},{4,5},{5,4},{6,7},{7,6},{8,9},{9,8},{10,11... | collective-permute-start | bytes 3145736 | tf_op jit(solution)/shard_map/ppermute | solution.py:38
  107.7 68.7 %collective-permute-start.10 = (f32[2,2,256,256]{3,2,1,0:T(8,128)S(1)}, f32[2,2,256,256]{3,2,1,0:T(8,128)S(1)}, u32[]{:S(2)}, u32[]{:S(2)}) collective-permute-start(f32[2,2,256,256]{3,2,1,0:T(8,128)S(1)} %get-tuple-element.39), channel_id=1, source_target_pairs={{0,2},{1,3},{2,0},{3,1},{4,6},{5,7},{6,4},{7,5},{8,10},{9,11},{10,... | collective-permute-start | bytes 3145736 | tf_op jit(solution)/shard_map/ppermute | solution.py:38
  127.9 48.5 %collective-permute-start.11 = (f32[2,2,256,256]{3,2,1,0:T(8,128)S(1)}, f32[2,2,256,256]{3,2,1,0:T(8,128)S(1)}, u32[]{:S(2)}, u32[]{:S(2)}) collective-permute-start(f32[2,2,256,256]{3,2,1,0:T(8,128)S(1)} %get-tuple-element.40), channel_id=1, source_target_pairs={{0,4},{1,5},{2,6},{3,7},{4,0},{5,1},{6,2},{7,3},{8,12},{9,13},{10,... | collective-permute-start | bytes 3145736 | tf_op jit(solution)/shard_map/ppermute | solution.py:38
  127.9 27.5 %collective-permute-start.9 = (f32[1,2,256,256]{3,2,1,0:T(8,128)S(1)}, f32[1,2,256,256]{3,2,1,0:T(8,128)S(1)}, u32[]{:S(2)}, u32[]{:S(2)}) collective-permute-start(f32[1,2,256,256]{3,2,1,0:T(8,128)S(1)} %get-tuple-element.38), channel_id=1, source_target_pairs={{0,8},{1,9},{2,10},{3,11},{4,12},{5,13},{6,14},{7,15},{8,0},{9,1},... | collective-permute-start | bytes 1572872 | tf_op jit(solution)/shard_map/ppermute | solution.py:38
  128.3 48.1 %collective-permute-start.12 = (f32[1,2,256,256]{3,2,1,0:T(8,128)S(1)}, f32[1,2,256,256]{3,2,1,0:T(8,128)S(1)}, u32[]{:S(2)}, u32[]{:S(2)}) collective-permute-start(f32[1,2,256,256]{3,2,1,0:T(8,128)S(1)} %get-tuple-element.41), channel_id=1, source_target_pairs={{0,12},{1,13},{2,14},{3,15},{4,8},{5,9},{6,10},{7,11},{8,4},{9,5},... | collective-permute-start | bytes 1572872 | tf_op jit(solution)/shard_map/ppermute | solution.py:38
  (2 other events, 10.8 us)

commit v8 on v7

--- a/solution.py
+++ b/solution.py
@@ -141,15 +141,19 @@
     )(*tables)
 
 
-def copy_slots(slots, source, sends, held, load_sems, sems):
+def copy_slots(slots, source, sends, sems, load_sems=None, held=None):
     loads, stores = [], []
     for at, (slot, (send, place)) in enumerate(zip(slots, sends)):
+        if held is None:
+            stores.append(pltpu.make_async_copy(source.at[slot], send.at[place], sems.at[at]))
+            continue
         loads.append(pltpu.make_async_copy(source.at[slot], held.at[at], load_sems.at[at]))
         stores.append(pltpu.make_async_copy(held.at[at], send.at[place], sems.at[at]))
     for load in loads:
         load.start()
-    for load, store in zip(loads, stores):
-        load.wait()
+    for at, store in enumerate(stores):
+        if loads:
+            loads[at].wait()
         store.start()
     for store in stores:
         store.wait()
@@ -163,28 +167,28 @@
     slots = []
     for exchange in plan:
         slots += outgoing_slots(exchange, me_ref[0], mats, left_ref, match_ref)
-    copy_slots(slots, source, places(plan, pairs, rest[:-3]), *rest[-3:])
+    copy_slots(slots, source, places(plan, pairs, rest[: len(plan)]), *rest[len(plan) :])
 
 
 def next_pack_kernel(plan, pairs, offset, whole, source, *rest):
-    sends = places(plan, pairs, rest[:-3])
-    copy_slots([whole[offset + at, 3] for at in range(len(sends))], source, sends, *rest[-3:])
-
-
-def pack_call(kernel, plan, pairs, grant, scalars, source):
+    sends = places(plan, pairs, rest[: len(plan)])
+    copy_slots([whole[offset + at, 3] for at in range(len(sends))], source, sends, *rest[len(plan) :])
+
+
+def pack_call(kernel, plan, pairs, grant, scalars, source, in_vmem=False):
     order = source.shape[-1]
     sent = sum(payload(e, pairs) for e in plan)
+    buffer = pltpu.VMEM if in_vmem else jax.ShapeDtypeStruct
+    scratch = [pltpu.SemaphoreType.DMA((sent,))]
+    if not in_vmem:
+        scratch += [pltpu.SemaphoreType.DMA((sent,)), pltpu.VMEM((sent, 2, order, order), F32)]
     return list(
         pl.pallas_call(
             kernel,
             in_specs=[SMEM] * len(scalars) + [HBM],
-            out_specs=[HBM] * len(plan),
-            out_shape=[jax.ShapeDtypeStruct((payload(e, pairs), 2, order, order), F32) for e in plan],
-            scratch_shapes=[
-                pltpu.VMEM((sent, 2, order, order), F32),
-                pltpu.SemaphoreType.DMA((sent,)),
-                pltpu.SemaphoreType.DMA((sent,)),
-            ],
+            out_specs=[pl.BlockSpec(memory_space=pltpu.VMEM) if in_vmem else HBM] * len(plan),
+            out_shape=[buffer((payload(e, pairs), 2, order, order), F32) for e in plan],
+            scratch_shapes=scratch,
             compiler_params=pltpu.CompilerParams(vmem_limit_bytes=grant),
             cost_estimate=pl.CostEstimate(flops=0, bytes_accessed=sent * 16 * order**2, transcendentals=0),
         )(*scalars, source)
@@ -357,7 +361,7 @@
 
     rest = plan[len(shifts) :]
     pack = functools.partial(first_pack_kernel, shifts, pairs, mats)
-    sends = pack_call(pack, shifts, pairs, LARGE_GRANT, first_tables, rho)
+    sends = pack_call(pack, shifts, pairs, LARGE_GRANT, first_tables, rho, in_vmem=True)
     pack = functools.partial(first_pack_kernel, rest, pairs, mats)
     sends += pack_call(pack, rest, pairs, GRANT, first_tables, rho)
     groups = [group for group in (shifts + early, middle, last) if group]
@@ -365,7 +369,7 @@
 
     pack = functools.partial(next_pack_kernel, rest, pairs, size(shifts))
     sends += pack_call(pack, rest, pairs, GRANT, scalars[:1], first)
-    groups = [group for group in (shifts + early, middle + last) if group]
+    groups = [group for group in (shifts + early, middle[:1], middle[1:] + last) if group]
     return gather(sends, local_call(damping, hamiltonian, first, rho), 0.5 * STEP * STEP, [], groups)[0]
 
 

time: 183 us -> 181 us (0.989)
  waiting for transfers between devices: 101 us -> 92.4 us
  Pallas kernels: 38.4 us -> 42.8 us
    ppermute x18, waiting for transfers between devices: 101 us -> 92.4 us  [permute(): lax.ppermute(value, 'tier', [(i, self.peer(i, True)) for i in range(self....]
    pallas_call x5 -> x6, Pallas kernels: 16.8 us -> 22.1 us  [rows_call(): pl.pallas_call(functools.partial(rows_kernel, plan, packs, pairs, offset,...]
  transfers between devices with their start and end apart: 18 -> 18, of which waited for: 9 -> 10; matrix products, arithmetic and copies ran while one was open for 0% -> 0% of each run, Pallas kernels for 15% -> 19%
where the time goes in v8:
time: 181 us; the launch traced here: 178 us
  waiting for transfers between devices  92.4 us (51%)
  Pallas kernels  42.8 us (24%)
  starting transfers between devices  42.3 us (23%)
    ppermute x18, waiting for transfers between devices, permute(): lax.ppermute(value, 'tier', [(i, self.peer(i, True)) for i in range(self....  92.4 us
    ppermute x18, starting transfers between devices, permute(): lax.ppermute(value, 'tier', [(i, self.peer(i, True)) for i in range(self....  42.3 us
    pallas_call x6, Pallas kernels, rows_call(): pl.pallas_call(functools.partial(rows_kernel, plan, packs, pairs, offset,...  22.1 us
    pallas_call x2, Pallas kernels, local_call(): pl.pallas_call(functools.partial(local_kernel, len(densities) == 2), grid...  12.2 us
    pallas_call x3, Pallas kernels, pack_call(): pl.pallas_call(kernel, in_specs=[SMEM] * len(scalars) + [HBM], out_specs=...  6.19 us
  transfers between devices with their start and end apart: 18, of which 10 were waited for; matrix products, arithmetic and copies ran while one was open for 0% of the time, Pallas kernels for 19%

profile of v8, /device:TPU:13, one launch (start us, length us, event | category | flops | bytes accessed | tf_op | source)
XLA Modules:
  0.0 178.0 jit_solution(10332312206067897606)
XLA Ops:
  0.0 2.6 %shard_map.84 = (f32[1,2,256,256]{3,2,1,0:T(8,128)S(1)}, f32[1,2,256,256]{3,2,1,0:T(8,128)S(1)}) custom-call(s32[1]{0:T(128)} %bitcast.me_ref, s32[5,6,16]{2,1,0:T(8,128)} %bitcast.6, s32[1,4,1,5]{3,2,1,0:T(1,128)} %match_ref.5, f32[8,2,256,256]{3,2,1,0:T(8,128)} %refs_0_.1), custom_call_target="tpu_custom_call" | custom-call | bytes 2097152 | tf_op jit(solution)/shard_map/pallas_call | solution.py:186
  9.7 6.6 %collective-permute-done.4.refs_0_ = f32[1,2,256,256]{3,2,1,0:T(8,128)S(1)} collective-permute-done((f32[1,2,256,256]{3,2,1,0:T(8,128)S(1)}, f32[1,2,256,256]{3,2,1,0:T(8,128)S(1)}, u32[]{:S(2)}, u32[]{:S(2)}) %collective-permute-start.4) | collective-permute-done | bytes 524320 | tf_op jit(solution)/shard_map/ppermute | solution.py:38
  18.0 11.4 %collective-permute-done.5.refs_1_ = f32[1,2,256,256]{3,2,1,0:T(8,128)S(1)} collective-permute-done((f32[1,2,256,256]{3,2,1,0:T(8,128)S(1)}, f32[1,2,256,256]{3,2,1,0:T(8,128)S(1)}, u32[]{:S(2)}, u32[]{:S(2)}) %collective-permute-start.5) | collective-permute-done | bytes 524320 | tf_op jit(solution)/shard_map/ppermute | solution.py:38
  30.6 3.7 %collective-permute-done.6.refs_2_ = f32[1,2,256,256]{3,2,1,0:T(8,128)S(1)} collective-permute-done((f32[1,2,256,256]{3,2,1,0:T(8,128)S(1)}, f32[1,2,256,256]{3,2,1,0:T(8,128)S(1)}, u32[]{:S(2)}, u32[]{:S(2)}) %collective-permute-start.6) | collective-permute-done | bytes 524320 | tf_op jit(solution)/shard_map/ppermute | solution.py:38
  34.3 3.0 %collective-permute-start.1 = (f32[1,2,256,256]{3,2,1,0:T(8,128)S(1)}, f32[1,2,256,256]{3,2,1,0:T(8,128)S(1)}, u32[]{:S(2)}, u32[]{:S(2)}) collective-permute-start(f32[1,2,256,256]{3,2,1,0:T(8,128)S(1)} %get-tuple-element.29), channel_id=1, source_target_pairs={{0,12},{1,13},{2,14},{3,15},{4,8},{5,9},{6,10},{7,11},{8,4},{9,5},... | collective-permute-start | bytes 1572872 | tf_op jit(solution)/shard_map/ppermute | solution.py:38
  37.3 4.8 %collective-permute-done.7.refs_3_ = f32[1,2,256,256]{3,2,1,0:T(8,128)S(1)} collective-permute-done((f32[1,2,256,256]{3,2,1,0:T(8,128)S(1)}, f32[1,2,256,256]{3,2,1,0:T(8,128)S(1)}, u32[]{:S(2)}, u32[]{:S(2)}) %collective-permute-start.7) | collective-permute-done | bytes 524320 | tf_op jit(solution)/shard_map/ppermute | solution.py:38
  43.8 2.4 %shard_map.82 = (s32[12,4]{1,0:T(8,128)S(1)}, f32[12,2]{1,0:T(8,128)S(1)}) custom-call(s32[1]{0:T(128)} %bitcast.me_ref, s32[5,6,16]{2,1,0:T(8,128)S(1)} %bitcast.9, s32[16]{0:T(128)S(1)} %copy-done.6, s32[1,4,1,5]{3,2,1,0:T(1,128)S(1)} %copy-done.4, f32[6,16]{1,0:T(8,128)S(1)} %fusion.1.left_root, f32[4,1]{1,0:T(4,128)S(1)} %bitcast.10, f32[2,4]{1,0:T(2,128)S(1)} %bitcast.11), custom_call_target="tpu_custom_call" | custom-call | tf_op jit(solution)/shard_map/pallas_call | solution.py:135
  46.2 5.4 %shard_map.85.refs_5_ = f32[8,2,256,256]{3,2,1,0:T(8,128)S(1)} custom-call(f32[8]{0:T(128)S(1)} %copy-done.7, f32[256,256]{1,0:T(8,128)S(1)} %copy-done.2, f32[8,2,256,256]{3,2,1,0:T(8,128)S(1)} %copy-done), custom_call_target="tpu_custom_call" | custom-call | flops 3221225472 | bytes 8388608 | tf_op jit(solution)/shard_map/pallas_call | solution.py:221
  51.6 3.3 %shard_map.86.refs_2_ = f32[8,2,256,256]{3,2,1,0:T(8,128)S(1)} custom-call(s32[12,4]{1,0:T(8,128)S(1)} %get-tuple-element.26.whole, f32[12,2]{1,0:T(8,128)S(1)} %get-tuple-element.27.real, f32[4,256,256]{2,1,0:T(8,128)S(1)} %copy-done.1, f32[1,2,256,256]{3,2,1,0:T(8,128)S(1)} %collective-permute-done.4.refs_0_, ...), custom_call_target="tpu_custom_call", output_to_operand_aliasing={{}: (8, {})} | custom-call | tf_op jit(solution)/shard_map/pallas_call | solution.py:315
  55.0 28.6 %collective-permute-done.2.refs_0_ = f32[1,2,256,256]{3,2,1,0:T(8,128)S(1)} collective-permute-done((f32[1,2,256,256]{3,2,1,0:T(8,128)S(1)}, f32[1,2,256,256]{3,2,1,0:T(8,128)S(1)}, u32[]{:S(2)}, u32[]{:S(2)}) %collective-permute-start.2) | collective-permute-done | bytes 524320 | tf_op jit(solution)/shard_map/ppermute | solution.py:38
  83.6 3.2 %shard_map.87.refs_2_ = f32[8,2,256,256]{3,2,1,0:T(8,128)S(1)} custom-call(s32[12,4]{1,0:T(8,128)S(1)} %get-tuple-element.26.whole, f32[12,2]{1,0:T(8,128)S(1)} %get-tuple-element.27.real, f32[4,256,256]{2,1,0:T(8,128)S(1)} %copy-done.1, f32[1,2,256,256]{3,2,1,0:T(8,128)S(1)} %collective-permute-done.2.refs_0_, ...), custom_call_target="tpu_custom_call", output_to_operand_aliasing={{}: (5, {})} | custom-call | tf_op jit(solution)/shard_map/pallas_call | solution.py:315
  86.9 2.2 %shard_map.88 = (f32[8,2,256,256]{3,2,1,0:T(8,128)S(1)}, f32[1,2,256,256]{3,2,1,0:T(8,128)S(1)}, f32[1,2,256,256]{3,2,1,0:T(8,128)S(1)}) custom-call(s32[12,4]{1,0:T(8,128)S(1)} %get-tuple-element.26.whole, f32[12,2]{1,0:T(8,128)S(1)} %get-tuple-element.27.real, f32[4,256,256]{2,1,0:T(8,128)S(1)} %copy-done.1, ...), custom_call_target="tpu_custom_call", output_to_operand_aliasing={{0}: (5, {})} | custom-call | tf_op jit(solution)/shard_map/pallas_call | solution.py:315
  89.1 3.2 %collective-permute-start.13 = (f32[1,2,256,256]{3,2,1,0:T(8,128)S(1)}, f32[1,2,256,256]{3,2,1,0:T(8,128)S(1)}, u32[]{:S(2)}, u32[]{:S(2)}) collective-permute-start(f32[1,2,256,256]{3,2,1,0:T(8,128)S(1)} %get-tuple-element.42), channel_id=1, source_target_pairs={{0,3},{1,4},{2,5},{3,6},{4,7},{5,8},{6,9},{7,10},{8,11},{9,12},{10... | collective-permute-start | bytes 1572872 | tf_op jit(solution)/shard_map/ppermute | solution.py:38
  97.2 10.7 %collective-permute-done.13.refs_0_ = f32[1,2,256,256]{3,2,1,0:T(8,128)S(1)} collective-permute-done((f32[1,2,256,256]{3,2,1,0:T(8,128)S(1)}, f32[1,2,256,256]{3,2,1,0:T(8,128)S(1)}, u32[]{:S(2)}, u32[]{:S(2)}) %collective-permute-start.13) | collective-permute-done | bytes 524320 | tf_op jit(solution)/shard_map/ppermute | solution.py:38
  107.9 8.1 %collective-permute-done.14.refs_1_ = f32[1,2,256,256]{3,2,1,0:T(8,128)S(1)} collective-permute-done((f32[1,2,256,256]{3,2,1,0:T(8,128)S(1)}, f32[1,2,256,256]{3,2,1,0:T(8,128)S(1)}, u32[]{:S(2)}, u32[]{:S(2)}) %collective-permute-start.14) | collective-permute-done | bytes 524320 | tf_op jit(solution)/shard_map/ppermute | solution.py:38
  117.2 3.9 %collective-permute-done.15.refs_2_ = f32[1,2,256,256]{3,2,1,0:T(8,128)S(1)} collective-permute-done((f32[1,2,256,256]{3,2,1,0:T(8,128)S(1)}, f32[1,2,256,256]{3,2,1,0:T(8,128)S(1)}, u32[]{:S(2)}, u32[]{:S(2)}) %collective-permute-start.15) | collective-permute-done | bytes 524320 | tf_op jit(solution)/shard_map/ppermute | solution.py:38
  121.1 7.8 %collective-permute-start.12 = (f32[1,2,256,256]{3,2,1,0:T(8,128)S(1)}, f32[1,2,256,256]{3,2,1,0:T(8,128)S(1)}, u32[]{:S(2)}, u32[]{:S(2)}) collective-permute-start(f32[1,2,256,256]{3,2,1,0:T(8,128)S(1)} %get-tuple-element.41), channel_id=1, source_target_pairs={{0,8},{1,9},{2,10},{3,11},{4,12},{5,13},{6,14},{7,15},{8,0},{9,1},... | collective-permute-start | bytes 1572872 | tf_op jit(solution)/shard_map/ppermute | solution.py:38
  128.9 14.3 %collective-permute-start.11 = (f32[1,2,256,256]{3,2,1,0:T(8,128)S(1)}, f32[1,2,256,256]{3,2,1,0:T(8,128)S(1)}, u32[]{:S(2)}, u32[]{:S(2)}) collective-permute-start(f32[1,2,256,256]{3,2,1,0:T(8,128)S(1)} %get-tuple-element.40), channel_id=1, source_target_pairs={{0,12},{1,13},{2,14},{3,15},{4,8},{5,9},{6,10},{7,11},{8,4},{9,5},... | collective-permute-start | bytes 1572872 | tf_op jit(solution)/shard_map/ppermute | solution.py:38
  143.1 6.8 %shard_map.90.refs_5_ = f32[8,2,256,256]{3,2,1,0:T(8,128)} custom-call(f32[8]{0:T(128)S(1)} %copy-done.7, f32[256,256]{1,0:T(8,128)S(1)} %copy-done.2, f32[8,2,256,256]{3,2,1,0:T(8,128)S(1)} %get-tuple-element.37.source.density_ref, f32[8,2,256,256]{3,2,1,0:T(8,128)S(1)} %copy-done), custom_call_target="tpu_custom_call" | custom-call | flops 3221225472 | bytes 12582912 | tf_op jit(solution)/shard_map/pallas_call | solution.py:221
  149.9 5.5 %shard_map.91.refs_1_ = f32[8,2,256,256]{3,2,1,0:T(8,128)} custom-call(s32[12,4]{1,0:T(8,128)S(1)} %get-tuple-element.26.whole, f32[12,2]{1,0:T(8,128)S(1)} %get-tuple-element.27.real, f32[4,256,256]{2,1,0:T(8,128)S(1)} %copy-done.1, f32[1,2,256,256]{3,2,1,0:T(8,128)S(1)} %collective-permute-done.13.refs_0_, ...), custom_call_target="tpu_custom_call", output_to_operand_aliasing={{}: (8, {})} | custom-call | tf_op jit(solution)/shard_map/pallas_call | solution.py:315
  155.4 3.3 %collective-permute-done.12.refs_0_ = f32[1,2,256,256]{3,2,1,0:T(8,128)S(1)} collective-permute-done((f32[1,2,256,256]{3,2,1,0:T(8,128)S(1)}, f32[1,2,256,256]{3,2,1,0:T(8,128)S(1)}, u32[]{:S(2)}, u32[]{:S(2)}) %collective-permute-start.12) | collective-permute-done | bytes 524320 | tf_op jit(solution)/shard_map/ppermute | solution.py:38
  158.8 2.8 %shard_map.92.refs_3_ = f32[8,2,256,256]{3,2,1,0:T(8,128)} custom-call(s32[12,4]{1,0:T(8,128)S(1)} %get-tuple-element.26.whole, f32[12,2]{1,0:T(8,128)S(1)} %get-tuple-element.27.real, f32[4,256,256]{2,1,0:T(8,128)S(1)} %copy-done.1, f32[1,2,256,256]{3,2,1,0:T(8,128)S(1)} %collective-permute-done.12.refs_0_, ...), custom_call_target="tpu_custom_call", output_to_operand_aliasing={{}: (4, {})} | custom-call | tf_op jit(solution)/shard_map/pallas_call | solution.py:315
  161.6 11.3 %collective-permute-done.11.refs_2_ = f32[1,2,256,256]{3,2,1,0:T(8,128)S(1)} collective-permute-done((f32[1,2,256,256]{3,2,1,0:T(8,128)S(1)}, f32[1,2,256,256]{3,2,1,0:T(8,128)S(1)}, u32[]{:S(2)}, u32[]{:S(2)}) %collective-permute-start.11) | collective-permute-done | bytes 524320 | tf_op jit(solution)/shard_map/ppermute | solution.py:38
  172.9 5.0 %shard_map.93 = f32[8,2,256,256]{3,2,1,0:T(8,128)} custom-call(s32[12,4]{1,0:T(8,128)S(1)} %get-tuple-element.26.whole, f32[12,2]{1,0:T(8,128)S(1)} %get-tuple-element.27.real, f32[4,256,256]{2,1,0:T(8,128)S(1)} %copy-done.1, f32[2,2,256,256]{3,2,1,0:T(8,128)S(1)} %collective-permute-done.9.refs_0_, ...), custom_call_target="tpu_custom_call", output_to_operand_aliasing={{}: (6, {})} | custom-call | tf_op jit(solution)/shard_map/pallas_call | solution.py:315
  (42 shorter events, 17.9 us)
Async XLA Ops:
  0.0 4.6 %copy-start = (f32[8,2,256,256]{3,2,1,0:T(8,128)S(1)}, f32[8,2,256,256]{3,2,1,0:T(8,128)}, u32[]{:S(2)}) copy-start(f32[8,2,256,256]{3,2,1,0:T(8,128)} %refs_0_.1) | copy-start | bytes 12582916
  0.0 43.7 %copy-start.5 = (f32[4,2]{0,1:T(2,128)S(1)}, f32[4,2]{0,1:T(2,128)}, u32[]{:S(2)}) copy-start(f32[4,2]{0,1:T(2,128)} %param.11) | copy-start | bytes 100
  0.0 43.7 %copy-start.6 = (s32[16]{0:T(128)S(1)}, s32[16]{0:T(128)}, u32[]{:S(2)}) copy-start(s32[16]{0:T(128)} %count_ref.1) | copy-start | bytes 196
  0.0 46.1 %copy-start.2 = (f32[256,256]{1,0:T(8,128)S(1)}, f32[256,256]{1,0:T(8,128)}, u32[]{:S(2)}) copy-start(f32[256,256]{1,0:T(8,128)} %hamiltonian_ref.3) | copy-start | bytes 786436
  0.0 46.1 %copy-start.7 = (f32[8]{0:T(128)S(1)}, f32[8]{0:T(128)}, u32[]{:S(2)}) copy-start(f32[8]{0:T(128)} %damping_ref.3) | copy-start | bytes 100
  2.6 13.6 %collective-permute-start.4 = (f32[1,2,256,256]{3,2,1,0:T(8,128)S(1)}, f32[1,2,256,256]{3,2,1,0:T(8,128)S(1)}, u32[]{:S(2)}, u32[]{:S(2)}) collective-permute-start(f32[1,2,256,256]{3,2,1,0:T(8,128)S(1)} %get-tuple-element.32), channel_id=1, source_target_pairs={{0,3},{1,4},{2,5},{3,6},{4,7},{5,8},{6,9},{7,10},{8,11},{9,12},{10... | collective-permute-start | bytes 1572872 | tf_op jit(solution)/shard_map/ppermute | solution.py:38
  4.6 24.9 %collective-permute-start.5 = (f32[1,2,256,256]{3,2,1,0:T(8,128)S(1)}, f32[1,2,256,256]{3,2,1,0:T(8,128)S(1)}, u32[]{:S(2)}, u32[]{:S(2)}) collective-permute-start(f32[1,2,256,256]{3,2,1,0:T(8,128)S(1)} %get-tuple-element.33), channel_id=1, source_target_pairs={{0,13},{1,14},{2,15},{3,0},{4,1},{5,2},{6,3},{7,4},{8,5},{9,6},{10... | collective-permute-start | bytes 1572872 | tf_op jit(solution)/shard_map/ppermute | solution.py:38
  6.6 27.7 %collective-permute-start.6 = (f32[1,2,256,256]{3,2,1,0:T(8,128)S(1)}, f32[1,2,256,256]{3,2,1,0:T(8,128)S(1)}, u32[]{:S(2)}, u32[]{:S(2)}) collective-permute-start(f32[1,2,256,256]{3,2,1,0:T(8,128)S(1)} %get-tuple-element.34), channel_id=1, source_target_pairs={{0,14},{1,15},{2,4},{3,5},{4,2},{5,3},{6,8},{7,9},{8,6},{9,7},{10,... | collective-permute-start | bytes 1572872 | tf_op jit(solution)/shard_map/ppermute | solution.py:38
  8.7 33.4 %collective-permute-start.7 = (f32[1,2,256,256]{3,2,1,0:T(8,128)S(1)}, f32[1,2,256,256]{3,2,1,0:T(8,128)S(1)}, u32[]{:S(2)}, u32[]{:S(2)}) collective-permute-start(f32[1,2,256,256]{3,2,1,0:T(8,128)S(1)} %get-tuple-element.35), channel_id=1, source_target_pairs={{0,15},{1,2},{2,1},{3,4},{4,3},{5,6},{6,5},{7,8},{8,7},{9,10},{10,... | collective-permute-start | bytes 1572872 | tf_op jit(solution)/shard_map/ppermute | solution.py:38
  9.7 41.9 %collective-permute-start.8 = (f32[2,2,256,256]{3,2,1,0:T(8,128)S(1)}, f32[2,2,256,256]{3,2,1,0:T(8,128)S(1)}, u32[]{:S(2)}, u32[]{:S(2)}) collective-permute-start(f32[2,2,256,256]{3,2,1,0:T(8,128)S(1)} %get-tuple-element.36), channel_id=1, source_target_pairs={{0,1},{1,0},{2,3},{3,2},{4,5},{5,4},{6,7},{7,6},{8,9},{9,8},{10,11... | collective-permute-start | bytes 3145736 | tf_op jit(solution)/shard_map/ppermute | solution.py:38
  16.3 67.3 %collective-permute-start.3 = (f32[2,2,256,256]{3,2,1,0:T(8,128)S(1)}, f32[2,2,256,256]{3,2,1,0:T(8,128)S(1)}, u32[]{:S(2)}, u32[]{:S(2)}) collective-permute-start(f32[2,2,256,256]{3,2,1,0:T(8,128)S(1)} %get-tuple-element.31), channel_id=1, source_target_pairs={{0,2},{1,3},{2,0},{3,1},{4,6},{5,7},{6,4},{7,5},{8,10},{9,11},{10,... | collective-permute-start | bytes 3145736 | tf_op jit(solution)/shard_map/ppermute | solution.py:38
  29.4 57.4 %collective-permute-start = (f32[2,2,256,256]{3,2,1,0:T(8,128)S(1)}, f32[2,2,256,256]{3,2,1,0:T(8,128)S(1)}, u32[]{:S(2)}, u32[]{:S(2)}) collective-permute-start(f32[2,2,256,256]{3,2,1,0:T(8,128)S(1)} %get-tuple-element.28), channel_id=1, source_target_pairs={{0,4},{1,5},{2,6},{3,7},{4,0},{5,1},{6,2},{7,3},{8,12},{9,13},{10,... | collective-permute-start | bytes 3145736 | tf_op jit(solution)/shard_map/ppermute | solution.py:38
  34.3 52.5 %collective-permute-start.1 = (f32[1,2,256,256]{3,2,1,0:T(8,128)S(1)}, f32[1,2,256,256]{3,2,1,0:T(8,128)S(1)}, u32[]{:S(2)}, u32[]{:S(2)}) collective-permute-start(f32[1,2,256,256]{3,2,1,0:T(8,128)S(1)} %get-tuple-element.29), channel_id=1, source_target_pairs={{0,12},{1,13},{2,14},{3,15},{4,8},{5,9},{6,10},{7,11},{8,4},{9,5},... | collective-permute-start | bytes 1572872 | tf_op jit(solution)/shard_map/ppermute | solution.py:38
  42.1 41.5 %collective-permute-start.2 = (f32[1,2,256,256]{3,2,1,0:T(8,128)S(1)}, f32[1,2,256,256]{3,2,1,0:T(8,128)S(1)}, u32[]{:S(2)}, u32[]{:S(2)}) collective-permute-start(f32[1,2,256,256]{3,2,1,0:T(8,128)S(1)} %get-tuple-element.30), channel_id=1, source_target_pairs={{0,8},{1,9},{2,10},{3,11},{4,12},{5,13},{6,14},{7,15},{8,0},{9,1},... | collective-permute-start | bytes 1572872 | tf_op jit(solution)/shard_map/ppermute | solution.py:38
  46.2 5.4 %copy-start.1 = (f32[4,256,256]{2,1,0:T(8,128)S(1)}, f32[4,256,256]{2,1,0:T(8,128)}, u32[]{:S(2)}) copy-start(f32[4,256,256]{2,1,0:T(8,128)} %couplings_ref.11) | copy-start | bytes 3145732
  89.1 18.8 %collective-permute-start.13 = (f32[1,2,256,256]{3,2,1,0:T(8,128)S(1)}, f32[1,2,256,256]{3,2,1,0:T(8,128)S(1)}, u32[]{:S(2)}, u32[]{:S(2)}) collective-permute-start(f32[1,2,256,256]{3,2,1,0:T(8,128)S(1)} %get-tuple-element.42), channel_id=1, source_target_pairs={{0,3},{1,4},{2,5},{3,6},{4,7},{5,8},{6,9},{7,10},{8,11},{9,12},{10... | collective-permute-start | bytes 1572872 | tf_op jit(solution)/shard_map/ppermute | solution.py:38
  92.2 23.7 %collective-permute-start.14 = (f32[1,2,256,256]{3,2,1,0:T(8,128)S(1)}, f32[1,2,256,256]{3,2,1,0:T(8,128)S(1)}, u32[]{:S(2)}, u32[]{:S(2)}) collective-permute-start(f32[1,2,256,256]{3,2,1,0:T(8,128)S(1)} %get-tuple-element.43), channel_id=1, source_target_pairs={{0,13},{1,14},{2,15},{3,0},{4,1},{5,2},{6,3},{7,4},{8,5},{9,6},{10... | collective-permute-start | bytes 1572872 | tf_op jit(solution)/shard_map/ppermute | solution.py:38
  93.8 27.2 %collective-permute-start.15 = (f32[1,2,256,256]{3,2,1,0:T(8,128)S(1)}, f32[1,2,256,256]{3,2,1,0:T(8,128)S(1)}, u32[]{:S(2)}, u32[]{:S(2)}) collective-permute-start(f32[1,2,256,256]{3,2,1,0:T(8,128)S(1)} %get-tuple-element.44), channel_id=1, source_target_pairs={{0,14},{1,15},{2,4},{3,5},{4,2},{5,3},{6,8},{7,9},{8,6},{9,7},{10,... | collective-permute-start | bytes 1572872 | tf_op jit(solution)/shard_map/ppermute | solution.py:38
  95.4 33.4 %collective-permute-start.16 = (f32[1,2,256,256]{3,2,1,0:T(8,128)S(1)}, f32[1,2,256,256]{3,2,1,0:T(8,128)S(1)}, u32[]{:S(2)}, u32[]{:S(2)}) collective-permute-start(f32[1,2,256,256]{3,2,1,0:T(8,128)S(1)} %get-tuple-element.45), channel_id=1, source_target_pairs={{0,15},{1,2},{2,1},{3,4},{4,3},{5,6},{6,5},{7,8},{8,7},{9,10},{10,... | collective-permute-start | bytes 1572872 | tf_op jit(solution)/shard_map/ppermute | solution.py:38
  97.2 52.7 %collective-permute-start.17 = (f32[2,2,256,256]{3,2,1,0:T(8,128)S(1)}, f32[2,2,256,256]{3,2,1,0:T(8,128)S(1)}, u32[]{:S(2)}, u32[]{:S(2)}) collective-permute-start(f32[2,2,256,256]{3,2,1,0:T(8,128)S(1)} %get-tuple-element.46), channel_id=1, source_target_pairs={{0,1},{1,0},{2,3},{3,2},{4,5},{5,4},{6,7},{7,6},{8,9},{9,8},{10,11... | collective-permute-start | bytes 3145736 | tf_op jit(solution)/shard_map/ppermute | solution.py:38
  107.9 65.0 %collective-permute-start.9 = (f32[2,2,256,256]{3,2,1,0:T(8,128)S(1)}, f32[2,2,256,256]{3,2,1,0:T(8,128)S(1)}, u32[]{:S(2)}, u32[]{:S(2)}) collective-permute-start(f32[2,2,256,256]{3,2,1,0:T(8,128)S(1)} %get-tuple-element.38), channel_id=1, source_target_pairs={{0,2},{1,3},{2,0},{3,1},{4,6},{5,7},{6,4},{7,5},{8,10},{9,11},{10,... | collective-permute-start | bytes 3145736 | tf_op jit(solution)/shard_map/ppermute | solution.py:38
  116.0 56.9 %collective-permute-start.10 = (f32[2,2,256,256]{3,2,1,0:T(8,128)S(1)}, f32[2,2,256,256]{3,2,1,0:T(8,128)S(1)}, u32[]{:S(2)}, u32[]{:S(2)}) collective-permute-start(f32[2,2,256,256]{3,2,1,0:T(8,128)S(1)} %get-tuple-element.39), channel_id=1, source_target_pairs={{0,4},{1,5},{2,6},{3,7},{4,0},{5,1},{6,2},{7,3},{8,12},{9,13},{10,... | collective-permute-start | bytes 3145736 | tf_op jit(solution)/shard_map/ppermute | solution.py:38
  121.1 37.7 %collective-permute-start.12 = (f32[1,2,256,256]{3,2,1,0:T(8,128)S(1)}, f32[1,2,256,256]{3,2,1,0:T(8,128)S(1)}, u32[]{:S(2)}, u32[]{:S(2)}) collective-permute-start(f32[1,2,256,256]{3,2,1,0:T(8,128)S(1)} %get-tuple-element.41), channel_id=1, source_target_pairs={{0,8},{1,9},{2,10},{3,11},{4,12},{5,13},{6,14},{7,15},{8,0},{9,1},... | collective-permute-start | bytes 1572872 | tf_op jit(solution)/shard_map/ppermute | solution.py:38
  128.9 44.0 %collective-permute-start.11 = (f32[1,2,256,256]{3,2,1,0:T(8,128)S(1)}, f32[1,2,256,256]{3,2,1,0:T(8,128)S(1)}, u32[]{:S(2)}, u32[]{:S(2)}) collective-permute-start(f32[1,2,256,256]{3,2,1,0:T(8,128)S(1)} %get-tuple-element.40), channel_id=1, source_target_pairs={{0,12},{1,13},{2,14},{3,15},{4,8},{5,9},{6,10},{7,11},{8,4},{9,5},... | collective-permute-start | bytes 1572872 | tf_op jit(solution)/shard_map/ppermute | solution.py:38
  (2 other events, 9.1 us)

commit v9 on v8

--- a/solution.py
+++ b/solution.py
@@ -39,22 +39,22 @@
 
 
 def exchanges(size, colours):
-    shifts, others, swaps, far, last = [], [], [], [], []
+    shifts, short, swaps, far, others = [], [], [], [], []
     for distance in range(1, REACH + 1):
         colour = distance.bit_length() - 1
         if distance != 1 << colour or colour >= colours:
             shifts += [Exchange("shift", distance, size), Exchange("shift", size - distance, size)]
             continue
-        pair = [Exchange("swap", distance, size, colour), Exchange("other", distance, size)]
+        swaps.append(Exchange("swap", distance, size, colour))
+        other = Exchange("other", distance, size)
         if distance == REACH:
-            last = pair
+            others.append(other)
         else:
-            swaps.append(pair[0])
-            others.insert(0, pair[1])
+            short.insert(0, other)
     for colour in range(colours):
         if 1 << colour > REACH:
             far.append(Exchange("swap", 1 << colour, size, colour, listed=False))
-    return shifts, others + swaps[:1], far + swaps[1:], last
+    return shifts, short + swaps[:1], far, swaps[1:], others
 
 
 def payload(exchange, pairs):
@@ -231,7 +231,7 @@
     )(damping, hamiltonian, *densities)
 
 
-def rows_kernel(plan, packs, pairs, offset, scale, whole, real, couplings_ref, *refs):
+def rows_kernel(plan, packs, pairs, offsets, scale, whole, real, couplings_ref, *refs):
     arrivals = refs[: len(plan)]
     acc_in = refs[len(plan)]
     rest = refs[len(plan) + 1 :]
@@ -239,10 +239,10 @@
     acc, landed, chosen, acc_sems, land_sems, mode_sems, send_sems = rest[1 + len(packs) :]
     mats = acc.shape[0]
     rows, lands, modes = [], [], []
-    for exchange, arrival in zip(plan, arrivals):
+    for exchange, offset, arrival in zip(plan, offsets, arrivals):
         for place in range(payload(exchange, pairs)):
             at = len(rows)
-            index = offset + at
+            index = offset + place
             live = whole[index, 0] == 1 if exchange.listed and place == payload(exchange, pairs) - 1 else None
             row = (live, whole[index, 1], whole[index, 2], real[index, 0], real[index, 1])
             lands.append(pltpu.make_async_copy(arrival.at[place], landed.at[at], land_sems.at[at]))
@@ -306,14 +306,14 @@
         when(touched[n], stores[n].wait)
 
 
-def rows_call(plan, packs, pairs, offset, scale, scalars, couplings, arrivals, acc):
+def rows_call(plan, packs, pairs, offsets, scale, scalars, couplings, arrivals, acc):
     mats, _, order, _ = acc.shape
     count = sum(payload(e, pairs) for e in plan)
     sent = sum(payload(e, pairs) for e in packs)
     shapes = [jax.ShapeDtypeStruct(acc.shape, F32)]
     shapes += [jax.ShapeDtypeStruct((payload(e, pairs), 2, order, order), F32) for e in packs]
     return pl.pallas_call(
-        functools.partial(rows_kernel, plan, packs, pairs, offset, scale),
+        functools.partial(rows_kernel, plan, packs, pairs, offsets, scale),
         in_specs=[SMEM] * 2 + [HBM] + [ANY] * len(plan) + [HBM],
         out_specs=[HBM] * len(shapes),
         out_shape=shapes,
@@ -334,8 +334,8 @@
 
 def body(rho, hamiltonian, couplings, bath_coef, damping, match_edges, left_rows, left_count):
     colours, pairs = match_edges.shape[1:3]
-    shifts, early, middle, last = exchanges(lax.axis_size("tier"), colours)
-    plan = shifts + early + middle + last
+    shifts, early, far, swaps, others = exchanges(lax.axis_size("tier"), colours)
+    plan = shifts + early + far + swaps + others
     mats = rho.shape[0]
     me = lax.axis_index("tier").astype(jnp.int32)[None]
     left_fields = jnp.transpose(left_rows, (2, 1, 0))
@@ -350,13 +350,12 @@
         return sum(payload(e, pairs) for e in group)
 
     def gather(sends, acc, scale, packs, groups):
-        arrived = [e.permute(s) for e, s in zip(plan, sends)]
-        at, offset = 0, 0
+        arrived = {e: e.permute(s) for e, s in zip(plan, sends)}
         for group in groups:
             sent = packs if group is groups[-1] else []
-            got = arrived[at : at + len(group)]
-            acc, *out = rows_call(group, sent, pairs, offset, scale, scalars, couplings, got, acc)
-            at, offset = at + len(group), offset + size(group)
+            offsets = [size(plan[: plan.index(e)]) for e in group]
+            got = [arrived[e] for e in group]
+            acc, *out = rows_call(group, sent, pairs, offsets, scale, scalars, couplings, got, acc)
         return acc, out
 
     rest = plan[len(shifts) :]
@@ -364,12 +363,12 @@
     sends = pack_call(pack, shifts, pairs, LARGE_GRANT, first_tables, rho, in_vmem=True)
     pack = functools.partial(first_pack_kernel, rest, pairs, mats)
     sends += pack_call(pack, rest, pairs, GRANT, first_tables, rho)
-    groups = [group for group in (shifts + early, middle, last) if group]
+    groups = [group for group in (shifts + early, swaps, far + others) if group]
     first, sends = gather(sends, local_call(damping, hamiltonian, rho), 1.0, shifts, groups)
 
     pack = functools.partial(next_pack_kernel, rest, pairs, size(shifts))
     sends += pack_call(pack, rest, pairs, GRANT, scalars[:1], first)
-    groups = [group for group in (shifts + early, middle[:1], middle[1:] + last) if group]
+    groups = [group for group in (shifts + early, far, swaps + others) if group]
     return gather(sends, local_call(damping, hamiltonian, first, rho), 0.5 * STEP * STEP, [], groups)[0]
 
 

time: 181 us -> 180 us (level)
  waiting for transfers between devices: 92.4 us -> 84.2 us
  starting transfers between devices: 42.3 us -> 50 us
    ppermute x18, waiting for transfers between devices: 92.4 us -> 84.2 us  [permute(): lax.ppermute(value, 'tier', [(i, self.peer(i, True)) for i in range(self....]
    ppermute x18, starting transfers between devices: 42.3 us -> 50 us  [permute(): lax.ppermute(value, 'tier', [(i, self.peer(i, True)) for i in range(self....]
  transfers between devices with their start and end apart: 18 -> 18, of which waited for: 10 -> 12; matrix products, arithmetic and copies ran while one was open for 0% -> 0% of each run, Pallas kernels for 19% -> 19%
where the time goes in v9:
time: 180 us; the launch traced here: 178 us
  waiting for transfers between devices  84.2 us (47%)
  starting transfers between devices  50 us (28%)
  Pallas kernels  42.8 us (24%)
    ppermute x18, waiting for transfers between devices, permute(): lax.ppermute(value, 'tier', [(i, self.peer(i, True)) for i in range(self....  84.2 us
    ppermute x18, starting transfers between devices, permute(): lax.ppermute(value, 'tier', [(i, self.peer(i, True)) for i in range(self....  50 us
    pallas_call x6, Pallas kernels, rows_call(): pl.pallas_call(functools.partial(rows_kernel, plan, packs, pairs, offsets...  22.1 us
    pallas_call x2, Pallas kernels, local_call(): pl.pallas_call(functools.partial(local_kernel, len(densities) == 2), grid...  12.2 us
    pallas_call x3, Pallas kernels, pack_call(): pl.pallas_call(kernel, in_specs=[SMEM] * len(scalars) + [HBM], out_specs=...  6.19 us
  transfers between devices with their start and end apart: 18, of which 12 were waited for; matrix products, arithmetic and copies ran while one was open for 0% of the time, Pallas kernels for 19%

profile of v9, /device:TPU:13, one launch (start us, length us, event | category | flops | bytes accessed | tf_op | source)
XLA Modules:
  0.0 177.5 jit_solution(8277110902369861078)
XLA Ops:
  0.0 2.6 %shard_map.84 = (f32[1,2,256,256]{3,2,1,0:T(8,128)S(1)}, f32[1,2,256,256]{3,2,1,0:T(8,128)S(1)}) custom-call(s32[1]{0:T(128)} %bitcast.me_ref, s32[5,6,16]{2,1,0:T(8,128)} %bitcast.6, s32[1,4,1,5]{3,2,1,0:T(1,128)} %match_ref.5, f32[8,2,256,256]{3,2,1,0:T(8,128)} %refs_0_.1), custom_call_target="tpu_custom_call" | custom-call | bytes 2097152 | tf_op jit(solution)/shard_map/pallas_call | solution.py:186
  9.7 6.6 %collective-permute-done.4.refs_0_ = f32[1,2,256,256]{3,2,1,0:T(8,128)S(1)} collective-permute-done((f32[1,2,256,256]{3,2,1,0:T(8,128)S(1)}, f32[1,2,256,256]{3,2,1,0:T(8,128)S(1)}, u32[]{:S(2)}, u32[]{:S(2)}) %collective-permute-start.4) | collective-permute-done | bytes 524320 | tf_op jit(solution)/shard_map/ppermute | solution.py:38
  18.0 11.4 %collective-permute-done.5.refs_1_ = f32[1,2,256,256]{3,2,1,0:T(8,128)S(1)} collective-permute-done((f32[1,2,256,256]{3,2,1,0:T(8,128)S(1)}, f32[1,2,256,256]{3,2,1,0:T(8,128)S(1)}, u32[]{:S(2)}, u32[]{:S(2)}) %collective-permute-start.5) | collective-permute-done | bytes 524320 | tf_op jit(solution)/shard_map/ppermute | solution.py:38
  30.6 3.7 %collective-permute-done.6.refs_2_ = f32[1,2,256,256]{3,2,1,0:T(8,128)S(1)} collective-permute-done((f32[1,2,256,256]{3,2,1,0:T(8,128)S(1)}, f32[1,2,256,256]{3,2,1,0:T(8,128)S(1)}, u32[]{:S(2)}, u32[]{:S(2)}) %collective-permute-start.6) | collective-permute-done | bytes 524320 | tf_op jit(solution)/shard_map/ppermute | solution.py:38
  34.3 5.2 %collective-permute-start = (f32[1,2,256,256]{3,2,1,0:T(8,128)S(1)}, f32[1,2,256,256]{3,2,1,0:T(8,128)S(1)}, u32[]{:S(2)}, u32[]{:S(2)}) collective-permute-start(f32[1,2,256,256]{3,2,1,0:T(8,128)S(1)} %get-tuple-element.28), channel_id=1, source_target_pairs={{0,8},{1,9},{2,10},{3,11},{4,12},{5,13},{6,14},{7,15},{8,0},{9,1},... | collective-permute-start | bytes 1572872 | tf_op jit(solution)/shard_map/ppermute | solution.py:38
  40.3 2.3 %collective-permute-start.1 = (f32[1,2,256,256]{3,2,1,0:T(8,128)S(1)}, f32[1,2,256,256]{3,2,1,0:T(8,128)S(1)}, u32[]{:S(2)}, u32[]{:S(2)}) collective-permute-start(f32[1,2,256,256]{3,2,1,0:T(8,128)S(1)} %get-tuple-element.29), channel_id=1, source_target_pairs={{0,12},{1,13},{2,14},{3,15},{4,8},{5,9},{6,10},{7,11},{8,4},{9,5},... | collective-permute-start | bytes 1572872 | tf_op jit(solution)/shard_map/ppermute | solution.py:38
  42.7 2.4 %shard_map.82 = (s32[12,4]{1,0:T(8,128)S(1)}, f32[12,2]{1,0:T(8,128)S(1)}) custom-call(s32[1]{0:T(128)} %bitcast.me_ref, s32[5,6,16]{2,1,0:T(8,128)S(1)} %bitcast.9, s32[16]{0:T(128)S(1)} %copy-done.6, s32[1,4,1,5]{3,2,1,0:T(1,128)S(1)} %copy-done.4, f32[6,16]{1,0:T(8,128)S(1)} %fusion.1.left_root, f32[4,1]{1,0:T(4,128)S(1)} %bitcast.10, f32[2,4]{1,0:T(2,128)S(1)} %bitcast.11), custom_call_target="tpu_custom_call" | custom-call | tf_op jit(solution)/shard_map/pallas_call | solution.py:135
  45.1 5.4 %shard_map.85.refs_5_ = f32[8,2,256,256]{3,2,1,0:T(8,128)S(1)} custom-call(f32[8]{0:T(128)S(1)} %copy-done.7, f32[256,256]{1,0:T(8,128)S(1)} %copy-done.2, f32[8,2,256,256]{3,2,1,0:T(8,128)S(1)} %copy-done), custom_call_target="tpu_custom_call" | custom-call | flops 3221225472 | bytes 8388608 | tf_op jit(solution)/shard_map/pallas_call | solution.py:221
  50.6 3.3 %shard_map.86.refs_2_ = f32[8,2,256,256]{3,2,1,0:T(8,128)S(1)} custom-call(s32[12,4]{1,0:T(8,128)S(1)} %get-tuple-element.26.whole, f32[12,2]{1,0:T(8,128)S(1)} %get-tuple-element.27.real, f32[4,256,256]{2,1,0:T(8,128)S(1)} %copy-done.1, f32[1,2,256,256]{3,2,1,0:T(8,128)S(1)} %collective-permute-done.4.refs_0_, ...), custom_call_target="tpu_custom_call", output_to_operand_aliasing={{}: (8, {})} | custom-call | tf_op jit(solution)/shard_map/pallas_call | solution.py:315
  53.9 8.3 %collective-permute-done.2.refs_0_ = f32[2,2,256,256]{3,2,1,0:T(8,128)S(1)} collective-permute-done((f32[2,2,256,256]{3,2,1,0:T(8,128)S(1)}, f32[2,2,256,256]{3,2,1,0:T(8,128)S(1)}, u32[]{:S(2)}, u32[]{:S(2)}) %collective-permute-start.2) | collective-permute-done | bytes 1048608 | tf_op jit(solution)/shard_map/ppermute | solution.py:38
  62.2 12.7 %collective-permute-done.3.refs_1_ = f32[2,2,256,256]{3,2,1,0:T(8,128)S(1)} collective-permute-done((f32[2,2,256,256]{3,2,1,0:T(8,128)S(1)}, f32[2,2,256,256]{3,2,1,0:T(8,128)S(1)}, u32[]{:S(2)}, u32[]{:S(2)}) %collective-permute-start.3) | collective-permute-done | bytes 1048608 | tf_op jit(solution)/shard_map/ppermute | solution.py:38
  74.9 3.3 %shard_map.87.refs_2_ = f32[8,2,256,256]{3,2,1,0:T(8,128)S(1)} custom-call(s32[12,4]{1,0:T(8,128)S(1)} %get-tuple-element.26.whole, f32[12,2]{1,0:T(8,128)S(1)} %get-tuple-element.27.real, f32[4,256,256]{2,1,0:T(8,128)S(1)} %copy-done.1, f32[2,2,256,256]{3,2,1,0:T(8,128)S(1)} %collective-permute-done.2.refs_0_, ...), custom_call_target="tpu_custom_call", output_to_operand_aliasing={{}: (5, {})} | custom-call | tf_op jit(solution)/shard_map/pallas_call | solution.py:315
  80.3 9.3 %collective-permute-start.13 = (f32[1,2,256,256]{3,2,1,0:T(8,128)S(1)}, f32[1,2,256,256]{3,2,1,0:T(8,128)S(1)}, u32[]{:S(2)}, u32[]{:S(2)}) collective-permute-start(f32[1,2,256,256]{3,2,1,0:T(8,128)S(1)} %get-tuple-element.42), channel_id=1, source_target_pairs={{0,3},{1,4},{2,5},{3,6},{4,7},{5,8},{6,9},{7,10},{8,11},{9,12},{10... | collective-permute-start | bytes 1572872 | tf_op jit(solution)/shard_map/ppermute | solution.py:38
  93.5 8.7 %collective-permute-done.13.refs_0_ = f32[1,2,256,256]{3,2,1,0:T(8,128)S(1)} collective-permute-done((f32[1,2,256,256]{3,2,1,0:T(8,128)S(1)}, f32[1,2,256,256]{3,2,1,0:T(8,128)S(1)}, u32[]{:S(2)}, u32[]{:S(2)}) %collective-permute-start.13) | collective-permute-done | bytes 524320 | tf_op jit(solution)/shard_map/ppermute | solution.py:38
  103.5 12.7 %collective-permute-done.14.refs_1_ = f32[1,2,256,256]{3,2,1,0:T(8,128)S(1)} collective-permute-done((f32[1,2,256,256]{3,2,1,0:T(8,128)S(1)}, f32[1,2,256,256]{3,2,1,0:T(8,128)S(1)}, u32[]{:S(2)}, u32[]{:S(2)}) %collective-permute-start.14) | collective-permute-done | bytes 524320 | tf_op jit(solution)/shard_map/ppermute | solution.py:38
  116.3 2.2 %collective-permute-done.15.refs_2_ = f32[1,2,256,256]{3,2,1,0:T(8,128)S(1)} collective-permute-done((f32[1,2,256,256]{3,2,1,0:T(8,128)S(1)}, f32[1,2,256,256]{3,2,1,0:T(8,128)S(1)}, u32[]{:S(2)}, u32[]{:S(2)}) %collective-permute-start.15) | collective-permute-done | bytes 524320 | tf_op jit(solution)/shard_map/ppermute | solution.py:38
  118.5 5.5 %collective-permute-start.12 = (f32[1,2,256,256]{3,2,1,0:T(8,128)S(1)}, f32[1,2,256,256]{3,2,1,0:T(8,128)S(1)}, u32[]{:S(2)}, u32[]{:S(2)}) collective-permute-start(f32[1,2,256,256]{3,2,1,0:T(8,128)S(1)} %get-tuple-element.41), channel_id=1, source_target_pairs={{0,8},{1,9},{2,10},{3,11},{4,12},{5,13},{6,14},{7,15},{8,0},{9,1},... | collective-permute-start | bytes 1572872 | tf_op jit(solution)/shard_map/ppermute | solution.py:38
  125.8 16.1 %collective-permute-start.11 = (f32[1,2,256,256]{3,2,1,0:T(8,128)S(1)}, f32[1,2,256,256]{3,2,1,0:T(8,128)S(1)}, u32[]{:S(2)}, u32[]{:S(2)}) collective-permute-start(f32[1,2,256,256]{3,2,1,0:T(8,128)S(1)} %get-tuple-element.40), channel_id=1, source_target_pairs={{0,12},{1,13},{2,14},{3,15},{4,8},{5,9},{6,10},{7,11},{8,4},{9,5},... | collective-permute-start | bytes 1572872 | tf_op jit(solution)/shard_map/ppermute | solution.py:38
  142.0 6.8 %shard_map.90.refs_5_ = f32[8,2,256,256]{3,2,1,0:T(8,128)} custom-call(f32[8]{0:T(128)S(1)} %copy-done.7, f32[256,256]{1,0:T(8,128)S(1)} %copy-done.2, f32[8,2,256,256]{3,2,1,0:T(8,128)S(1)} %get-tuple-element.37.source.density_ref, f32[8,2,256,256]{3,2,1,0:T(8,128)S(1)} %copy-done), custom_call_target="tpu_custom_call" | custom-call | flops 3221225472 | bytes 12582912 | tf_op jit(solution)/shard_map/pallas_call | solution.py:221
  148.8 5.5 %shard_map.91.refs_1_ = f32[8,2,256,256]{3,2,1,0:T(8,128)} custom-call(s32[12,4]{1,0:T(8,128)S(1)} %get-tuple-element.26.whole, f32[12,2]{1,0:T(8,128)S(1)} %get-tuple-element.27.real, f32[4,256,256]{2,1,0:T(8,128)S(1)} %copy-done.1, f32[1,2,256,256]{3,2,1,0:T(8,128)S(1)} %collective-permute-done.13.refs_0_, ...), custom_call_target="tpu_custom_call", output_to_operand_aliasing={{}: (8, {})} | custom-call | tf_op jit(solution)/shard_map/pallas_call | solution.py:315
  154.3 5.2 %collective-permute-done.12.refs_0_ = f32[1,2,256,256]{3,2,1,0:T(8,128)S(1)} collective-permute-done((f32[1,2,256,256]{3,2,1,0:T(8,128)S(1)}, f32[1,2,256,256]{3,2,1,0:T(8,128)S(1)}, u32[]{:S(2)}, u32[]{:S(2)}) %collective-permute-start.12) | collective-permute-done | bytes 524320 | tf_op jit(solution)/shard_map/ppermute | solution.py:38
  159.5 2.8 %shard_map.92.refs_3_ = f32[8,2,256,256]{3,2,1,0:T(8,128)} custom-call(s32[12,4]{1,0:T(8,128)S(1)} %get-tuple-element.26.whole, f32[12,2]{1,0:T(8,128)S(1)} %get-tuple-element.27.real, f32[4,256,256]{2,1,0:T(8,128)S(1)} %copy-done.1, f32[1,2,256,256]{3,2,1,0:T(8,128)S(1)} %collective-permute-done.12.refs_0_, ...), custom_call_target="tpu_custom_call", output_to_operand_aliasing={{}: (4, {})} | custom-call | tf_op jit(solution)/shard_map/pallas_call | solution.py:315
  162.3 10.0 %collective-permute-done.11.refs_2_ = f32[1,2,256,256]{3,2,1,0:T(8,128)S(1)} collective-permute-done((f32[1,2,256,256]{3,2,1,0:T(8,128)S(1)}, f32[1,2,256,256]{3,2,1,0:T(8,128)S(1)}, u32[]{:S(2)}, u32[]{:S(2)}) %collective-permute-start.11) | collective-permute-done | bytes 524320 | tf_op jit(solution)/shard_map/ppermute | solution.py:38
  172.4 5.0 %shard_map.93 = f32[8,2,256,256]{3,2,1,0:T(8,128)} custom-call(s32[12,4]{1,0:T(8,128)S(1)} %get-tuple-element.26.whole, f32[12,2]{1,0:T(8,128)S(1)} %get-tuple-element.27.real, f32[4,256,256]{2,1,0:T(8,128)S(1)} %copy-done.1, f32[2,2,256,256]{3,2,1,0:T(8,128)S(1)} %collective-permute-done.9.refs_0_, ...), custom_call_target="tpu_custom_call", output_to_operand_aliasing={{}: (6, {})} | custom-call | tf_op jit(solution)/shard_map/pallas_call | solution.py:315
  (42 shorter events, 20.0 us)
Async XLA Ops:
  0.0 4.6 %copy-start = (f32[8,2,256,256]{3,2,1,0:T(8,128)S(1)}, f32[8,2,256,256]{3,2,1,0:T(8,128)}, u32[]{:S(2)}) copy-start(f32[8,2,256,256]{3,2,1,0:T(8,128)} %refs_0_.1) | copy-start | bytes 12582916
  0.0 42.7 %copy-start.5 = (f32[4,2]{0,1:T(2,128)S(1)}, f32[4,2]{0,1:T(2,128)}, u32[]{:S(2)}) copy-start(f32[4,2]{0,1:T(2,128)} %param.11) | copy-start | bytes 100
  0.0 42.7 %copy-start.6 = (s32[16]{0:T(128)S(1)}, s32[16]{0:T(128)}, u32[]{:S(2)}) copy-start(s32[16]{0:T(128)} %count_ref.1) | copy-start | bytes 196
  0.0 45.1 %copy-start.2 = (f32[256,256]{1,0:T(8,128)S(1)}, f32[256,256]{1,0:T(8,128)}, u32[]{:S(2)}) copy-start(f32[256,256]{1,0:T(8,128)} %hamiltonian_ref.3) | copy-start | bytes 786436
  0.0 45.1 %copy-start.7 = (f32[8]{0:T(128)S(1)}, f32[8]{0:T(128)}, u32[]{:S(2)}) copy-start(f32[8]{0:T(128)} %damping_ref.3) | copy-start | bytes 100
  2.6 13.6 %collective-permute-start.4 = (f32[1,2,256,256]{3,2,1,0:T(8,128)S(1)}, f32[1,2,256,256]{3,2,1,0:T(8,128)S(1)}, u32[]{:S(2)}, u32[]{:S(2)}) collective-permute-start(f32[1,2,256,256]{3,2,1,0:T(8,128)S(1)} %get-tuple-element.32), channel_id=1, source_target_pairs={{0,3},{1,4},{2,5},{3,6},{4,7},{5,8},{6,9},{7,10},{8,11},{9,12},{10... | collective-permute-start | bytes 1572872 | tf_op jit(solution)/shard_map/ppermute | solution.py:38
  4.6 24.9 %collective-permute-start.5 = (f32[1,2,256,256]{3,2,1,0:T(8,128)S(1)}, f32[1,2,256,256]{3,2,1,0:T(8,128)S(1)}, u32[]{:S(2)}, u32[]{:S(2)}) collective-permute-start(f32[1,2,256,256]{3,2,1,0:T(8,128)S(1)} %get-tuple-element.33), channel_id=1, source_target_pairs={{0,13},{1,14},{2,15},{3,0},{4,1},{5,2},{6,3},{7,4},{8,5},{9,6},{10... | collective-permute-start | bytes 1572872 | tf_op jit(solution)/shard_map/ppermute | solution.py:38
  6.6 27.7 %collective-permute-start.6 = (f32[1,2,256,256]{3,2,1,0:T(8,128)S(1)}, f32[1,2,256,256]{3,2,1,0:T(8,128)S(1)}, u32[]{:S(2)}, u32[]{:S(2)}) collective-permute-start(f32[1,2,256,256]{3,2,1,0:T(8,128)S(1)} %get-tuple-element.34), channel_id=1, source_target_pairs={{0,14},{1,15},{2,4},{3,5},{4,2},{5,3},{6,8},{7,9},{8,6},{9,7},{10,... | collective-permute-start | bytes 1572872 | tf_op jit(solution)/shard_map/ppermute | solution.py:38
  8.7 31.6 %collective-permute-start.7 = (f32[1,2,256,256]{3,2,1,0:T(8,128)S(1)}, f32[1,2,256,256]{3,2,1,0:T(8,128)S(1)}, u32[]{:S(2)}, u32[]{:S(2)}) collective-permute-start(f32[1,2,256,256]{3,2,1,0:T(8,128)S(1)} %get-tuple-element.35), channel_id=1, source_target_pairs={{0,15},{1,2},{2,1},{3,4},{4,3},{5,6},{6,5},{7,8},{8,7},{9,10},{10,... | collective-permute-start | bytes 1572872 | tf_op jit(solution)/shard_map/ppermute | solution.py:38
  9.7 40.8 %collective-permute-start.8 = (f32[2,2,256,256]{3,2,1,0:T(8,128)S(1)}, f32[2,2,256,256]{3,2,1,0:T(8,128)S(1)}, u32[]{:S(2)}, u32[]{:S(2)}) collective-permute-start(f32[2,2,256,256]{3,2,1,0:T(8,128)S(1)} %get-tuple-element.36), channel_id=1, source_target_pairs={{0,1},{1,0},{2,3},{3,2},{4,5},{5,4},{6,7},{7,6},{8,9},{9,8},{10,11... | collective-permute-start | bytes 3145736 | tf_op jit(solution)/shard_map/ppermute | solution.py:38
  16.3 45.9 %collective-permute-start.2 = (f32[2,2,256,256]{3,2,1,0:T(8,128)S(1)}, f32[2,2,256,256]{3,2,1,0:T(8,128)S(1)}, u32[]{:S(2)}, u32[]{:S(2)}) collective-permute-start(f32[2,2,256,256]{3,2,1,0:T(8,128)S(1)} %get-tuple-element.30), channel_id=1, source_target_pairs={{0,2},{1,3},{2,0},{3,1},{4,6},{5,7},{6,4},{7,5},{8,10},{9,11},{10,... | collective-permute-start | bytes 3145736 | tf_op jit(solution)/shard_map/ppermute | solution.py:38
  29.4 45.4 %collective-permute-start.3 = (f32[2,2,256,256]{3,2,1,0:T(8,128)S(1)}, f32[2,2,256,256]{3,2,1,0:T(8,128)S(1)}, u32[]{:S(2)}, u32[]{:S(2)}) collective-permute-start(f32[2,2,256,256]{3,2,1,0:T(8,128)S(1)} %get-tuple-element.31), channel_id=1, source_target_pairs={{0,4},{1,5},{2,6},{3,7},{4,0},{5,1},{6,2},{7,3},{8,12},{9,13},{10,... | collective-permute-start | bytes 3145736 | tf_op jit(solution)/shard_map/ppermute | solution.py:38
  34.3 43.8 %collective-permute-start = (f32[1,2,256,256]{3,2,1,0:T(8,128)S(1)}, f32[1,2,256,256]{3,2,1,0:T(8,128)S(1)}, u32[]{:S(2)}, u32[]{:S(2)}) collective-permute-start(f32[1,2,256,256]{3,2,1,0:T(8,128)S(1)} %get-tuple-element.28), channel_id=1, source_target_pairs={{0,8},{1,9},{2,10},{3,11},{4,12},{5,13},{6,14},{7,15},{8,0},{9,1},... | collective-permute-start | bytes 1572872 | tf_op jit(solution)/shard_map/ppermute | solution.py:38
  40.3 37.9 %collective-permute-start.1 = (f32[1,2,256,256]{3,2,1,0:T(8,128)S(1)}, f32[1,2,256,256]{3,2,1,0:T(8,128)S(1)}, u32[]{:S(2)}, u32[]{:S(2)}) collective-permute-start(f32[1,2,256,256]{3,2,1,0:T(8,128)S(1)} %get-tuple-element.29), channel_id=1, source_target_pairs={{0,12},{1,13},{2,14},{3,15},{4,8},{5,9},{6,10},{7,11},{8,4},{9,5},... | collective-permute-start | bytes 1572872 | tf_op jit(solution)/shard_map/ppermute | solution.py:38
  45.1 5.4 %copy-start.1 = (f32[4,256,256]{2,1,0:T(8,128)S(1)}, f32[4,256,256]{2,1,0:T(8,128)}, u32[]{:S(2)}) copy-start(f32[4,256,256]{2,1,0:T(8,128)} %couplings_ref.11) | copy-start | bytes 3145732
  80.3 21.9 %collective-permute-start.13 = (f32[1,2,256,256]{3,2,1,0:T(8,128)S(1)}, f32[1,2,256,256]{3,2,1,0:T(8,128)S(1)}, u32[]{:S(2)}, u32[]{:S(2)}) collective-permute-start(f32[1,2,256,256]{3,2,1,0:T(8,128)S(1)} %get-tuple-element.42), channel_id=1, source_target_pairs={{0,3},{1,4},{2,5},{3,6},{4,7},{5,8},{6,9},{7,10},{8,11},{9,12},{10... | collective-permute-start | bytes 1572872 | tf_op jit(solution)/shard_map/ppermute | solution.py:38
  89.6 26.6 %collective-permute-start.14 = (f32[1,2,256,256]{3,2,1,0:T(8,128)S(1)}, f32[1,2,256,256]{3,2,1,0:T(8,128)S(1)}, u32[]{:S(2)}, u32[]{:S(2)}) collective-permute-start(f32[1,2,256,256]{3,2,1,0:T(8,128)S(1)} %get-tuple-element.43), channel_id=1, source_target_pairs={{0,13},{1,14},{2,15},{3,0},{4,1},{5,2},{6,3},{7,4},{8,5},{9,6},{10... | collective-permute-start | bytes 1572872 | tf_op jit(solution)/shard_map/ppermute | solution.py:38
  91.2 27.3 %collective-permute-start.15 = (f32[1,2,256,256]{3,2,1,0:T(8,128)S(1)}, f32[1,2,256,256]{3,2,1,0:T(8,128)S(1)}, u32[]{:S(2)}, u32[]{:S(2)}) collective-permute-start(f32[1,2,256,256]{3,2,1,0:T(8,128)S(1)} %get-tuple-element.44), channel_id=1, source_target_pairs={{0,14},{1,15},{2,4},{3,5},{4,2},{5,3},{6,8},{7,9},{8,6},{9,7},{10,... | collective-permute-start | bytes 1572872 | tf_op jit(solution)/shard_map/ppermute | solution.py:38
  91.7 34.1 %collective-permute-start.16 = (f32[1,2,256,256]{3,2,1,0:T(8,128)S(1)}, f32[1,2,256,256]{3,2,1,0:T(8,128)S(1)}, u32[]{:S(2)}, u32[]{:S(2)}) collective-permute-start(f32[1,2,256,256]{3,2,1,0:T(8,128)S(1)} %get-tuple-element.45), channel_id=1, source_target_pairs={{0,15},{1,2},{2,1},{3,4},{4,3},{5,6},{6,5},{7,8},{8,7},{9,10},{10,... | collective-permute-start | bytes 1572872 | tf_op jit(solution)/shard_map/ppermute | solution.py:38
  93.5 55.3 %collective-permute-start.17 = (f32[2,2,256,256]{3,2,1,0:T(8,128)S(1)}, f32[2,2,256,256]{3,2,1,0:T(8,128)S(1)}, u32[]{:S(2)}, u32[]{:S(2)}) collective-permute-start(f32[2,2,256,256]{3,2,1,0:T(8,128)S(1)} %get-tuple-element.46), channel_id=1, source_target_pairs={{0,1},{1,0},{2,3},{3,2},{4,5},{5,4},{6,7},{7,6},{8,9},{9,8},{10,11... | collective-permute-start | bytes 3145736 | tf_op jit(solution)/shard_map/ppermute | solution.py:38
  102.2 70.2 %collective-permute-start.9 = (f32[2,2,256,256]{3,2,1,0:T(8,128)S(1)}, f32[2,2,256,256]{3,2,1,0:T(8,128)S(1)}, u32[]{:S(2)}, u32[]{:S(2)}) collective-permute-start(f32[2,2,256,256]{3,2,1,0:T(8,128)S(1)} %get-tuple-element.38), channel_id=1, source_target_pairs={{0,2},{1,3},{2,0},{3,1},{4,6},{5,7},{6,4},{7,5},{8,10},{9,11},{10,... | collective-permute-start | bytes 3145736 | tf_op jit(solution)/shard_map/ppermute | solution.py:38
  116.3 56.1 %collective-permute-start.10 = (f32[2,2,256,256]{3,2,1,0:T(8,128)S(1)}, f32[2,2,256,256]{3,2,1,0:T(8,128)S(1)}, u32[]{:S(2)}, u32[]{:S(2)}) collective-permute-start(f32[2,2,256,256]{3,2,1,0:T(8,128)S(1)} %get-tuple-element.39), channel_id=1, source_target_pairs={{0,4},{1,5},{2,6},{3,7},{4,0},{5,1},{6,2},{7,3},{8,12},{9,13},{10,... | collective-permute-start | bytes 3145736 | tf_op jit(solution)/shard_map/ppermute | solution.py:38
  118.5 41.0 %collective-permute-start.12 = (f32[1,2,256,256]{3,2,1,0:T(8,128)S(1)}, f32[1,2,256,256]{3,2,1,0:T(8,128)S(1)}, u32[]{:S(2)}, u32[]{:S(2)}) collective-permute-start(f32[1,2,256,256]{3,2,1,0:T(8,128)S(1)} %get-tuple-element.41), channel_id=1, source_target_pairs={{0,8},{1,9},{2,10},{3,11},{4,12},{5,13},{6,14},{7,15},{8,0},{9,1},... | collective-permute-start | bytes 1572872 | tf_op jit(solution)/shard_map/ppermute | solution.py:38
  125.8 46.6 %collective-permute-start.11 = (f32[1,2,256,256]{3,2,1,0:T(8,128)S(1)}, f32[1,2,256,256]{3,2,1,0:T(8,128)S(1)}, u32[]{:S(2)}, u32[]{:S(2)}) collective-permute-start(f32[1,2,256,256]{3,2,1,0:T(8,128)S(1)} %get-tuple-element.40), channel_id=1, source_target_pairs={{0,12},{1,13},{2,14},{3,15},{4,8},{5,9},{6,10},{7,11},{8,4},{9,5},... | collective-permute-start | bytes 1572872 | tf_op jit(solution)/shard_map/ppermute | solution.py:38
  (2 other events, 9.1 us)

commit v10 on v9

--- a/solution.py
+++ b/solution.py
@@ -127,6 +127,8 @@
             whole[at, 0] = jnp.int32(1) if live is None else live.astype(jnp.int32)
             whole[at, 1], whole[at, 2], whole[at, 3] = target, mode, slot
             real[at, 0], real[at, 1] = a, b
+            for field in range(4):
+                real[at, 2 + field] = whole[at, field].astype(F32)
             at += 1
 
 
@@ -136,7 +138,7 @@
         functools.partial(tables_kernel, plan, mats),
         in_specs=[SMEM] * 7,
         out_specs=[SMEM] * 2,
-        out_shape=[jax.ShapeDtypeStruct((count, 4), jnp.int32), jax.ShapeDtypeStruct((count, 2), F32)],
+        out_shape=[jax.ShapeDtypeStruct((count, 4), jnp.int32), jax.ShapeDtypeStruct((count, 6), F32)],
         compiler_params=pltpu.CompilerParams(vmem_limit_bytes=GRANT),
     )(*tables)
 
@@ -231,8 +233,12 @@
     )(damping, hamiltonian, *densities)
 
 
-def rows_kernel(plan, packs, pairs, offsets, scale, whole, real, couplings_ref, *refs):
+def rows_kernel(plan, packs, pairs, offsets, scale, real, couplings_ref, *refs):
     arrivals = refs[: len(plan)]
+
+    def whole(index, field):
+        return real[index, 2 + field].astype(jnp.int32)
+
     acc_in = refs[len(plan)]
     rest = refs[len(plan) + 1 :]
     acc_out, sends = rest[0], rest[1 : 1 + len(packs)]
@@ -243,8 +249,8 @@
         for place in range(payload(exchange, pairs)):
             at = len(rows)
             index = offset + place
-            live = whole[index, 0] == 1 if exchange.listed and place == payload(exchange, pairs) - 1 else None
-            row = (live, whole[index, 1], whole[index, 2], real[index, 0], real[index, 1])
+            live = whole(index, 0) == 1 if exchange.listed and place == payload(exchange, pairs) - 1 else None
+            row = (live, whole(index, 1), whole(index, 2), real[index, 0], real[index, 1])
             lands.append(pltpu.make_async_copy(arrival.at[place], landed.at[at], land_sems.at[at]))
             modes.append(pltpu.make_async_copy(couplings_ref.at[row[2]], chosen.at[at], mode_sems.at[at]))
             rows.append(row)
@@ -271,7 +277,7 @@
 
     early, late, copies = [], [], []
     for at, (send, place) in enumerate(places(packs, pairs, sends)):
-        slot = whole[at, 3]
+        slot = whole(at, 3)
         copy = pltpu.make_async_copy(acc.at[slot], send.at[place], send_sems.at[at])
         busy = touches(slot)
         copies.append(copy)
@@ -314,10 +320,10 @@
     shapes += [jax.ShapeDtypeStruct((payload(e, pairs), 2, order, order), F32) for e in packs]
     return pl.pallas_call(
         functools.partial(rows_kernel, plan, packs, pairs, offsets, scale),
-        in_specs=[SMEM] * 2 + [HBM] + [ANY] * len(plan) + [HBM],
+        in_specs=[SMEM] + [HBM] + [ANY] * len(plan) + [HBM],
         out_specs=[HBM] * len(shapes),
         out_shape=shapes,
-        input_output_aliases={3 + len(plan): 0},
+        input_output_aliases={2 + len(plan): 0},
         scratch_shapes=[
             pltpu.VMEM((mats, 2, order, order), F32),
             pltpu.VMEM((count, 2, order, order), F32),
@@ -329,7 +335,7 @@
         ],
         compiler_params=pltpu.CompilerParams(vmem_limit_bytes=GRANT),
         cost_estimate=pl.CostEstimate(flops=0, bytes_accessed=0, transcendentals=0),
-    )(*scalars, couplings, *arrivals, acc)
+    )(scalars[1], couplings, *arrivals, acc)
 
 
 def body(rho, hamiltonian, couplings, bath_coef, damping, match_edges, left_rows, left_count):

time: 180 us -> 179 us (level)
  waiting for transfers between devices: 84.2 us -> 86.4 us
    ppermute x18, waiting for transfers between devices: 84.2 us -> 86.4 us  [permute(): lax.ppermute(value, 'tier', [(i, self.peer(i, True)) for i in range(self....]
  transfers between devices with their start and end apart: 18 -> 18, of which waited for: 12 -> 12; matrix products, arithmetic and copies ran while one was open for 0% -> 0% of each run, Pallas kernels for 19% -> 17%
where the time goes in v10:
time: 179 us; the launch traced here: 178 us
  waiting for transfers between devices  86.4 us (48%)
  starting transfers between devices  49.5 us (28%)
  Pallas kernels  41.1 us (23%)
    ppermute x18, waiting for transfers between devices, permute(): lax.ppermute(value, 'tier', [(i, self.peer(i, True)) for i in range(self....  86.4 us
    ppermute x18, starting transfers between devices, permute(): lax.ppermute(value, 'tier', [(i, self.peer(i, True)) for i in range(self....  49.5 us
    pallas_call x6, Pallas kernels, rows_call(): pl.pallas_call(functools.partial(rows_kernel, plan, packs, pairs, offsets...  20.3 us
    pallas_call x2, Pallas kernels, local_call(): pl.pallas_call(functools.partial(local_kernel, len(densities) == 2), grid...  12.1 us
    pallas_call x3, Pallas kernels, pack_call(): pl.pallas_call(kernel, in_specs=[SMEM] * len(scalars) + [HBM], out_specs=...  6.19 us
  transfers between devices with their start and end apart: 18, of which 12 were waited for; matrix products, arithmetic and copies ran while one was open for 0% of the time, Pallas kernels for 17%

profile of v10, /device:TPU:13, one launch (start us, length us, event | category | flops | bytes accessed | tf_op | source)
XLA Modules:
  0.0 177.5 jit_solution(7632171681085073824)
XLA Ops:
  0.0 2.6 %shard_map.84 = (f32[1,2,256,256]{3,2,1,0:T(8,128)S(1)}, f32[1,2,256,256]{3,2,1,0:T(8,128)S(1)}) custom-call(s32[1]{0:T(128)} %bitcast.me_ref, s32[5,6,16]{2,1,0:T(8,128)} %bitcast.6, s32[1,4,1,5]{3,2,1,0:T(1,128)} %match_ref.5, f32[8,2,256,256]{3,2,1,0:T(8,128)} %refs_0_.1), custom_call_target="tpu_custom_call" | custom-call | bytes 2097152 | tf_op jit(solution)/shard_map/pallas_call | solution.py:188
  9.7 6.6 %collective-permute-done.4.refs_0_ = f32[1,2,256,256]{3,2,1,0:T(8,128)S(1)} collective-permute-done((f32[1,2,256,256]{3,2,1,0:T(8,128)S(1)}, f32[1,2,256,256]{3,2,1,0:T(8,128)S(1)}, u32[]{:S(2)}, u32[]{:S(2)}) %collective-permute-start.4) | collective-permute-done | bytes 524320 | tf_op jit(solution)/shard_map/ppermute | solution.py:38
  18.0 11.4 %collective-permute-done.5.refs_1_ = f32[1,2,256,256]{3,2,1,0:T(8,128)S(1)} collective-permute-done((f32[1,2,256,256]{3,2,1,0:T(8,128)S(1)}, f32[1,2,256,256]{3,2,1,0:T(8,128)S(1)}, u32[]{:S(2)}, u32[]{:S(2)}) %collective-permute-start.5) | collective-permute-done | bytes 524320 | tf_op jit(solution)/shard_map/ppermute | solution.py:38
  30.6 3.7 %collective-permute-done.6.refs_2_ = f32[1,2,256,256]{3,2,1,0:T(8,128)S(1)} collective-permute-done((f32[1,2,256,256]{3,2,1,0:T(8,128)S(1)}, f32[1,2,256,256]{3,2,1,0:T(8,128)S(1)}, u32[]{:S(2)}, u32[]{:S(2)}) %collective-permute-start.6) | collective-permute-done | bytes 524320 | tf_op jit(solution)/shard_map/ppermute | solution.py:38
  34.3 5.2 %collective-permute-start = (f32[1,2,256,256]{3,2,1,0:T(8,128)S(1)}, f32[1,2,256,256]{3,2,1,0:T(8,128)S(1)}, u32[]{:S(2)}, u32[]{:S(2)}) collective-permute-start(f32[1,2,256,256]{3,2,1,0:T(8,128)S(1)} %get-tuple-element.28), channel_id=1, source_target_pairs={{0,8},{1,9},{2,10},{3,11},{4,12},{5,13},{6,14},{7,15},{8,0},{9,1},... | collective-permute-start | bytes 1572872 | tf_op jit(solution)/shard_map/ppermute | solution.py:38
  42.7 2.5 %shard_map.82 = (s32[12,4]{1,0:T(8,128)S(1)}, f32[12,6]{1,0:T(8,128)S(1)}) custom-call(s32[1]{0:T(128)} %bitcast.me_ref, s32[5,6,16]{2,1,0:T(8,128)S(1)} %bitcast.9, s32[16]{0:T(128)S(1)} %copy-done.6, s32[1,4,1,5]{3,2,1,0:T(1,128)S(1)} %copy-done.4, f32[6,16]{1,0:T(8,128)S(1)} %fusion.1.left_root, f32[4,1]{1,0:T(4,128)S(1)} %bitcast.10, f32[2,4]{1,0:T(2,128)S(1)} %bitcast.11), custom_call_target="tpu_custom_call" | custom-call | tf_op jit(solution)/shard_map/pallas_call | solution.py:137
  45.2 5.3 %shard_map.85.refs_5_ = f32[8,2,256,256]{3,2,1,0:T(8,128)S(1)} custom-call(f32[8]{0:T(128)S(1)} %copy-done.7, f32[256,256]{1,0:T(8,128)S(1)} %copy-done.2, f32[8,2,256,256]{3,2,1,0:T(8,128)S(1)} %copy-done), custom_call_target="tpu_custom_call" | custom-call | flops 3221225472 | bytes 8388608 | tf_op jit(solution)/shard_map/pallas_call | solution.py:223
  50.6 2.5 %shard_map.86.refs_2_ = f32[8,2,256,256]{3,2,1,0:T(8,128)S(1)} custom-call(f32[12,6]{1,0:T(8,128)S(1)} %get-tuple-element.26.real, f32[4,256,256]{2,1,0:T(8,128)S(1)} %copy-done.1, f32[1,2,256,256]{3,2,1,0:T(8,128)S(1)} %collective-permute-done.4.refs_0_, f32[1,2,256,256]{3,2,1,0:T(8,128)S(1)} %collective-permute-done.5.refs_1_, ...), custom_call_target="tpu_custom_call", output_to_operand_aliasing={{}: (7, {})} | custom-call | tf_op jit(solution)/shard_map/pallas_call | solution.py:321
  53.1 9.1 %collective-permute-done.2.refs_0_ = f32[2,2,256,256]{3,2,1,0:T(8,128)S(1)} collective-permute-done((f32[2,2,256,256]{3,2,1,0:T(8,128)S(1)}, f32[2,2,256,256]{3,2,1,0:T(8,128)S(1)}, u32[]{:S(2)}, u32[]{:S(2)}) %collective-permute-start.2) | collective-permute-done | bytes 1048608 | tf_op jit(solution)/shard_map/ppermute | solution.py:38
  62.2 12.7 %collective-permute-done.3.refs_1_ = f32[2,2,256,256]{3,2,1,0:T(8,128)S(1)} collective-permute-done((f32[2,2,256,256]{3,2,1,0:T(8,128)S(1)}, f32[2,2,256,256]{3,2,1,0:T(8,128)S(1)}, u32[]{:S(2)}, u32[]{:S(2)}) %collective-permute-start.3) | collective-permute-done | bytes 1048608 | tf_op jit(solution)/shard_map/ppermute | solution.py:38
  74.9 3.1 %shard_map.87.refs_2_ = f32[8,2,256,256]{3,2,1,0:T(8,128)S(1)} custom-call(f32[12,6]{1,0:T(8,128)S(1)} %get-tuple-element.26.real, f32[4,256,256]{2,1,0:T(8,128)S(1)} %copy-done.1, f32[2,2,256,256]{3,2,1,0:T(8,128)S(1)} %collective-permute-done.2.refs_0_, f32[2,2,256,256]{3,2,1,0:T(8,128)S(1)} %collective-permute-done.3.refs_1_, ...), custom_call_target="tpu_custom_call", output_to_operand_aliasing={{}: (4, {})} | custom-call | tf_op jit(solution)/shard_map/pallas_call | solution.py:321
  78.0 2.7 %shard_map.88 = (f32[8,2,256,256]{3,2,1,0:T(8,128)S(1)}, f32[1,2,256,256]{3,2,1,0:T(8,128)S(1)}, f32[1,2,256,256]{3,2,1,0:T(8,128)S(1)}) custom-call(f32[12,6]{1,0:T(8,128)S(1)} %get-tuple-element.26.real, f32[4,256,256]{2,1,0:T(8,128)S(1)} %copy-done.1, f32[1,2,256,256]{3,2,1,0:T(8,128)S(1)} %collective-permute-done.refs_0_, ...), custom_call_target="tpu_custom_call", output_to_operand_aliasing={{0}: (4, {})} | custom-call | tf_op jit(solution)/shard_map/pallas_call | solution.py:321
  80.7 9.5 %collective-permute-start.13 = (f32[1,2,256,256]{3,2,1,0:T(8,128)S(1)}, f32[1,2,256,256]{3,2,1,0:T(8,128)S(1)}, u32[]{:S(2)}, u32[]{:S(2)}) collective-permute-start(f32[1,2,256,256]{3,2,1,0:T(8,128)S(1)} %get-tuple-element.42), channel_id=1, source_target_pairs={{0,3},{1,4},{2,5},{3,6},{4,7},{5,8},{6,9},{7,10},{8,11},{9,12},{10... | collective-permute-start | bytes 1572872 | tf_op jit(solution)/shard_map/ppermute | solution.py:38
  93.4 9.5 %collective-permute-done.13.refs_0_ = f32[1,2,256,256]{3,2,1,0:T(8,128)S(1)} collective-permute-done((f32[1,2,256,256]{3,2,1,0:T(8,128)S(1)}, f32[1,2,256,256]{3,2,1,0:T(8,128)S(1)}, u32[]{:S(2)}, u32[]{:S(2)}) %collective-permute-start.13) | collective-permute-done | bytes 524320 | tf_op jit(solution)/shard_map/ppermute | solution.py:38
  102.9 12.9 %collective-permute-done.14.refs_1_ = f32[1,2,256,256]{3,2,1,0:T(8,128)S(1)} collective-permute-done((f32[1,2,256,256]{3,2,1,0:T(8,128)S(1)}, f32[1,2,256,256]{3,2,1,0:T(8,128)S(1)}, u32[]{:S(2)}, u32[]{:S(2)}) %collective-permute-start.14) | collective-permute-done | bytes 524320 | tf_op jit(solution)/shard_map/ppermute | solution.py:38
  115.8 2.6 %collective-permute-done.15.refs_2_ = f32[1,2,256,256]{3,2,1,0:T(8,128)S(1)} collective-permute-done((f32[1,2,256,256]{3,2,1,0:T(8,128)S(1)}, f32[1,2,256,256]{3,2,1,0:T(8,128)S(1)}, u32[]{:S(2)}, u32[]{:S(2)}) %collective-permute-start.15) | collective-permute-done | bytes 524320 | tf_op jit(solution)/shard_map/ppermute | solution.py:38
  118.4 5.6 %collective-permute-start.12 = (f32[1,2,256,256]{3,2,1,0:T(8,128)S(1)}, f32[1,2,256,256]{3,2,1,0:T(8,128)S(1)}, u32[]{:S(2)}, u32[]{:S(2)}) collective-permute-start(f32[1,2,256,256]{3,2,1,0:T(8,128)S(1)} %get-tuple-element.41), channel_id=1, source_target_pairs={{0,8},{1,9},{2,10},{3,11},{4,12},{5,13},{6,14},{7,15},{8,0},{9,1},... | collective-permute-start | bytes 1572872 | tf_op jit(solution)/shard_map/ppermute | solution.py:38
  125.7 17.5 %collective-permute-start.11 = (f32[1,2,256,256]{3,2,1,0:T(8,128)S(1)}, f32[1,2,256,256]{3,2,1,0:T(8,128)S(1)}, u32[]{:S(2)}, u32[]{:S(2)}) collective-permute-start(f32[1,2,256,256]{3,2,1,0:T(8,128)S(1)} %get-tuple-element.40), channel_id=1, source_target_pairs={{0,12},{1,13},{2,14},{3,15},{4,8},{5,9},{6,10},{7,11},{8,4},{9,5},... | collective-permute-start | bytes 1572872 | tf_op jit(solution)/shard_map/ppermute | solution.py:38
  143.2 6.8 %shard_map.90.refs_5_ = f32[8,2,256,256]{3,2,1,0:T(8,128)} custom-call(f32[8]{0:T(128)S(1)} %copy-done.7, f32[256,256]{1,0:T(8,128)S(1)} %copy-done.2, f32[8,2,256,256]{3,2,1,0:T(8,128)S(1)} %get-tuple-element.37.source.density_ref, f32[8,2,256,256]{3,2,1,0:T(8,128)S(1)} %copy-done), custom_call_target="tpu_custom_call" | custom-call | flops 3221225472 | bytes 12582912 | tf_op jit(solution)/shard_map/pallas_call | solution.py:223
  149.9 4.2 %shard_map.91.refs_1_ = f32[8,2,256,256]{3,2,1,0:T(8,128)} custom-call(f32[12,6]{1,0:T(8,128)S(1)} %get-tuple-element.26.real, f32[4,256,256]{2,1,0:T(8,128)S(1)} %copy-done.1, f32[1,2,256,256]{3,2,1,0:T(8,128)S(1)} %collective-permute-done.13.refs_0_, f32[1,2,256,256]{3,2,1,0:T(8,128)S(1)} %collective-permute-done.14.refs_1_, ...), custom_call_target="tpu_custom_call", output_to_operand_aliasing={{}: (7, {})} | custom-call | tf_op jit(solution)/shard_map/pallas_call | solution.py:321
  154.1 4.7 %collective-permute-done.12.refs_0_ = f32[1,2,256,256]{3,2,1,0:T(8,128)S(1)} collective-permute-done((f32[1,2,256,256]{3,2,1,0:T(8,128)S(1)}, f32[1,2,256,256]{3,2,1,0:T(8,128)S(1)}, u32[]{:S(2)}, u32[]{:S(2)}) %collective-permute-start.12) | collective-permute-done | bytes 524320 | tf_op jit(solution)/shard_map/ppermute | solution.py:38
  158.8 2.7 %shard_map.92.refs_3_ = f32[8,2,256,256]{3,2,1,0:T(8,128)} custom-call(f32[12,6]{1,0:T(8,128)S(1)} %get-tuple-element.26.real, f32[4,256,256]{2,1,0:T(8,128)S(1)} %copy-done.1, f32[1,2,256,256]{3,2,1,0:T(8,128)S(1)} %collective-permute-done.12.refs_0_, f32[8,2,256,256]{3,2,1,0:T(8,128)} %shard_map.91.refs_1_), custom_call_target="tpu_custom_call", output_to_operand_aliasing={{}: (3, {})} | custom-call | tf_op jit(solution)/shard_map/pallas_call | solution.py:321
  161.6 10.6 %collective-permute-done.11.refs_2_ = f32[1,2,256,256]{3,2,1,0:T(8,128)S(1)} collective-permute-done((f32[1,2,256,256]{3,2,1,0:T(8,128)S(1)}, f32[1,2,256,256]{3,2,1,0:T(8,128)S(1)}, u32[]{:S(2)}, u32[]{:S(2)}) %collective-permute-start.11) | collective-permute-done | bytes 524320 | tf_op jit(solution)/shard_map/ppermute | solution.py:38
  172.2 5.2 %shard_map.93 = f32[8,2,256,256]{3,2,1,0:T(8,128)} custom-call(f32[12,6]{1,0:T(8,128)S(1)} %get-tuple-element.26.real, f32[4,256,256]{2,1,0:T(8,128)S(1)} %copy-done.1, f32[2,2,256,256]{3,2,1,0:T(8,128)S(1)} %collective-permute-done.9.refs_0_, f32[2,2,256,256]{3,2,1,0:T(8,128)S(1)} %collective-permute-done.10.refs_1_, ...), custom_call_target="tpu_custom_call", output_to_operand_aliasing={{}: (5, {})} | custom-call | tf_op jit(solution)/shard_map/pallas_call | solution.py:321
  (42 shorter events, 18.1 us)
Async XLA Ops:
  0.0 4.6 %copy-start = (f32[8,2,256,256]{3,2,1,0:T(8,128)S(1)}, f32[8,2,256,256]{3,2,1,0:T(8,128)}, u32[]{:S(2)}) copy-start(f32[8,2,256,256]{3,2,1,0:T(8,128)} %refs_0_.1) | copy-start | bytes 12582916
  0.0 42.7 %copy-start.5 = (f32[4,2]{0,1:T(2,128)S(1)}, f32[4,2]{0,1:T(2,128)}, u32[]{:S(2)}) copy-start(f32[4,2]{0,1:T(2,128)} %param.11) | copy-start | bytes 100
  0.0 42.7 %copy-start.6 = (s32[16]{0:T(128)S(1)}, s32[16]{0:T(128)}, u32[]{:S(2)}) copy-start(s32[16]{0:T(128)} %count_ref.1) | copy-start | bytes 196
  0.0 45.2 %copy-start.2 = (f32[256,256]{1,0:T(8,128)S(1)}, f32[256,256]{1,0:T(8,128)}, u32[]{:S(2)}) copy-start(f32[256,256]{1,0:T(8,128)} %hamiltonian_ref.3) | copy-start | bytes 786436
  0.0 45.2 %copy-start.7 = (f32[8]{0:T(128)S(1)}, f32[8]{0:T(128)}, u32[]{:S(2)}) copy-start(f32[8]{0:T(128)} %damping_ref.3) | copy-start | bytes 100
  2.6 13.6 %collective-permute-start.4 = (f32[1,2,256,256]{3,2,1,0:T(8,128)S(1)}, f32[1,2,256,256]{3,2,1,0:T(8,128)S(1)}, u32[]{:S(2)}, u32[]{:S(2)}) collective-permute-start(f32[1,2,256,256]{3,2,1,0:T(8,128)S(1)} %get-tuple-element.32), channel_id=1, source_target_pairs={{0,3},{1,4},{2,5},{3,6},{4,7},{5,8},{6,9},{7,10},{8,11},{9,12},{10... | collective-permute-start | bytes 1572872 | tf_op jit(solution)/shard_map/ppermute | solution.py:38
  4.6 24.9 %collective-permute-start.5 = (f32[1,2,256,256]{3,2,1,0:T(8,128)S(1)}, f32[1,2,256,256]{3,2,1,0:T(8,128)S(1)}, u32[]{:S(2)}, u32[]{:S(2)}) collective-permute-start(f32[1,2,256,256]{3,2,1,0:T(8,128)S(1)} %get-tuple-element.33), channel_id=1, source_target_pairs={{0,13},{1,14},{2,15},{3,0},{4,1},{5,2},{6,3},{7,4},{8,5},{9,6},{10... | collective-permute-start | bytes 1572872 | tf_op jit(solution)/shard_map/ppermute | solution.py:38
  6.6 27.7 %collective-permute-start.6 = (f32[1,2,256,256]{3,2,1,0:T(8,128)S(1)}, f32[1,2,256,256]{3,2,1,0:T(8,128)S(1)}, u32[]{:S(2)}, u32[]{:S(2)}) collective-permute-start(f32[1,2,256,256]{3,2,1,0:T(8,128)S(1)} %get-tuple-element.34), channel_id=1, source_target_pairs={{0,14},{1,15},{2,4},{3,5},{4,2},{5,3},{6,8},{7,9},{8,6},{9,7},{10,... | collective-permute-start | bytes 1572872 | tf_op jit(solution)/shard_map/ppermute | solution.py:38
  8.7 31.6 %collective-permute-start.7 = (f32[1,2,256,256]{3,2,1,0:T(8,128)S(1)}, f32[1,2,256,256]{3,2,1,0:T(8,128)S(1)}, u32[]{:S(2)}, u32[]{:S(2)}) collective-permute-start(f32[1,2,256,256]{3,2,1,0:T(8,128)S(1)} %get-tuple-element.35), channel_id=1, source_target_pairs={{0,15},{1,2},{2,1},{3,4},{4,3},{5,6},{6,5},{7,8},{8,7},{9,10},{10,... | collective-permute-start | bytes 1572872 | tf_op jit(solution)/shard_map/ppermute | solution.py:38
  9.7 40.9 %collective-permute-start.8 = (f32[2,2,256,256]{3,2,1,0:T(8,128)S(1)}, f32[2,2,256,256]{3,2,1,0:T(8,128)S(1)}, u32[]{:S(2)}, u32[]{:S(2)}) collective-permute-start(f32[2,2,256,256]{3,2,1,0:T(8,128)S(1)} %get-tuple-element.36), channel_id=1, source_target_pairs={{0,1},{1,0},{2,3},{3,2},{4,5},{5,4},{6,7},{7,6},{8,9},{9,8},{10,11... | collective-permute-start | bytes 3145736 | tf_op jit(solution)/shard_map/ppermute | solution.py:38
  16.3 45.9 %collective-permute-start.2 = (f32[2,2,256,256]{3,2,1,0:T(8,128)S(1)}, f32[2,2,256,256]{3,2,1,0:T(8,128)S(1)}, u32[]{:S(2)}, u32[]{:S(2)}) collective-permute-start(f32[2,2,256,256]{3,2,1,0:T(8,128)S(1)} %get-tuple-element.30), channel_id=1, source_target_pairs={{0,2},{1,3},{2,0},{3,1},{4,6},{5,7},{6,4},{7,5},{8,10},{9,11},{10,... | collective-permute-start | bytes 3145736 | tf_op jit(solution)/shard_map/ppermute | solution.py:38
  29.4 45.4 %collective-permute-start.3 = (f32[2,2,256,256]{3,2,1,0:T(8,128)S(1)}, f32[2,2,256,256]{3,2,1,0:T(8,128)S(1)}, u32[]{:S(2)}, u32[]{:S(2)}) collective-permute-start(f32[2,2,256,256]{3,2,1,0:T(8,128)S(1)} %get-tuple-element.31), channel_id=1, source_target_pairs={{0,4},{1,5},{2,6},{3,7},{4,0},{5,1},{6,2},{7,3},{8,12},{9,13},{10,... | collective-permute-start | bytes 3145736 | tf_op jit(solution)/shard_map/ppermute | solution.py:38
  34.3 43.7 %collective-permute-start = (f32[1,2,256,256]{3,2,1,0:T(8,128)S(1)}, f32[1,2,256,256]{3,2,1,0:T(8,128)S(1)}, u32[]{:S(2)}, u32[]{:S(2)}) collective-permute-start(f32[1,2,256,256]{3,2,1,0:T(8,128)S(1)} %get-tuple-element.28), channel_id=1, source_target_pairs={{0,8},{1,9},{2,10},{3,11},{4,12},{5,13},{6,14},{7,15},{8,0},{9,1},... | collective-permute-start | bytes 1572872 | tf_op jit(solution)/shard_map/ppermute | solution.py:38
  40.3 37.7 %collective-permute-start.1 = (f32[1,2,256,256]{3,2,1,0:T(8,128)S(1)}, f32[1,2,256,256]{3,2,1,0:T(8,128)S(1)}, u32[]{:S(2)}, u32[]{:S(2)}) collective-permute-start(f32[1,2,256,256]{3,2,1,0:T(8,128)S(1)} %get-tuple-element.29), channel_id=1, source_target_pairs={{0,12},{1,13},{2,14},{3,15},{4,8},{5,9},{6,10},{7,11},{8,4},{9,5},... | collective-permute-start | bytes 1572872 | tf_op jit(solution)/shard_map/ppermute | solution.py:38
  45.2 5.4 %copy-start.1 = (f32[4,256,256]{2,1,0:T(8,128)S(1)}, f32[4,256,256]{2,1,0:T(8,128)}, u32[]{:S(2)}) copy-start(f32[4,256,256]{2,1,0:T(8,128)} %couplings_ref.11) | copy-start | bytes 3145732
  80.7 22.2 %collective-permute-start.13 = (f32[1,2,256,256]{3,2,1,0:T(8,128)S(1)}, f32[1,2,256,256]{3,2,1,0:T(8,128)S(1)}, u32[]{:S(2)}, u32[]{:S(2)}) collective-permute-start(f32[1,2,256,256]{3,2,1,0:T(8,128)S(1)} %get-tuple-element.42), channel_id=1, source_target_pairs={{0,3},{1,4},{2,5},{3,6},{4,7},{5,8},{6,9},{7,10},{8,11},{9,12},{10... | collective-permute-start | bytes 1572872 | tf_op jit(solution)/shard_map/ppermute | solution.py:38
  90.2 25.6 %collective-permute-start.14 = (f32[1,2,256,256]{3,2,1,0:T(8,128)S(1)}, f32[1,2,256,256]{3,2,1,0:T(8,128)S(1)}, u32[]{:S(2)}, u32[]{:S(2)}) collective-permute-start(f32[1,2,256,256]{3,2,1,0:T(8,128)S(1)} %get-tuple-element.43), channel_id=1, source_target_pairs={{0,13},{1,14},{2,15},{3,0},{4,1},{5,2},{6,3},{7,4},{8,5},{9,6},{10... | collective-permute-start | bytes 1572872 | tf_op jit(solution)/shard_map/ppermute | solution.py:38
  91.8 26.6 %collective-permute-start.15 = (f32[1,2,256,256]{3,2,1,0:T(8,128)S(1)}, f32[1,2,256,256]{3,2,1,0:T(8,128)S(1)}, u32[]{:S(2)}, u32[]{:S(2)}) collective-permute-start(f32[1,2,256,256]{3,2,1,0:T(8,128)S(1)} %get-tuple-element.44), channel_id=1, source_target_pairs={{0,14},{1,15},{2,4},{3,5},{4,2},{5,3},{6,8},{7,9},{8,6},{9,7},{10,... | collective-permute-start | bytes 1572872 | tf_op jit(solution)/shard_map/ppermute | solution.py:38
  91.9 33.8 %collective-permute-start.16 = (f32[1,2,256,256]{3,2,1,0:T(8,128)S(1)}, f32[1,2,256,256]{3,2,1,0:T(8,128)S(1)}, u32[]{:S(2)}, u32[]{:S(2)}) collective-permute-start(f32[1,2,256,256]{3,2,1,0:T(8,128)S(1)} %get-tuple-element.45), channel_id=1, source_target_pairs={{0,15},{1,2},{2,1},{3,4},{4,3},{5,6},{6,5},{7,8},{8,7},{9,10},{10,... | collective-permute-start | bytes 1572872 | tf_op jit(solution)/shard_map/ppermute | solution.py:38
  93.4 56.5 %collective-permute-start.17 = (f32[2,2,256,256]{3,2,1,0:T(8,128)S(1)}, f32[2,2,256,256]{3,2,1,0:T(8,128)S(1)}, u32[]{:S(2)}, u32[]{:S(2)}) collective-permute-start(f32[2,2,256,256]{3,2,1,0:T(8,128)S(1)} %get-tuple-element.46), channel_id=1, source_target_pairs={{0,1},{1,0},{2,3},{3,2},{4,5},{5,4},{6,7},{7,6},{8,9},{9,8},{10,11... | collective-permute-start | bytes 3145736 | tf_op jit(solution)/shard_map/ppermute | solution.py:38
  102.9 69.3 %collective-permute-start.9 = (f32[2,2,256,256]{3,2,1,0:T(8,128)S(1)}, f32[2,2,256,256]{3,2,1,0:T(8,128)S(1)}, u32[]{:S(2)}, u32[]{:S(2)}) collective-permute-start(f32[2,2,256,256]{3,2,1,0:T(8,128)S(1)} %get-tuple-element.38), channel_id=1, source_target_pairs={{0,2},{1,3},{2,0},{3,1},{4,6},{5,7},{6,4},{7,5},{8,10},{9,11},{10,... | collective-permute-start | bytes 3145736 | tf_op jit(solution)/shard_map/ppermute | solution.py:38
  115.7 56.5 %collective-permute-start.10 = (f32[2,2,256,256]{3,2,1,0:T(8,128)S(1)}, f32[2,2,256,256]{3,2,1,0:T(8,128)S(1)}, u32[]{:S(2)}, u32[]{:S(2)}) collective-permute-start(f32[2,2,256,256]{3,2,1,0:T(8,128)S(1)} %get-tuple-element.39), channel_id=1, source_target_pairs={{0,4},{1,5},{2,6},{3,7},{4,0},{5,1},{6,2},{7,3},{8,12},{9,13},{10,... | collective-permute-start | bytes 3145736 | tf_op jit(solution)/shard_map/ppermute | solution.py:38
  118.4 40.4 %collective-permute-start.12 = (f32[1,2,256,256]{3,2,1,0:T(8,128)S(1)}, f32[1,2,256,256]{3,2,1,0:T(8,128)S(1)}, u32[]{:S(2)}, u32[]{:S(2)}) collective-permute-start(f32[1,2,256,256]{3,2,1,0:T(8,128)S(1)} %get-tuple-element.41), channel_id=1, source_target_pairs={{0,8},{1,9},{2,10},{3,11},{4,12},{5,13},{6,14},{7,15},{8,0},{9,1},... | collective-permute-start | bytes 1572872 | tf_op jit(solution)/shard_map/ppermute | solution.py:38
  125.7 46.5 %collective-permute-start.11 = (f32[1,2,256,256]{3,2,1,0:T(8,128)S(1)}, f32[1,2,256,256]{3,2,1,0:T(8,128)S(1)}, u32[]{:S(2)}, u32[]{:S(2)}) collective-permute-start(f32[1,2,256,256]{3,2,1,0:T(8,128)S(1)} %get-tuple-element.40), channel_id=1, source_target_pairs={{0,12},{1,13},{2,14},{3,15},{4,8},{5,9},{6,10},{7,11},{8,4},{9,5},... | collective-permute-start | bytes 1572872 | tf_op jit(solution)/shard_map/ppermute | solution.py:38
  (2 other events, 9.1 us)
